TPU v7x, 128 devices: a whole 4x4x4 slice. The times are simulated.
128 devices in a mesh: tm: 16 (over z, y), head: 8 (over x, core).
Axes of the slice: x: 4, y: 4, z: 4, core: 2. Of those that a mesh axis runs over, the one named last changes fastest.
Arguments:
- query: bfloat16 [4096, 3072], P(('tm', 'head')), may hold values from -100 to 100
- key_cur: bfloat16 [4096, 3072], P(('tm', 'head')), may hold values from -6 to 6
- value_cur: bfloat16 [4096, 3072], P(('tm', 'head')), may hold values from -6 to 6
- d_out: bfloat16 [4096, 3072], P(('tm', 'head')), may hold values from -6 to 6
- key_hist: bfloat16 [4096, 3072], P('tm', 'head'), may hold values from -10 to 10
- value_hist: bfloat16 [4096, 3072], P('tm', 'head'), may hold values from -6 to 6
- hist_len: int32 [16], P('tm'), may hold values from 1 to 256, 2048 in all
Outputs:
- grad_query: bfloat16 [4096, 3072], P(('tm', 'head'))
- grad_key_cur: bfloat16 [4096, 3072], P(('tm', 'head'))
- grad_value_cur: bfloat16 [4096, 3072], P(('tm', 'head'))
- grad_key_hist: bfloat16 [4096, 3072], P('tm', 'head')
- grad_value_hist: bfloat16 [4096, 3072], P('tm', 'head')
Inputs may be any that keep to these rules, and one draw needn't show every extreme that they name: `hist_len`: every time shard has at least one filled slot; filled slots come first.
All inputs are finite; a program needn't handle non-finite values.
Results may differ from a plain program's by a relative error of at most 0.019.
Values may be sent and summed in bfloat16 or wider, within the bound.
No kernel may reach another device: no remote copies, remote signals or barrier semaphores. Data moves between devices by JAX's collectives and lax.ppermute only.
A program may use at most 128 MiB of HBM per device.

v0:
```python
import math

import jax
import jax.numpy as jnp
from jax import lax
from jax.sharding import PartitionSpec as P

HS = 128


def block_stats(queries, grads, key_block, value_block, live_mask, score_scale):
    scores = (
        jnp.einsum("qhd,khd->hqk", queries, key_block, preferred_element_type=jnp.float32)
        * score_scale
    )
    row_max = jnp.max(jnp.where(live_mask, scores, -jnp.inf), axis=2)
    weights = jnp.where(live_mask, jnp.exp(scores - row_max[:, :, None]), 0.0)
    grad_scores = jnp.einsum("qhd,khd->hqk", grads, value_block, preferred_element_type=jnp.float32)
    return (row_max, jnp.sum(weights, axis=2), jnp.sum(weights * grad_scores, axis=2))


def prob_terms(
    queries, grads, key_block, value_block, live_mask, row_max, row_total, row_delta, score_scale
):
    scores = (
        jnp.einsum("qhd,khd->hqk", queries, key_block, preferred_element_type=jnp.float32)
        * score_scale
    )
    grad_scores = jnp.einsum("qhd,khd->hqk", grads, value_block, preferred_element_type=jnp.float32)
    full_prob = jnp.where(
        live_mask, jnp.exp(scores - row_max[:, :, None]) / row_total[:, :, None], 0.0
    )
    score_grad = (score_scale * full_prob * (grad_scores - row_delta[:, :, None])).astype(
        jnp.bfloat16
    )
    return (full_prob.astype(jnp.bfloat16), score_grad)


def shards(query, key_cur, value_cur, d_out, key_hist, value_hist, hist_len):
    local_query, local_key, local_value, local_grad = (
        lax.all_to_all(query, "head", split_axis=1, concat_axis=0, tiled=True),
        lax.all_to_all(key_cur, "head", split_axis=1, concat_axis=0, tiled=True),
        lax.all_to_all(value_cur, "head", split_axis=1, concat_axis=0, tiled=True),
        lax.all_to_all(d_out, "head", split_axis=1, concat_axis=0, tiled=True),
    )
    row_count = local_query.shape[0]
    feat_width = local_query.shape[1]
    head_count = feat_width // HS
    score_scale = 1.0 / math.sqrt(HS)
    own_keys = jnp.concatenate([local_key, key_hist], axis=0).reshape(-1, head_count, HS)
    own_values = jnp.concatenate([local_value, value_hist], axis=0).reshape(-1, head_count, HS)
    key_count = own_keys.shape[0]
    slot_index = jnp.arange(key_count)
    query_heads = local_query.reshape(row_count, head_count, HS)
    grad_heads = local_grad.reshape(row_count, head_count, HS)

    def live_of(filled):
        return (slot_index < row_count) | (slot_index - row_count < filled)

    gathered_keys, gathered_values, hist_counts = (
        lax.all_gather(own_keys, "tm", axis=0, tiled=True),
        lax.all_gather(own_values, "tm", axis=0, tiled=True),
        lax.all_gather(hist_len, "tm", axis=0, tiled=True),
    )
    block_count = hist_counts.shape[0]

    def key_slice(block_id):
        start_row = block_id * key_count
        return (
            lax.dynamic_slice_in_dim(gathered_keys, start_row, key_count, 0),
            lax.dynamic_slice_in_dim(gathered_values, start_row, key_count, 0),
            live_of(hist_counts[block_id]),
        )

    def stat_block(block_id):
        key_block, value_block, live_mask = key_slice(block_id)
        return block_stats(query_heads, grad_heads, key_block, value_block, live_mask, score_scale)

    block_max, block_total, block_dots = lax.map(stat_block, jnp.arange(block_count))
    row_max = jnp.max(block_max, axis=0)
    rescale = jnp.exp(block_max - row_max[None])
    row_total = jnp.sum(block_total * rescale, axis=0)
    row_delta = jnp.sum(block_dots * rescale, axis=0) / row_total

    def add_query(accum, block_id):
        key_block, value_block, live_mask = key_slice(block_id)
        prob_low, score_grad = prob_terms(
            query_heads,
            grad_heads,
            key_block,
            value_block,
            live_mask,
            row_max,
            row_total,
            row_delta,
            score_scale,
        )
        return (
            accum
            + jnp.einsum("hqk,khd->qhd", score_grad, key_block, preferred_element_type=jnp.float32),
            None,
        )

    summed_query, _ = lax.scan(
        add_query, jnp.zeros((row_count, head_count, HS), jnp.float32), jnp.arange(block_count)
    )
    grad_query = summed_query.reshape(row_count, feat_width)

    def block_terms(inner_id):
        key_block, value_block, live_mask = key_slice(inner_id)
        prob_low, score_grad = prob_terms(
            query_heads,
            grad_heads,
            key_block,
            value_block,
            live_mask,
            row_max,
            row_total,
            row_delta,
            score_scale,
        )
        grad_k = jnp.einsum(
            "hqk,qhd->khd", score_grad, query_heads, preferred_element_type=jnp.float32
        )
        grad_v = jnp.einsum(
            "hqk,qhd->khd", prob_low, grad_heads, preferred_element_type=jnp.float32
        )
        return jnp.concatenate(
            [grad_k.reshape(key_count, feat_width), grad_v.reshape(key_count, feat_width)], axis=1
        )

    summed_keys = lax.psum_scatter(
        lax.map(block_terms, jnp.arange(key_count * lax.axis_size("tm") // key_count))
        .reshape(key_count * lax.axis_size("tm"), 2 * feat_width)
        .astype(jnp.bfloat16),
        "tm",
        scatter_dimension=0,
        tiled=True,
    ).astype(jnp.float32)
    grad_keys = summed_keys[:, :feat_width]
    grad_values = summed_keys[:, feat_width:]
    query_low = grad_query.astype(jnp.bfloat16)
    keys_low = grad_keys.astype(jnp.bfloat16)
    values_low = grad_values.astype(jnp.bfloat16)
    back_query, back_key, back_value = (
        lax.all_to_all(query_low, "head", split_axis=0, concat_axis=1, tiled=True),
        lax.all_to_all(keys_low[:row_count], "head", split_axis=0, concat_axis=1, tiled=True),
        lax.all_to_all(values_low[:row_count], "head", split_axis=0, concat_axis=1, tiled=True),
    )
    return (back_query, back_key, back_value, keys_low[row_count:], values_low[row_count:])


def solution(mesh):
    in_specs = (
        P(("tm", "head"), None),
        P(("tm", "head"), None),
        P(("tm", "head"), None),
        P(("tm", "head"), None),
        P("tm", "head"),
        P("tm", "head"),
        P("tm"),
    )
    out_specs = (
        P(("tm", "head"), None),
        P(("tm", "head"), None),
        P(("tm", "head"), None),
        P("tm", "head"),
        P("tm", "head"),
    )
    return jax.shard_map(shards, mesh=mesh, in_specs=in_specs, out_specs=out_specs, check_vma=False)
```

profile of v0, /device:TPU:1, one launch (start us, length us, event | category | flops | bytes accessed | tf_op | source)
XLA Modules:
  0.0 593.6 jit_solution(16398517295192034907)
XLA Ops:
  8.8 5.8 all-to-all-start
  15.9 4.6 all-to-all-done
  22.4 4.2 all-to-all-start.2
  27.0 5.6 all-to-all-done.2
  34.6 4.2 all-to-all-start.1
  39.5 5.2 all-to-all-done.1
  44.8 4.2 all-to-all-start.3
  51.0 14.9 %all-reduce = s32[16]{0:T(128)S(1)} all-reduce(s32[16]{0:T(128)S(1)} %dynamic-update-slice), channel_id=1, replica_groups=mesh['tm'=16,'head'=8] {'tm'}, use_global_device_ids=true, to_apply=%add | all-reduce | flops 16 | bytes 128
  66.5 17.7 %all-gather.3.cloned.1.call-done = bf16[8192,3,128]{2,0,1:T(8,128)(2,1)} async-done(((bf16[512,3,128]{2,0,1:T(8,128)(2,1)}), bf16[8192,3,128]{2,0,1:T(8,128)(2,1)}) %all-gather.3.cloned.1.call-update) | async-done | bytes 6291472 | tf_op jit(solution)/shard_map/all_gather | solution.py:61
  84.2 63.3 %all-gather.5.cloned.1.call-done = bf16[8192,3,128]{2,0,1:T(8,128)(2,1)} async-done(((bf16[512,3,128]{2,0,1:T(8,128)(2,1)}), bf16[8192,3,128]{2,0,1:T(8,128)(2,1)}) %all-gather.5.cloned.1.call-update) | async-done | bytes 6291472 | tf_op jit(solution)/shard_map/all_gather | solution.py:62
  147.4 122.7 %while.46 = (s32[]{:T(128)}, f32[16,3,256]{2,1,0:T(4,128)S(1)}, f32[16,3,256]{2,1,0:T(4,128)S(1)}, f32[16,3,256]{2,1,0:T(4,128)S(1)}, s32[16]{0:T(128)S(1)}, /*i...) while((s32[]{:T(128)}, f32[16,3,256]{2,1,0:T(4,128)S(1)}, ...), condition=%wide.region_4.5_spmd.clone.clone, body=%wide.region_0.4_spmd.clone.clone.sunk | while | flops 205258496 | bytes 5940497 | solution.py:79
  270.3 141.9 %while.47 = (s32[]{:T(128)}, bf16[16,512,768]{1,2,0:T(8,128)(2,1)}, s32[16]{0:T(128)S(1)}, s32[16]{0:T(128)S(1)}, bf16[8192,3,128]{2,0,1:T(8,128)(2,1)}, /*index...) while((s32[]{:T(128)}, bf16[16,512,768]{1,2,0:T(8,128)(2,1)}, ...), condition=%wide.region_11.12_spmd.clone.clone, body=%wide.region_10.11_spmd.clone.clone.sunk | while | flops 407767040 | bytes 8661269 | solution.py:133
  412.2 16.6 %copy.97 = bf16[16,512,768]{2,1,0:T(8,128)(2,1)} copy(bf16[16,512,768]{1,2,0:T(8,128)(2,1)} %get-tuple-element.455) | data formatting | bytes 25165824 | tf_op jit(solution)/shard_map/convert_element_type | solution.py:135
  428.8 126.3 %while.48 = (s32[]{:T(128)}, f32[256,3,128]{0,2,1:T(8,128)S(1)}, s32[16]{0:T(128)S(1)}, bf16[8192,3,128]{2,0,1:T(8,128)(2,1)}, s32[16]{0:T(128)S(1)}, /*index=5*...) while((s32[]{:T(128)}, f32[256,3,128]{0,2,1:T(8,128)S(1)}, ...), condition=%wide.region_9.10_spmd.clone.clone, body=%wide.region_8.9_spmd.clone.clone.sunk | while | flops 305334272 | bytes 5517078 | solution.py:104
  434.7 2.0 fusion.105
  442.5 2.0 fusion.105
  450.4 2.1 fusion.105
  458.3 2.1 fusion.105
  466.3 2.1 fusion.105
  474.2 2.1 fusion.105
  482.1 2.1 fusion.105
  490.0 2.1 fusion.105
  497.9 2.0 fusion.105
  513.8 2.1 fusion.105
  521.7 2.1 fusion.105
  529.5 2.0 fusion.105
  556.2 4.9 all-to-all-start.4
  561.2 2.0 fusion.49
  563.2 3.8 all-to-all-done.4
  567.0 9.2 %all_to_all.118 = bf16[8,32,384]{2,1,0:T(8,128)(2,1)S(1)} all-to-all(bf16[8,32,384]{2,1,0:T(8,128)(2,1)S(1)} %bitcast.129), channel_id=1, replica_groups=mesh['tm'=16,'head'=8] {'head'}, dimensions={0} | all-to-all | bytes 393216 | tf_op jit(solution)/shard_map/all_to_all | solution.py:148
  576.3 4.2 all-to-all-start.5
  581.9 4.5 all-to-all-done.5
  (366 shorter events, 252.8 us)
Async XLA Ops:
  8.8 11.7 %all-to-all-start = ((bf16[32,8,384]{2,0,1:T(8,128)(2,1)}), bf16[32,8,384]{2,0,1:T(8,128)(2,1)S(1)}, u32[]{:S(2)}, u32[]{:S(2)}) async-start(bf16[32,8,384]{2,0,1:T(8,128)(2,1)} %bitcast.75), calls=%async_computation | async-start | bytes 393216 | tf_op jit(solution)/shard_map/all_to_all | solution.py:42
  14.6 69.6 %all-gather.3.cloned.1.call-start = ((), (), s32[]{:S(2)}) async-start(), calls=%async_computation.8 | async-start | bytes 6684672 | tf_op jit(solution)/shard_map/all_gather | solution.py:61
  15.7 6.1 %copy-start = (bf16[32,3072]{1,0:T(8,128)(2,1)S(1)}, bf16[32,3072]{1,0:T(8,128)(2,1)}, u32[]{:S(2)}) copy-start(bf16[32,3072]{1,0:T(8,128)(2,1)} %param.15) | copy-start | bytes 589828
  20.5 6.1 %copy-start.1 = (bf16[256,384]{1,0:T(8,128)(2,1)S(1)}, bf16[256,384]{1,0:T(8,128)(2,1)}, u32[]{:S(2)}) copy-start(bf16[256,384]{1,0:T(8,128)(2,1)} %param.18) | copy-start | bytes 589828
  22.4 10.2 %all-to-all-start.2 = ((bf16[32,8,384]{2,0,1:T(8,128)(2,1)}), bf16[32,8,384]{2,0,1:T(8,128)(2,1)S(1)}, u32[]{:S(2)}, u32[]{:S(2)}) async-start(bf16[32,8,384]{2,0,1:T(8,128)(2,1)} %bitcast.73), calls=%async_computation.2 | async-start | bytes 393216 | tf_op jit(solution)/shard_map/all_to_all | solution.py:43
  26.7 120.8 %all-gather.5.cloned.1.call-start = ((), (), s32[]{:S(2)}) async-start(), calls=%async_computation.9 | async-start | bytes 6684672 | tf_op jit(solution)/shard_map/all_gather | solution.py:62
  26.8 7.0 %copy-start.2 = (bf16[32,3072]{1,0:T(8,128)(2,1)S(1)}, bf16[32,3072]{1,0:T(8,128)(2,1)}, u32[]{:S(2)}) copy-start(bf16[32,3072]{1,0:T(8,128)(2,1)} %param.13) | copy-start | bytes 589828
  32.6 6.2 %copy-start.3 = (bf16[32,3072]{1,0:T(8,128)(2,1)S(1)}, bf16[32,3072]{1,0:T(8,128)(2,1)}, u32[]{:S(2)}) copy-start(bf16[32,3072]{1,0:T(8,128)(2,1)} %param.16) | copy-start | bytes 589828
  33.0 16.6 %copy-start.4 = (u32[128]{0:T(128)S(1)}, u32[128]{0:T(128)}, u32[]{:S(2)}) copy-start(u32[128]{0:T(128)} %constant.171) | copy-start | bytes 1540
  34.6 10.2 %all-to-all-start.1 = ((bf16[32,8,384]{2,0,1:T(8,128)(2,1)}), bf16[32,8,384]{2,0,1:T(8,128)(2,1)S(1)}, u32[]{:S(2)}, u32[]{:S(2)}) async-start(bf16[32,8,384]{2,0,1:T(8,128)(2,1)} %bitcast.74), calls=%async_computation.1 | async-start | bytes 393216 | tf_op jit(solution)/shard_map/all_to_all | solution.py:41
  44.8 21.4 %all-to-all-start.3 = ((bf16[32,8,384]{2,0,1:T(8,128)(2,1)}), bf16[32,8,384]{2,0,1:T(8,128)(2,1)S(1)}, u32[]{:S(2)}, u32[]{:S(2)}) async-start(bf16[32,8,384]{2,0,1:T(8,128)(2,1)} %bitcast.72), calls=%async_computation.3 | async-start | bytes 393216 | tf_op jit(solution)/shard_map/all_to_all | solution.py:44
  49.0 512.2 %reduce-scatter.2.cloned.1.call-start = ((), (), s32[]{:S(2)}) async-start(), calls=%async_computation.10 | async-start | bytes 13369344 | tf_op jit(solution)/shard_map/reduce_scatter | solution.py:132
  556.2 10.8 %all-to-all-start.4 = ((bf16[8,32,384]{2,1,0:T(8,128)(2,1)}), bf16[8,32,384]{2,1,0:T(8,128)(2,1)S(1)}, u32[]{:S(2)}, u32[]{:S(2)}) async-start(bf16[8,32,384]{2,1,0:T(8,128)(2,1)} %convert_element_type.35), calls=%async_computation.4 | async-start | bytes 393216 | tf_op jit(solution)/shard_map/all_to_all | solution.py:146
  576.3 10.2 %all-to-all-start.5 = ((bf16[8,32,384]{2,1,0:T(8,128)(2,1)}), bf16[8,32,384]{2,1,0:T(8,128)(2,1)S(1)}, u32[]{:S(2)}, u32[]{:S(2)}) async-start(bf16[8,32,384]{2,1,0:T(8,128)(2,1)} %bitcast.9), calls=%async_computation.6 | async-start | bytes 393216 | tf_op jit(solution)/shard_map/all_to_all | solution.py:147
Sparse Core Ops, SparseCore 0:
  21.8 62.2 all-gather.2
  86.3 61.0 all-gather.4
  428.9 94.1 reduce-scatter.1
where the time goes:
time: 601 us; the launch traced here: 594 us
  matrix products  157 us (26%)
  loops' own time  126 us (21%)
  waiting for transfers between devices  105 us (17%)
  local copies, waits for them, and re-layouts  87.4 us (15%)
  other arithmetic  52.2 us (9%)
  starting transfers between devices  27.7 us (5%)
  blocking collectives  24.1 us (4%)
  between operations  14.6 us (2%)
    all_gather x1, waiting for transfers between devices, shards(): lax.all_gather(own_values, 'tm', axis=0, tiled=True)  63.3 us
    dot_general x32, matrix products, prob_terms(): jnp.einsum('qhd,khd->hqk', queries, key_block, preferred_element_type=jnp...  46 us
    another operation x1, loops' own time, shards(): lax.scan(add_query, jnp.zeros((row_count, head_count, HS), jnp.float32),...  42.1 us
    another operation x1, loops' own time, shards(): lax.map(stat_block, jnp.arange(block_count))  42.1 us
    another operation x1, loops' own time, shards(): lax.map(block_terms, jnp.arange(key_count * lax.axis_size('tm') // key_co...  42 us
    dot_general x16, matrix products, add_query(): jnp.einsum('hqk,khd->qhd', score_grad, key_block, preferred_element_type=...  32.9 us
    or x48, other arithmetic, live_of(): return (slot_index < row_count) | (slot_index - row_count < filled)  31.2 us
    dynamic_slice x48, local copies, waits for them, and re-layouts, key_slice(): hist_counts[block_id]  28.2 us
  transfers between devices with their start and end apart: 9, of which 7 were waited for; matrix products, arithmetic and copies ran while one was open for 16% of the time, Pallas kernels for 0%

commit v1 on v0

v1 whole, which is shorter than its diff:
```python
import math

import jax
import jax.numpy as jnp
from jax import lax
from jax.experimental import pallas as pl
from jax.experimental.pallas import tpu as pltpu
from jax.sharding import Mesh
from jax.sharding import PartitionSpec as P

HS = 128
SCALE = 1.0 / math.sqrt(HS)
EXP2_SCALE = SCALE * math.log2(math.e)
LOW = -1e30
VMEM_LIMIT = 48 * 1024 * 1024
AXES = ("z", "y", "x", "c")
F32 = jnp.float32
BF16 = jnp.bfloat16


def rows_dot(a, b):
    return lax.dot_general(a, b, (((1,), (1,)), ((), ())), preferred_element_type=F32)


def plain_dot(a, b):
    return lax.dot_general(a, b, (((1,), (0,)), ((), ())), preferred_element_type=F32)


def left_dot(a, b):
    return lax.dot_general(a, b, (((0,), (0,)), ((), ())), preferred_element_type=F32)


def load_all(sources, targets, sem):
    copies = [
        pltpu.make_async_copy(s, t, sem.at[i]) for i, (s, t) in enumerate(zip(sources, targets))
    ]
    for copy in copies:
        copy.start()
    for copy in copies:
        copy.wait()


def live_mask(hist_buf, block, rows, width):
    count = hist_buf[block, 2 * rows : 2 * rows + 16, 0:width].astype(F32)[0:1]
    slot = lax.broadcasted_iota(jnp.int32, (rows, width), 0).astype(F32)
    return slot < count


def stat_step(keys, values, queries, grads, state, mask):
    top, total, dots = state
    scores = rows_dot(keys, queries)
    if mask is not None:
        scores = jnp.where(mask, scores, LOW)
    new_top = jnp.maximum(top, jnp.max(scores, axis=0, keepdims=True))
    shrink = jnp.exp2((top - new_top) * EXP2_SCALE)
    weights = jnp.exp2((scores - new_top) * EXP2_SCALE)
    grad_scores = rows_dot(values, grads)
    total = total * shrink + jnp.sum(weights, axis=0, keepdims=True)
    dots = dots * shrink + jnp.sum(weights * grad_scores, axis=0, keepdims=True)
    return new_top, total, dots


def stat_kernel(nk, nq, todo, *refs):
    cur_in, hist_in, query_in = refs[:nk], refs[nk : 2 * nk], refs[2 * nk : 2 * nk + nq]
    rest = refs[2 * nk + nq :]
    has_state = any(not fresh for fresh, _ in todo)
    if has_state:
        state_in, rest = rest[0], rest[1:]
    out_ref, cur, hist, query, sem = rest
    load_all(
        list(cur_in) + list(hist_in) + list(query_in),
        [cur.at[i] for i in range(nk)]
        + [hist.at[i] for i in range(nk)]
        + [query.at[i] for i in range(nq)],
        sem,
    )
    rows = cur.shape[2]
    width = query.shape[2]
    heads = cur.shape[3] // HS

    def one(head, block, fresh, key_blocks):
        lanes = pl.ds(pl.multiple_of(head * HS, HS), HS)
        queries, grads = query[block, 0, :, lanes], query[block, 1, :, lanes]
        row = head * 4 + block
        if fresh:
            state = (
                jnp.full((1, width), LOW, F32),
                jnp.zeros((1, width), F32),
                jnp.zeros((1, width), F32),
            )
        else:
            state = tuple(state_in[i, pl.ds(row, 1), :] for i in range(3))
        for kb in key_blocks:
            state = stat_step(
                cur[kb, 0, :, lanes], cur[kb, 1, :, lanes], queries, grads, state, None
            )
            state = stat_step(
                hist[kb, 0:rows, lanes],
                hist[kb, rows : 2 * rows, lanes],
                queries,
                grads,
                state,
                live_mask(hist, kb, rows, width),
            )
        for i in range(3):
            out_ref[i, pl.ds(row, 1), :] = state[i]

    groups = []
    for block, (fresh, key_blocks) in enumerate(todo):
        if groups and groups[-1][1:] == (fresh, key_blocks):
            groups[-1][0].append(block)
        else:
            groups.append(([block], fresh, key_blocks))
    for blocks, fresh, key_blocks in groups:
        first, count = blocks[0], len(blocks)

        def step(i, _, first=first, count=count, fresh=fresh, key_blocks=key_blocks):
            one(i // count, first + i % count, fresh, key_blocks)
            return 0

        lax.fori_loop(0, heads * count, step, 0)


def stats_call(curs, hists, queries, todo, state=None):
    nk, nq = len(curs), len(queries)
    rows, width = curs[0].shape[1], queries[0].shape[1]
    feat = curs[0].shape[2]
    any_spec = pl.BlockSpec(memory_space=pl.ANY)
    vmem = pl.BlockSpec(memory_space=pltpu.VMEM)
    args = list(curs) + list(hists) + list(queries)
    in_specs = [any_spec] * len(args)
    if state is not None:
        args.append(state)
        in_specs.append(vmem)
    pairs = sum(len(k) for _, k in todo)
    flops = 2 * 2 * pairs * (2 * rows) * width * feat

    def kernel(*refs):
        stat_kernel(nk, nq, todo, *refs)

    return pl.pallas_call(
        kernel,
        out_shape=jax.ShapeDtypeStruct((3, 16, width), F32),
        in_specs=in_specs,
        out_specs=vmem,
        scratch_shapes=[
            pltpu.VMEM((nk, 2, rows, feat), BF16),
            pltpu.VMEM((nk, 2 * rows + 16, feat), BF16),
            pltpu.VMEM((nq, 2, width, feat), BF16),
            pltpu.SemaphoreType.DMA((2 * nk + nq,)),
        ],
        compiler_params=pltpu.CompilerParams(vmem_limit_bytes=VMEM_LIMIT),
        cost_estimate=pl.CostEstimate(
            flops=2 * flops,
            bytes_accessed=sum(a.size * a.dtype.itemsize for a in args),
            transcendentals=pairs * 2 * rows * width * (feat // HS),
        ),
    )(*args)


OFFSETS = (0, -1, 1, 2)


def combine_stats(stats, base_ref, delta_ref, heads):
    for head in range(heads):
        for block, offset in enumerate(OFFSETS):
            parts = []
            for ref, step in zip(stats, OFFSETS):
                there = [o % 4 for o in OFFSETS].index((offset - step) % 4)
                row = head * 4 + there
                parts.append([ref[i, row : row + 1, :] for i in range(3)])
            top = jnp.maximum(
                jnp.maximum(parts[0][0], parts[1][0]), jnp.maximum(parts[2][0], parts[3][0])
            )
            total = jnp.zeros_like(top)
            dots = jnp.zeros_like(top)
            for part in parts:
                shrink = jnp.exp2((part[0] - top) * EXP2_SCALE)
                total = total + part[1] * shrink
                dots = dots + part[2] * shrink
            row = head * 4 + block
            base_ref[row : row + 1, :] = top + jnp.log2(total) * (1.0 / EXP2_SCALE)
            delta_ref[row : row + 1, :] = dots / total


def grad_kernel(nk, nq, last, *refs):
    cur_in, hist_in, query_in = refs[:nk], refs[nk : 2 * nk], refs[2 * nk : 2 * nk + nq]
    refs = refs[2 * nk + nq :]
    stats, refs = refs[:4], refs[4:]
    sum_in = None
    if len(refs) > 2 * nk + 1 + 9:
        sum_in, refs = refs[0], refs[1:]
    cur_out, hist_out, sum_out = refs[:nk], refs[nk : 2 * nk], refs[2 * nk]
    cur, hist, query, cur_grad, hist_grad, sums, base, delta, sem = refs[2 * nk + 1 :]
    load_all(
        list(cur_in) + list(hist_in) + list(query_in),
        [cur.at[i] for i in range(nk)]
        + [hist.at[i] for i in range(nk)]
        + [query.at[i] for i in range(nq)],
        sem,
    )
    rows = cur.shape[2]
    width = query.shape[2]
    heads = cur.shape[3] // HS
    combine_stats(stats, base, delta, heads)
    if sum_in is None:
        sums[...] = jnp.zeros_like(sums)
    else:
        sums[...] = sum_in[...]

    def part(head, lanes, keys, values, mask):
        grad_k = grad_v = None
        for block in range(nq):
            queries, grads = query[block, 0, :, lanes], query[block, 1, :, lanes]
            row = pl.ds(head * 4 + block, 1)
            scores = rows_dot(keys, queries)
            prob = jnp.exp2((scores - base[row, :]) * EXP2_SCALE)
            if mask is not None:
                prob = jnp.where(mask, prob, 0.0)
            grad_scores = rows_dot(values, grads)
            score_grad = (prob * (grad_scores - delta[row, :])).astype(BF16)
            add_v = plain_dot(prob.astype(BF16), grads)
            add_k = plain_dot(score_grad, queries)
            grad_v = add_v if grad_v is None else grad_v + add_v
            grad_k = add_k if grad_k is None else grad_k + add_k
            sums[block, :, lanes] += left_dot(score_grad, keys)
        return (grad_k * SCALE).astype(BF16), grad_v.astype(BF16)

    def step(i, _):
        head, kb = i // nk, i % nk
        lanes = pl.ds(pl.multiple_of(head * HS, HS), HS)
        grad_k, grad_v = part(head, lanes, cur[kb, 0, :, lanes], cur[kb, 1, :, lanes], None)
        cur_grad[kb, 0, :, lanes] = grad_k
        cur_grad[kb, 1, :, lanes] = grad_v
        grad_k, grad_v = part(
            head,
            lanes,
            hist[kb, 0:rows, lanes],
            hist[kb, rows : 2 * rows, lanes],
            live_mask(hist, kb, rows, width),
        )
        hist_grad[kb, 0, :, lanes] = grad_k
        hist_grad[kb, 1, :, lanes] = grad_v
        return 0

    lax.fori_loop(0, heads * nk, step, 0)
    if last:
        sum_out[...] = (sums[...] * SCALE).astype(BF16)
    else:
        sum_out[...] = sums[...]
    load_all(
        [cur_grad.at[i] for i in range(nk)] + [hist_grad.at[i] for i in range(nk)],
        list(cur_out) + list(hist_out),
        sem,
    )


def grads_call(curs, hists, queries, stats, sums=None, last=False):
    nk, nq = len(curs), len(queries)
    rows, width = curs[0].shape[1], queries[0].shape[1]
    feat = curs[0].shape[2]
    any_spec = pl.BlockSpec(memory_space=pl.ANY)
    vmem = pl.BlockSpec(memory_space=pltpu.VMEM)
    args = list(curs) + list(hists) + list(queries)
    in_specs = [any_spec] * len(args)
    args += list(stats)
    in_specs += [vmem] * 4
    if sums is not None:
        args.append(sums)
        in_specs.append(vmem)
    block = jax.ShapeDtypeStruct((2, rows, feat), BF16)
    flops = 5 * 2 * nk * nq * (2 * rows) * width * feat

    def kernel(*refs):
        grad_kernel(nk, nq, last, *refs)

    outs = pl.pallas_call(
        kernel,
        out_shape=[block] * (2 * nk)
        + [jax.ShapeDtypeStruct((nq, width, feat), BF16 if last else F32)],
        in_specs=in_specs,
        out_specs=[any_spec] * (2 * nk) + [vmem],
        scratch_shapes=[
            pltpu.VMEM((nk, 2, rows, feat), BF16),
            pltpu.VMEM((nk, 2 * rows + 16, feat), BF16),
            pltpu.VMEM((nq, 2, width, feat), BF16),
            pltpu.VMEM((nk, 2, rows, feat), BF16),
            pltpu.VMEM((nk, 2, rows, feat), BF16),
            pltpu.VMEM((nq, width, feat), F32),
            pltpu.VMEM((16, width), F32),
            pltpu.VMEM((16, width), F32),
            pltpu.SemaphoreType.DMA((2 * nk + nq,)),
        ],
        compiler_params=pltpu.CompilerParams(vmem_limit_bytes=VMEM_LIMIT),
        cost_estimate=pl.CostEstimate(
            flops=2 * flops,
            bytes_accessed=sum(a.size * a.dtype.itemsize for a in args),
            transcendentals=nk * nq * 2 * rows * width * (feat // HS),
        ),
    )(*args)
    return outs[:nk], outs[nk : 2 * nk], outs[2 * nk]


def ring_moves(sizes):
    nz, ny, nx, nc = sizes

    def table(target):
        pairs = []
        for z in range(nz):
            for y in range(ny):
                for x in range(nx):
                    for c in range(nc):
                        tz, ty = target(z, y, c)
                        src = ((z * ny + y) * nx + x) * nc + c
                        pairs.append((src, (((tz % nz) * ny + ty % ny) * nx + x) * nc + c))
        return pairs

    def keys(step):
        return table(lambda z, y, c: (z, y + step) if c == 0 else (z + step, y))

    def queries(step):
        return table(lambda z, y, c: (z + step, y) if c == 0 else (z, y + step))

    return keys, queries


def make_shards(sizes):
    key_move, query_move = ring_moves(sizes)

    def to_key(value, step):
        return lax.ppermute(value, AXES, key_move(step))

    def to_query(value, step):
        return lax.ppermute(value, AXES, query_move(step))

    def shards(query, key_cur, value_cur, d_out, key_hist, value_hist, hist_len):
        tokens = query.shape[0]
        head_dev = sizes[2] * sizes[3]
        feat = key_hist.shape[1]
        rows = key_hist.shape[0]
        count = jnp.broadcast_to(hist_len.astype(BF16)[:, None], (16, feat))
        hist0 = jnp.concatenate([key_hist, value_hist, count], axis=0)
        hist_m, hist_p = to_key(hist0, 1), to_key(hist0, -1)
        hist2 = to_key(hist_m, 1)

        packed = jnp.stack([query, d_out, key_cur, value_cur])
        packed = packed.reshape(4, tokens, head_dev, feat).transpose(2, 0, 1, 3)
        moved = lax.all_to_all(
            packed.reshape(head_dev, 4 * tokens, feat), ("x", "c"), 0, 0, tiled=True
        )
        moved = moved.reshape(head_dev, 4, tokens, feat).transpose(1, 0, 2, 3)
        moved = moved.reshape(4, head_dev * tokens, feat)
        query0, cur0 = moved[:2], moved[2:]

        cur_m, cur_p = to_key(cur0, 1), to_key(cur0, -1)
        query_m, query_p = to_query(query0, 1), to_query(query0, -1)
        cur2 = to_key(cur_p, -1)
        query2 = jnp.stack([to_query(query_p[0], -1), to_query(query_m[1], 1)])

        curs, hists = [cur0, cur_m, cur_p, cur2], [hist0, hist_m, hist_p, hist2]
        queries = [query0, query_m, query_p, query2]
        state = stats_call(curs[:3], hists[:3], queries[:3], [(True, (0, 1, 2))] * 3)
        state = stats_call(
            curs, hists, queries, [(False, (3,))] * 3 + [(True, (0, 1, 2, 3))], state
        )
        stats = [state, to_query(state, 1), to_query(state, -1), to_query(state, 2)]

        far_cur, far_hist, sums = grads_call(curs[3:], hists[3:], queries, stats)
        got_cur, got_hist = to_key(far_cur[0], 1), to_key(far_hist[0], -1)
        near_cur, near_hist, sums = grads_call(curs[1:3], hists[1:3], queries, stats, sums)
        send_cur_p = (near_cur[1].astype(F32) + got_cur.astype(F32)).astype(BF16)
        send_hist_m = (near_hist[0].astype(F32) + got_hist.astype(F32)).astype(BF16)
        cur_a, cur_b = to_key(send_cur_p, 1), to_key(near_cur[0], -1)
        hist_a, hist_b = to_key(near_hist[1], 1), to_key(send_hist_m, -1)
        own_cur, own_hist, sums = grads_call(
            curs[:1], hists[:1], queries, stats, sums, last=True
        )
        query_a, query_b, query_c = (
            to_query(sums[1], -1),
            to_query(sums[2], 1),
            to_query(sums[3], 2),
        )

        def total(*parts):
            return sum(part.astype(F32) for part in parts).astype(BF16)

        grad_query = total(sums[0], query_a, query_b, query_c)
        grad_cur = total(own_cur[0], cur_a, cur_b)
        grad_hist = total(own_hist[0], hist_a, hist_b)
        back = jnp.concatenate([grad_query[None], grad_cur], axis=0)
        back = back.reshape(3, head_dev, tokens, feat).transpose(1, 0, 2, 3)
        back = lax.all_to_all(
            back.reshape(head_dev, 3 * tokens, feat), ("x", "c"), 0, 0, tiled=True
        )
        back = back.reshape(head_dev, 3, tokens, feat).transpose(1, 2, 0, 3)
        back = back.reshape(3, tokens, head_dev * feat)
        return back[0], back[1], back[2], grad_hist[0], grad_hist[1]

    return shards


def solution(mesh):
    sizes = (4, 4, 4, 2)
    grid = Mesh(mesh.devices.reshape(sizes), AXES)
    token = P(AXES, None)
    hist = P(("z", "y"), ("x", "c"))
    return jax.shard_map(
        make_shards(sizes),
        mesh=grid,
        in_specs=(token, token, token, token, hist, hist, P(("z", "y"))),
        out_specs=(token, token, token, hist, hist),
        check_vma=False,
    )
```

time: 601 us -> 157 us (0.26)
  matrix products: 157 us -> 0 us
  loops' own time: 126 us -> 0 us
  local copies, waits for them, and re-layouts: 87.4 us -> 7.93 us
  waiting for transfers between devices: 105 us -> 41.5 us
  Pallas kernels: 0 us -> 57.8 us
  other arithmetic: 52.2 us -> 2.68 us
  blocking collectives: 24.1 us -> 0 us
  starting transfers between devices: 27.7 us -> 43.8 us
  between operations: 14.6 us -> 1.61 us
    dot_general x112 -> x0, matrix products: 157 us -> none  [the longest x32 46 us: prob_terms(): jnp.einsum('qhd,khd->hqk', queries, key_block, preferred_element_type=jnp...]
    another operation x3 -> x0, loops' own time: 126 us -> none  [the longest x1 42.1 us: shards(): lax.scan(add_query, jnp.zeros((row_count, head_count, HS), jnp.float32),...]
    all_gather x2 -> x0, waiting for transfers between devices: 81 us -> none  [the longest x1 63.3 us: shards(): lax.all_gather(own_values, 'tm', axis=0, tiled=True)]
    pallas_call x0 -> x5, Pallas kernels: none -> 57.8 us  [the longest x3 40.1 us: grads_call(): pl.pallas_call(kernel, out_shape=[block] * (2 * nk) + [jax.ShapeDtypeStru...]
    dynamic_slice x96 -> x0, local copies, waits for them, and re-layouts: 56.3 us -> none  [the longest x48 28.2 us: key_slice(): hist_counts[block_id]]
    or x48 -> x0, other arithmetic: 31.2 us -> none  [live_of(): return (slot_index < row_count) | (slot_index - row_count < filled)]
    ppermute x0 -> x22, starting transfers between devices: none -> 29.7 us  [the longest x12 16.7 us: to_key(): return lax.ppermute(value, AXES, key_move(step))]
    ppermute x0 -> x22, waiting for transfers between devices: none -> 22.4 us  [the longest x12 11.7 us: to_key(): return lax.ppermute(value, AXES, key_move(step))]
  transfers between devices with their start and end apart: 9 -> 24, of which waited for: 7 -> 13; matrix products, arithmetic and copies ran while one was open for 16% -> 1% of each run, Pallas kernels for 0% -> 12%
where the time goes in v1:
time: 157 us; the launch traced here: 155 us
  Pallas kernels  57.8 us (37%)
  starting transfers between devices  43.8 us (28%)
  waiting for transfers between devices  41.5 us (26%)
  local copies, waits for them, and re-layouts  7.93 us (5%)
  other arithmetic  2.68 us (2%)
  between operations  1.61 us (1%)
    pallas_call x3, Pallas kernels, grads_call(): pl.pallas_call(kernel, out_shape=[block] * (2 * nk) + [jax.ShapeDtypeStru...  40.1 us
    pallas_call x2, Pallas kernels, stats_call(): pl.pallas_call(kernel, out_shape=jax.ShapeDtypeStruct((3, 16, width), F32...  17.7 us
    ppermute x12, starting transfers between devices, to_key(): return lax.ppermute(value, AXES, key_move(step))  16.7 us
    ppermute x10, starting transfers between devices, to_query(): return lax.ppermute(value, AXES, query_move(step))  13 us
    ppermute x12, waiting for transfers between devices, to_key(): return lax.ppermute(value, AXES, key_move(step))  11.7 us
    ppermute x10, waiting for transfers between devices, to_query(): return lax.ppermute(value, AXES, query_move(step))  10.7 us
    all_to_all x1, waiting for transfers between devices, shards(): lax.all_to_all(packed.reshape(head_dev, 4 * tokens, feat), ('x', 'c'), 0,...  9.74 us
    all_to_all x1, waiting for transfers between devices, shards(): lax.all_to_all(back.reshape(head_dev, 3 * tokens, feat), ('x', 'c'), 0, 0...  9.42 us
  transfers between devices with their start and end apart: 24, of which 13 were waited for; matrix products, arithmetic and copies ran while one was open for 1% of the time, Pallas kernels for 12%

profile of v1, /device:TPU:1, one launch (start us, length us, event | category | flops | bytes accessed | tf_op | source)
XLA Modules:
  0.0 155.4 jit_solution(3307476083706945312)
XLA Ops:
  0.7 1.0 copy.23
  1.7 1.0 copy.25
  2.8 1.0 pad_maximum_fusion
  3.8 5.9 %all-to-all-start = ((bf16[8,128,384]{2,1,0:T(8,128)(2,1)}), bf16[8,128,384]{2,1,0:T(8,128)(2,1)S(1)}, u32[]{:S(2)}, u32[]{:S(2)}) async-start(bf16[8,128,384]{2,1,0:T(8,128)(2,1)} %bitcast.1), calls=%async_computation | async-start | bytes 1572864 | tf_op jit(solution)/shard_map/all_to_all | solution.py:348
  10.6 1.7 %collective-permute-start.7 = (bf16[528,384]{1,0:T(8,128)(2,1)S(1)}, bf16[528,384]{1,0:T(8,128)(2,1)S(1)}, u32[]{:S(2)}, u32[]{:S(2)}) collective-permute-start(bf16[528,384]{1,0:T(8,128)(2,1)S(1)} %maximum_maximum_fusion.refs_3_.refs_4_.refs_1_), channel_id=1, source_target_pairs={{0,8},{1,33},{2,10},{3,35},{4,12},{5,37},{6,14},{7,39},{8,16},{9,4... | collective-permute-start | bytes 1216520 | tf_op jit(solution)/shard_map/ppermute | solution.py:331
  12.3 9.7 %all-to-all-done = bf16[8,128,384]{2,1,0:T(8,128)(2,1)S(1)} async-done(((bf16[8,128,384]{2,1,0:T(8,128)(2,1)}), bf16[8,128,384]{2,1,0:T(8,128)(2,1)S(1)}, u32[]{:S(2)}, u32[]{:S(2)}) %all-to-all-start) | async-done | bytes 786464 | tf_op jit(solution)/shard_map/all_to_all | solution.py:348
  22.2 2.8 %collective-permute-start.1 = (bf16[2,256,384]{2,1,0:T(8,128)(2,1)S(1)}, bf16[2,256,384]{2,1,0:T(8,128)(2,1)S(1)}, u32[]{:S(2)}, u32[]{:S(2)}) collective-permute-start(bf16[2,256,384]{2,1,0:T(8,128)(2,1)S(1)} %bitcast.62), channel_id=1, source_target_pairs={{0,96},{1,25},{2,98},{3,27},{4,100},{5,29},{6,102},{7,31},{8,104},... | collective-permute-start | bytes 1179656 | tf_op jit(solution)/shard_map/ppermute | solution.py:334
  25.0 3.8 %collective-permute-start.8 = (bf16[528,384]{1,0:T(8,128)(2,1)S(1)}, bf16[528,384]{1,0:T(8,128)(2,1)S(1)}, u32[]{:S(2)}, u32[]{:S(2)}) collective-permute-start(bf16[528,384]{1,0:T(8,128)(2,1)S(1)} %maximum_maximum_fusion.refs_3_.refs_4_.refs_1_), channel_id=1, source_target_pairs={{0,24},{1,97},{2,26},{3,99},{4,28},{5,101},{6,30},{7,103},{8,0},{9... | collective-permute-start | bytes 1216520 | tf_op jit(solution)/shard_map/ppermute | solution.py:331
  28.8 2.7 %collective-permute-start.5 = (bf16[2,256,384]{2,1,0:T(8,128)(2,1)S(1)}, bf16[2,256,384]{2,1,0:T(8,128)(2,1)S(1)}, u32[]{:S(2)}, u32[]{:S(2)}) collective-permute-start(bf16[2,256,384]{2,1,0:T(8,128)(2,1)S(1)} %bitcast.69), channel_id=1, source_target_pairs={{0,24},{1,97},{2,26},{3,99},{4,28},{5,101},{6,30},{7,103},{8,0},{9... | collective-permute-start | bytes 1179656 | tf_op jit(solution)/shard_map/ppermute | solution.py:331
  32.2 1.0 collective-permute-done.refs_7_.refs_9_.refs_3_.refs_5_
  33.1 2.5 %collective-permute-start.2 = (bf16[256,384]{1,0:T(8,128)(2,1)S(1)}, bf16[256,384]{1,0:T(8,128)(2,1)S(1)}, u32[]{:S(2)}, u32[]{:S(2)}) collective-permute-start(bf16[256,384]{1,0:T(8,128)(2,1)S(1)} %slice_bitcast_fusion.3), channel_id=1, source_target_pairs={{0,96},{1,25},{2,98},{3,27},{4,100},{5,29},{6,102},{7,31},{8,104},... | collective-permute-start | bytes 589832 | tf_op jit(solution)/shard_map/ppermute | solution.py:334
  36.4 1.3 collective-permute-start.3
  37.7 2.9 %collective-permute-done.5.refs_2_.refs_1_ = bf16[2,256,384]{2,1,0:T(8,128)(2,1)S(1)} collective-permute-done((bf16[2,256,384]{2,1,0:T(8,128)(2,1)S(1)}, bf16[2,256,384]{2,1,0:T(8,128)(2,1)S(1)}, u32[]{:S(2)}, u32[]{:S(2)}) %collective-permute-start.5) | collective-permute-done | bytes 393248 | tf_op jit(solution)/shard_map/ppermute | solution.py:331
  40.6 3.4 %collective-permute-start.6 = (bf16[2,256,384]{2,1,0:T(8,128)(2,1)S(1)}, bf16[2,256,384]{2,1,0:T(8,128)(2,1)S(1)}, u32[]{:S(2)}, u32[]{:S(2)}) collective-permute-start(bf16[2,256,384]{2,1,0:T(8,128)(2,1)S(1)} %collective-permute-done.5.refs_2_.refs_1_), channel_id=1, source_target_pairs={{0,24},{1,97},{2,26},{3,99},{4,28},{5,101},{6,30},{7,103},{8,0},{9... | collective-permute-start | bytes 1179656 | tf_op jit(solution)/shard_map/ppermute | solution.py:331
  44.3 8.7 %shard_map.110.refs_12_ = f32[3,16,256]{2,1,0:T(8,128)S(1)} custom-call(bf16[2,256,384]{2,1,0:T(8,128)(2,1)S(1)} %bitcast.71, bf16[2,256,384]{2,1,0:T(8,128)(2,1)S(1)} %collective-permute-done.4.refs_1_.refs_0_, bf16[2,256,384]{2,1,0:T(8,128)(2,1)S(1)} %collective-permute-done.5.refs_2_.refs_1_, ...), custom_call_target="tpu_custom_call" | custom-call | flops 3623878656 | bytes 3575808 | tf_op jit(solution)/shard_map/pallas_call | solution.py:141
  53.1 9.0 %shard_map.111.refs_6_.refs_8_ = f32[3,16,256]{2,1,0:T(8,128)S(1)} custom-call(bf16[2,256,384]{2,1,0:T(8,128)(2,1)S(1)} %bitcast.72, bf16[2,256,384]{2,1,0:T(8,128)(2,1)S(1)} %collective-permute-done.4.refs_1_.refs_0_, bf16[2,256,384]{2,1,0:T(8,128)(2,1)S(1)} %collective-permute-done.5.refs_2_.refs_1_, ...), custom_call_target="tpu_custom_call" | custom-call | flops 2818572288 | bytes 4816896 | tf_op jit(solution)/shard_map/pallas_call | solution.py:141
  62.1 2.6 %collective-permute-start.12 = (f32[3,16,256]{2,1,0:T(8,128)S(1)}, f32[3,16,256]{2,1,0:T(8,128)S(1)}, u32[]{:S(2)}, u32[]{:S(2)}) collective-permute-start(f32[3,16,256]{2,1,0:T(8,128)S(1)} %shard_map.111.refs_6_.refs_8_), channel_id=1, source_target_pairs={{0,64},{1,17},{2,66},{3,19},{4,68},{5,21},{6,70},{7,23},{8,72},{9,... | collective-permute-start | bytes 147464 | tf_op jit(solution)/shard_map/ppermute | solution.py:334
  66.6 1.3 collective-permute-done.11.refs_8_.refs_10_
  68.0 1.7 %collective-permute-done.10.refs_7_.refs_9_ = f32[3,16,256]{2,1,0:T(8,128)S(1)} collective-permute-done((f32[3,16,256]{2,1,0:T(8,128)S(1)}, f32[3,16,256]{2,1,0:T(8,128)S(1)}, u32[]{:S(2)}, u32[]{:S(2)}) %collective-permute-start.10) | collective-permute-done | bytes 49184 | tf_op jit(solution)/shard_map/ppermute | solution.py:334
  69.6 9.6 %shard_map.112 = (bf16[2,256,384]{2,1,0:T(8,128)(2,1)S(1)}, bf16[2,256,384]{2,1,0:T(8,128)(2,1)S(1)}, f32[4,256,384]{2,1,0:T(8,128)S(1)}) custom-call(bf16[2,256,384]{2,1,0:T(8,128)(2,1)S(1)} %collective-permute-done.6.refs_3_.refs_0_, bf16[528,384]{1,0:T(8,128)(2,1)S(1)} %collective-permute-done.9.refs_7_.refs_1_, bf16[2,256,384]{2,1,0:T(8,128)(2,1)S(1)} %bitcast.66, ...), custom_call_target="tpu_custom_call" | custom-call | flops 4026531840 | bytes 2568192 | tf_op jit(solution)/shard_map/pallas_call | solution.py:277
  79.3 1.2 copy-done.1
  80.4 20.9 %shard_map.113 = (bf16[2,256,384]{2,1,0:T(8,128)(2,1)S(1)}, bf16[2,256,384]{2,1,0:T(8,128)(2,1)S(1)}, bf16[2,256,384]{2,1,0:T(8,128)(2,1)S(1)}, bf16[2,256,384]{2,1,0:T(8,128)(2,1)S(1)}, f32[4,256,384]{2,1,0:T(8,128)}) custom-call(bf16[2,256,384]{2,1,0:T(8,128)(2,1)S(1)} %collective-permute-done.4.refs_1_.refs_0_, ...), custom_call_target="tpu_custom_call" | custom-call | flops 8053063680 | bytes 4939776 | tf_op jit(solution)/shard_map/pallas_call | solution.py:277
  101.4 1.5 collective-permute-start.19
  102.9 2.6 %collective-permute-start.20 = (bf16[2,256,384]{2,1,0:T(8,128)(2,1)S(1)}, bf16[2,256,384]{2,1,0:T(8,128)(2,1)S(1)}, u32[]{:S(2)}, u32[]{:S(2)}) collective-permute-start(bf16[2,256,384]{2,1,0:T(8,128)(2,1)S(1)} %get-tuple-element.26), channel_id=1, source_target_pairs={{0,24},{1,97},{2,26},{3,99},{4,28},{5,101},{6,30},{7,103},{8,0},{9... | collective-permute-start | bytes 1179656 | tf_op jit(solution)/shard_map/ppermute | solution.py:331
  105.5 1.4 copy-done
  106.9 9.7 %shard_map.114 = (bf16[2,256,384]{2,1,0:T(8,128)(2,1)S(1)}, bf16[2,256,384]{2,1,0:T(8,128)(2,1)S(1)}, bf16[4,256,384]{2,1,0:T(8,128)(2,1)S(1)}) custom-call(bf16[2,256,384]{2,1,0:T(8,128)(2,1)S(1)} %bitcast.73, bf16[528,384]{1,0:T(8,128)(2,1)S(1)} %maximum_maximum_fusion.refs_3_.refs_4_.refs_1_, bf16[2,256,384]{2,1,0:T(8,128)(2,1)S(1)} %bitcast.68, ...), custom_call_target="tpu_custom_call" | custom-call | flops 4026531840 | bytes 4141056 | tf_op jit(solution)/shard_map/pallas_call | solution.py:277
  119.3 2.0 %collective-permute-done.13 = bf16[256,384]{1,0:T(8,128)(2,1)S(1)} collective-permute-done((bf16[256,384]{1,0:T(8,128)(2,1)S(1)}, bf16[256,384]{1,0:T(8,128)(2,1)S(1)}, u32[]{:S(2)}, u32[]{:S(2)}) %collective-permute-start.13) | collective-permute-done | bytes 196640 | tf_op jit(solution)/shard_map/ppermute | solution.py:334
  121.3 2.4 %collective-permute-done.15 = bf16[256,384]{1,0:T(8,128)(2,1)S(1)} collective-permute-done((bf16[256,384]{1,0:T(8,128)(2,1)S(1)}, bf16[256,384]{1,0:T(8,128)(2,1)S(1)}, u32[]{:S(2)}, u32[]{:S(2)}) %collective-permute-start.15) | collective-permute-done | bytes 196640 | tf_op jit(solution)/shard_map/ppermute | solution.py:334
  123.9 1.8 %collective-permute-done.14 = bf16[256,384]{1,0:T(8,128)(2,1)S(1)} collective-permute-done((bf16[256,384]{1,0:T(8,128)(2,1)S(1)}, bf16[256,384]{1,0:T(8,128)(2,1)S(1)}, u32[]{:S(2)}, u32[]{:S(2)}) %collective-permute-start.14) | collective-permute-done | bytes 196640 | tf_op jit(solution)/shard_map/ppermute | solution.py:334
  125.8 7.7 %collective-permute-done.17 = bf16[2,256,384]{2,1,0:T(8,128)(2,1)S(1)} collective-permute-done((bf16[2,256,384]{2,1,0:T(8,128)(2,1)S(1)}, bf16[2,256,384]{2,1,0:T(8,128)(2,1)S(1)}, u32[]{:S(2)}, u32[]{:S(2)}) %collective-permute-start.17) | collective-permute-done | bytes 393248 | tf_op jit(solution)/shard_map/ppermute | solution.py:331
  134.8 8.2 %all-to-all-start.1 = ((bf16[8,96,384]{2,1,0:T(8,128)(2,1)}), bf16[8,96,384]{2,1,0:T(8,128)(2,1)S(1)}, u32[]{:S(2)}, u32[]{:S(2)}) async-start(bf16[8,96,384]{2,1,0:T(8,128)(2,1)} %bitcast.20), calls=%async_computation.1 | async-start | bytes 1179648 | tf_op jit(solution)/shard_map/all_to_all | solution.py:392
  143.8 9.4 %all-to-all-done.1 = bf16[8,96,384]{2,1,0:T(8,128)(2,1)S(1)} async-done(((bf16[8,96,384]{2,1,0:T(8,128)(2,1)}), bf16[8,96,384]{2,1,0:T(8,128)(2,1)S(1)}, u32[]{:S(2)}, u32[]{:S(2)}) %all-to-all-start.1) | async-done | bytes 589856 | tf_op jit(solution)/shard_map/all_to_all | solution.py:392
  (62 shorter events, 11.4 us)
Async XLA Ops:
  0.6 2.0 %copy-start.2 = (bf16[32,3072]{1,0:T(8,128)(2,1)S(1)}, bf16[32,3072]{1,0:T(8,128)(2,1)}, u32[]{:S(2)}) copy-start(bf16[32,3072]{1,0:T(8,128)(2,1)} %param.9) | copy-start | bytes 589828
  0.6 2.1 %copy-start.3 = (bf16[32,3072]{1,0:T(8,128)(2,1)S(1)}, bf16[32,3072]{1,0:T(8,128)(2,1)}, u32[]{:S(2)}) copy-start(bf16[32,3072]{1,0:T(8,128)(2,1)} %param.10) | copy-start | bytes 589828
  3.8 6.6 %copy-start.4 = (bf16[256,384]{1,0:T(8,128)(2,1)S(1)}, bf16[256,384]{1,0:T(8,128)(2,1)}, u32[]{:S(2)}) copy-start(bf16[256,384]{1,0:T(8,128)(2,1)} %param.12) | copy-start | bytes 589828
  3.8 6.6 %copy-start.5 = (bf16[256,384]{1,0:T(8,128)(2,1)S(1)}, bf16[256,384]{1,0:T(8,128)(2,1)}, u32[]{:S(2)}) copy-start(bf16[256,384]{1,0:T(8,128)(2,1)} %param.11) | copy-start | bytes 589828
  3.8 18.2 %all-to-all-start = ((bf16[8,128,384]{2,1,0:T(8,128)(2,1)}), bf16[8,128,384]{2,1,0:T(8,128)(2,1)S(1)}, u32[]{:S(2)}, u32[]{:S(2)}) async-start(bf16[8,128,384]{2,1,0:T(8,128)(2,1)} %bitcast.1), calls=%async_computation | async-start | bytes 1572864 | tf_op jit(solution)/shard_map/all_to_all | solution.py:348
  10.6 18.1 %collective-permute-start.7 = (bf16[528,384]{1,0:T(8,128)(2,1)S(1)}, bf16[528,384]{1,0:T(8,128)(2,1)S(1)}, u32[]{:S(2)}, u32[]{:S(2)}) collective-permute-start(bf16[528,384]{1,0:T(8,128)(2,1)S(1)} %maximum_maximum_fusion.refs_3_.refs_4_.refs_1_), channel_id=1, source_target_pairs={{0,8},{1,33},{2,10},{3,35},{4,12},{5,37},{6,14},{7,39},{8,16},{9,4... | collective-permute-start | bytes 1216520 | tf_op jit(solution)/shard_map/ppermute | solution.py:331
  22.2 9.4 %collective-permute-start.1 = (bf16[2,256,384]{2,1,0:T(8,128)(2,1)S(1)}, bf16[2,256,384]{2,1,0:T(8,128)(2,1)S(1)}, u32[]{:S(2)}, u32[]{:S(2)}) collective-permute-start(bf16[2,256,384]{2,1,0:T(8,128)(2,1)S(1)} %bitcast.62), channel_id=1, source_target_pairs={{0,96},{1,25},{2,98},{3,27},{4,100},{5,29},{6,102},{7,31},{8,104},... | collective-permute-start | bytes 1179656 | tf_op jit(solution)/shard_map/ppermute | solution.py:334
  25.0 8.1 %collective-permute-start = (bf16[2,256,384]{2,1,0:T(8,128)(2,1)S(1)}, bf16[2,256,384]{2,1,0:T(8,128)(2,1)S(1)}, u32[]{:S(2)}, u32[]{:S(2)}) collective-permute-start(bf16[2,256,384]{2,1,0:T(8,128)(2,1)S(1)} %bitcast.63), channel_id=1, source_target_pairs={{0,32},{1,9},{2,34},{3,11},{4,36},{5,13},{6,38},{7,15},{8,40},{9,1... | collective-permute-start | bytes 1179656 | tf_op jit(solution)/shard_map/ppermute | solution.py:334
  25.0 11.4 %collective-permute-start.8 = (bf16[528,384]{1,0:T(8,128)(2,1)S(1)}, bf16[528,384]{1,0:T(8,128)(2,1)S(1)}, u32[]{:S(2)}, u32[]{:S(2)}) collective-permute-start(bf16[528,384]{1,0:T(8,128)(2,1)S(1)} %maximum_maximum_fusion.refs_3_.refs_4_.refs_1_), channel_id=1, source_target_pairs={{0,24},{1,97},{2,26},{3,99},{4,28},{5,101},{6,30},{7,103},{8,0},{9... | collective-permute-start | bytes 1216520 | tf_op jit(solution)/shard_map/ppermute | solution.py:331
  28.8 24.3 %collective-permute-start.9 = (bf16[528,384]{1,0:T(8,128)(2,1)S(1)}, bf16[528,384]{1,0:T(8,128)(2,1)S(1)}, u32[]{:S(2)}, u32[]{:S(2)}) collective-permute-start(bf16[528,384]{1,0:T(8,128)(2,1)S(1)} %collective-permute-done.7.refs_4_.refs_5_.refs_2_), channel_id=1, source_target_pairs={{0,8},{1,33},{2,10},{3,35},{4,12},{5,37},{6,14},{7,39},{8,16},{9,4... | collective-permute-start | bytes 1216520 | tf_op jit(solution)/shard_map/ppermute | solution.py:331
  28.8 11.8 %collective-permute-start.5 = (bf16[2,256,384]{2,1,0:T(8,128)(2,1)S(1)}, bf16[2,256,384]{2,1,0:T(8,128)(2,1)S(1)}, u32[]{:S(2)}, u32[]{:S(2)}) collective-permute-start(bf16[2,256,384]{2,1,0:T(8,128)(2,1)S(1)} %bitcast.69), channel_id=1, source_target_pairs={{0,24},{1,97},{2,26},{3,99},{4,28},{5,101},{6,30},{7,103},{8,0},{9... | collective-permute-start | bytes 1179656 | tf_op jit(solution)/shard_map/ppermute | solution.py:331
  31.6 12.8 %collective-permute-start.4 = (bf16[2,256,384]{2,1,0:T(8,128)(2,1)S(1)}, bf16[2,256,384]{2,1,0:T(8,128)(2,1)S(1)}, u32[]{:S(2)}, u32[]{:S(2)}) collective-permute-start(bf16[2,256,384]{2,1,0:T(8,128)(2,1)S(1)} %bitcast.70), channel_id=1, source_target_pairs={{0,8},{1,33},{2,10},{3,35},{4,12},{5,37},{6,14},{7,39},{8,16},{9,4... | collective-permute-start | bytes 1179656 | tf_op jit(solution)/shard_map/ppermute | solution.py:331
  33.1 19.9 %collective-permute-start.2 = (bf16[256,384]{1,0:T(8,128)(2,1)S(1)}, bf16[256,384]{1,0:T(8,128)(2,1)S(1)}, u32[]{:S(2)}, u32[]{:S(2)}) collective-permute-start(bf16[256,384]{1,0:T(8,128)(2,1)S(1)} %slice_bitcast_fusion.3), channel_id=1, source_target_pairs={{0,96},{1,25},{2,98},{3,27},{4,100},{5,29},{6,102},{7,31},{8,104},... | collective-permute-start | bytes 589832 | tf_op jit(solution)/shard_map/ppermute | solution.py:334
  36.4 16.6 %collective-permute-start.3 = (bf16[256,384]{1,0:T(8,128)(2,1)S(1)}, bf16[256,384]{1,0:T(8,128)(2,1)S(1)}, u32[]{:S(2)}, u32[]{:S(2)}) collective-permute-start(bf16[256,384]{1,0:T(8,128)(2,1)S(1)} %slice_bitcast_fusion.2), channel_id=1, source_target_pairs={{0,32},{1,9},{2,34},{3,11},{4,36},{5,13},{6,38},{7,15},{8,40},{9,1... | collective-permute-start | bytes 589832 | tf_op jit(solution)/shard_map/ppermute | solution.py:334
  40.6 12.5 %collective-permute-start.6 = (bf16[2,256,384]{2,1,0:T(8,128)(2,1)S(1)}, bf16[2,256,384]{2,1,0:T(8,128)(2,1)S(1)}, u32[]{:S(2)}, u32[]{:S(2)}) collective-permute-start(bf16[2,256,384]{2,1,0:T(8,128)(2,1)S(1)} %collective-permute-done.5.refs_2_.refs_1_), channel_id=1, source_target_pairs={{0,24},{1,97},{2,26},{3,99},{4,28},{5,101},{6,30},{7,103},{8,0},{9... | collective-permute-start | bytes 1179656 | tf_op jit(solution)/shard_map/ppermute | solution.py:331
  62.1 4.5 %collective-permute-start.12 = (f32[3,16,256]{2,1,0:T(8,128)S(1)}, f32[3,16,256]{2,1,0:T(8,128)S(1)}, u32[]{:S(2)}, u32[]{:S(2)}) collective-permute-start(f32[3,16,256]{2,1,0:T(8,128)S(1)} %shard_map.111.refs_6_.refs_8_), channel_id=1, source_target_pairs={{0,64},{1,17},{2,66},{3,19},{4,68},{5,21},{6,70},{7,23},{8,72},{9,... | collective-permute-start | bytes 147464 | tf_op jit(solution)/shard_map/ppermute | solution.py:334
  64.7 3.3 %collective-permute-start.11 = (f32[3,16,256]{2,1,0:T(8,128)S(1)}, f32[3,16,256]{2,1,0:T(8,128)S(1)}, u32[]{:S(2)}, u32[]{:S(2)}) collective-permute-start(f32[3,16,256]{2,1,0:T(8,128)S(1)} %shard_map.111.refs_6_.refs_8_), channel_id=1, source_target_pairs={{0,96},{1,25},{2,98},{3,27},{4,100},{5,29},{6,102},{7,31},{8,104},... | collective-permute-start | bytes 147464 | tf_op jit(solution)/shard_map/ppermute | solution.py:334
  65.5 4.2 %collective-permute-start.10 = (f32[3,16,256]{2,1,0:T(8,128)S(1)}, f32[3,16,256]{2,1,0:T(8,128)S(1)}, u32[]{:S(2)}, u32[]{:S(2)}) collective-permute-start(f32[3,16,256]{2,1,0:T(8,128)S(1)} %shard_map.111.refs_6_.refs_8_), channel_id=1, source_target_pairs={{0,32},{1,9},{2,34},{3,11},{4,36},{5,13},{6,38},{7,15},{8,40},{9,1... | collective-permute-start | bytes 147464 | tf_op jit(solution)/shard_map/ppermute | solution.py:334
  79.2 1.2 copy-start.1
  101.3 24.5 %collective-permute-start.18 = (bf16[2,256,384]{2,1,0:T(8,128)(2,1)S(1)}, bf16[2,256,384]{2,1,0:T(8,128)(2,1)S(1)}, u32[]{:S(2)}, u32[]{:S(2)}) collective-permute-start(bf16[2,256,384]{2,1,0:T(8,128)(2,1)S(1)} %get-tuple-element.22), channel_id=1, source_target_pairs={{0,24},{1,97},{2,26},{3,99},{4,28},{5,101},{6,30},{7,103},{8,0},{9... | collective-permute-start | bytes 1179656 | tf_op jit(solution)/shard_map/ppermute | solution.py:331
  101.4 24.4 %collective-permute-start.19 = (bf16[2,256,384]{2,1,0:T(8,128)(2,1)S(1)}, bf16[2,256,384]{2,1,0:T(8,128)(2,1)S(1)}, u32[]{:S(2)}, u32[]{:S(2)}) collective-permute-start(bf16[2,256,384]{2,1,0:T(8,128)(2,1)S(1)} %get-tuple-element.24), channel_id=1, source_target_pairs={{0,8},{1,33},{2,10},{3,35},{4,12},{5,37},{6,14},{7,39},{8,16},{9,4... | collective-permute-start | bytes 1179656 | tf_op jit(solution)/shard_map/ppermute | solution.py:331
  102.9 14.7 %collective-permute-start.16 = (bf16[2,256,384]{2,1,0:T(8,128)(2,1)S(1)}, bf16[2,256,384]{2,1,0:T(8,128)(2,1)S(1)}, u32[]{:S(2)}, u32[]{:S(2)}) collective-permute-start(bf16[2,256,384]{2,1,0:T(8,128)(2,1)S(1)} %get-tuple-element.21), channel_id=1, source_target_pairs={{0,8},{1,33},{2,10},{3,35},{4,12},{5,37},{6,14},{7,39},{8,16},{9,4... | collective-permute-start | bytes 1179656 | tf_op jit(solution)/shard_map/ppermute | solution.py:331
  102.9 15.5 %collective-permute-start.20 = (bf16[2,256,384]{2,1,0:T(8,128)(2,1)S(1)}, bf16[2,256,384]{2,1,0:T(8,128)(2,1)S(1)}, u32[]{:S(2)}, u32[]{:S(2)}) collective-permute-start(bf16[2,256,384]{2,1,0:T(8,128)(2,1)S(1)} %get-tuple-element.26), channel_id=1, source_target_pairs={{0,24},{1,97},{2,26},{3,99},{4,28},{5,101},{6,30},{7,103},{8,0},{9... | collective-permute-start | bytes 1179656 | tf_op jit(solution)/shard_map/ppermute | solution.py:331
  105.5 1.4 copy-start
  116.7 4.6 %collective-permute-start.13 = (bf16[256,384]{1,0:T(8,128)(2,1)S(1)}, bf16[256,384]{1,0:T(8,128)(2,1)S(1)}, u32[]{:S(2)}, u32[]{:S(2)}) collective-permute-start(bf16[256,384]{1,0:T(8,128)(2,1)S(1)} %get-tuple-element.27), channel_id=1, source_target_pairs={{0,96},{1,25},{2,98},{3,27},{4,100},{5,29},{6,102},{7,31},{8,104},... | collective-permute-start | bytes 589832 | tf_op jit(solution)/shard_map/ppermute | solution.py:334
  117.6 6.1 %collective-permute-start.15 = (bf16[256,384]{1,0:T(8,128)(2,1)S(1)}, bf16[256,384]{1,0:T(8,128)(2,1)S(1)}, u32[]{:S(2)}, u32[]{:S(2)}) collective-permute-start(bf16[256,384]{1,0:T(8,128)(2,1)S(1)} %get-tuple-element.28), channel_id=1, source_target_pairs={{0,64},{1,17},{2,66},{3,19},{4,68},{5,21},{6,70},{7,23},{8,72},{9,... | collective-permute-start | bytes 589832 | tf_op jit(solution)/shard_map/ppermute | solution.py:334
  118.4 7.3 %collective-permute-start.14 = (bf16[256,384]{1,0:T(8,128)(2,1)S(1)}, bf16[256,384]{1,0:T(8,128)(2,1)S(1)}, u32[]{:S(2)}, u32[]{:S(2)}) collective-permute-start(bf16[256,384]{1,0:T(8,128)(2,1)S(1)} %get-tuple-element.29), channel_id=1, source_target_pairs={{0,32},{1,9},{2,34},{3,11},{4,36},{5,13},{6,38},{7,15},{8,40},{9,1... | collective-permute-start | bytes 589832 | tf_op jit(solution)/shard_map/ppermute | solution.py:334
  121.3 12.3 %collective-permute-start.17 = (bf16[2,256,384]{2,1,0:T(8,128)(2,1)S(1)}, bf16[2,256,384]{2,1,0:T(8,128)(2,1)S(1)}, u32[]{:S(2)}, u32[]{:S(2)}) collective-permute-start(bf16[2,256,384]{2,1,0:T(8,128)(2,1)S(1)} %add_convert_fusion.3), channel_id=1, source_target_pairs={{0,8},{1,33},{2,10},{3,35},{4,12},{5,37},{6,14},{7,39},{8,16},{9,4... | collective-permute-start | bytes 1179656 | tf_op jit(solution)/shard_map/ppermute | solution.py:331
  123.7 9.9 %collective-permute-start.21 = (bf16[2,256,384]{2,1,0:T(8,128)(2,1)S(1)}, bf16[2,256,384]{2,1,0:T(8,128)(2,1)S(1)}, u32[]{:S(2)}, u32[]{:S(2)}) collective-permute-start(bf16[2,256,384]{2,1,0:T(8,128)(2,1)S(1)} %add_convert_fusion.1), channel_id=1, source_target_pairs={{0,24},{1,97},{2,26},{3,99},{4,28},{5,101},{6,30},{7,103},{8,0},{9... | collective-permute-start | bytes 1179656 | tf_op jit(solution)/shard_map/ppermute | solution.py:331
  134.8 18.4 %all-to-all-start.1 = ((bf16[8,96,384]{2,1,0:T(8,128)(2,1)}), bf16[8,96,384]{2,1,0:T(8,128)(2,1)S(1)}, u32[]{:S(2)}, u32[]{:S(2)}) async-start(bf16[8,96,384]{2,1,0:T(8,128)(2,1)} %bitcast.20), calls=%async_computation.1 | async-start | bytes 1179648 | tf_op jit(solution)/shard_map/all_to_all | solution.py:392

commit v2 on v0

v2 whole, which is shorter than its diff:
```python
import math

import jax
import jax.numpy as jnp
from jax import lax
from jax.experimental import pallas as pl
from jax.experimental.pallas import tpu as pltpu
from jax.sharding import Mesh
from jax.sharding import PartitionSpec as P

HS = 128
SCALE = 1.0 / math.sqrt(HS)
EXP2_SCALE = SCALE * math.log2(math.e)
LOW = -1e30
VMEM_LIMIT = 24 * 1024 * 1024
AXES = ("z", "y", "x", "c")
OFFSETS = (0, -1, 1, 2)
F32 = jnp.float32
BF16 = jnp.bfloat16
VMEM = pl.BlockSpec(memory_space=pltpu.VMEM)


def rows_dot(a, b):
    return lax.dot_general(a, b, (((1,), (1,)), ((), ())), preferred_element_type=F32)


def plain_dot(a, b):
    return lax.dot_general(a, b, (((1,), (0,)), ((), ())), preferred_element_type=F32)


def call(kernel, outs, args, flops=0, exps=0, scratch=()):
    size = sum(a.size * a.dtype.itemsize for a in args)
    return pl.pallas_call(
        kernel,
        out_shape=outs,
        in_specs=[VMEM] * len(args),
        out_specs=jax.tree.map(lambda _: VMEM, outs),
        scratch_shapes=list(scratch),
        compiler_params=pltpu.CompilerParams(vmem_limit_bytes=VMEM_LIMIT),
        cost_estimate=pl.CostEstimate(flops=flops // 64, bytes_accessed=size // 64, transcendentals=0),
    )(*args)


def head_lanes(head):
    return pl.ds(pl.multiple_of(head * HS, HS), HS)


def dead_bias(hist, rows, width):
    count = hist[2 * rows : 2 * rows + 16, 0:HS].astype(F32)[0:1]
    slot = lax.broadcasted_iota(jnp.int32, (rows, HS), 0).astype(F32)
    bias = jnp.where(slot < count, 0.0, LOW)
    return jnp.concatenate([bias] * (width // HS), axis=1)


def wide(refs, which, lanes):
    return jnp.concatenate([ref[which, :, lanes] for ref in refs], axis=0)


def stat_step(keys, values, queries, grads, state, bias):
    top, total, dots = state
    scores = rows_dot(keys, queries)
    if bias is not None:
        scores = scores + bias
    new_top = jnp.maximum(top, jnp.max(scores, axis=0, keepdims=True))
    shrink = jnp.exp2((top - new_top) * EXP2_SCALE)
    weights = jnp.exp2((scores - new_top) * EXP2_SCALE)
    grad_scores = rows_dot(values, grads)
    total = total * shrink + jnp.sum(weights, axis=0, keepdims=True)
    dots = dots * shrink + jnp.sum(weights * grad_scores, axis=0, keepdims=True)
    return new_top, total, dots


def stats_call(curs, hists, queries, groups, state_in=None):
    nk, nq = len(curs), len(queries)
    rows, feat = curs[0].shape[1:]
    tokens = queries[0].shape[1]
    heads = feat // HS

    def kernel(*refs):
        cur, hist, query = refs[:nk], refs[nk : 2 * nk], refs[2 * nk : 2 * nk + nq]
        old, out = refs[2 * nk + nq], refs[-1]

        def step(head, _):
            lanes = head_lanes(head)
            for blocks, key_blocks, fresh in groups:
                width = tokens * len(blocks)
                queries = wide([query[b] for b in blocks], 0, lanes)
                grads = wide([query[b] for b in blocks], 1, lanes)
                if fresh:
                    state = (
                        jnp.full((1, width), LOW, F32),
                        jnp.zeros((1, width), F32),
                        jnp.zeros((1, width), F32),
                    )
                else:
                    state = tuple(
                        jnp.concatenate(
                            [old[i, pl.ds(head * 4 + b, 1), :] for b in blocks], axis=1
                        )
                        for i in range(3)
                    )
                for kb in key_blocks:
                    state = stat_step(
                        cur[kb][0, :, lanes], cur[kb][1, :, lanes], queries, grads, state, None
                    )
                    state = stat_step(
                        hist[kb][0:rows, lanes],
                        hist[kb][rows : 2 * rows, lanes],
                        queries,
                        grads,
                        state,
                        dead_bias(hist[kb], rows, width),
                    )
                for i in range(3):
                    for j, b in enumerate(blocks):
                        out[i, pl.ds(head * 4 + b, 1), :] = state[i][
                            :, j * tokens : (j + 1) * tokens
                        ]
            return 0

        lax.fori_loop(0, heads, step, 0)

    args = list(curs) + list(hists) + list(queries) + ([] if state_in is None else [state_in])
    pairs = sum(len(b) * len(k) for b, k, _ in groups)
    work = pairs * 2 * rows * tokens
    out = jax.ShapeDtypeStruct((3, 16, tokens), F32)
    return call(kernel, out, args, flops=2 * 2 * 2 * work * feat, exps=work * heads)


def combine_stats(stats, base_ref, delta_ref, heads):
    for head in range(heads):
        for block, offset in enumerate(OFFSETS):
            parts = []
            for ref, step in zip(stats, OFFSETS):
                there = [o % 4 for o in OFFSETS].index((offset - step) % 4)
                row = head * 4 + there
                parts.append([ref[i, row : row + 1, :] for i in range(3)])
            top = jnp.maximum(
                jnp.maximum(parts[0][0], parts[1][0]), jnp.maximum(parts[2][0], parts[3][0])
            )
            total = jnp.zeros_like(top)
            dots = jnp.zeros_like(top)
            for part in parts:
                shrink = jnp.exp2((part[0] - top) * EXP2_SCALE)
                total = total + part[1] * shrink
                dots = dots + part[2] * shrink
            at = slice(block * top.shape[1], (block + 1) * top.shape[1])
            base_ref[head, 0:1, at] = top + jnp.log2(total) * (1.0 / EXP2_SCALE)
            delta_ref[head, 0:1, at] = dots / total


def grads_call(curs, hists, queries, stats, sums_in=None, far=None):
    nk, nq = len(curs), len(queries)
    rows, feat = curs[0].shape[1:]
    tokens = queries[0].shape[1]
    heads = feat // HS
    width = nq * tokens
    last = far is not None

    def kernel(*refs):
        cur, hist, query = refs[:nk], refs[nk : 2 * nk], refs[2 * nk : 2 * nk + nq]
        refs = refs[2 * nk + nq :]
        stat, refs = refs[:4], refs[4:]
        if sums_in is not None:
            old, refs = refs[0], refs[1:]
        if last:
            far_in, refs = refs[0], refs[1:]
        key_out, sum_out = refs[:nk], refs[nk:-2]
        base, delta = refs[-2:]
        combine_stats(stat, base, delta, heads)

        def part(keys, values, queries, grads, lift, shift, bias):
            scores = rows_dot(keys, queries) - lift
            if bias is not None:
                scores = scores + bias
            prob = jnp.exp2(scores * EXP2_SCALE)
            grad_scores = rows_dot(values, grads)
            score_grad = (prob * (grad_scores - shift)).astype(BF16)
            grad_v = plain_dot(prob.astype(BF16), grads)
            grad_k = plain_dot(score_grad, queries) * SCALE
            return score_grad, grad_k, grad_v

        def store(kb, i, lanes, value):
            if last:
                value = value + far_in[i, :, lanes].astype(F32)
            key_out[kb][i, :, lanes] = value.astype(BF16)

        def step(head, _):
            lanes = head_lanes(head)
            queries, grads = wide(query, 0, lanes), wide(query, 1, lanes)
            lift, shift = base[head, 0:1, :], delta[head, 0:1, :]
            total = None if sums_in is None else old[head]
            for kb in range(nk):
                keys = cur[kb][0, :, lanes]
                score_a, grad_k, grad_v = part(
                    keys, cur[kb][1, :, lanes], queries, grads, lift, shift, None
                )
                store(kb, 0, lanes, grad_k)
                store(kb, 1, lanes, grad_v)
                old_keys = hist[kb][0:rows, lanes]
                score_b, grad_k, grad_v = part(
                    old_keys,
                    hist[kb][rows : 2 * rows, lanes],
                    queries,
                    grads,
                    lift,
                    shift,
                    dead_bias(hist[kb], rows, width),
                )
                store(kb, 2, lanes, grad_k)
                store(kb, 3, lanes, grad_v)
                add = plain_dot(
                    jnp.concatenate([keys, old_keys], axis=0).T,
                    jnp.concatenate([score_a, score_b], axis=0),
                )
                total = add if total is None else total + add
            if last:
                for b in range(nq):
                    piece = total[:, b * tokens : (b + 1) * tokens] * SCALE
                    sum_out[b][:, lanes] = piece.T.astype(BF16)
            else:
                sum_out[0][head] = total
            return 0

        lax.fori_loop(0, heads, step, 0)

    block = jax.ShapeDtypeStruct((4, rows, feat), BF16)
    if last:
        sums = [jax.ShapeDtypeStruct((tokens, feat), BF16)] * nq
    else:
        sums = [jax.ShapeDtypeStruct((heads, HS, width), F32)]
    args = list(curs) + list(hists) + list(queries) + list(stats)
    args += [a for a in (sums_in, far) if a is not None]
    work = nk * 2 * rows * width
    outs = call(
        kernel,
        [block] * nk + sums,
        args,
        flops=2 * 5 * 2 * work * feat,
        exps=work * heads,
        scratch=[pltpu.VMEM((heads, 8, width), F32)] * 2,
    )
    return list(outs[:nk]), list(outs[nk:])


def pack_call(arrays, parts):
    rows, columns = arrays[0].shape
    feat = columns // parts

    def kernel(*refs):
        out = refs[-1]
        for i, ref in enumerate(refs[:-1]):
            for p in range(parts):
                out[p, i * rows : (i + 1) * rows, :] = ref[:, p * feat : (p + 1) * feat]

    shape = jax.ShapeDtypeStruct((parts, len(arrays) * rows, feat), BF16)
    return call(kernel, shape, arrays)


def unpack_call(array, count):
    parts, rows, feat = array.shape
    rows //= count

    def kernel(ref, *outs):
        for i, out in enumerate(outs):
            for p in range(parts):
                out[:, p * feat : (p + 1) * feat] = ref[p, i * rows : (i + 1) * rows, :]

    return call(kernel, [jax.ShapeDtypeStruct((rows, parts * feat), BF16)] * count, [array])


def split_call(array, count):
    parts, rows, feat = array.shape
    rows //= count

    def kernel(ref, *outs):
        for i in range(count):
            for p in range(parts):
                outs[i // 2][i % 2, p * rows : (p + 1) * rows, :] = ref[
                    p, i * rows : (i + 1) * rows, :
                ]

    block = jax.ShapeDtypeStruct((2, parts * rows, feat), BF16)
    return call(kernel, [block] * (count // 2), [array])


def add_call(query_parts, cur_parts, parts):
    tokens, feat = query_parts[0].shape
    rows = tokens // parts
    nq = len(query_parts)

    def kernel(*refs):
        out = refs[-1]
        sums = [
            sum(ref[...].astype(F32) for ref in refs[:nq]),
            sum(ref[0].astype(F32) for ref in refs[nq:-1]),
            sum(ref[1].astype(F32) for ref in refs[nq:-1]),
        ]
        for i, total in enumerate(sums):
            low = total.astype(BF16)
            for p in range(parts):
                out[p, i * rows : (i + 1) * rows, :] = low[p * rows : (p + 1) * rows]

    shape = jax.ShapeDtypeStruct((parts, 3 * rows, feat), BF16)
    return call(kernel, shape, list(query_parts) + list(cur_parts))


def add_hist_call(key_parts):
    _, rows, feat = key_parts[0].shape

    def kernel(*refs):
        for i, out in enumerate(refs[-2:]):
            out[...] = sum(ref[2 + i].astype(F32) for ref in refs[:-2]).astype(BF16)

    return call(kernel, [jax.ShapeDtypeStruct((rows, feat), BF16)] * 2, list(key_parts))


def ring_moves(sizes):
    nz, ny, nx, nc = sizes

    def table(target):
        pairs = []
        for z in range(nz):
            for y in range(ny):
                for x in range(nx):
                    for c in range(nc):
                        tz, ty = target(z, y, c)
                        src = ((z * ny + y) * nx + x) * nc + c
                        pairs.append((src, (((tz % nz) * ny + ty % ny) * nx + x) * nc + c))
        return pairs

    def keys(step):
        return table(lambda z, y, c: (z, y + step) if c == 0 else (z + step, y))

    def queries(step):
        return table(lambda z, y, c: (z + step, y) if c == 0 else (z, y + step))

    return keys, queries


def make_shards(sizes):
    key_move, query_move = ring_moves(sizes)

    def to_key(value, step):
        return lax.ppermute(value, AXES, key_move(step))

    def to_query(value, step):
        return lax.ppermute(value, AXES, query_move(step))

    def shards(query, key_cur, value_cur, d_out, key_hist, value_hist, hist_len):
        parts = sizes[2] * sizes[3]
        feat = key_hist.shape[1]
        count = jnp.broadcast_to(hist_len.astype(BF16)[:, None], (16, feat))
        hist0 = jnp.concatenate([key_hist, value_hist, count], axis=0)
        hists = [hist0] + [to_key(hist0, -o) for o in OFFSETS[1:]]

        packed = pack_call([query, d_out, key_cur, value_cur], parts)
        moved = lax.all_to_all(packed, ("x", "c"), 0, 0, tiled=True)
        moved, hists = lax.optimization_barrier((moved, hists))
        query0, cur0 = split_call(moved, 4)

        curs = [cur0] + [to_key(cur0, -o) for o in OFFSETS[1:]]
        queries = [query0] + [to_query(query0, -o) for o in OFFSETS[1:]]
        near = (0, 1, 2)
        state = stats_call(curs[:3], hists[:3], queries[:3], [(near, near, True)])
        state = stats_call(
            curs, hists, queries, [(near, (3,), False), ((3,), (0, 1, 2, 3), True)], state
        )
        stats = [state] + [to_query(state, -o) for o in OFFSETS[1:]]

        far, sums = grads_call(curs[3:], hists[3:], queries, stats)
        far = to_key(far[0], 2)
        near, sums = grads_call(curs[1:3], hists[1:3], queries, stats, sums[0])
        near = [to_key(block, offset) for block, offset in zip(near, OFFSETS[1:3])]
        own, sums = grads_call(curs[:1], hists[:1], queries, stats, sums[0], far)
        query_parts = [sums[0]] + [to_query(sums[i], OFFSETS[i]) for i in range(1, 4)]

        back = add_call(query_parts, own + near, parts)
        back = lax.all_to_all(back, ("x", "c"), 0, 0, tiled=True)
        outs = unpack_call(back, 3)
        grad_k, grad_v = add_hist_call(own + near)
        return outs[0], outs[1], outs[2], grad_k, grad_v

    return shards


def solution(mesh):
    sizes = (4, 4, 4, 2)
    grid = Mesh(mesh.devices.reshape(sizes), AXES)
    token = P(AXES, None)
    hist = P(("z", "y"), ("x", "c"))
    return jax.shard_map(
        make_shards(sizes),
        mesh=grid,
        in_specs=(token, token, token, token, hist, hist, P(("z", "y"))),
        out_specs=(token, token, token, hist, hist),
        check_vma=False,
    )
```

time: 601 us -> 122 us (0.20); the launches traced: 594 us -> 122 us
  matrix products: 157 us -> 0 us
  loops' own time: 126 us -> 0 us
  local copies, waits for them, and re-layouts: 87.4 us -> 3.72 us
  waiting for transfers between devices: 105 us -> 44.4 us
  other arithmetic: 52.2 us -> 0.14 us
  Pallas kernels: 0 us -> 31.5 us
  blocking collectives: 24.1 us -> 0 us
  starting transfers between devices: 27.7 us -> 40.9 us
  between operations: 14.6 us -> 1.44 us
    dot_general x112 -> x0, matrix products: 157 us -> none  [the longest x32 46 us: prob_terms(): jnp.einsum('qhd,khd->hqk', queries, key_block, preferred_element_type=jnp...]
    another operation x3 -> x0, loops' own time: 126 us -> none  [the longest x1 42.1 us: shards(): lax.scan(add_query, jnp.zeros((row_count, head_count, HS), jnp.float32),...]
    all_gather x2 -> x0, waiting for transfers between devices: 81 us -> none  [the longest x1 63.3 us: shards(): lax.all_gather(own_values, 'tm', axis=0, tiled=True)]
    dynamic_slice x96 -> x0, local copies, waits for them, and re-layouts: 56.3 us -> none  [the longest x48 28.2 us: key_slice(): hist_counts[block_id]]
    ppermute x0 -> x18, waiting for transfers between devices: none -> 35.1 us  [the longest x9 19.4 us: to_query(): return lax.ppermute(value, AXES, query_move(step))]
    pallas_call x0 -> x10, Pallas kernels: none -> 31.5 us  [call(): pl.pallas_call(kernel, out_shape=outs, in_specs=[VMEM] * len(args), out_s...]
    or x48 -> x0, other arithmetic: 31.2 us -> none  [live_of(): return (slot_index < row_count) | (slot_index - row_count < filled)]
    ppermute x0 -> x18, starting transfers between devices: none -> 25.4 us  [the longest x9 14.6 us: to_key(): return lax.ppermute(value, AXES, key_move(step))]
  transfers between devices with their start and end apart: 9 -> 20, of which waited for: 7 -> 14; matrix products, arithmetic and copies ran while one was open for 16% -> 0% of each run, Pallas kernels for 0% -> 16%
where the time goes in v2:
time: 122 us
  waiting for transfers between devices  44.4 us (36%)
  starting transfers between devices  40.9 us (34%)
  Pallas kernels  31.5 us (26%)
  local copies, waits for them, and re-layouts  3.72 us (3%)
  between operations  1.44 us (1%)
    pallas_call x10, Pallas kernels, call(): pl.pallas_call(kernel, out_shape=outs, in_specs=[VMEM] * len(args), out_s...  31.5 us
    ppermute x9, waiting for transfers between devices, to_query(): return lax.ppermute(value, AXES, query_move(step))  19.4 us
    ppermute x9, waiting for transfers between devices, to_key(): return lax.ppermute(value, AXES, key_move(step))  15.7 us
    ppermute x9, starting transfers between devices, to_key(): return lax.ppermute(value, AXES, key_move(step))  14.6 us
    ppermute x9, starting transfers between devices, to_query(): return lax.ppermute(value, AXES, query_move(step))  10.9 us
    all_to_all x1, starting transfers between devices, shards(): back = lax.all_to_all(back, ('x', 'c'), 0, 0, tiled=True)  9.64 us
    all_to_all x1, waiting for transfers between devices, shards(): back = lax.all_to_all(back, ('x', 'c'), 0, 0, tiled=True)  9.36 us
    all_to_all x1, starting transfers between devices, shards(): moved = lax.all_to_all(packed, ('x', 'c'), 0, 0, tiled=True)  5.8 us
  transfers between devices with their start and end apart: 20, of which 14 were waited for; matrix products, arithmetic and copies ran while one was open for 0% of the time, Pallas kernels for 16%

profile of v2, /device:TPU:1, one launch (start us, length us, event | category | flops | bytes accessed | tf_op | source)
XLA Modules:
  0.0 122.1 jit_solution(1422708656555229080)
XLA Ops:
  1.6 0.9 copy-done.1
  4.3 1.0 shard_map.110
  5.3 5.8 %all-to-all-start = ((bf16[8,128,384]{2,1,0:T(8,128)(2,1)}), bf16[8,128,384]{2,1,0:T(8,128)(2,1)S(1)}, u32[]{:S(2)}, u32[]{:S(2)}) async-start(bf16[8,128,384]{2,1,0:T(8,128)(2,1)} %shard_map.110), calls=%async_computation | async-start | bytes 1572864 | tf_op jit(solution)/shard_map/all_to_all | solution.py:358
  12.0 3.7 %collective-permute-start.2 = (bf16[528,384]{1,0:T(8,128)(2,1)S(1)}, bf16[528,384]{1,0:T(8,128)(2,1)S(1)}, u32[]{:S(2)}, u32[]{:S(2)}) collective-permute-start(bf16[528,384]{1,0:T(8,128)(2,1)S(1)} %maximum_maximum_fusion.refs_3_.refs_4_.refs_1_), channel_id=1, source_target_pairs={{0,16},{1,65},{2,18},{3,67},{4,20},{5,69},{6,22},{7,71},{8,24},{9,... | collective-permute-start | bytes 1216520 | tf_op jit(solution)/shard_map/ppermute | solution.py:345
  16.1 1.0 collective-permute-start
  17.1 4.0 %collective-permute-done.2.refs_7_.refs_1_ = bf16[528,384]{1,0:T(8,128)(2,1)S(1)} collective-permute-done((bf16[528,384]{1,0:T(8,128)(2,1)S(1)}, bf16[528,384]{1,0:T(8,128)(2,1)S(1)}, u32[]{:S(2)}, u32[]{:S(2)}) %collective-permute-start.2) | collective-permute-done | bytes 405536 | tf_op jit(solution)/shard_map/ppermute | solution.py:345
  21.1 5.0 %collective-permute-done.1.refs_5_.refs_6_.refs_3_ = bf16[528,384]{1,0:T(8,128)(2,1)S(1)} collective-permute-done((bf16[528,384]{1,0:T(8,128)(2,1)S(1)}, bf16[528,384]{1,0:T(8,128)(2,1)S(1)}, u32[]{:S(2)}, u32[]{:S(2)}) %collective-permute-start.1) | collective-permute-done | bytes 405536 | tf_op jit(solution)/shard_map/ppermute | solution.py:345
  26.1 2.7 %collective-permute-start.7 = (bf16[2,256,384]{2,1,0:T(8,128)(2,1)S(1)}, bf16[2,256,384]{2,1,0:T(8,128)(2,1)S(1)}, u32[]{:S(2)}, u32[]{:S(2)}) collective-permute-start(bf16[2,256,384]{2,1,0:T(8,128)(2,1)S(1)} %get-tuple-element.28.refs_0_), channel_id=1, source_target_pairs={{0,24},{1,97},{2,26},{3,99},{4,28},{5,101},{6,30},{7,103},{8,0},{9... | collective-permute-start | bytes 1179656 | tf_op jit(solution)/shard_map/ppermute | solution.py:345
  28.8 2.7 %collective-permute-start.4 = (bf16[2,256,384]{2,1,0:T(8,128)(2,1)S(1)}, bf16[2,256,384]{2,1,0:T(8,128)(2,1)S(1)}, u32[]{:S(2)}, u32[]{:S(2)}) collective-permute-start(bf16[2,256,384]{2,1,0:T(8,128)(2,1)S(1)} %get-tuple-element.30.refs_6_.refs_8_.refs_2_.refs_4_), channel_id=1, source_target_pairs={{0,96},{1,25},{2,98},{3,27},{4,100},{5,29},{6,102},{7,31},{8,104},... | collective-permute-start | bytes 1179656 | tf_op jit(solution)/shard_map/ppermute | solution.py:348
  31.6 1.3 %collective-permute-start.8 = (bf16[2,256,384]{2,1,0:T(8,128)(2,1)S(1)}, bf16[2,256,384]{2,1,0:T(8,128)(2,1)S(1)}, u32[]{:S(2)}, u32[]{:S(2)}) collective-permute-start(bf16[2,256,384]{2,1,0:T(8,128)(2,1)S(1)} %get-tuple-element.28.refs_0_), channel_id=1, source_target_pairs={{0,16},{1,65},{2,18},{3,67},{4,20},{5,69},{6,22},{7,71},{8,24},{9,... | collective-permute-start | bytes 1179656 | tf_op jit(solution)/shard_map/ppermute | solution.py:345
  32.9 1.2 collective-permute-done.7.refs_2_.refs_1_
  34.1 3.9 %collective-permute-start.5 = (bf16[2,256,384]{2,1,0:T(8,128)(2,1)S(1)}, bf16[2,256,384]{2,1,0:T(8,128)(2,1)S(1)}, u32[]{:S(2)}, u32[]{:S(2)}) collective-permute-start(bf16[2,256,384]{2,1,0:T(8,128)(2,1)S(1)} %get-tuple-element.30.refs_6_.refs_8_.refs_2_.refs_4_), channel_id=1, source_target_pairs={{0,64},{1,17},{2,66},{3,19},{4,68},{5,21},{6,70},{7,23},{8,72},{9,... | collective-permute-start | bytes 1179656 | tf_op jit(solution)/shard_map/ppermute | solution.py:348
  38.0 1.3 %collective-permute-done.6.refs_1_.refs_0_ = bf16[2,256,384]{2,1,0:T(8,128)(2,1)S(1)} collective-permute-done((bf16[2,256,384]{2,1,0:T(8,128)(2,1)S(1)}, bf16[2,256,384]{2,1,0:T(8,128)(2,1)S(1)}, u32[]{:S(2)}, u32[]{:S(2)}) %collective-permute-start.6) | collective-permute-done | bytes 393248 | tf_op jit(solution)/shard_map/ppermute | solution.py:345
  39.2 7.3 %collective-permute-done.4.refs_8_.refs_10_.refs_4_.refs_6_ = bf16[2,256,384]{2,1,0:T(8,128)(2,1)S(1)} collective-permute-done((bf16[2,256,384]{2,1,0:T(8,128)(2,1)S(1)}, bf16[2,256,384]{2,1,0:T(8,128)(2,1)S(1)}, u32[]{:S(2)}, u32[]{:S(2)}) %collective-permute-start.4) | collective-permute-done | bytes 393248 | tf_op jit(solution)/shard_map/ppermute | solution.py:348
  46.5 3.4 %collective-permute-done.3.refs_7_.refs_9_.refs_3_.refs_5_ = bf16[2,256,384]{2,1,0:T(8,128)(2,1)S(1)} collective-permute-done((bf16[2,256,384]{2,1,0:T(8,128)(2,1)S(1)}, bf16[2,256,384]{2,1,0:T(8,128)(2,1)S(1)}, u32[]{:S(2)}, u32[]{:S(2)}) %collective-permute-start.3) | collective-permute-done | bytes 393248 | tf_op jit(solution)/shard_map/ppermute | solution.py:348
  49.9 5.2 %shard_map.112.refs_12_ = f32[3,16,256]{2,1,0:T(8,128)S(1)} custom-call(bf16[2,256,384]{2,1,0:T(8,128)(2,1)S(1)} %get-tuple-element.28.refs_0_, bf16[2,256,384]{2,1,0:T(8,128)(2,1)S(1)} %collective-permute-done.6.refs_1_.refs_0_, bf16[2,256,384]{2,1,0:T(8,128)(2,1)S(1)} %collective-permute-done.7.refs_2_.refs_1_, ...), custom_call_target="tpu_custom_call" | custom-call | flops 56623104 | bytes 55872 | tf_op jit(solution)/shard_map/pallas_call | solution.py:33
  55.1 4.5 %shard_map.113.refs_6_.refs_8_ = f32[3,16,256]{2,1,0:T(8,128)S(1)} custom-call(bf16[2,256,384]{2,1,0:T(8,128)(2,1)S(1)} %get-tuple-element.28.refs_0_, bf16[2,256,384]{2,1,0:T(8,128)(2,1)S(1)} %collective-permute-done.6.refs_1_.refs_0_, bf16[2,256,384]{2,1,0:T(8,128)(2,1)S(1)} %collective-permute-done.7.refs_2_.refs_1_, ...), custom_call_target="tpu_custom_call" | custom-call | flops 44040192 | bytes 75264 | tf_op jit(solution)/shard_map/pallas_call | solution.py:33
  59.8 1.5 %collective-permute-start.9 = (f32[3,16,256]{2,1,0:T(8,128)S(1)}, f32[3,16,256]{2,1,0:T(8,128)S(1)}, u32[]{:S(2)}, u32[]{:S(2)}) collective-permute-start(f32[3,16,256]{2,1,0:T(8,128)S(1)} %shard_map.113.refs_6_.refs_8_), channel_id=1, source_target_pairs={{0,32},{1,9},{2,34},{3,11},{4,36},{5,13},{6,38},{7,15},{8,40},{9,1... | collective-permute-start | bytes 147464 | tf_op jit(solution)/shard_map/ppermute | solution.py:348
  61.2 2.9 %collective-permute-done.11.refs_9_.refs_11_ = f32[3,16,256]{2,1,0:T(8,128)S(1)} collective-permute-done((f32[3,16,256]{2,1,0:T(8,128)S(1)}, f32[3,16,256]{2,1,0:T(8,128)S(1)}, u32[]{:S(2)}, u32[]{:S(2)}) %collective-permute-start.11) | collective-permute-done | bytes 49184 | tf_op jit(solution)/shard_map/ppermute | solution.py:348
  64.7 4.6 %shard_map.114 = (bf16[4,256,384]{2,1,0:T(8,128)(2,1)S(1)}, f32[3,128,1024]{2,1,0:T(8,128)S(1)}) custom-call(bf16[2,256,384]{2,1,0:T(8,128)(2,1)S(1)} %collective-permute-done.8.refs_3_.refs_0_, bf16[528,384]{1,0:T(8,128)(2,1)S(1)} %collective-permute-done.2.refs_7_.refs_1_, bf16[2,256,384]{2,1,0:T(8,128)(2,1)S(1)} %get-tuple-element.30.refs_6_.refs_8_.refs_2_.refs_4_, ...), custom_call_target="tpu_custom_call" | custom-call | flops 62914560 | bytes 40128 | tf_op jit(solution)/shard_map/pallas_call | solution.py:33
  69.3 3.9 %collective-permute-start.12 = (bf16[4,256,384]{2,1,0:T(8,128)(2,1)S(1)}, bf16[4,256,384]{2,1,0:T(8,128)(2,1)S(1)}, u32[]{:S(2)}, u32[]{:S(2)}) collective-permute-start(bf16[4,256,384]{2,1,0:T(8,128)(2,1)S(1)} %get-tuple-element.36), channel_id=1, source_target_pairs={{0,16},{1,65},{2,18},{3,67},{4,20},{5,69},{6,22},{7,71},{8,24},{9,... | collective-permute-start | bytes 2359304 | tf_op jit(solution)/shard_map/ppermute | solution.py:345
  73.2 8.7 %shard_map.115 = (bf16[4,256,384]{2,1,0:T(8,128)(2,1)S(1)}, bf16[4,256,384]{2,1,0:T(8,128)(2,1)S(1)}, f32[3,128,1024]{2,1,0:T(8,128)S(1)}) custom-call(bf16[2,256,384]{2,1,0:T(8,128)(2,1)S(1)} %collective-permute-done.6.refs_1_.refs_0_, bf16[2,256,384]{2,1,0:T(8,128)(2,1)S(1)} %collective-permute-done.7.refs_2_.refs_1_, ...), custom_call_target="tpu_custom_call" | custom-call | flops 125829120 | bytes 77184 | tf_op jit(solution)/shard_map/pallas_call | solution.py:33
  83.4 4.7 %shard_map.116 = (bf16[4,256,384]{2,1,0:T(8,128)(2,1)S(1)}, bf16[256,384]{1,0:T(8,128)(2,1)S(1)}, bf16[256,384]{1,0:T(8,128)(2,1)S(1)}, bf16[256,384]{1,0:T(8,128)(2,1)S(1)}, bf16[256,384]{1,0:T(8,128)(2,1)S(1)}) custom-call(bf16[2,256,384]{2,1,0:T(8,128)(2,1)S(1)} %get-tuple-element.28.refs_0_, ...), custom_call_target="tpu_custom_call" | custom-call | flops 62914560 | bytes 76992 | tf_op jit(solution)/shard_map/pallas_call | solution.py:33
  88.1 1.3 %collective-permute-start.13 = (bf16[256,384]{1,0:T(8,128)(2,1)S(1)}, bf16[256,384]{1,0:T(8,128)(2,1)S(1)}, u32[]{:S(2)}, u32[]{:S(2)}) collective-permute-start(bf16[256,384]{1,0:T(8,128)(2,1)S(1)} %get-tuple-element.38), channel_id=1, source_target_pairs={{0,96},{1,25},{2,98},{3,27},{4,100},{5,29},{6,102},{7,31},{8,104},... | collective-permute-start | bytes 589832 | tf_op jit(solution)/shard_map/ppermute | solution.py:348
  89.7 1.1 collective-permute-start.15
  90.7 2.3 %collective-permute-done.16.refs_5_.refs_1_ = bf16[4,256,384]{2,1,0:T(8,128)(2,1)S(1)} collective-permute-done((bf16[4,256,384]{2,1,0:T(8,128)(2,1)S(1)}, bf16[4,256,384]{2,1,0:T(8,128)(2,1)S(1)}, u32[]{:S(2)}, u32[]{:S(2)}) %collective-permute-start.16) | collective-permute-done | bytes 786464 | tf_op jit(solution)/shard_map/ppermute | solution.py:345
  93.1 2.0 %collective-permute-done.17.refs_6_.refs_2_ = bf16[4,256,384]{2,1,0:T(8,128)(2,1)S(1)} collective-permute-done((bf16[4,256,384]{2,1,0:T(8,128)(2,1)S(1)}, bf16[4,256,384]{2,1,0:T(8,128)(2,1)S(1)}, u32[]{:S(2)}, u32[]{:S(2)}) %collective-permute-start.17) | collective-permute-done | bytes 786464 | tf_op jit(solution)/shard_map/ppermute | solution.py:345
  95.2 3.9 %collective-permute-done.14.refs_2_ = bf16[256,384]{1,0:T(8,128)(2,1)S(1)} collective-permute-done((bf16[256,384]{1,0:T(8,128)(2,1)S(1)}, bf16[256,384]{1,0:T(8,128)(2,1)S(1)}, u32[]{:S(2)}, u32[]{:S(2)}) %collective-permute-start.14) | collective-permute-done | bytes 196640 | tf_op jit(solution)/shard_map/ppermute | solution.py:348
  99.1 1.2 collective-permute-done.15.refs_3_
  100.3 1.1 shard_map.117
  101.4 9.6 %all-to-all-start.1 = ((bf16[8,96,384]{2,1,0:T(8,128)(2,1)}), bf16[8,96,384]{2,1,0:T(8,128)(2,1)S(1)}, u32[]{:S(2)}, u32[]{:S(2)}) async-start(bf16[8,96,384]{2,1,0:T(8,128)(2,1)} %shard_map.117), calls=%async_computation.1 | async-start | bytes 1179648 | tf_op jit(solution)/shard_map/all_to_all | solution.py:379
  111.8 9.4 %all-to-all-done.1.ref = bf16[8,96,384]{2,1,0:T(8,128)(2,1)S(1)} async-done(((bf16[8,96,384]{2,1,0:T(8,128)(2,1)}), bf16[8,96,384]{2,1,0:T(8,128)(2,1)S(1)}, u32[]{:S(2)}, u32[]{:S(2)}) %all-to-all-start.1) | async-done | bytes 589856 | tf_op jit(solution)/shard_map/all_to_all | solution.py:379
  (33 shorter events, 7.7 us)
Async XLA Ops:
  0.6 0.9 copy-start
  1.6 0.9 copy-start.1
  2.5 0.9 copy-start.2
  3.4 0.9 copy-start.3
  4.3 7.5 %copy-start.4 = (bf16[256,384]{1,0:T(8,128)(2,1)S(1)}, bf16[256,384]{1,0:T(8,128)(2,1)}, u32[]{:S(2)}) copy-start(bf16[256,384]{1,0:T(8,128)(2,1)} %param.12) | copy-start | bytes 589828
  4.3 7.5 %copy-start.5 = (bf16[256,384]{1,0:T(8,128)(2,1)S(1)}, bf16[256,384]{1,0:T(8,128)(2,1)}, u32[]{:S(2)}) copy-start(bf16[256,384]{1,0:T(8,128)(2,1)} %param.11) | copy-start | bytes 589828
  5.3 20.7 %all-to-all-start = ((bf16[8,128,384]{2,1,0:T(8,128)(2,1)}), bf16[8,128,384]{2,1,0:T(8,128)(2,1)S(1)}, u32[]{:S(2)}, u32[]{:S(2)}) async-start(bf16[8,128,384]{2,1,0:T(8,128)(2,1)} %shard_map.110), calls=%async_computation | async-start | bytes 1572864 | tf_op jit(solution)/shard_map/all_to_all | solution.py:358
  12.0 9.1 %collective-permute-start.2 = (bf16[528,384]{1,0:T(8,128)(2,1)S(1)}, bf16[528,384]{1,0:T(8,128)(2,1)S(1)}, u32[]{:S(2)}, u32[]{:S(2)}) collective-permute-start(bf16[528,384]{1,0:T(8,128)(2,1)S(1)} %maximum_maximum_fusion.refs_3_.refs_4_.refs_1_), channel_id=1, source_target_pairs={{0,16},{1,65},{2,18},{3,67},{4,20},{5,69},{6,22},{7,71},{8,24},{9,... | collective-permute-start | bytes 1216520 | tf_op jit(solution)/shard_map/ppermute | solution.py:345
  15.6 10.4 %collective-permute-start.1 = (bf16[528,384]{1,0:T(8,128)(2,1)S(1)}, bf16[528,384]{1,0:T(8,128)(2,1)S(1)}, u32[]{:S(2)}, u32[]{:S(2)}) collective-permute-start(bf16[528,384]{1,0:T(8,128)(2,1)S(1)} %maximum_maximum_fusion.refs_3_.refs_4_.refs_1_), channel_id=1, source_target_pairs={{0,24},{1,97},{2,26},{3,99},{4,28},{5,101},{6,30},{7,103},{8,0},{9... | collective-permute-start | bytes 1216520 | tf_op jit(solution)/shard_map/ppermute | solution.py:345
  16.1 10.0 %collective-permute-start = (bf16[528,384]{1,0:T(8,128)(2,1)S(1)}, bf16[528,384]{1,0:T(8,128)(2,1)S(1)}, u32[]{:S(2)}, u32[]{:S(2)}) collective-permute-start(bf16[528,384]{1,0:T(8,128)(2,1)S(1)} %maximum_maximum_fusion.refs_3_.refs_4_.refs_1_), channel_id=1, source_target_pairs={{0,8},{1,33},{2,10},{3,35},{4,12},{5,37},{6,14},{7,39},{8,16},{9,4... | collective-permute-start | bytes 1216520 | tf_op jit(solution)/shard_map/ppermute | solution.py:345
  26.1 7.9 %collective-permute-start.7 = (bf16[2,256,384]{2,1,0:T(8,128)(2,1)S(1)}, bf16[2,256,384]{2,1,0:T(8,128)(2,1)S(1)}, u32[]{:S(2)}, u32[]{:S(2)}) collective-permute-start(bf16[2,256,384]{2,1,0:T(8,128)(2,1)S(1)} %get-tuple-element.28.refs_0_), channel_id=1, source_target_pairs={{0,24},{1,97},{2,26},{3,99},{4,28},{5,101},{6,30},{7,103},{8,0},{9... | collective-permute-start | bytes 1179656 | tf_op jit(solution)/shard_map/ppermute | solution.py:345
  28.8 10.4 %collective-permute-start.6 = (bf16[2,256,384]{2,1,0:T(8,128)(2,1)S(1)}, bf16[2,256,384]{2,1,0:T(8,128)(2,1)S(1)}, u32[]{:S(2)}, u32[]{:S(2)}) collective-permute-start(bf16[2,256,384]{2,1,0:T(8,128)(2,1)S(1)} %get-tuple-element.28.refs_0_), channel_id=1, source_target_pairs={{0,8},{1,33},{2,10},{3,35},{4,12},{5,37},{6,14},{7,39},{8,16},{9,4... | collective-permute-start | bytes 1179656 | tf_op jit(solution)/shard_map/ppermute | solution.py:345
  28.8 17.7 %collective-permute-start.4 = (bf16[2,256,384]{2,1,0:T(8,128)(2,1)S(1)}, bf16[2,256,384]{2,1,0:T(8,128)(2,1)S(1)}, u32[]{:S(2)}, u32[]{:S(2)}) collective-permute-start(bf16[2,256,384]{2,1,0:T(8,128)(2,1)S(1)} %get-tuple-element.30.refs_6_.refs_8_.refs_2_.refs_4_), channel_id=1, source_target_pairs={{0,96},{1,25},{2,98},{3,27},{4,100},{5,29},{6,102},{7,31},{8,104},... | collective-permute-start | bytes 1179656 | tf_op jit(solution)/shard_map/ppermute | solution.py:348
  31.6 18.3 %collective-permute-start.3 = (bf16[2,256,384]{2,1,0:T(8,128)(2,1)S(1)}, bf16[2,256,384]{2,1,0:T(8,128)(2,1)S(1)}, u32[]{:S(2)}, u32[]{:S(2)}) collective-permute-start(bf16[2,256,384]{2,1,0:T(8,128)(2,1)S(1)} %get-tuple-element.30.refs_6_.refs_8_.refs_2_.refs_4_), channel_id=1, source_target_pairs={{0,32},{1,9},{2,34},{3,11},{4,36},{5,13},{6,38},{7,15},{8,40},{9,1... | collective-permute-start | bytes 1179656 | tf_op jit(solution)/shard_map/ppermute | solution.py:348
  31.6 23.5 %collective-permute-start.8 = (bf16[2,256,384]{2,1,0:T(8,128)(2,1)S(1)}, bf16[2,256,384]{2,1,0:T(8,128)(2,1)S(1)}, u32[]{:S(2)}, u32[]{:S(2)}) collective-permute-start(bf16[2,256,384]{2,1,0:T(8,128)(2,1)S(1)} %get-tuple-element.28.refs_0_), channel_id=1, source_target_pairs={{0,16},{1,65},{2,18},{3,67},{4,20},{5,69},{6,22},{7,71},{8,24},{9,... | collective-permute-start | bytes 1179656 | tf_op jit(solution)/shard_map/ppermute | solution.py:345
  34.1 21.0 %collective-permute-start.5 = (bf16[2,256,384]{2,1,0:T(8,128)(2,1)S(1)}, bf16[2,256,384]{2,1,0:T(8,128)(2,1)S(1)}, u32[]{:S(2)}, u32[]{:S(2)}) collective-permute-start(bf16[2,256,384]{2,1,0:T(8,128)(2,1)S(1)} %get-tuple-element.30.refs_6_.refs_8_.refs_2_.refs_4_), channel_id=1, source_target_pairs={{0,64},{1,17},{2,66},{3,19},{4,68},{5,21},{6,70},{7,23},{8,72},{9,... | collective-permute-start | bytes 1179656 | tf_op jit(solution)/shard_map/ppermute | solution.py:348
  59.6 4.5 %collective-permute-start.11 = (f32[3,16,256]{2,1,0:T(8,128)S(1)}, f32[3,16,256]{2,1,0:T(8,128)S(1)}, u32[]{:S(2)}, u32[]{:S(2)}) collective-permute-start(f32[3,16,256]{2,1,0:T(8,128)S(1)} %shard_map.113.refs_6_.refs_8_), channel_id=1, source_target_pairs={{0,64},{1,17},{2,66},{3,19},{4,68},{5,21},{6,70},{7,23},{8,72},{9,... | collective-permute-start | bytes 147464 | tf_op jit(solution)/shard_map/ppermute | solution.py:348
  59.7 4.5 %collective-permute-start.10 = (f32[3,16,256]{2,1,0:T(8,128)S(1)}, f32[3,16,256]{2,1,0:T(8,128)S(1)}, u32[]{:S(2)}, u32[]{:S(2)}) collective-permute-start(f32[3,16,256]{2,1,0:T(8,128)S(1)} %shard_map.113.refs_6_.refs_8_), channel_id=1, source_target_pairs={{0,96},{1,25},{2,98},{3,27},{4,100},{5,29},{6,102},{7,31},{8,104},... | collective-permute-start | bytes 147464 | tf_op jit(solution)/shard_map/ppermute | solution.py:348
  59.8 4.9 %collective-permute-start.9 = (f32[3,16,256]{2,1,0:T(8,128)S(1)}, f32[3,16,256]{2,1,0:T(8,128)S(1)}, u32[]{:S(2)}, u32[]{:S(2)}) collective-permute-start(f32[3,16,256]{2,1,0:T(8,128)S(1)} %shard_map.113.refs_6_.refs_8_), channel_id=1, source_target_pairs={{0,32},{1,9},{2,34},{3,11},{4,36},{5,13},{6,38},{7,15},{8,40},{9,1... | collective-permute-start | bytes 147464 | tf_op jit(solution)/shard_map/ppermute | solution.py:348
  69.3 14.1 %collective-permute-start.12 = (bf16[4,256,384]{2,1,0:T(8,128)(2,1)S(1)}, bf16[4,256,384]{2,1,0:T(8,128)(2,1)S(1)}, u32[]{:S(2)}, u32[]{:S(2)}) collective-permute-start(bf16[4,256,384]{2,1,0:T(8,128)(2,1)S(1)} %get-tuple-element.36), channel_id=1, source_target_pairs={{0,16},{1,65},{2,18},{3,67},{4,20},{5,69},{6,22},{7,71},{8,24},{9,... | collective-permute-start | bytes 2359304 | tf_op jit(solution)/shard_map/ppermute | solution.py:345
  81.9 11.2 %collective-permute-start.16 = (bf16[4,256,384]{2,1,0:T(8,128)(2,1)S(1)}, bf16[4,256,384]{2,1,0:T(8,128)(2,1)S(1)}, u32[]{:S(2)}, u32[]{:S(2)}) collective-permute-start(bf16[4,256,384]{2,1,0:T(8,128)(2,1)S(1)} %get-tuple-element.42), channel_id=1, source_target_pairs={{0,24},{1,97},{2,26},{3,99},{4,28},{5,101},{6,30},{7,103},{8,0},{9... | collective-permute-start | bytes 2359304 | tf_op jit(solution)/shard_map/ppermute | solution.py:345
  82.7 12.3 %collective-permute-start.17 = (bf16[4,256,384]{2,1,0:T(8,128)(2,1)S(1)}, bf16[4,256,384]{2,1,0:T(8,128)(2,1)S(1)}, u32[]{:S(2)}, u32[]{:S(2)}) collective-permute-start(bf16[4,256,384]{2,1,0:T(8,128)(2,1)S(1)} %get-tuple-element.43), channel_id=1, source_target_pairs={{0,8},{1,33},{2,10},{3,35},{4,12},{5,37},{6,14},{7,39},{8,16},{9,4... | collective-permute-start | bytes 2359304 | tf_op jit(solution)/shard_map/ppermute | solution.py:345
  88.1 7.0 %collective-permute-start.13 = (bf16[256,384]{1,0:T(8,128)(2,1)S(1)}, bf16[256,384]{1,0:T(8,128)(2,1)S(1)}, u32[]{:S(2)}, u32[]{:S(2)}) collective-permute-start(bf16[256,384]{1,0:T(8,128)(2,1)S(1)} %get-tuple-element.38), channel_id=1, source_target_pairs={{0,96},{1,25},{2,98},{3,27},{4,100},{5,29},{6,102},{7,31},{8,104},... | collective-permute-start | bytes 589832 | tf_op jit(solution)/shard_map/ppermute | solution.py:348
  89.4 9.7 %collective-permute-start.14 = (bf16[256,384]{1,0:T(8,128)(2,1)S(1)}, bf16[256,384]{1,0:T(8,128)(2,1)S(1)}, u32[]{:S(2)}, u32[]{:S(2)}) collective-permute-start(bf16[256,384]{1,0:T(8,128)(2,1)S(1)} %get-tuple-element.39), channel_id=1, source_target_pairs={{0,32},{1,9},{2,34},{3,11},{4,36},{5,13},{6,38},{7,15},{8,40},{9,1... | collective-permute-start | bytes 589832 | tf_op jit(solution)/shard_map/ppermute | solution.py:348
  89.7 10.7 %collective-permute-start.15 = (bf16[256,384]{1,0:T(8,128)(2,1)S(1)}, bf16[256,384]{1,0:T(8,128)(2,1)S(1)}, u32[]{:S(2)}, u32[]{:S(2)}) collective-permute-start(bf16[256,384]{1,0:T(8,128)(2,1)S(1)} %get-tuple-element.40), channel_id=1, source_target_pairs={{0,64},{1,17},{2,66},{3,19},{4,68},{5,21},{6,70},{7,23},{8,72},{9,... | collective-permute-start | bytes 589832 | tf_op jit(solution)/shard_map/ppermute | solution.py:348
  101.4 19.8 %all-to-all-start.1 = ((bf16[8,96,384]{2,1,0:T(8,128)(2,1)}), bf16[8,96,384]{2,1,0:T(8,128)(2,1)S(1)}, u32[]{:S(2)}, u32[]{:S(2)}) async-start(bf16[8,96,384]{2,1,0:T(8,128)(2,1)} %shard_map.117), calls=%async_computation.1 | async-start | bytes 1179648 | tf_op jit(solution)/shard_map/all_to_all | solution.py:379

commit v3 on v2

--- a/solution.py
+++ b/solution.py
@@ -13,6 +13,7 @@
 EXP2_SCALE = SCALE * math.log2(math.e)
 LOW = -1e30
 VMEM_LIMIT = 24 * 1024 * 1024
+PACK_LIMIT = 56 * 1024 * 1024
 AXES = ("z", "y", "x", "c")
 OFFSETS = (0, -1, 1, 2)
 F32 = jnp.float32
@@ -52,8 +53,21 @@
     return jnp.concatenate([bias] * (width // HS), axis=1)
 
 
-def wide(refs, which, lanes):
-    return jnp.concatenate([ref[which, :, lanes] for ref in refs], axis=0)
+def flatten(blocks):
+    return [a for block in blocks for a in (block if isinstance(block, list) else [block])]
+
+
+def regroup(refs, blocks):
+    refs = list(refs)
+    return [[refs.pop(0) for _ in block] if isinstance(block, list) else refs.pop(0) for block in blocks]
+
+
+def take(block, which, lanes):
+    return block[which][:, lanes] if isinstance(block, list) else block[which, :, lanes]
+
+
+def wide(blocks, which, lanes):
+    return jnp.concatenate([take(block, which, lanes) for block in blocks], axis=0)
 
 
 def stat_step(keys, values, queries, grads, state, bias):
@@ -71,20 +85,21 @@
 
 
 def stats_call(curs, hists, queries, groups, state_in=None):
-    nk, nq = len(curs), len(queries)
-    rows, feat = curs[0].shape[1:]
+    nk, nh, nq = len(flatten(curs)), len(hists), len(flatten(queries))
+    rows, feat = hists[0].shape[0] // 2 - 8, hists[0].shape[1]
     tokens = queries[0].shape[1]
     heads = feat // HS
 
     def kernel(*refs):
-        cur, hist, query = refs[:nk], refs[nk : 2 * nk], refs[2 * nk : 2 * nk + nq]
-        old, out = refs[2 * nk + nq], refs[-1]
+        cur, hist = regroup(refs[:nk], curs), refs[nk : nk + nh]
+        query = regroup(refs[nk + nh : nk + nh + nq], queries)
+        old, out = refs[nk + nh + nq], refs[-1]
 
         def step(head, _):
             lanes = head_lanes(head)
-            for blocks, key_blocks, fresh in groups:
+            for blocks, cur_blocks, hist_blocks, fresh in groups:
                 width = tokens * len(blocks)
-                queries = wide([query[b] for b in blocks], 0, lanes)
+                asked = wide([query[b] for b in blocks], 0, lanes)
                 grads = wide([query[b] for b in blocks], 1, lanes)
                 if fresh:
                     state = (
@@ -99,14 +114,15 @@
                         )
                         for i in range(3)
                     )
-                for kb in key_blocks:
+                for kb in cur_blocks:
                     state = stat_step(
-                        cur[kb][0, :, lanes], cur[kb][1, :, lanes], queries, grads, state, None
+                        take(cur[kb], 0, lanes), take(cur[kb], 1, lanes), asked, grads, state, None
                     )
+                for kb in hist_blocks:
                     state = stat_step(
                         hist[kb][0:rows, lanes],
                         hist[kb][rows : 2 * rows, lanes],
-                        queries,
+                        asked,
                         grads,
                         state,
                         dead_bias(hist[kb], rows, width),
@@ -120,9 +136,8 @@
 
         lax.fori_loop(0, heads, step, 0)
 
-    args = list(curs) + list(hists) + list(queries) + ([] if state_in is None else [state_in])
-    pairs = sum(len(b) * len(k) for b, k, _ in groups)
-    work = pairs * 2 * rows * tokens
+    args = flatten(curs) + list(hists) + flatten(queries) + ([] if state_in is None else [state_in])
+    work = sum(len(b) * (len(c) + len(h)) for b, c, h, _ in groups) * rows * tokens
     out = jax.ShapeDtypeStruct((3, 16, tokens), F32)
     return call(kernel, out, args, flops=2 * 2 * 2 * work * feat, exps=work * heads)
 
@@ -151,15 +166,17 @@
 
 def grads_call(curs, hists, queries, stats, sums_in=None, far=None):
     nk, nq = len(curs), len(queries)
-    rows, feat = curs[0].shape[1:]
+    rows, feat = hists[0].shape[0] // 2 - 8, hists[0].shape[1]
     tokens = queries[0].shape[1]
     heads = feat // HS
     width = nq * tokens
+    n_cur, n_query = len(flatten(curs)), len(flatten(queries))
     last = far is not None
 
     def kernel(*refs):
-        cur, hist, query = refs[:nk], refs[nk : 2 * nk], refs[2 * nk : 2 * nk + nq]
-        refs = refs[2 * nk + nq :]
+        cur, refs = regroup(refs[:n_cur], curs), refs[n_cur:]
+        hist, refs = refs[:nk], refs[nk:]
+        query, refs = regroup(refs[:n_query], queries), refs[n_query:]
         stat, refs = refs[:4], refs[4:]
         if sums_in is not None:
             old, refs = refs[0], refs[1:]
@@ -187,13 +204,13 @@
 
         def step(head, _):
             lanes = head_lanes(head)
-            queries, grads = wide(query, 0, lanes), wide(query, 1, lanes)
+            asked, grads = wide(query, 0, lanes), wide(query, 1, lanes)
             lift, shift = base[head, 0:1, :], delta[head, 0:1, :]
             total = None if sums_in is None else old[head]
             for kb in range(nk):
-                keys = cur[kb][0, :, lanes]
+                keys = take(cur[kb], 0, lanes)
                 score_a, grad_k, grad_v = part(
-                    keys, cur[kb][1, :, lanes], queries, grads, lift, shift, None
+                    keys, take(cur[kb], 1, lanes), asked, grads, lift, shift, None
                 )
                 store(kb, 0, lanes, grad_k)
                 store(kb, 1, lanes, grad_v)
@@ -201,7 +218,7 @@
                 score_b, grad_k, grad_v = part(
                     old_keys,
                     hist[kb][rows : 2 * rows, lanes],
-                    queries,
+                    asked,
                     grads,
                     lift,
                     shift,
@@ -229,7 +246,7 @@
         sums = [jax.ShapeDtypeStruct((tokens, feat), BF16)] * nq
     else:
         sums = [jax.ShapeDtypeStruct((heads, HS, width), F32)]
-    args = list(curs) + list(hists) + list(queries) + list(stats)
+    args = flatten(curs) + list(hists) + flatten(queries) + list(stats)
     args += [a for a in (sums_in, far) if a is not None]
     work = nk * 2 * rows * width
     outs = call(
@@ -243,30 +260,44 @@
     return list(outs[:nk]), list(outs[nk:])
 
 
-def pack_call(arrays, parts):
+def pack_call(arrays, key_hist, value_hist, hist_len, parts):
     rows, columns = arrays[0].shape
     feat = columns // parts
+    old = key_hist.shape[0]
+    n = len(arrays)
 
     def kernel(*refs):
-        out = refs[-1]
-        for i, ref in enumerate(refs[:-1]):
+        ins, (key_in, value_in, count), outs = refs[:n], refs[n : n + 3], refs[n + 3 :]
+        outs, (hist, held, sem) = outs[:-3], outs[-3:]
+        copies = [pltpu.make_async_copy(ref, held.at[i], sem.at[i]) for i, ref in enumerate(ins)]
+        copies.append(pltpu.make_async_copy(key_in, hist.at[pl.ds(0, old)], sem.at[n]))
+        copies.append(pltpu.make_async_copy(value_in, hist.at[pl.ds(old, old)], sem.at[n + 1]))
+        for copy in copies:
+            copy.start()
+        filled = jnp.full((16, feat), count[0], jnp.int32).astype(F32)
+        hist[2 * old :, :] = filled.astype(BF16)
+        for i in range(n):
+            copies[i].wait()
             for p in range(parts):
-                out[p, i * rows : (i + 1) * rows, :] = ref[:, p * feat : (p + 1) * feat]
-
-    shape = jax.ShapeDtypeStruct((parts, len(arrays) * rows, feat), BF16)
-    return call(kernel, shape, arrays)
-
-
-def unpack_call(array, count):
-    parts, rows, feat = array.shape
-    rows //= count
-
-    def kernel(ref, *outs):
-        for i, out in enumerate(outs):
-            for p in range(parts):
-                out[:, p * feat : (p + 1) * feat] = ref[p, i * rows : (i + 1) * rows, :]
-
-    return call(kernel, [jax.ShapeDtypeStruct((rows, parts * feat), BF16)] * count, [array])
+                outs[i // 2][p, i % 2 * rows : (i % 2 + 1) * rows, :] = held[
+                    i, :, p * feat : (p + 1) * feat
+                ]
+        copies[n].wait()
+        copies[n + 1].wait()
+
+    pair = jax.ShapeDtypeStruct((parts, 2 * rows, feat), BF16)
+    return pl.pallas_call(
+        kernel,
+        out_shape=[pair] * (n // 2) + [jax.ShapeDtypeStruct((2 * old + 16, feat), BF16)],
+        in_specs=[pl.BlockSpec(memory_space=pl.ANY)] * (n + 2)
+        + [pl.BlockSpec(memory_space=pltpu.SMEM)],
+        out_specs=[VMEM] * (n // 2 + 1),
+        scratch_shapes=[
+            pltpu.VMEM((n, rows, columns), BF16),
+            pltpu.SemaphoreType.DMA((n + 2,)),
+        ],
+        compiler_params=pltpu.CompilerParams(vmem_limit_bytes=PACK_LIMIT),
+    )(*arrays, key_hist, value_hist, hist_len)
 
 
 def split_call(array, count):
@@ -282,6 +313,18 @@
 
     block = jax.ShapeDtypeStruct((2, parts * rows, feat), BF16)
     return call(kernel, [block] * (count // 2), [array])
+
+
+def unpack_call(array, count):
+    parts, rows, feat = array.shape
+    rows //= count
+
+    def kernel(ref, *outs):
+        for i, out in enumerate(outs):
+            for p in range(parts):
+                out[:, p * feat : (p + 1) * feat] = ref[p, i * rows : (i + 1) * rows, :]
+
+    return call(kernel, [jax.ShapeDtypeStruct((rows, parts * feat), BF16)] * count, [array])
 
 
 def add_call(query_parts, cur_parts, parts):
@@ -324,16 +367,17 @@
             for y in range(ny):
                 for x in range(nx):
                     for c in range(nc):
-                        tz, ty = target(z, y, c)
+                        tz, ty, tx, tc = target(z, y, x, c)
                         src = ((z * ny + y) * nx + x) * nc + c
-                        pairs.append((src, (((tz % nz) * ny + ty % ny) * nx + x) * nc + c))
+                        dst = ((tz % nz) * ny + ty % ny) * nx + tx % nx
+                        pairs.append((src, dst * nc + tc % nc))
         return pairs
 
     def keys(step):
-        return table(lambda z, y, c: (z, y + step) if c == 0 else (z + step, y))
+        return table(lambda z, y, x, c: (z, y + step, x, c) if c == 0 else (z + step, y, x, c))
 
     def queries(step):
-        return table(lambda z, y, c: (z + step, y) if c == 0 else (z, y + step))
+        return table(lambda z, y, x, c: (z + step, y, x, c) if c == 0 else (z, y + step, x, c))
 
     return keys, queries
 
@@ -349,23 +393,20 @@
 
     def shards(query, key_cur, value_cur, d_out, key_hist, value_hist, hist_len):
         parts = sizes[2] * sizes[3]
-        feat = key_hist.shape[1]
-        count = jnp.broadcast_to(hist_len.astype(BF16)[:, None], (16, feat))
-        hist0 = jnp.concatenate([key_hist, value_hist, count], axis=0)
+        asked, kept, hist0 = pack_call(
+            [query, d_out, key_cur, value_cur], key_hist, value_hist, hist_len, parts
+        )
         hists = [hist0] + [to_key(hist0, -o) for o in OFFSETS[1:]]
-
-        packed = pack_call([query, d_out, key_cur, value_cur], parts)
-        moved = lax.all_to_all(packed, ("x", "c"), 0, 0, tiled=True)
-        moved, hists = lax.optimization_barrier((moved, hists))
-        query0, cur0 = split_call(moved, 4)
-
+        asked = lax.all_to_all(asked, ("x", "c"), 0, 0, tiled=True)
+        kept, asked = lax.optimization_barrier((kept, asked))
+        kept = lax.all_to_all(kept, ("x", "c"), 0, 0, tiled=True)
+        query0 = split_call(asked, 2)[0]
+        queries = [query0] + [to_query(query0, -o) for o in OFFSETS[1:]]
+        cur0 = split_call(kept, 2)[0]
         curs = [cur0] + [to_key(cur0, -o) for o in OFFSETS[1:]]
-        queries = [query0] + [to_query(query0, -o) for o in OFFSETS[1:]]
-        near = (0, 1, 2)
-        state = stats_call(curs[:3], hists[:3], queries[:3], [(near, near, True)])
-        state = stats_call(
-            curs, hists, queries, [(near, (3,), False), ((3,), (0, 1, 2, 3), True)], state
-        )
+        every = (0, 1, 2, 3)
+        state = stats_call(curs[:1], hists, queries, [(every, (0,), every, True)])
+        state = stats_call(curs, hists[:1], queries, [(every, (1, 2, 3), (), False)], state)
         stats = [state] + [to_query(state, -o) for o in OFFSETS[1:]]
 
         far, sums = grads_call(curs[3:], hists[3:], queries, stats)

time: 122 us -> 115 us (0.943)
  waiting for transfers between devices: 44.4 us -> 34.3 us
  starting transfers between devices: 40.9 us -> 43.3 us
  Pallas kernels: 31.5 us -> 33.4 us
  local copies, waits for them, and re-layouts: 3.72 us -> 2.03 us
    ppermute x9, waiting for transfers between devices: 19.4 us -> 9.05 us  [to_query(): return lax.ppermute(value, AXES, query_move(step))]
    all_to_all x1 -> x2, waiting for transfers between devices: 0.01 us -> 8.47 us  [the longest x1 5.46 us: shards(): kept = lax.all_to_all(kept, ('x', 'c'), 0, 0, tiled=True)]
    ppermute x9, waiting for transfers between devices: 15.7 us -> 8.56 us  [to_key(): return lax.ppermute(value, AXES, key_move(step))]
    all_to_all x1 -> x2, starting transfers between devices: 5.8 us -> 11.7 us  [the longest x1 5.94 us: shards(): asked = lax.all_to_all(asked, ('x', 'c'), 0, 0, tiled=True)]
    ppermute x9, starting transfers between devices: 14.6 us -> 11.6 us  [to_key(): return lax.ppermute(value, AXES, key_move(step))]
    pallas_call x0 -> x1, Pallas kernels: none -> 2.42 us  [pack_call(): pl.pallas_call(kernel, out_shape=[pair] * (n // 2) + [jax.ShapeDtypeStruc...]
    unnamed x12 -> x6, local copies, waits for them, and re-layouts: 3.71 us -> 2.03 us
    all_to_all x1, starting transfers between devices: 9.64 us -> 8 us  [shards(): back = lax.all_to_all(back, ('x', 'c'), 0, 0, tiled=True)]
  transfers between devices with their start and end apart: 20 -> 21, of which waited for: 14 -> 14; matrix products, arithmetic and copies ran while one was open for 0% -> 0% of each run, Pallas kernels for 16% -> 19%
where the time goes in v3:
time: 115 us; the launch traced here: 114 us
  starting transfers between devices  43.3 us (38%)
  waiting for transfers between devices  34.3 us (30%)
  Pallas kernels  33.4 us (29%)
  local copies, waits for them, and re-layouts  2.03 us (2%)
  between operations  1.4 us (1%)
    pallas_call x10, Pallas kernels, call(): pl.pallas_call(kernel, out_shape=outs, in_specs=[VMEM] * len(args), out_s...  30.9 us
    ppermute x9, starting transfers between devices, to_query(): return lax.ppermute(value, AXES, query_move(step))  11.9 us
    ppermute x9, starting transfers between devices, to_key(): return lax.ppermute(value, AXES, key_move(step))  11.6 us
    ppermute x9, waiting for transfers between devices, to_query(): return lax.ppermute(value, AXES, query_move(step))  9.05 us
    ppermute x9, waiting for transfers between devices, to_key(): return lax.ppermute(value, AXES, key_move(step))  8.56 us
    all_to_all x1, waiting for transfers between devices, shards(): back = lax.all_to_all(back, ('x', 'c'), 0, 0, tiled=True)  8.24 us
    all_to_all x1, starting transfers between devices, shards(): back = lax.all_to_all(back, ('x', 'c'), 0, 0, tiled=True)  8 us
    all_to_all x1, starting transfers between devices, shards(): asked = lax.all_to_all(asked, ('x', 'c'), 0, 0, tiled=True)  5.94 us
  transfers between devices with their start and end apart: 21, of which 14 were waited for; matrix products, arithmetic and copies ran while one was open for 0% of the time, Pallas kernels for 19%

profile of v3, /device:TPU:1, one launch (start us, length us, event | category | flops | bytes accessed | tf_op | source)
XLA Modules:
  0.0 114.4 jit_solution(11470701517746111903)
XLA Ops:
  1.3 2.4 %shard_map.110 = (bf16[8,64,384]{2,1,0:T(8,128)(2,1)}, bf16[8,64,384]{2,1,0:T(8,128)(2,1)}, bf16[528,384]{1,0:T(8,128)(2,1)}) custom-call(bf16[32,3072]{1,0:T(8,128)(2,1)} %refs_0_.1, bf16[32,3072]{1,0:T(8,128)(2,1)} %refs_1_.1, bf16[32,3072]{1,0:T(8,128)(2,1)} %refs_2_.1, bf16[32,3072]{1,0:T(8,128)(2,1)} %refs_3_.1, bf16[256,384]{1,0:T(8,128)(2,1)} %refs_4_.1, ...), custom_call_target="tpu_custom_call" | custom-call | tf_op jit(solution)/shard_map/pallas_call | solution.py:289
  3.7 5.9 %all-to-all-start = ((bf16[8,64,384]{2,1,0:T(8,128)(2,1)}), bf16[8,64,384]{2,1,0:T(8,128)(2,1)S(1)}, u32[]{:S(2)}, u32[]{:S(2)}) async-start(bf16[8,64,384]{2,1,0:T(8,128)(2,1)} %get-tuple-element.26), calls=%async_computation | async-start | bytes 786432 | tf_op jit(solution)/shard_map/all_to_all | solution.py:400
  9.7 3.6 %collective-permute-start.8 = (bf16[528,384]{1,0:T(8,128)(2,1)}, bf16[528,384]{1,0:T(8,128)(2,1)S(1)}, u32[]{:S(2)}, u32[]{:S(2)}) collective-permute-start(bf16[528,384]{1,0:T(8,128)(2,1)} %get-tuple-element.28.refs_1_.refs_4_), channel_id=1, source_target_pairs={{0,16},{1,65},{2,18},{3,67},{4,20},{5,69},{6,22},{7,71},{8,24},{9,... | collective-permute-start | bytes 1216520 | tf_op jit(solution)/shard_map/ppermute | solution.py:389
  13.7 1.0 collective-permute-start.6
  14.7 3.0 %all-to-all-done.ref = bf16[8,64,384]{2,1,0:T(8,128)(2,1)S(1)} async-done(((bf16[8,64,384]{2,1,0:T(8,128)(2,1)}), bf16[8,64,384]{2,1,0:T(8,128)(2,1)S(1)}, u32[]{:S(2)}, u32[]{:S(2)}) %all-to-all-start) | async-done | bytes 393248 | tf_op jit(solution)/shard_map/all_to_all | solution.py:400
  17.8 3.0 %collective-permute-start.2 = (bf16[2,256,384]{2,1,0:T(8,128)(2,1)S(1)}, bf16[2,256,384]{2,1,0:T(8,128)(2,1)S(1)}, u32[]{:S(2)}, u32[]{:S(2)}) collective-permute-start(bf16[2,256,384]{2,1,0:T(8,128)(2,1)S(1)} %shard_map.112.refs_5_.refs_2_.refs_4_), channel_id=1, source_target_pairs={{0,64},{1,17},{2,66},{3,19},{4,68},{5,21},{6,70},{7,23},{8,72},{9,... | collective-permute-start | bytes 1179656 | tf_op jit(solution)/shard_map/ppermute | solution.py:392
  20.8 5.8 %all-to-all-start.1 = ((bf16[8,64,384]{2,1,0:T(8,128)(2,1)}), bf16[8,64,384]{2,1,0:T(8,128)(2,1)}, u32[]{:S(2)}, u32[]{:S(2)}) async-start(bf16[8,64,384]{2,1,0:T(8,128)(2,1)} %get-tuple-element.27), calls=%async_computation.1 | async-start | bytes 786432 | tf_op jit(solution)/shard_map/all_to_all | solution.py:402
  26.6 2.7 %collective-permute-start.1 = (bf16[2,256,384]{2,1,0:T(8,128)(2,1)S(1)}, bf16[2,256,384]{2,1,0:T(8,128)(2,1)S(1)}, u32[]{:S(2)}, u32[]{:S(2)}) collective-permute-start(bf16[2,256,384]{2,1,0:T(8,128)(2,1)S(1)} %shard_map.112.refs_5_.refs_2_.refs_4_), channel_id=1, source_target_pairs={{0,96},{1,25},{2,98},{3,27},{4,100},{5,29},{6,102},{7,31},{8,104},... | collective-permute-start | bytes 1179656 | tf_op jit(solution)/shard_map/ppermute | solution.py:392
  29.3 5.5 %all-to-all-done.1.ref = bf16[8,64,384]{2,1,0:T(8,128)(2,1)} async-done(((bf16[8,64,384]{2,1,0:T(8,128)(2,1)}), bf16[8,64,384]{2,1,0:T(8,128)(2,1)}, u32[]{:S(2)}, u32[]{:S(2)}) %all-to-all-start.1) | async-done | bytes 393248 | tf_op jit(solution)/shard_map/all_to_all | solution.py:402
  34.8 1.0 shard_map.111.refs_0_
  36.2 2.8 %collective-permute-start.4 = (bf16[2,256,384]{2,1,0:T(8,128)(2,1)S(1)}, bf16[2,256,384]{2,1,0:T(8,128)(2,1)S(1)}, u32[]{:S(2)}, u32[]{:S(2)}) collective-permute-start(bf16[2,256,384]{2,1,0:T(8,128)(2,1)S(1)} %shard_map.111.refs_0_), channel_id=1, source_target_pairs={{0,24},{1,97},{2,26},{3,99},{4,28},{5,101},{6,30},{7,103},{8,0},{9... | collective-permute-start | bytes 1179656 | tf_op jit(solution)/shard_map/ppermute | solution.py:389
  39.1 6.1 %shard_map.113.refs_9_ = f32[3,16,256]{2,1,0:T(8,128)S(1)} custom-call(bf16[2,256,384]{2,1,0:T(8,128)(2,1)S(1)} %shard_map.111.refs_0_, bf16[528,384]{1,0:T(8,128)(2,1)S(1)} %copy-done, bf16[528,384]{1,0:T(8,128)(2,1)S(1)} %collective-permute-done.6.refs_2_, bf16[528,384]{1,0:T(8,128)(2,1)S(1)} %collective-permute-done.7.refs_3_, ...), custom_call_target="tpu_custom_call" | custom-call | flops 62914560 | bytes 56064 | tf_op jit(solution)/shard_map/pallas_call | solution.py:34
  45.1 1.5 %collective-permute-done.4.refs_2_.refs_1_ = bf16[2,256,384]{2,1,0:T(8,128)(2,1)S(1)} collective-permute-done((bf16[2,256,384]{2,1,0:T(8,128)(2,1)S(1)}, bf16[2,256,384]{2,1,0:T(8,128)(2,1)S(1)}, u32[]{:S(2)}, u32[]{:S(2)}) %collective-permute-start.4) | collective-permute-done | bytes 393248 | tf_op jit(solution)/shard_map/ppermute | solution.py:389
  46.7 1.9 %collective-permute-done.3.refs_1_.refs_0_ = bf16[2,256,384]{2,1,0:T(8,128)(2,1)S(1)} collective-permute-done((bf16[2,256,384]{2,1,0:T(8,128)(2,1)S(1)}, bf16[2,256,384]{2,1,0:T(8,128)(2,1)S(1)}, u32[]{:S(2)}, u32[]{:S(2)}) %collective-permute-start.3) | collective-permute-done | bytes 393248 | tf_op jit(solution)/shard_map/ppermute | solution.py:389
  48.5 3.3 %shard_map.114.refs_6_.refs_8_ = f32[3,16,256]{2,1,0:T(8,128)S(1)} custom-call(bf16[2,256,384]{2,1,0:T(8,128)(2,1)S(1)} %shard_map.111.refs_0_, bf16[2,256,384]{2,1,0:T(8,128)(2,1)S(1)} %collective-permute-done.3.refs_1_.refs_0_, bf16[2,256,384]{2,1,0:T(8,128)(2,1)S(1)} %collective-permute-done.4.refs_2_.refs_1_, ...), custom_call_target="tpu_custom_call" | custom-call | flops 37748736 | bytes 56256 | tf_op jit(solution)/shard_map/pallas_call | solution.py:34
  51.8 2.7 %collective-permute-start.11 = (f32[3,16,256]{2,1,0:T(8,128)S(1)}, f32[3,16,256]{2,1,0:T(8,128)S(1)}, u32[]{:S(2)}, u32[]{:S(2)}) collective-permute-start(f32[3,16,256]{2,1,0:T(8,128)S(1)} %shard_map.114.refs_6_.refs_8_), channel_id=1, source_target_pairs={{0,64},{1,17},{2,66},{3,19},{4,68},{5,21},{6,70},{7,23},{8,72},{9,... | collective-permute-start | bytes 147464 | tf_op jit(solution)/shard_map/ppermute | solution.py:392
  56.4 1.4 %collective-permute-done.10.refs_8_.refs_10_ = f32[3,16,256]{2,1,0:T(8,128)S(1)} collective-permute-done((f32[3,16,256]{2,1,0:T(8,128)S(1)}, f32[3,16,256]{2,1,0:T(8,128)S(1)}, u32[]{:S(2)}, u32[]{:S(2)}) %collective-permute-start.10) | collective-permute-done | bytes 49184 | tf_op jit(solution)/shard_map/ppermute | solution.py:392
  57.8 1.7 %collective-permute-done.9.refs_7_.refs_9_ = f32[3,16,256]{2,1,0:T(8,128)S(1)} collective-permute-done((f32[3,16,256]{2,1,0:T(8,128)S(1)}, f32[3,16,256]{2,1,0:T(8,128)S(1)}, u32[]{:S(2)}, u32[]{:S(2)}) %collective-permute-start.9) | collective-permute-done | bytes 49184 | tf_op jit(solution)/shard_map/ppermute | solution.py:392
  59.5 4.5 %shard_map.115 = (bf16[4,256,384]{2,1,0:T(8,128)(2,1)S(1)}, f32[3,128,1024]{2,1,0:T(8,128)S(1)}) custom-call(bf16[2,256,384]{2,1,0:T(8,128)(2,1)S(1)} %collective-permute-done.5.refs_3_.refs_0_, bf16[528,384]{1,0:T(8,128)(2,1)S(1)} %collective-permute-done.8.refs_4_.refs_1_, bf16[2,256,384]{2,1,0:T(8,128)(2,1)S(1)} %shard_map.112.refs_5_.refs_2_.refs_4_, ...), custom_call_target="tpu_custom_call" | custom-call | flops 62914560 | bytes 40128 | tf_op jit(solution)/shard_map/pallas_call | solution.py:34
  64.0 1.8 %collective-permute-start.12 = (bf16[4,256,384]{2,1,0:T(8,128)(2,1)S(1)}, bf16[4,256,384]{2,1,0:T(8,128)(2,1)S(1)}, u32[]{:S(2)}, u32[]{:S(2)}) collective-permute-start(bf16[4,256,384]{2,1,0:T(8,128)(2,1)S(1)} %get-tuple-element.32), channel_id=1, source_target_pairs={{0,16},{1,65},{2,18},{3,67},{4,20},{5,69},{6,22},{7,71},{8,24},{9,... | collective-permute-start | bytes 2359304 | tf_op jit(solution)/shard_map/ppermute | solution.py:389
  65.8 8.6 %shard_map.116 = (bf16[4,256,384]{2,1,0:T(8,128)(2,1)S(1)}, bf16[4,256,384]{2,1,0:T(8,128)(2,1)S(1)}, f32[3,128,1024]{2,1,0:T(8,128)S(1)}) custom-call(bf16[2,256,384]{2,1,0:T(8,128)(2,1)S(1)} %collective-permute-done.3.refs_1_.refs_0_, bf16[2,256,384]{2,1,0:T(8,128)(2,1)S(1)} %collective-permute-done.4.refs_2_.refs_1_, ...), custom_call_target="tpu_custom_call" | custom-call | flops 125829120 | bytes 77184 | tf_op jit(solution)/shard_map/pallas_call | solution.py:34
  74.4 1.1 collective-permute-start.16
  76.9 4.7 %shard_map.117 = (bf16[4,256,384]{2,1,0:T(8,128)(2,1)S(1)}, bf16[256,384]{1,0:T(8,128)(2,1)S(1)}, bf16[256,384]{1,0:T(8,128)(2,1)S(1)}, bf16[256,384]{1,0:T(8,128)(2,1)S(1)}, bf16[256,384]{1,0:T(8,128)(2,1)S(1)}) custom-call(bf16[2,256,384]{2,1,0:T(8,128)(2,1)S(1)} %shard_map.111.refs_0_, bf16[528,384]{1,0:T(8,128)(2,1)S(1)} %copy-done, ...), custom_call_target="tpu_custom_call" | custom-call | flops 62914560 | bytes 76992 | tf_op jit(solution)/shard_map/pallas_call | solution.py:34
  81.8 1.3 %collective-permute-start.14 = (bf16[256,384]{1,0:T(8,128)(2,1)S(1)}, bf16[256,384]{1,0:T(8,128)(2,1)S(1)}, u32[]{:S(2)}, u32[]{:S(2)}) collective-permute-start(bf16[256,384]{1,0:T(8,128)(2,1)S(1)} %get-tuple-element.35), channel_id=1, source_target_pairs={{0,32},{1,9},{2,34},{3,11},{4,36},{5,13},{6,38},{7,15},{8,40},{9,1... | collective-permute-start | bytes 589832 | tf_op jit(solution)/shard_map/ppermute | solution.py:392
  83.6 2.0 %collective-permute-done.16.refs_5_.refs_1_ = bf16[4,256,384]{2,1,0:T(8,128)(2,1)S(1)} collective-permute-done((bf16[4,256,384]{2,1,0:T(8,128)(2,1)S(1)}, bf16[4,256,384]{2,1,0:T(8,128)(2,1)S(1)}, u32[]{:S(2)}, u32[]{:S(2)}) %collective-permute-start.16) | collective-permute-done | bytes 786464 | tf_op jit(solution)/shard_map/ppermute | solution.py:389
  85.6 2.2 %collective-permute-done.17.refs_6_.refs_2_ = bf16[4,256,384]{2,1,0:T(8,128)(2,1)S(1)} collective-permute-done((bf16[4,256,384]{2,1,0:T(8,128)(2,1)S(1)}, bf16[4,256,384]{2,1,0:T(8,128)(2,1)S(1)}, u32[]{:S(2)}, u32[]{:S(2)}) %collective-permute-start.17) | collective-permute-done | bytes 786464 | tf_op jit(solution)/shard_map/ppermute | solution.py:389
  88.6 2.1 %collective-permute-done.14.refs_2_ = bf16[256,384]{1,0:T(8,128)(2,1)S(1)} collective-permute-done((bf16[256,384]{1,0:T(8,128)(2,1)S(1)}, bf16[256,384]{1,0:T(8,128)(2,1)S(1)}, u32[]{:S(2)}, u32[]{:S(2)}) %collective-permute-start.14) | collective-permute-done | bytes 196640 | tf_op jit(solution)/shard_map/ppermute | solution.py:392
  90.7 2.6 %collective-permute-done.15.refs_3_ = bf16[256,384]{1,0:T(8,128)(2,1)S(1)} collective-permute-done((bf16[256,384]{1,0:T(8,128)(2,1)S(1)}, bf16[256,384]{1,0:T(8,128)(2,1)S(1)}, u32[]{:S(2)}, u32[]{:S(2)}) %collective-permute-start.15) | collective-permute-done | bytes 196640 | tf_op jit(solution)/shard_map/ppermute | solution.py:392
  93.3 1.1 shard_map.118
  95.3 8.0 %all-to-all-start.2 = ((bf16[8,96,384]{2,1,0:T(8,128)(2,1)}), bf16[8,96,384]{2,1,0:T(8,128)(2,1)S(1)}, u32[]{:S(2)}, u32[]{:S(2)}) async-start(bf16[8,96,384]{2,1,0:T(8,128)(2,1)} %shard_map.118), calls=%async_computation.2 | async-start | bytes 1179648 | tf_op jit(solution)/shard_map/all_to_all | solution.py:420
  103.3 1.1 copy-done.2
  105.3 8.2 %all-to-all-done.2.ref = bf16[8,96,384]{2,1,0:T(8,128)(2,1)S(1)} async-done(((bf16[8,96,384]{2,1,0:T(8,128)(2,1)}), bf16[8,96,384]{2,1,0:T(8,128)(2,1)S(1)}, u32[]{:S(2)}, u32[]{:S(2)}) %all-to-all-start.2) | async-done | bytes 589856 | tf_op jit(solution)/shard_map/all_to_all | solution.py:420
  (27 shorter events, 8.4 us)
Async XLA Ops:
  3.7 35.4 %copy-start = (bf16[528,384]{1,0:T(8,128)(2,1)S(1)}, bf16[528,384]{1,0:T(8,128)(2,1)}, u32[]{:S(2)}) copy-start(bf16[528,384]{1,0:T(8,128)(2,1)} %get-tuple-element.28.refs_1_.refs_4_) | copy-start | bytes 1216516
  3.7 14.0 %all-to-all-start = ((bf16[8,64,384]{2,1,0:T(8,128)(2,1)}), bf16[8,64,384]{2,1,0:T(8,128)(2,1)S(1)}, u32[]{:S(2)}, u32[]{:S(2)}) async-start(bf16[8,64,384]{2,1,0:T(8,128)(2,1)} %get-tuple-element.26), calls=%async_computation | async-start | bytes 786432 | tf_op jit(solution)/shard_map/all_to_all | solution.py:400
  9.7 19.7 %collective-permute-start.8 = (bf16[528,384]{1,0:T(8,128)(2,1)}, bf16[528,384]{1,0:T(8,128)(2,1)S(1)}, u32[]{:S(2)}, u32[]{:S(2)}) collective-permute-start(bf16[528,384]{1,0:T(8,128)(2,1)} %get-tuple-element.28.refs_1_.refs_4_), channel_id=1, source_target_pairs={{0,16},{1,65},{2,18},{3,67},{4,20},{5,69},{6,22},{7,71},{8,24},{9,... | collective-permute-start | bytes 1216520 | tf_op jit(solution)/shard_map/ppermute | solution.py:389
  13.3 22.6 %collective-permute-start.7 = (bf16[528,384]{1,0:T(8,128)(2,1)}, bf16[528,384]{1,0:T(8,128)(2,1)S(1)}, u32[]{:S(2)}, u32[]{:S(2)}) collective-permute-start(bf16[528,384]{1,0:T(8,128)(2,1)} %get-tuple-element.28.refs_1_.refs_4_), channel_id=1, source_target_pairs={{0,24},{1,97},{2,26},{3,99},{4,28},{5,101},{6,30},{7,103},{8,0},{9... | collective-permute-start | bytes 1216520 | tf_op jit(solution)/shard_map/ppermute | solution.py:389
  13.7 22.5 %collective-permute-start.6 = (bf16[528,384]{1,0:T(8,128)(2,1)}, bf16[528,384]{1,0:T(8,128)(2,1)S(1)}, u32[]{:S(2)}, u32[]{:S(2)}) collective-permute-start(bf16[528,384]{1,0:T(8,128)(2,1)} %get-tuple-element.28.refs_1_.refs_4_), channel_id=1, source_target_pairs={{0,8},{1,33},{2,10},{3,35},{4,12},{5,37},{6,14},{7,39},{8,16},{9,4... | collective-permute-start | bytes 1216520 | tf_op jit(solution)/shard_map/ppermute | solution.py:389
  17.8 21.3 %collective-permute-start.2 = (bf16[2,256,384]{2,1,0:T(8,128)(2,1)S(1)}, bf16[2,256,384]{2,1,0:T(8,128)(2,1)S(1)}, u32[]{:S(2)}, u32[]{:S(2)}) collective-permute-start(bf16[2,256,384]{2,1,0:T(8,128)(2,1)S(1)} %shard_map.112.refs_5_.refs_2_.refs_4_), channel_id=1, source_target_pairs={{0,64},{1,17},{2,66},{3,19},{4,68},{5,21},{6,70},{7,23},{8,72},{9,... | collective-permute-start | bytes 1179656 | tf_op jit(solution)/shard_map/ppermute | solution.py:392
  20.8 14.0 %all-to-all-start.1 = ((bf16[8,64,384]{2,1,0:T(8,128)(2,1)}), bf16[8,64,384]{2,1,0:T(8,128)(2,1)}, u32[]{:S(2)}, u32[]{:S(2)}) async-start(bf16[8,64,384]{2,1,0:T(8,128)(2,1)} %get-tuple-element.27), calls=%async_computation.1 | async-start | bytes 786432 | tf_op jit(solution)/shard_map/all_to_all | solution.py:402
  26.6 12.5 %collective-permute-start.1 = (bf16[2,256,384]{2,1,0:T(8,128)(2,1)S(1)}, bf16[2,256,384]{2,1,0:T(8,128)(2,1)S(1)}, u32[]{:S(2)}, u32[]{:S(2)}) collective-permute-start(bf16[2,256,384]{2,1,0:T(8,128)(2,1)S(1)} %shard_map.112.refs_5_.refs_2_.refs_4_), channel_id=1, source_target_pairs={{0,96},{1,25},{2,98},{3,27},{4,100},{5,29},{6,102},{7,31},{8,104},... | collective-permute-start | bytes 1179656 | tf_op jit(solution)/shard_map/ppermute | solution.py:392
  29.3 9.7 %collective-permute-start = (bf16[2,256,384]{2,1,0:T(8,128)(2,1)S(1)}, bf16[2,256,384]{2,1,0:T(8,128)(2,1)S(1)}, u32[]{:S(2)}, u32[]{:S(2)}) collective-permute-start(bf16[2,256,384]{2,1,0:T(8,128)(2,1)S(1)} %shard_map.112.refs_5_.refs_2_.refs_4_), channel_id=1, source_target_pairs={{0,32},{1,9},{2,34},{3,11},{4,36},{5,13},{6,38},{7,15},{8,40},{9,1... | collective-permute-start | bytes 1179656 | tf_op jit(solution)/shard_map/ppermute | solution.py:392
  35.8 9.3 %collective-permute-start.5 = (bf16[2,256,384]{2,1,0:T(8,128)(2,1)S(1)}, bf16[2,256,384]{2,1,0:T(8,128)(2,1)S(1)}, u32[]{:S(2)}, u32[]{:S(2)}) collective-permute-start(bf16[2,256,384]{2,1,0:T(8,128)(2,1)S(1)} %shard_map.111.refs_0_), channel_id=1, source_target_pairs={{0,16},{1,65},{2,18},{3,67},{4,20},{5,69},{6,22},{7,71},{8,24},{9,... | collective-permute-start | bytes 1179656 | tf_op jit(solution)/shard_map/ppermute | solution.py:389
  36.2 10.4 %collective-permute-start.4 = (bf16[2,256,384]{2,1,0:T(8,128)(2,1)S(1)}, bf16[2,256,384]{2,1,0:T(8,128)(2,1)S(1)}, u32[]{:S(2)}, u32[]{:S(2)}) collective-permute-start(bf16[2,256,384]{2,1,0:T(8,128)(2,1)S(1)} %shard_map.111.refs_0_), channel_id=1, source_target_pairs={{0,24},{1,97},{2,26},{3,99},{4,28},{5,101},{6,30},{7,103},{8,0},{9... | collective-permute-start | bytes 1179656 | tf_op jit(solution)/shard_map/ppermute | solution.py:389
  39.0 9.5 %collective-permute-start.3 = (bf16[2,256,384]{2,1,0:T(8,128)(2,1)S(1)}, bf16[2,256,384]{2,1,0:T(8,128)(2,1)S(1)}, u32[]{:S(2)}, u32[]{:S(2)}) collective-permute-start(bf16[2,256,384]{2,1,0:T(8,128)(2,1)S(1)} %shard_map.111.refs_0_), channel_id=1, source_target_pairs={{0,8},{1,33},{2,10},{3,35},{4,12},{5,37},{6,14},{7,39},{8,16},{9,4... | collective-permute-start | bytes 1179656 | tf_op jit(solution)/shard_map/ppermute | solution.py:389
  51.8 4.5 %collective-permute-start.11 = (f32[3,16,256]{2,1,0:T(8,128)S(1)}, f32[3,16,256]{2,1,0:T(8,128)S(1)}, u32[]{:S(2)}, u32[]{:S(2)}) collective-permute-start(f32[3,16,256]{2,1,0:T(8,128)S(1)} %shard_map.114.refs_6_.refs_8_), channel_id=1, source_target_pairs={{0,64},{1,17},{2,66},{3,19},{4,68},{5,21},{6,70},{7,23},{8,72},{9,... | collective-permute-start | bytes 147464 | tf_op jit(solution)/shard_map/ppermute | solution.py:392
  54.5 3.2 %collective-permute-start.10 = (f32[3,16,256]{2,1,0:T(8,128)S(1)}, f32[3,16,256]{2,1,0:T(8,128)S(1)}, u32[]{:S(2)}, u32[]{:S(2)}) collective-permute-start(f32[3,16,256]{2,1,0:T(8,128)S(1)} %shard_map.114.refs_6_.refs_8_), channel_id=1, source_target_pairs={{0,96},{1,25},{2,98},{3,27},{4,100},{5,29},{6,102},{7,31},{8,104},... | collective-permute-start | bytes 147464 | tf_op jit(solution)/shard_map/ppermute | solution.py:392
  55.3 4.2 %collective-permute-start.9 = (f32[3,16,256]{2,1,0:T(8,128)S(1)}, f32[3,16,256]{2,1,0:T(8,128)S(1)}, u32[]{:S(2)}, u32[]{:S(2)}) collective-permute-start(f32[3,16,256]{2,1,0:T(8,128)S(1)} %shard_map.114.refs_6_.refs_8_), channel_id=1, source_target_pairs={{0,32},{1,9},{2,34},{3,11},{4,36},{5,13},{6,38},{7,15},{8,40},{9,1... | collective-permute-start | bytes 147464 | tf_op jit(solution)/shard_map/ppermute | solution.py:392
  64.0 12.9 %collective-permute-start.12 = (bf16[4,256,384]{2,1,0:T(8,128)(2,1)S(1)}, bf16[4,256,384]{2,1,0:T(8,128)(2,1)S(1)}, u32[]{:S(2)}, u32[]{:S(2)}) collective-permute-start(bf16[4,256,384]{2,1,0:T(8,128)(2,1)S(1)} %get-tuple-element.32), channel_id=1, source_target_pairs={{0,16},{1,65},{2,18},{3,67},{4,20},{5,69},{6,22},{7,71},{8,24},{9,... | collective-permute-start | bytes 2359304 | tf_op jit(solution)/shard_map/ppermute | solution.py:389
  74.4 11.2 %collective-permute-start.16 = (bf16[4,256,384]{2,1,0:T(8,128)(2,1)S(1)}, bf16[4,256,384]{2,1,0:T(8,128)(2,1)S(1)}, u32[]{:S(2)}, u32[]{:S(2)}) collective-permute-start(bf16[4,256,384]{2,1,0:T(8,128)(2,1)S(1)} %get-tuple-element.38), channel_id=1, source_target_pairs={{0,24},{1,97},{2,26},{3,99},{4,28},{5,101},{6,30},{7,103},{8,0},{9... | collective-permute-start | bytes 2359304 | tf_op jit(solution)/shard_map/ppermute | solution.py:389
  75.4 12.3 %collective-permute-start.17 = (bf16[4,256,384]{2,1,0:T(8,128)(2,1)S(1)}, bf16[4,256,384]{2,1,0:T(8,128)(2,1)S(1)}, u32[]{:S(2)}, u32[]{:S(2)}) collective-permute-start(bf16[4,256,384]{2,1,0:T(8,128)(2,1)S(1)} %get-tuple-element.39), channel_id=1, source_target_pairs={{0,8},{1,33},{2,10},{3,35},{4,12},{5,37},{6,14},{7,39},{8,16},{9,4... | collective-permute-start | bytes 2359304 | tf_op jit(solution)/shard_map/ppermute | solution.py:389
  81.6 7.1 %collective-permute-start.13 = (bf16[256,384]{1,0:T(8,128)(2,1)S(1)}, bf16[256,384]{1,0:T(8,128)(2,1)S(1)}, u32[]{:S(2)}, u32[]{:S(2)}) collective-permute-start(bf16[256,384]{1,0:T(8,128)(2,1)S(1)} %get-tuple-element.34), channel_id=1, source_target_pairs={{0,96},{1,25},{2,98},{3,27},{4,100},{5,29},{6,102},{7,31},{8,104},... | collective-permute-start | bytes 589832 | tf_op jit(solution)/shard_map/ppermute | solution.py:392
  81.8 8.9 %collective-permute-start.14 = (bf16[256,384]{1,0:T(8,128)(2,1)S(1)}, bf16[256,384]{1,0:T(8,128)(2,1)S(1)}, u32[]{:S(2)}, u32[]{:S(2)}) collective-permute-start(bf16[256,384]{1,0:T(8,128)(2,1)S(1)} %get-tuple-element.35), channel_id=1, source_target_pairs={{0,32},{1,9},{2,34},{3,11},{4,36},{5,13},{6,38},{7,15},{8,40},{9,1... | collective-permute-start | bytes 589832 | tf_op jit(solution)/shard_map/ppermute | solution.py:392
  83.1 10.2 %collective-permute-start.15 = (bf16[256,384]{1,0:T(8,128)(2,1)S(1)}, bf16[256,384]{1,0:T(8,128)(2,1)S(1)}, u32[]{:S(2)}, u32[]{:S(2)}) collective-permute-start(bf16[256,384]{1,0:T(8,128)(2,1)S(1)} %get-tuple-element.36), channel_id=1, source_target_pairs={{0,64},{1,17},{2,66},{3,19},{4,68},{5,21},{6,70},{7,23},{8,72},{9,... | collective-permute-start | bytes 589832 | tf_op jit(solution)/shard_map/ppermute | solution.py:392
  94.4 0.9 copy-start.1
  95.3 18.2 %all-to-all-start.2 = ((bf16[8,96,384]{2,1,0:T(8,128)(2,1)}), bf16[8,96,384]{2,1,0:T(8,128)(2,1)S(1)}, u32[]{:S(2)}, u32[]{:S(2)}) async-start(bf16[8,96,384]{2,1,0:T(8,128)(2,1)} %shard_map.118), calls=%async_computation.2 | async-start | bytes 1179648 | tf_op jit(solution)/shard_map/all_to_all | solution.py:420
  103.3 1.1 copy-start.2

commit v4 on v3

--- a/solution.py
+++ b/solution.py
@@ -16,6 +16,7 @@
 PACK_LIMIT = 56 * 1024 * 1024
 AXES = ("z", "y", "x", "c")
 OFFSETS = (0, -1, 1, 2)
+X_STEPS = (0, 1, 3, 2)
 F32 = jnp.float32
 BF16 = jnp.bfloat16
 VMEM = pl.BlockSpec(memory_space=pltpu.VMEM)
@@ -84,7 +85,7 @@
     return new_top, total, dots
 
 
-def stats_call(curs, hists, queries, groups, state_in=None):
+def stats_call(curs, hists, queries, groups, state_in=None, at=(0, 1, 2, 3)):
     nk, nh, nq = len(flatten(curs)), len(hists), len(flatten(queries))
     rows, feat = hists[0].shape[0] // 2 - 8, hists[0].shape[1]
     tokens = queries[0].shape[1]
@@ -94,6 +95,8 @@
         cur, hist = regroup(refs[:nk], curs), refs[nk : nk + nh]
         query = regroup(refs[nk + nh : nk + nh + nq], queries)
         old, out = refs[nk + nh + nq], refs[-1]
+        if state_in is not None:
+            out[...] = old[...]
 
         def step(head, _):
             lanes = head_lanes(head)
@@ -110,7 +113,7 @@
                 else:
                     state = tuple(
                         jnp.concatenate(
-                            [old[i, pl.ds(head * 4 + b, 1), :] for b in blocks], axis=1
+                            [old[i, pl.ds(head * 4 + at[b], 1), :] for b in blocks], axis=1
                         )
                         for i in range(3)
                     )
@@ -129,7 +132,7 @@
                     )
                 for i in range(3):
                     for j, b in enumerate(blocks):
-                        out[i, pl.ds(head * 4 + b, 1), :] = state[i][
+                        out[i, pl.ds(head * 4 + at[b], 1), :] = state[i][
                             :, j * tokens : (j + 1) * tokens
                         ]
             return 0
@@ -260,15 +263,15 @@
     return list(outs[:nk]), list(outs[nk:])
 
 
-def pack_call(arrays, key_hist, value_hist, hist_len, parts):
+def pack_call(arrays, key_hist, value_hist, hist_len, sizes):
     rows, columns = arrays[0].shape
-    feat = columns // parts
-    old = key_hist.shape[0]
+    nx, nc = sizes[2:]
+    old, feat = key_hist.shape
     n = len(arrays)
 
     def kernel(*refs):
         ins, (key_in, value_in, count), outs = refs[:n], refs[n : n + 3], refs[n + 3 :]
-        outs, (hist, held, sem) = outs[:-3], outs[-3:]
+        same, other, hist, held, sem = outs
         copies = [pltpu.make_async_copy(ref, held.at[i], sem.at[i]) for i, ref in enumerate(ins)]
         copies.append(pltpu.make_async_copy(key_in, hist.at[pl.ds(0, old)], sem.at[n]))
         copies.append(pltpu.make_async_copy(value_in, hist.at[pl.ds(old, old)], sem.at[n + 1]))
@@ -276,22 +279,24 @@
             copy.start()
         filled = jnp.full((16, feat), count[0], jnp.int32).astype(F32)
         hist[2 * old :, :] = filled.astype(BF16)
+        x, core = lax.axis_index("x"), lax.axis_index("c")
         for i in range(n):
             copies[i].wait()
-            for p in range(parts):
-                outs[i // 2][p, i % 2 * rows : (i % 2 + 1) * rows, :] = held[
-                    i, :, p * feat : (p + 1) * feat
-                ]
+            for j, step in enumerate(X_STEPS):
+                for k, out in enumerate((same, other)):
+                    part = lax.rem(x + step, nx) * nc + lax.rem(core + k, nc)
+                    at = pl.ds(pl.multiple_of(part * feat, feat), feat)
+                    out[i // 2, j, i % 2] = held[i, :, at]
         copies[n].wait()
         copies[n + 1].wait()
 
-    pair = jax.ShapeDtypeStruct((parts, 2 * rows, feat), BF16)
+    shape = jax.ShapeDtypeStruct((n // 2, nx, 2, rows, feat), BF16)
     return pl.pallas_call(
         kernel,
-        out_shape=[pair] * (n // 2) + [jax.ShapeDtypeStruct((2 * old + 16, feat), BF16)],
+        out_shape=[shape, shape, jax.ShapeDtypeStruct((2 * old + 16, feat), BF16)],
         in_specs=[pl.BlockSpec(memory_space=pl.ANY)] * (n + 2)
         + [pl.BlockSpec(memory_space=pltpu.SMEM)],
-        out_specs=[VMEM] * (n // 2 + 1),
+        out_specs=[VMEM] * 3,
         scratch_shapes=[
             pltpu.VMEM((n, rows, columns), BF16),
             pltpu.SemaphoreType.DMA((n + 2,)),
@@ -300,19 +305,29 @@
     )(*arrays, key_hist, value_hist, hist_len)
 
 
-def split_call(array, count):
-    parts, rows, feat = array.shape
-    rows //= count
-
-    def kernel(ref, *outs):
-        for i in range(count):
-            for p in range(parts):
-                outs[i // 2][i % 2, p * rows : (p + 1) * rows, :] = ref[
-                    p, i * rows : (i + 1) * rows, :
-                ]
-
-    block = jax.ShapeDtypeStruct((2, parts * rows, feat), BF16)
-    return call(kernel, [block] * (count // 2), [array])
+def merge_call(same, other):
+    pairs, nx, two, rows, feat = same.shape
+
+    def kernel(a, b, *outs):
+        for i in range(pairs):
+            for j in range(nx):
+                outs[i * nx + j][:, 0:rows, :] = a[i, j]
+                outs[i * nx + j][:, rows : 2 * rows, :] = b[i, j]
+
+    shape = jax.ShapeDtypeStruct((two, 2 * rows, feat), BF16)
+    outs = call(kernel, [shape] * (pairs * nx), [same, other])
+    return [list(outs[i * nx : (i + 1) * nx]) for i in range(pairs)]
+
+
+def stack_call(blocks):
+    two, rows, feat = blocks[0].shape
+
+    def kernel(*refs):
+        for j, ref in enumerate(refs[:-1]):
+            refs[-1][:, j * rows : (j + 1) * rows, :] = ref[...]
+
+    shape = jax.ShapeDtypeStruct((two, len(blocks) * rows, feat), BF16)
+    return call(kernel, shape, blocks)
 
 
 def unpack_call(array, count):
@@ -327,13 +342,16 @@
     return call(kernel, [jax.ShapeDtypeStruct((rows, parts * feat), BF16)] * count, [array])
 
 
-def add_call(query_parts, cur_parts, parts):
+def add_call(query_parts, cur_parts, sizes):
     tokens, feat = query_parts[0].shape
+    nx, nc = sizes[2:]
+    parts = nx * nc
     rows = tokens // parts
     nq = len(query_parts)
 
     def kernel(*refs):
         out = refs[-1]
+        x, core = lax.axis_index("x"), lax.axis_index("c")
         sums = [
             sum(ref[...].astype(F32) for ref in refs[:nq]),
             sum(ref[0].astype(F32) for ref in refs[nq:-1]),
@@ -341,8 +359,11 @@
         ]
         for i, total in enumerate(sums):
             low = total.astype(BF16)
-            for p in range(parts):
-                out[p, i * rows : (i + 1) * rows, :] = low[p * rows : (p + 1) * rows]
+            for j, step in enumerate(X_STEPS):
+                for k in range(nc):
+                    owner = lax.rem(x + nx - step, nx) * nc + lax.rem(core + k, nc)
+                    first = (j * nc + k) * rows
+                    out[owner, i * rows : (i + 1) * rows, :] = low[first : first + rows]
 
     shape = jax.ShapeDtypeStruct((parts, 3 * rows, feat), BF16)
     return call(kernel, shape, list(query_parts) + list(cur_parts))
@@ -379,11 +400,17 @@
     def queries(step):
         return table(lambda z, y, x, c: (z + step, y, x, c) if c == 0 else (z, y + step, x, c))
 
-    return keys, queries
+    def chips(step):
+        return table(lambda z, y, x, c: (z, y, x + step, c))
+
+    def cores():
+        return table(lambda z, y, x, c: (z, y, x, c + 1))
+
+    return keys, queries, chips, cores
 
 
 def make_shards(sizes):
-    key_move, query_move = ring_moves(sizes)
+    key_move, query_move, chip_move, core_move = ring_moves(sizes)
 
     def to_key(value, step):
         return lax.ppermute(value, AXES, key_move(step))
@@ -392,20 +419,31 @@
         return lax.ppermute(value, AXES, query_move(step))
 
     def shards(query, key_cur, value_cur, d_out, key_hist, value_hist, hist_len):
-        parts = sizes[2] * sizes[3]
-        asked, kept, hist0 = pack_call(
-            [query, d_out, key_cur, value_cur], key_hist, value_hist, hist_len, parts
+        same, other, hist0 = pack_call(
+            [query, d_out, key_cur, value_cur], key_hist, value_hist, hist_len, sizes
         )
+        other = lax.ppermute(other, AXES, core_move())
         hists = [hist0] + [to_key(hist0, -o) for o in OFFSETS[1:]]
-        asked = lax.all_to_all(asked, ("x", "c"), 0, 0, tiled=True)
-        kept, asked = lax.optimization_barrier((kept, asked))
-        kept = lax.all_to_all(kept, ("x", "c"), 0, 0, tiled=True)
-        query0 = split_call(asked, 2)[0]
+        asked, kept = merge_call(same, other)
+        kept, hists[1], hists[2] = lax.optimization_barrier((kept, hists[1], hists[2]))
+
+        def exchange(pieces):
+            moved = [
+                lax.ppermute(p, AXES, chip_move(d)) for p, d in zip(pieces[1:], X_STEPS[1:])
+            ]
+            return stack_call(pieces[:1] + moved)
+
+        query0 = exchange(asked)
         queries = [query0] + [to_query(query0, -o) for o in OFFSETS[1:]]
-        cur0 = split_call(kept, 2)[0]
+        cur0 = exchange(kept)
         curs = [cur0] + [to_key(cur0, -o) for o in OFFSETS[1:]]
         every = (0, 1, 2, 3)
-        state = stats_call(curs[:1], hists, queries, [(every, (0,), every, True)])
+        state = stats_call(
+            curs[:1], hists, [queries[0], queries[3]], [((0, 1), (0,), every, True)], at=(0, 3)
+        )
+        state = stats_call(
+            curs[:1], hists, queries[1:3], [((0, 1), (0,), every, True)], state, at=(1, 2)
+        )
         state = stats_call(curs, hists[:1], queries, [(every, (1, 2, 3), (), False)], state)
         stats = [state] + [to_query(state, -o) for o in OFFSETS[1:]]
 
@@ -416,7 +454,7 @@
         own, sums = grads_call(curs[:1], hists[:1], queries, stats, sums[0], far)
         query_parts = [sums[0]] + [to_query(sums[i], OFFSETS[i]) for i in range(1, 4)]
 
-        back = add_call(query_parts, own + near, parts)
+        back = add_call(query_parts, own + near, sizes)
         back = lax.all_to_all(back, ("x", "c"), 0, 0, tiled=True)
         outs = unpack_call(back, 3)
         grad_k, grad_v = add_hist_call(own + near)

time: 115 us -> 112 us (0.974)
  starting transfers between devices: 43.3 us -> 39.5 us
  waiting for transfers between devices: 34.3 us -> 36.1 us
    all_to_all x2 -> x0, starting transfers between devices: 11.7 us -> none  [the longest x1 5.94 us: shards(): asked = lax.all_to_all(asked, ('x', 'c'), 0, 0, tiled=True)]
    ppermute x0 -> x7, starting transfers between devices: none -> 8.78 us  [the longest x6 7.28 us: exchange(): lax.ppermute(p, AXES, chip_move(d))]
    all_to_all x2 -> x0, waiting for transfers between devices: 8.47 us -> none  [the longest x1 5.46 us: shards(): kept = lax.all_to_all(kept, ('x', 'c'), 0, 0, tiled=True)]
    ppermute x0 -> x7, waiting for transfers between devices: none -> 7.56 us  [the longest x6 7.55 us: exchange(): lax.ppermute(p, AXES, chip_move(d))]
    ppermute x9, starting transfers between devices: 11.9 us -> 8.9 us  [to_query(): return lax.ppermute(value, AXES, query_move(step))]
    ppermute x9, waiting for transfers between devices: 8.56 us -> 10.6 us  [to_key(): return lax.ppermute(value, AXES, key_move(step))]
    all_to_all x1, starting transfers between devices: 8 us -> 9.72 us  [shards(): back = lax.all_to_all(back, ('x', 'c'), 0, 0, tiled=True)]
    pallas_call x10 -> x12, Pallas kernels: 30.9 us -> 31.2 us  [call(): pl.pallas_call(kernel, out_shape=outs, in_specs=[VMEM] * len(args), out_s...]
  transfers between devices with their start and end apart: 21 -> 26, of which waited for: 14 -> 16; matrix products, arithmetic and copies ran while one was open for 0% -> 0% of each run, Pallas kernels for 19% -> 19%
where the time goes in v4:
time: 112 us
  starting transfers between devices  39.5 us (35%)
  waiting for transfers between devices  36.1 us (32%)
  Pallas kernels  33.6 us (30%)
  between operations  1.42 us (1%)
    pallas_call x12, Pallas kernels, call(): pl.pallas_call(kernel, out_shape=outs, in_specs=[VMEM] * len(args), out_s...  31.2 us
    ppermute x9, starting transfers between devices, to_key(): return lax.ppermute(value, AXES, key_move(step))  12.1 us
    ppermute x9, waiting for transfers between devices, to_key(): return lax.ppermute(value, AXES, key_move(step))  10.6 us
    all_to_all x1, starting transfers between devices, shards(): back = lax.all_to_all(back, ('x', 'c'), 0, 0, tiled=True)  9.72 us
    all_to_all x1, waiting for transfers between devices, shards(): back = lax.all_to_all(back, ('x', 'c'), 0, 0, tiled=True)  9.38 us
    ppermute x9, starting transfers between devices, to_query(): return lax.ppermute(value, AXES, query_move(step))  8.9 us
    ppermute x9, waiting for transfers between devices, to_query(): return lax.ppermute(value, AXES, query_move(step))  8.52 us
    ppermute x6, waiting for transfers between devices, exchange(): lax.ppermute(p, AXES, chip_move(d))  7.55 us
  transfers between devices with their start and end apart: 26, of which 16 were waited for; matrix products, arithmetic and copies ran while one was open for 0% of the time, Pallas kernels for 19%

profile of v4, /device:TPU:1, one launch (start us, length us, event | category | flops | bytes accessed | tf_op | source)
XLA Modules:
  0.0 111.6 jit_solution(10629019573444819890)
XLA Ops:
  1.3 2.4 %shard_map.110 = (bf16[2,4,2,32,384]{4,3,2,1,0:T(8,128)(2,1)}, bf16[2,4,2,32,384]{4,3,2,1,0:T(8,128)(2,1)}, bf16[528,384]{1,0:T(8,128)(2,1)}) custom-call(bf16[32,3072]{1,0:T(8,128)(2,1)} %refs_0_.1, bf16[32,3072]{1,0:T(8,128)(2,1)} %refs_1_.1, bf16[32,3072]{1,0:T(8,128)(2,1)} %refs_2_.1, bf16[32,3072]{1,0:T(8,128)(2,1)} %refs_3_.1, ...), custom_call_target="tpu_custom_call" | custom-call | tf_op jit(solution)/shard_map/pallas_call | solution.py:294
  3.7 1.5 %collective-permute-start = (bf16[2,4,2,32,384]{4,3,2,1,0:T(8,128)(2,1)}, bf16[2,4,2,32,384]{4,3,2,1,0:T(8,128)(2,1)S(1)}, u32[]{:S(2)}, u32[]{:S(2)}) collective-permute-start(bf16[2,4,2,32,384]{4,3,2,1,0:T(8,128)(2,1)} %get-tuple-element.38), channel_id=1, source_target_pairs={{0,1},{1,0},{2,3},{3,2},{4,5},{5,4},{6,7},{7,6},{8,9},{9,8},{10,11... | collective-permute-start | bytes 1179656 | tf_op jit(solution)/shard_map/ppermute | solution.py:425
  5.2 3.8 %collective-permute-start.2 = (bf16[528,384]{1,0:T(8,128)(2,1)}, bf16[528,384]{1,0:T(8,128)(2,1)S(1)}, u32[]{:S(2)}, u32[]{:S(2)}) collective-permute-start(bf16[528,384]{1,0:T(8,128)(2,1)} %get-tuple-element.43.refs_1_.refs_4_), channel_id=1, source_target_pairs={{0,24},{1,97},{2,26},{3,99},{4,28},{5,101},{6,30},{7,103},{8,0},{9... | collective-permute-start | bytes 1216520 | tf_op jit(solution)/shard_map/ppermute | solution.py:416
  10.1 1.3 %collective-permute-start.6 = (bf16[2,64,384]{2,1,0:T(8,128)(2,1)S(1)}, bf16[2,64,384]{2,1,0:T(8,128)(2,1)S(1)}, u32[]{:S(2)}, u32[]{:S(2)}) collective-permute-start(bf16[2,64,384]{2,1,0:T(8,128)(2,1)S(1)} %get-tuple-element.49), channel_id=1, source_target_pairs={{0,2},{1,3},{2,4},{3,5},{4,6},{5,7},{6,0},{7,1},{8,10},{9,11},{10,... | collective-permute-start | bytes 294920 | tf_op jit(solution)/shard_map/ppermute | solution.py:432
  11.4 1.5 %collective-permute-start.7 = (bf16[2,64,384]{2,1,0:T(8,128)(2,1)S(1)}, bf16[2,64,384]{2,1,0:T(8,128)(2,1)S(1)}, u32[]{:S(2)}, u32[]{:S(2)}) collective-permute-start(bf16[2,64,384]{2,1,0:T(8,128)(2,1)S(1)} %get-tuple-element.50), channel_id=1, source_target_pairs={{0,6},{1,7},{2,0},{3,1},{4,2},{5,3},{6,4},{7,5},{8,14},{9,15},{10,... | collective-permute-start | bytes 294920 | tf_op jit(solution)/shard_map/ppermute | solution.py:432
  12.9 1.5 %collective-permute-start.8 = (bf16[2,64,384]{2,1,0:T(8,128)(2,1)S(1)}, bf16[2,64,384]{2,1,0:T(8,128)(2,1)S(1)}, u32[]{:S(2)}, u32[]{:S(2)}) collective-permute-start(bf16[2,64,384]{2,1,0:T(8,128)(2,1)S(1)} %get-tuple-element.51), channel_id=1, source_target_pairs={{0,4},{1,5},{2,6},{3,7},{4,0},{5,1},{6,2},{7,3},{8,12},{9,13},{10,... | collective-permute-start | bytes 294920 | tf_op jit(solution)/shard_map/ppermute | solution.py:432
  14.4 1.6 %collective-permute-done.6.refs_1_ = bf16[2,64,384]{2,1,0:T(8,128)(2,1)S(1)} collective-permute-done((bf16[2,64,384]{2,1,0:T(8,128)(2,1)S(1)}, bf16[2,64,384]{2,1,0:T(8,128)(2,1)S(1)}, u32[]{:S(2)}, u32[]{:S(2)}) %collective-permute-start.6) | collective-permute-done | bytes 98336 | tf_op jit(solution)/shard_map/ppermute | solution.py:432
  16.3 2.7 %collective-permute-done.8.refs_3_ = bf16[2,64,384]{2,1,0:T(8,128)(2,1)S(1)} collective-permute-done((bf16[2,64,384]{2,1,0:T(8,128)(2,1)S(1)}, bf16[2,64,384]{2,1,0:T(8,128)(2,1)S(1)}, u32[]{:S(2)}, u32[]{:S(2)}) %collective-permute-start.8) | collective-permute-done | bytes 98336 | tf_op jit(solution)/shard_map/ppermute | solution.py:432
  19.0 2.3 %collective-permute-start.11 = (bf16[2,256,384]{2,1,0:T(8,128)(2,1)S(1)}, bf16[2,256,384]{2,1,0:T(8,128)(2,1)S(1)}, u32[]{:S(2)}, u32[]{:S(2)}) collective-permute-start(bf16[2,256,384]{2,1,0:T(8,128)(2,1)S(1)} %shard_map.113.refs_5_.refs_2_.refs_4_), channel_id=1, source_target_pairs={{0,64},{1,17},{2,66},{3,19},{4,68},{5,21},{6,70},{7,23},{8,72},{9,... | collective-permute-start | bytes 1179656 | tf_op jit(solution)/shard_map/ppermute | solution.py:419
  22.3 1.7 %collective-permute-start.4 = (bf16[2,64,384]{2,1,0:T(8,128)(2,1)S(1)}, bf16[2,64,384]{2,1,0:T(8,128)(2,1)S(1)}, u32[]{:S(2)}, u32[]{:S(2)}) collective-permute-start(bf16[2,64,384]{2,1,0:T(8,128)(2,1)S(1)} %get-tuple-element.46), channel_id=1, source_target_pairs={{0,6},{1,7},{2,0},{3,1},{4,2},{5,3},{6,4},{7,5},{8,14},{9,15},{10,... | collective-permute-start | bytes 294920 | tf_op jit(solution)/shard_map/ppermute | solution.py:432
  24.3 2.0 %collective-permute-done.3.refs_1_ = bf16[2,64,384]{2,1,0:T(8,128)(2,1)S(1)} collective-permute-done((bf16[2,64,384]{2,1,0:T(8,128)(2,1)S(1)}, bf16[2,64,384]{2,1,0:T(8,128)(2,1)S(1)}, u32[]{:S(2)}, u32[]{:S(2)}) %collective-permute-start.3) | collective-permute-done | bytes 98336 | tf_op jit(solution)/shard_map/ppermute | solution.py:432
  27.8 1.3 %collective-permute-done.5.refs_3_ = bf16[2,64,384]{2,1,0:T(8,128)(2,1)S(1)} collective-permute-done((bf16[2,64,384]{2,1,0:T(8,128)(2,1)S(1)}, bf16[2,64,384]{2,1,0:T(8,128)(2,1)S(1)}, u32[]{:S(2)}, u32[]{:S(2)}) %collective-permute-start.5) | collective-permute-done | bytes 98336 | tf_op jit(solution)/shard_map/ppermute | solution.py:432
  29.1 1.4 %collective-permute-start.14 = (bf16[2,256,384]{2,1,0:T(8,128)(2,1)S(1)}, bf16[2,256,384]{2,1,0:T(8,128)(2,1)S(1)}, u32[]{:S(2)}, u32[]{:S(2)}) collective-permute-start(bf16[2,256,384]{2,1,0:T(8,128)(2,1)S(1)} %shard_map.112.refs_0_), channel_id=1, source_target_pairs={{0,16},{1,65},{2,18},{3,67},{4,20},{5,69},{6,22},{7,71},{8,24},{9,... | collective-permute-start | bytes 1179656 | tf_op jit(solution)/shard_map/ppermute | solution.py:416
  30.5 3.0 %collective-permute-start.13 = (bf16[2,256,384]{2,1,0:T(8,128)(2,1)S(1)}, bf16[2,256,384]{2,1,0:T(8,128)(2,1)S(1)}, u32[]{:S(2)}, u32[]{:S(2)}) collective-permute-start(bf16[2,256,384]{2,1,0:T(8,128)(2,1)S(1)} %shard_map.112.refs_0_), channel_id=1, source_target_pairs={{0,24},{1,97},{2,26},{3,99},{4,28},{5,101},{6,30},{7,103},{8,0},{9... | collective-permute-start | bytes 1179656 | tf_op jit(solution)/shard_map/ppermute | solution.py:416
  34.1 3.4 %shard_map.114.refs_7_ = f32[3,16,256]{2,1,0:T(8,128)S(1)} custom-call(bf16[2,256,384]{2,1,0:T(8,128)(2,1)S(1)} %shard_map.112.refs_0_, bf16[528,384]{1,0:T(8,128)(2,1)S(1)} %copy-done, bf16[528,384]{1,0:T(8,128)(2,1)S(1)} %collective-permute-done.1.refs_2_, bf16[528,384]{1,0:T(8,128)(2,1)S(1)} %collective-permute-done.2.refs_3_, ...), custom_call_target="tpu_custom_call" | custom-call | flops 31457280 | bytes 43776 | tf_op jit(solution)/shard_map/pallas_call | solution.py:35
  37.5 3.4 %shard_map.115.refs_9_ = f32[3,16,256]{2,1,0:T(8,128)S(1)} custom-call(bf16[2,256,384]{2,1,0:T(8,128)(2,1)S(1)} %shard_map.112.refs_0_, bf16[528,384]{1,0:T(8,128)(2,1)S(1)} %copy-done, bf16[528,384]{1,0:T(8,128)(2,1)S(1)} %collective-permute-done.1.refs_2_, bf16[528,384]{1,0:T(8,128)(2,1)S(1)} %collective-permute-done.2.refs_3_, ...), custom_call_target="tpu_custom_call" | custom-call | flops 31457280 | bytes 44544 | tf_op jit(solution)/shard_map/pallas_call | solution.py:35
  41.0 4.7 %collective-permute-done.13.refs_2_.refs_1_ = bf16[2,256,384]{2,1,0:T(8,128)(2,1)S(1)} collective-permute-done((bf16[2,256,384]{2,1,0:T(8,128)(2,1)S(1)}, bf16[2,256,384]{2,1,0:T(8,128)(2,1)S(1)}, u32[]{:S(2)}, u32[]{:S(2)}) %collective-permute-start.13) | collective-permute-done | bytes 393248 | tf_op jit(solution)/shard_map/ppermute | solution.py:416
  45.8 3.4 %shard_map.116.refs_6_.refs_8_ = f32[3,16,256]{2,1,0:T(8,128)S(1)} custom-call(bf16[2,256,384]{2,1,0:T(8,128)(2,1)S(1)} %shard_map.112.refs_0_, bf16[2,256,384]{2,1,0:T(8,128)(2,1)S(1)} %collective-permute-done.12.refs_1_.refs_0_, bf16[2,256,384]{2,1,0:T(8,128)(2,1)S(1)} %collective-permute-done.13.refs_2_.refs_1_, ...), custom_call_target="tpu_custom_call" | custom-call | flops 37748736 | bytes 56256 | tf_op jit(solution)/shard_map/pallas_call | solution.py:35
  49.1 1.9 %collective-permute-start.18 = (f32[3,16,256]{2,1,0:T(8,128)S(1)}, f32[3,16,256]{2,1,0:T(8,128)S(1)}, u32[]{:S(2)}, u32[]{:S(2)}) collective-permute-start(f32[3,16,256]{2,1,0:T(8,128)S(1)} %shard_map.116.refs_6_.refs_8_), channel_id=1, source_target_pairs={{0,64},{1,17},{2,66},{3,19},{4,68},{5,21},{6,70},{7,23},{8,72},{9,... | collective-permute-start | bytes 147464 | tf_op jit(solution)/shard_map/ppermute | solution.py:419
  51.0 1.7 %collective-permute-start.17 = (f32[3,16,256]{2,1,0:T(8,128)S(1)}, f32[3,16,256]{2,1,0:T(8,128)S(1)}, u32[]{:S(2)}, u32[]{:S(2)}) collective-permute-start(f32[3,16,256]{2,1,0:T(8,128)S(1)} %shard_map.116.refs_6_.refs_8_), channel_id=1, source_target_pairs={{0,96},{1,25},{2,98},{3,27},{4,100},{5,29},{6,102},{7,31},{8,104},... | collective-permute-start | bytes 147464 | tf_op jit(solution)/shard_map/ppermute | solution.py:419
  53.9 3.0 %collective-permute-done.16.refs_7_.refs_9_ = f32[3,16,256]{2,1,0:T(8,128)S(1)} collective-permute-done((f32[3,16,256]{2,1,0:T(8,128)S(1)}, f32[3,16,256]{2,1,0:T(8,128)S(1)}, u32[]{:S(2)}, u32[]{:S(2)}) %collective-permute-start.16) | collective-permute-done | bytes 49184 | tf_op jit(solution)/shard_map/ppermute | solution.py:419
  57.0 4.6 %shard_map.117 = (bf16[4,256,384]{2,1,0:T(8,128)(2,1)S(1)}, f32[3,128,1024]{2,1,0:T(8,128)S(1)}) custom-call(bf16[2,256,384]{2,1,0:T(8,128)(2,1)S(1)} %collective-permute-done.14.refs_3_.refs_0_, bf16[528,384]{1,0:T(8,128)(2,1)S(1)} %collective-permute-done.15.refs_4_.refs_1_, bf16[2,256,384]{2,1,0:T(8,128)(2,1)S(1)} %shard_map.113.refs_5_.refs_2_.refs_4_, ...), custom_call_target="tpu_custom_call" | custom-call | flops 62914560 | bytes 40128 | tf_op jit(solution)/shard_map/pallas_call | solution.py:35
  61.6 1.6 %collective-permute-start.19 = (bf16[4,256,384]{2,1,0:T(8,128)(2,1)S(1)}, bf16[4,256,384]{2,1,0:T(8,128)(2,1)S(1)}, u32[]{:S(2)}, u32[]{:S(2)}) collective-permute-start(bf16[4,256,384]{2,1,0:T(8,128)(2,1)S(1)} %get-tuple-element.56), channel_id=1, source_target_pairs={{0,16},{1,65},{2,18},{3,67},{4,20},{5,69},{6,22},{7,71},{8,24},{9,... | collective-permute-start | bytes 2359304 | tf_op jit(solution)/shard_map/ppermute | solution.py:416
  63.1 8.7 %shard_map.118 = (bf16[4,256,384]{2,1,0:T(8,128)(2,1)S(1)}, bf16[4,256,384]{2,1,0:T(8,128)(2,1)S(1)}, f32[3,128,1024]{2,1,0:T(8,128)S(1)}) custom-call(bf16[2,256,384]{2,1,0:T(8,128)(2,1)S(1)} %collective-permute-done.12.refs_1_.refs_0_, bf16[2,256,384]{2,1,0:T(8,128)(2,1)S(1)} %collective-permute-done.13.refs_2_.refs_1_, ...), custom_call_target="tpu_custom_call" | custom-call | flops 125829120 | bytes 77184 | tf_op jit(solution)/shard_map/pallas_call | solution.py:35
  71.9 1.3 %collective-permute-start.23 = (bf16[4,256,384]{2,1,0:T(8,128)(2,1)S(1)}, bf16[4,256,384]{2,1,0:T(8,128)(2,1)S(1)}, u32[]{:S(2)}, u32[]{:S(2)}) collective-permute-start(bf16[4,256,384]{2,1,0:T(8,128)(2,1)S(1)} %get-tuple-element.62), channel_id=1, source_target_pairs={{0,24},{1,97},{2,26},{3,99},{4,28},{5,101},{6,30},{7,103},{8,0},{9... | collective-permute-start | bytes 2359304 | tf_op jit(solution)/shard_map/ppermute | solution.py:416
  74.5 4.7 %shard_map.119 = (bf16[4,256,384]{2,1,0:T(8,128)(2,1)S(1)}, bf16[256,384]{1,0:T(8,128)(2,1)S(1)}, bf16[256,384]{1,0:T(8,128)(2,1)S(1)}, bf16[256,384]{1,0:T(8,128)(2,1)S(1)}, bf16[256,384]{1,0:T(8,128)(2,1)S(1)}) custom-call(bf16[2,256,384]{2,1,0:T(8,128)(2,1)S(1)} %shard_map.112.refs_0_, bf16[528,384]{1,0:T(8,128)(2,1)S(1)} %copy-done, ...), custom_call_target="tpu_custom_call" | custom-call | flops 62914560 | bytes 76992 | tf_op jit(solution)/shard_map/pallas_call | solution.py:35
  79.3 1.5 %collective-permute-start.21 = (bf16[256,384]{1,0:T(8,128)(2,1)S(1)}, bf16[256,384]{1,0:T(8,128)(2,1)S(1)}, u32[]{:S(2)}, u32[]{:S(2)}) collective-permute-start(bf16[256,384]{1,0:T(8,128)(2,1)S(1)} %get-tuple-element.59), channel_id=1, source_target_pairs={{0,32},{1,9},{2,34},{3,11},{4,36},{5,13},{6,38},{7,15},{8,40},{9,1... | collective-permute-start | bytes 589832 | tf_op jit(solution)/shard_map/ppermute | solution.py:419
  80.7 2.3 %collective-permute-done.23.refs_5_.refs_1_ = bf16[4,256,384]{2,1,0:T(8,128)(2,1)S(1)} collective-permute-done((bf16[4,256,384]{2,1,0:T(8,128)(2,1)S(1)}, bf16[4,256,384]{2,1,0:T(8,128)(2,1)S(1)}, u32[]{:S(2)}, u32[]{:S(2)}) %collective-permute-start.23) | collective-permute-done | bytes 786464 | tf_op jit(solution)/shard_map/ppermute | solution.py:416
  83.1 2.4 %collective-permute-done.24.refs_6_.refs_2_ = bf16[4,256,384]{2,1,0:T(8,128)(2,1)S(1)} collective-permute-done((bf16[4,256,384]{2,1,0:T(8,128)(2,1)S(1)}, bf16[4,256,384]{2,1,0:T(8,128)(2,1)S(1)}, u32[]{:S(2)}, u32[]{:S(2)}) %collective-permute-start.24) | collective-permute-done | bytes 786464 | tf_op jit(solution)/shard_map/ppermute | solution.py:416
  86.3 2.9 %collective-permute-done.21.refs_2_ = bf16[256,384]{1,0:T(8,128)(2,1)S(1)} collective-permute-done((bf16[256,384]{1,0:T(8,128)(2,1)S(1)}, bf16[256,384]{1,0:T(8,128)(2,1)S(1)}, u32[]{:S(2)}, u32[]{:S(2)}) %collective-permute-start.21) | collective-permute-done | bytes 196640 | tf_op jit(solution)/shard_map/ppermute | solution.py:419
  90.8 9.7 %all-to-all-start = ((bf16[8,96,384]{2,1,0:T(8,128)(2,1)}), bf16[8,96,384]{2,1,0:T(8,128)(2,1)S(1)}, u32[]{:S(2)}, u32[]{:S(2)}) async-start(bf16[8,96,384]{2,1,0:T(8,128)(2,1)} %shard_map.120), calls=%async_computation | async-start | bytes 1179648 | tf_op jit(solution)/shard_map/all_to_all | solution.py:458
  101.4 9.4 %all-to-all-done.ref = bf16[8,96,384]{2,1,0:T(8,128)(2,1)S(1)} async-done(((bf16[8,96,384]{2,1,0:T(8,128)(2,1)}), bf16[8,96,384]{2,1,0:T(8,128)(2,1)S(1)}, u32[]{:S(2)}, u32[]{:S(2)}) %all-to-all-start) | async-done | bytes 589856 | tf_op jit(solution)/shard_map/all_to_all | solution.py:458
  (37 shorter events, 11.6 us)
Async XLA Ops:
  3.7 30.4 %copy-start = (bf16[528,384]{1,0:T(8,128)(2,1)S(1)}, bf16[528,384]{1,0:T(8,128)(2,1)}, u32[]{:S(2)}) copy-start(bf16[528,384]{1,0:T(8,128)(2,1)} %get-tuple-element.43.refs_1_.refs_4_) | copy-start | bytes 1216516
  3.7 5.3 %collective-permute-start = (bf16[2,4,2,32,384]{4,3,2,1,0:T(8,128)(2,1)}, bf16[2,4,2,32,384]{4,3,2,1,0:T(8,128)(2,1)S(1)}, u32[]{:S(2)}, u32[]{:S(2)}) collective-permute-start(bf16[2,4,2,32,384]{4,3,2,1,0:T(8,128)(2,1)} %get-tuple-element.38), channel_id=1, source_target_pairs={{0,1},{1,0},{2,3},{3,2},{4,5},{5,4},{6,7},{7,6},{8,9},{9,8},{10,11... | collective-permute-start | bytes 1179656 | tf_op jit(solution)/shard_map/ppermute | solution.py:425
  5.2 16.1 %collective-permute-start.2 = (bf16[528,384]{1,0:T(8,128)(2,1)}, bf16[528,384]{1,0:T(8,128)(2,1)S(1)}, u32[]{:S(2)}, u32[]{:S(2)}) collective-permute-start(bf16[528,384]{1,0:T(8,128)(2,1)} %get-tuple-element.43.refs_1_.refs_4_), channel_id=1, source_target_pairs={{0,24},{1,97},{2,26},{3,99},{4,28},{5,101},{6,30},{7,103},{8,0},{9... | collective-permute-start | bytes 1216520 | tf_op jit(solution)/shard_map/ppermute | solution.py:416
  9.1 12.3 %collective-permute-start.1 = (bf16[528,384]{1,0:T(8,128)(2,1)}, bf16[528,384]{1,0:T(8,128)(2,1)S(1)}, u32[]{:S(2)}, u32[]{:S(2)}) collective-permute-start(bf16[528,384]{1,0:T(8,128)(2,1)} %get-tuple-element.43.refs_1_.refs_4_), channel_id=1, source_target_pairs={{0,8},{1,33},{2,10},{3,35},{4,12},{5,37},{6,14},{7,39},{8,16},{9,4... | collective-permute-start | bytes 1216520 | tf_op jit(solution)/shard_map/ppermute | solution.py:416
  9.1 1.0 copy-start.1
  10.1 5.9 %collective-permute-start.6 = (bf16[2,64,384]{2,1,0:T(8,128)(2,1)S(1)}, bf16[2,64,384]{2,1,0:T(8,128)(2,1)S(1)}, u32[]{:S(2)}, u32[]{:S(2)}) collective-permute-start(bf16[2,64,384]{2,1,0:T(8,128)(2,1)S(1)} %get-tuple-element.49), channel_id=1, source_target_pairs={{0,2},{1,3},{2,4},{3,5},{4,6},{5,7},{6,0},{7,1},{8,10},{9,11},{10,... | collective-permute-start | bytes 294920 | tf_op jit(solution)/shard_map/ppermute | solution.py:432
  11.4 4.9 %collective-permute-start.7 = (bf16[2,64,384]{2,1,0:T(8,128)(2,1)S(1)}, bf16[2,64,384]{2,1,0:T(8,128)(2,1)S(1)}, u32[]{:S(2)}, u32[]{:S(2)}) collective-permute-start(bf16[2,64,384]{2,1,0:T(8,128)(2,1)S(1)} %get-tuple-element.50), channel_id=1, source_target_pairs={{0,6},{1,7},{2,0},{3,1},{4,2},{5,3},{6,4},{7,5},{8,14},{9,15},{10,... | collective-permute-start | bytes 294920 | tf_op jit(solution)/shard_map/ppermute | solution.py:432
  12.9 6.1 %collective-permute-start.8 = (bf16[2,64,384]{2,1,0:T(8,128)(2,1)S(1)}, bf16[2,64,384]{2,1,0:T(8,128)(2,1)S(1)}, u32[]{:S(2)}, u32[]{:S(2)}) collective-permute-start(bf16[2,64,384]{2,1,0:T(8,128)(2,1)S(1)} %get-tuple-element.51), channel_id=1, source_target_pairs={{0,4},{1,5},{2,6},{3,7},{4,0},{5,1},{6,2},{7,3},{8,12},{9,13},{10,... | collective-permute-start | bytes 294920 | tf_op jit(solution)/shard_map/ppermute | solution.py:432
  16.0 14.4 %collective-permute-start.15 = (bf16[528,384]{1,0:T(8,128)(2,1)}, bf16[528,384]{1,0:T(8,128)(2,1)S(1)}, u32[]{:S(2)}, u32[]{:S(2)}) collective-permute-start(bf16[528,384]{1,0:T(8,128)(2,1)} %get-tuple-element.43.refs_1_.refs_4_), channel_id=1, source_target_pairs={{0,16},{1,65},{2,18},{3,67},{4,20},{5,69},{6,22},{7,71},{8,24},{9,... | collective-permute-start | bytes 1216520 | tf_op jit(solution)/shard_map/ppermute | solution.py:416
  19.0 14.5 %collective-permute-start.11 = (bf16[2,256,384]{2,1,0:T(8,128)(2,1)S(1)}, bf16[2,256,384]{2,1,0:T(8,128)(2,1)S(1)}, u32[]{:S(2)}, u32[]{:S(2)}) collective-permute-start(bf16[2,256,384]{2,1,0:T(8,128)(2,1)S(1)} %shard_map.113.refs_5_.refs_2_.refs_4_), channel_id=1, source_target_pairs={{0,64},{1,17},{2,66},{3,19},{4,68},{5,21},{6,70},{7,23},{8,72},{9,... | collective-permute-start | bytes 1179656 | tf_op jit(solution)/shard_map/ppermute | solution.py:419
  21.3 5.0 %collective-permute-start.3 = (bf16[2,64,384]{2,1,0:T(8,128)(2,1)S(1)}, bf16[2,64,384]{2,1,0:T(8,128)(2,1)S(1)}, u32[]{:S(2)}, u32[]{:S(2)}) collective-permute-start(bf16[2,64,384]{2,1,0:T(8,128)(2,1)S(1)} %get-tuple-element.45), channel_id=1, source_target_pairs={{0,2},{1,3},{2,4},{3,5},{4,6},{5,7},{6,0},{7,1},{8,10},{9,11},{10,... | collective-permute-start | bytes 294920 | tf_op jit(solution)/shard_map/ppermute | solution.py:432
  22.3 4.8 %collective-permute-start.4 = (bf16[2,64,384]{2,1,0:T(8,128)(2,1)S(1)}, bf16[2,64,384]{2,1,0:T(8,128)(2,1)S(1)}, u32[]{:S(2)}, u32[]{:S(2)}) collective-permute-start(bf16[2,64,384]{2,1,0:T(8,128)(2,1)S(1)} %get-tuple-element.46), channel_id=1, source_target_pairs={{0,6},{1,7},{2,0},{3,1},{4,2},{5,3},{6,4},{7,5},{8,14},{9,15},{10,... | collective-permute-start | bytes 294920 | tf_op jit(solution)/shard_map/ppermute | solution.py:432
  24.0 5.1 %collective-permute-start.5 = (bf16[2,64,384]{2,1,0:T(8,128)(2,1)S(1)}, bf16[2,64,384]{2,1,0:T(8,128)(2,1)S(1)}, u32[]{:S(2)}, u32[]{:S(2)}) collective-permute-start(bf16[2,64,384]{2,1,0:T(8,128)(2,1)S(1)} %get-tuple-element.47), channel_id=1, source_target_pairs={{0,4},{1,5},{2,6},{3,7},{4,0},{5,1},{6,2},{7,3},{8,12},{9,13},{10,... | collective-permute-start | bytes 294920 | tf_op jit(solution)/shard_map/ppermute | solution.py:432
  26.3 11.2 %collective-permute-start.10 = (bf16[2,256,384]{2,1,0:T(8,128)(2,1)S(1)}, bf16[2,256,384]{2,1,0:T(8,128)(2,1)S(1)}, u32[]{:S(2)}, u32[]{:S(2)}) collective-permute-start(bf16[2,256,384]{2,1,0:T(8,128)(2,1)S(1)} %shard_map.113.refs_5_.refs_2_.refs_4_), channel_id=1, source_target_pairs={{0,96},{1,25},{2,98},{3,27},{4,100},{5,29},{6,102},{7,31},{8,104},... | collective-permute-start | bytes 1179656 | tf_op jit(solution)/shard_map/ppermute | solution.py:419
  27.1 10.5 %collective-permute-start.9 = (bf16[2,256,384]{2,1,0:T(8,128)(2,1)S(1)}, bf16[2,256,384]{2,1,0:T(8,128)(2,1)S(1)}, u32[]{:S(2)}, u32[]{:S(2)}) collective-permute-start(bf16[2,256,384]{2,1,0:T(8,128)(2,1)S(1)} %shard_map.113.refs_5_.refs_2_.refs_4_), channel_id=1, source_target_pairs={{0,32},{1,9},{2,34},{3,11},{4,36},{5,13},{6,38},{7,15},{8,40},{9,1... | collective-permute-start | bytes 1179656 | tf_op jit(solution)/shard_map/ppermute | solution.py:419
  29.1 11.9 %collective-permute-start.14 = (bf16[2,256,384]{2,1,0:T(8,128)(2,1)S(1)}, bf16[2,256,384]{2,1,0:T(8,128)(2,1)S(1)}, u32[]{:S(2)}, u32[]{:S(2)}) collective-permute-start(bf16[2,256,384]{2,1,0:T(8,128)(2,1)S(1)} %shard_map.112.refs_0_), channel_id=1, source_target_pairs={{0,16},{1,65},{2,18},{3,67},{4,20},{5,69},{6,22},{7,71},{8,24},{9,... | collective-permute-start | bytes 1179656 | tf_op jit(solution)/shard_map/ppermute | solution.py:416
  30.5 15.2 %collective-permute-start.13 = (bf16[2,256,384]{2,1,0:T(8,128)(2,1)S(1)}, bf16[2,256,384]{2,1,0:T(8,128)(2,1)S(1)}, u32[]{:S(2)}, u32[]{:S(2)}) collective-permute-start(bf16[2,256,384]{2,1,0:T(8,128)(2,1)S(1)} %shard_map.112.refs_0_), channel_id=1, source_target_pairs={{0,24},{1,97},{2,26},{3,99},{4,28},{5,101},{6,30},{7,103},{8,0},{9... | collective-permute-start | bytes 1179656 | tf_op jit(solution)/shard_map/ppermute | solution.py:416
  33.5 12.3 %collective-permute-start.12 = (bf16[2,256,384]{2,1,0:T(8,128)(2,1)S(1)}, bf16[2,256,384]{2,1,0:T(8,128)(2,1)S(1)}, u32[]{:S(2)}, u32[]{:S(2)}) collective-permute-start(bf16[2,256,384]{2,1,0:T(8,128)(2,1)S(1)} %shard_map.112.refs_0_), channel_id=1, source_target_pairs={{0,8},{1,33},{2,10},{3,35},{4,12},{5,37},{6,14},{7,39},{8,16},{9,4... | collective-permute-start | bytes 1179656 | tf_op jit(solution)/shard_map/ppermute | solution.py:416
  49.1 4.5 %collective-permute-start.18 = (f32[3,16,256]{2,1,0:T(8,128)S(1)}, f32[3,16,256]{2,1,0:T(8,128)S(1)}, u32[]{:S(2)}, u32[]{:S(2)}) collective-permute-start(f32[3,16,256]{2,1,0:T(8,128)S(1)} %shard_map.116.refs_6_.refs_8_), channel_id=1, source_target_pairs={{0,64},{1,17},{2,66},{3,19},{4,68},{5,21},{6,70},{7,23},{8,72},{9,... | collective-permute-start | bytes 147464 | tf_op jit(solution)/shard_map/ppermute | solution.py:419
  51.0 2.9 %collective-permute-start.17 = (f32[3,16,256]{2,1,0:T(8,128)S(1)}, f32[3,16,256]{2,1,0:T(8,128)S(1)}, u32[]{:S(2)}, u32[]{:S(2)}) collective-permute-start(f32[3,16,256]{2,1,0:T(8,128)S(1)} %shard_map.116.refs_6_.refs_8_), channel_id=1, source_target_pairs={{0,96},{1,25},{2,98},{3,27},{4,100},{5,29},{6,102},{7,31},{8,104},... | collective-permute-start | bytes 147464 | tf_op jit(solution)/shard_map/ppermute | solution.py:419
  52.7 4.3 %collective-permute-start.16 = (f32[3,16,256]{2,1,0:T(8,128)S(1)}, f32[3,16,256]{2,1,0:T(8,128)S(1)}, u32[]{:S(2)}, u32[]{:S(2)}) collective-permute-start(f32[3,16,256]{2,1,0:T(8,128)S(1)} %shard_map.116.refs_6_.refs_8_), channel_id=1, source_target_pairs={{0,32},{1,9},{2,34},{3,11},{4,36},{5,13},{6,38},{7,15},{8,40},{9,1... | collective-permute-start | bytes 147464 | tf_op jit(solution)/shard_map/ppermute | solution.py:419
  61.6 12.9 %collective-permute-start.19 = (bf16[4,256,384]{2,1,0:T(8,128)(2,1)S(1)}, bf16[4,256,384]{2,1,0:T(8,128)(2,1)S(1)}, u32[]{:S(2)}, u32[]{:S(2)}) collective-permute-start(bf16[4,256,384]{2,1,0:T(8,128)(2,1)S(1)} %get-tuple-element.56), channel_id=1, source_target_pairs={{0,16},{1,65},{2,18},{3,67},{4,20},{5,69},{6,22},{7,71},{8,24},{9,... | collective-permute-start | bytes 2359304 | tf_op jit(solution)/shard_map/ppermute | solution.py:416
  71.9 11.2 %collective-permute-start.23 = (bf16[4,256,384]{2,1,0:T(8,128)(2,1)S(1)}, bf16[4,256,384]{2,1,0:T(8,128)(2,1)S(1)}, u32[]{:S(2)}, u32[]{:S(2)}) collective-permute-start(bf16[4,256,384]{2,1,0:T(8,128)(2,1)S(1)} %get-tuple-element.62), channel_id=1, source_target_pairs={{0,24},{1,97},{2,26},{3,99},{4,28},{5,101},{6,30},{7,103},{8,0},{9... | collective-permute-start | bytes 2359304 | tf_op jit(solution)/shard_map/ppermute | solution.py:416
  73.1 12.3 %collective-permute-start.24 = (bf16[4,256,384]{2,1,0:T(8,128)(2,1)S(1)}, bf16[4,256,384]{2,1,0:T(8,128)(2,1)S(1)}, u32[]{:S(2)}, u32[]{:S(2)}) collective-permute-start(bf16[4,256,384]{2,1,0:T(8,128)(2,1)S(1)} %get-tuple-element.63), channel_id=1, source_target_pairs={{0,8},{1,33},{2,10},{3,35},{4,12},{5,37},{6,14},{7,39},{8,16},{9,4... | collective-permute-start | bytes 2359304 | tf_op jit(solution)/shard_map/ppermute | solution.py:416
  79.2 7.1 %collective-permute-start.20 = (bf16[256,384]{1,0:T(8,128)(2,1)S(1)}, bf16[256,384]{1,0:T(8,128)(2,1)S(1)}, u32[]{:S(2)}, u32[]{:S(2)}) collective-permute-start(bf16[256,384]{1,0:T(8,128)(2,1)S(1)} %get-tuple-element.58), channel_id=1, source_target_pairs={{0,96},{1,25},{2,98},{3,27},{4,100},{5,29},{6,102},{7,31},{8,104},... | collective-permute-start | bytes 589832 | tf_op jit(solution)/shard_map/ppermute | solution.py:419
  79.3 9.9 %collective-permute-start.21 = (bf16[256,384]{1,0:T(8,128)(2,1)S(1)}, bf16[256,384]{1,0:T(8,128)(2,1)S(1)}, u32[]{:S(2)}, u32[]{:S(2)}) collective-permute-start(bf16[256,384]{1,0:T(8,128)(2,1)S(1)} %get-tuple-element.59), channel_id=1, source_target_pairs={{0,32},{1,9},{2,34},{3,11},{4,36},{5,13},{6,38},{7,15},{8,40},{9,1... | collective-permute-start | bytes 589832 | tf_op jit(solution)/shard_map/ppermute | solution.py:419
  80.7 9.0 %collective-permute-start.22 = (bf16[256,384]{1,0:T(8,128)(2,1)S(1)}, bf16[256,384]{1,0:T(8,128)(2,1)S(1)}, u32[]{:S(2)}, u32[]{:S(2)}) collective-permute-start(bf16[256,384]{1,0:T(8,128)(2,1)S(1)} %get-tuple-element.60), channel_id=1, source_target_pairs={{0,64},{1,17},{2,66},{3,19},{4,68},{5,21},{6,70},{7,23},{8,72},{9,... | collective-permute-start | bytes 589832 | tf_op jit(solution)/shard_map/ppermute | solution.py:419
  90.8 19.9 %all-to-all-start = ((bf16[8,96,384]{2,1,0:T(8,128)(2,1)}), bf16[8,96,384]{2,1,0:T(8,128)(2,1)S(1)}, u32[]{:S(2)}, u32[]{:S(2)}) async-start(bf16[8,96,384]{2,1,0:T(8,128)(2,1)} %shard_map.120), calls=%async_computation | async-start | bytes 1179648 | tf_op jit(solution)/shard_map/all_to_all | solution.py:458

commit v5 on v4

--- a/solution.py
+++ b/solution.py
@@ -12,8 +12,9 @@
 SCALE = 1.0 / math.sqrt(HS)
 EXP2_SCALE = SCALE * math.log2(math.e)
 LOW = -1e30
-VMEM_LIMIT = 24 * 1024 * 1024
+VMEM_LIMIT = 12 * 1024 * 1024
 PACK_LIMIT = 56 * 1024 * 1024
+SAVED = (0, 1, 4)
 AXES = ("z", "y", "x", "c")
 OFFSETS = (0, -1, 1, 2)
 X_STEPS = (0, 1, 3, 2)
@@ -54,24 +55,11 @@
     return jnp.concatenate([bias] * (width // HS), axis=1)
 
 
-def flatten(blocks):
-    return [a for block in blocks for a in (block if isinstance(block, list) else [block])]
-
-
-def regroup(refs, blocks):
-    refs = list(refs)
-    return [[refs.pop(0) for _ in block] if isinstance(block, list) else refs.pop(0) for block in blocks]
-
-
-def take(block, which, lanes):
-    return block[which][:, lanes] if isinstance(block, list) else block[which, :, lanes]
-
-
 def wide(blocks, which, lanes):
-    return jnp.concatenate([take(block, which, lanes) for block in blocks], axis=0)
-
-
-def stat_step(keys, values, queries, grads, state, bias):
+    return jnp.concatenate([block[which, :, lanes] for block in blocks], axis=0)
+
+
+def stat_step(keys, values, queries, grads, state, bias, keep):
     top, total, dots = state
     scores = rows_dot(keys, queries)
     if bias is not None:
@@ -82,67 +70,71 @@
     grad_scores = rows_dot(values, grads)
     total = total * shrink + jnp.sum(weights, axis=0, keepdims=True)
     dots = dots * shrink + jnp.sum(weights * grad_scores, axis=0, keepdims=True)
+    if keep is not None:
+        keep(scores, grad_scores)
     return new_top, total, dots
 
 
-def stats_call(curs, hists, queries, groups, state_in=None, at=(0, 1, 2, 3)):
-    nk, nh, nq = len(flatten(curs)), len(hists), len(flatten(queries))
-    rows, feat = hists[0].shape[0] // 2 - 8, hists[0].shape[1]
-    tokens = queries[0].shape[1]
+def stats_call(curs, hists, queries, at, state_in=None, fresh=True, saved=()):
+    nk, nh, nq = len(curs), len(hists), len(queries)
+    tokens, feat = queries[0].shape[1:]
+    rows = tokens
     heads = feat // HS
-
-    def kernel(*refs):
-        cur, hist = regroup(refs[:nk], curs), refs[nk : nk + nh]
-        query = regroup(refs[nk + nh : nk + nh + nq], queries)
-        old, out = refs[nk + nh + nq], refs[-1]
+    width = tokens * nq
+
+    def kernel(*refs):
+        cur, refs = refs[:nk], refs[nk:]
+        hist, refs = refs[:nh], refs[nh:]
+        query, refs = refs[:nq], refs[nq:]
+        if state_in is not None:
+            old, refs = refs[0], refs[1:]
+        out, tiles = refs[0], refs[1:]
         if state_in is not None:
             out[...] = old[...]
 
         def step(head, _):
             lanes = head_lanes(head)
-            for blocks, cur_blocks, hist_blocks, fresh in groups:
-                width = tokens * len(blocks)
-                asked = wide([query[b] for b in blocks], 0, lanes)
-                grads = wide([query[b] for b in blocks], 1, lanes)
-                if fresh:
-                    state = (
-                        jnp.full((1, width), LOW, F32),
-                        jnp.zeros((1, width), F32),
-                        jnp.zeros((1, width), F32),
-                    )
-                else:
-                    state = tuple(
-                        jnp.concatenate(
-                            [old[i, pl.ds(head * 4 + at[b], 1), :] for b in blocks], axis=1
-                        )
-                        for i in range(3)
-                    )
-                for kb in cur_blocks:
-                    state = stat_step(
-                        take(cur[kb], 0, lanes), take(cur[kb], 1, lanes), asked, grads, state, None
-                    )
-                for kb in hist_blocks:
-                    state = stat_step(
-                        hist[kb][0:rows, lanes],
-                        hist[kb][rows : 2 * rows, lanes],
-                        asked,
-                        grads,
-                        state,
-                        dead_bias(hist[kb], rows, width),
-                    )
-                for i in range(3):
-                    for j, b in enumerate(blocks):
-                        out[i, pl.ds(head * 4 + at[b], 1), :] = state[i][
-                            :, j * tokens : (j + 1) * tokens
-                        ]
+            asked, grads = wide(query, 0, lanes), wide(query, 1, lanes)
+            places = [pl.ds(head * 4 + b, 1) for b in at]
+            if fresh:
+                low, zero = jnp.full((1, width), LOW, F32), jnp.zeros((1, width), F32)
+                state = (low, zero, zero)
+            else:
+                state = tuple(
+                    jnp.concatenate([old[i, row, :] for row in places], axis=1) for i in range(3)
+                )
+
+            def keep_of(block):
+                if block not in saved:
+                    return None
+                i = saved.index(block)
+
+                def keep(scores, grad_scores):
+                    tiles[2 * i][head] = scores
+                    tiles[2 * i + 1][head] = grad_scores
+
+                return keep
+
+            for i in range(nk):
+                keys, values = cur[i][0, :, lanes], cur[i][1, :, lanes]
+                state = stat_step(keys, values, asked, grads, state, None, keep_of(i))
+            for i in range(nh):
+                keys, values = hist[i][0:rows, lanes], hist[i][rows : 2 * rows, lanes]
+                bias = dead_bias(hist[i], rows, width)
+                state = stat_step(keys, values, asked, grads, state, bias, keep_of(nk + i))
+            for i in range(3):
+                for j, row in enumerate(places):
+                    out[i, row, :] = state[i][:, j * tokens : (j + 1) * tokens]
             return 0
 
         lax.fori_loop(0, heads, step, 0)
 
-    args = flatten(curs) + list(hists) + flatten(queries) + ([] if state_in is None else [state_in])
-    work = sum(len(b) * (len(c) + len(h)) for b, c, h, _ in groups) * rows * tokens
-    out = jax.ShapeDtypeStruct((3, 16, tokens), F32)
-    return call(kernel, out, args, flops=2 * 2 * 2 * work * feat, exps=work * heads)
+    args = list(curs) + list(hists) + list(queries) + ([] if state_in is None else [state_in])
+    work = (nk + nh) * rows * width
+    outs = [jax.ShapeDtypeStruct((3, 16, tokens), F32)]
+    outs += [jax.ShapeDtypeStruct((heads, rows, width), F32)] * (2 * len(saved))
+    outs = call(kernel, outs, args, flops=2 * 2 * 2 * work * feat, exps=work * heads)
+    return outs[0], [tuple(outs[1 + 2 * i : 3 + 2 * i]) for i in range(len(saved))]
 
 
 def combine_stats(stats, base_ref, delta_ref, heads):
@@ -167,20 +159,25 @@
             delta_ref[head, 0:1, at] = dots / total
 
 
-def grads_call(curs, hists, queries, stats, sums_in=None, far=None):
+def grads_call(curs, hists, queries, stats, tiles, sums_in=None, far=None):
     nk, nq = len(curs), len(queries)
-    rows, feat = hists[0].shape[0] // 2 - 8, hists[0].shape[1]
-    tokens = queries[0].shape[1]
+    tokens, feat = queries[0].shape[1:]
+    rows = tokens
     heads = feat // HS
     width = nq * tokens
-    n_cur, n_query = len(flatten(curs)), len(flatten(queries))
     last = far is not None
-
-    def kernel(*refs):
-        cur, refs = regroup(refs[:n_cur], curs), refs[n_cur:]
+    held = [a for pieces in tiles.values() for pair, _ in pieces for a in pair]
+
+    def kernel(*refs):
+        cur, refs = refs[:nk], refs[nk:]
         hist, refs = refs[:nk], refs[nk:]
-        query, refs = regroup(refs[:n_query], queries), refs[n_query:]
+        query, refs = refs[:nq], refs[nq:]
         stat, refs = refs[:4], refs[4:]
+        held_refs, refs = list(refs[: len(held)]), refs[len(held) :]
+        found = {
+            block: [(held_refs.pop(0), held_refs.pop(0), blocks) for _, blocks in pieces]
+            for block, pieces in tiles.items()
+        }
         if sums_in is not None:
             old, refs = refs[0], refs[1:]
         if last:
@@ -189,21 +186,25 @@
         base, delta = refs[-2:]
         combine_stats(stat, base, delta, heads)
 
-        def part(keys, values, queries, grads, lift, shift, bias):
-            scores = rows_dot(keys, queries) - lift
-            if bias is not None:
-                scores = scores + bias
-            prob = jnp.exp2(scores * EXP2_SCALE)
-            grad_scores = rows_dot(values, grads)
+        def saved_tile(block, which, head):
+            parts = {}
+            for *pair, blocks in found[block]:
+                for j, b in enumerate(blocks):
+                    parts[b] = pair[which][head, :, j * tokens : (j + 1) * tokens]
+            return jnp.concatenate([parts[b] for b in range(nq)], axis=1)
+
+        def part(block, head, keys, values, asked, grads, lift, shift, bias):
+            if block in found:
+                scores, grad_scores = saved_tile(block, 0, head), saved_tile(block, 1, head)
+            else:
+                scores, grad_scores = rows_dot(keys, asked), rows_dot(values, grads)
+                if bias is not None:
+                    scores = scores + bias
+            prob = jnp.exp2((scores - lift) * EXP2_SCALE)
             score_grad = (prob * (grad_scores - shift)).astype(BF16)
             grad_v = plain_dot(prob.astype(BF16), grads)
-            grad_k = plain_dot(score_grad, queries) * SCALE
-            return score_grad, grad_k, grad_v
-
-        def store(kb, i, lanes, value):
-            if last:
-                value = value + far_in[i, :, lanes].astype(F32)
-            key_out[kb][i, :, lanes] = value.astype(BF16)
+            grad_k = plain_dot(score_grad, asked) * SCALE
+            return score_grad, (grad_k, grad_v)
 
         def step(head, _):
             lanes = head_lanes(head)
@@ -211,27 +212,28 @@
             lift, shift = base[head, 0:1, :], delta[head, 0:1, :]
             total = None if sums_in is None else old[head]
             for kb in range(nk):
-                keys = take(cur[kb], 0, lanes)
-                score_a, grad_k, grad_v = part(
-                    keys, take(cur[kb], 1, lanes), asked, grads, lift, shift, None
-                )
-                store(kb, 0, lanes, grad_k)
-                store(kb, 1, lanes, grad_v)
-                old_keys = hist[kb][0:rows, lanes]
-                score_b, grad_k, grad_v = part(
-                    old_keys,
-                    hist[kb][rows : 2 * rows, lanes],
-                    asked,
-                    grads,
-                    lift,
-                    shift,
-                    dead_bias(hist[kb], rows, width),
-                )
-                store(kb, 2, lanes, grad_k)
-                store(kb, 3, lanes, grad_v)
+                blocks = [
+                    (cur[kb][0, :, lanes], cur[kb][1, :, lanes], None),
+                    (
+                        hist[kb][0:rows, lanes],
+                        hist[kb][rows : 2 * rows, lanes],
+                        dead_bias(hist[kb], rows, width),
+                    ),
+                ]
+                all_scores = []
+                for i, (keys, values, bias) in enumerate(blocks):
+                    score_grad, both = part(
+                        2 * kb + i, head, keys, values, asked, grads, lift, shift, bias
+                    )
+                    all_scores.append(score_grad)
+                    for j in range(2):
+                        value = both[j]
+                        if last:
+                            value = value + far_in[2 * i + j, :, lanes].astype(F32)
+                        key_out[kb][2 * i + j, :, lanes] = value.astype(BF16)
                 add = plain_dot(
-                    jnp.concatenate([keys, old_keys], axis=0).T,
-                    jnp.concatenate([score_a, score_b], axis=0),
+                    jnp.concatenate([keys for keys, _, _ in blocks], axis=0).T,
+                    jnp.concatenate(all_scores, axis=0),
                 )
                 total = add if total is None else total + add
             if last:
@@ -249,7 +251,7 @@
         sums = [jax.ShapeDtypeStruct((tokens, feat), BF16)] * nq
     else:
         sums = [jax.ShapeDtypeStruct((heads, HS, width), F32)]
-    args = flatten(curs) + list(hists) + flatten(queries) + list(stats)
+    args = list(curs) + list(hists) + list(queries) + list(stats) + held
     args += [a for a in (sums_in, far) if a is not None]
     work = nk * 2 * rows * width
     outs = call(
@@ -438,20 +440,29 @@
         cur0 = exchange(kept)
         curs = [cur0] + [to_key(cur0, -o) for o in OFFSETS[1:]]
         every = (0, 1, 2, 3)
-        state = stats_call(
-            curs[:1], hists, [queries[0], queries[3]], [((0, 1), (0,), every, True)], at=(0, 3)
+        ends, middle = (0, 3), (1, 2)
+        state, kept_a = stats_call(
+            curs[:1], hists, [queries[0], queries[3]], ends, saved=SAVED
         )
-        state = stats_call(
-            curs[:1], hists, queries[1:3], [((0, 1), (0,), every, True)], state, at=(1, 2)
+        state, kept_b = stats_call(curs[:1], hists, queries[1:3], middle, state, saved=SAVED)
+        state, kept_c = stats_call(
+            curs[1:], [], queries, every, state, fresh=False, saved=(0, 1, 2)
         )
-        state = stats_call(curs, hists[:1], queries, [(every, (1, 2, 3), (), False)], state)
         stats = [state] + [to_query(state, -o) for o in OFFSETS[1:]]
-
-        far, sums = grads_call(curs[3:], hists[3:], queries, stats)
+        held = {("cur", 1 + i): [(pair, every)] for i, pair in enumerate(kept_c)}
+        for i, a, b in zip(SAVED, kept_a, kept_b):
+            name = ("hist", i - 1) if i else ("cur", 0)
+            held[name] = [(a, ends), (b, middle)]
+
+        def tiles(*blocks):
+            names = [(kind, b) for b in blocks for kind in ("cur", "hist")]
+            return {i: held[name] for i, name in enumerate(names) if name in held}
+
+        far, sums = grads_call(curs[3:], hists[3:], queries, stats, tiles(3))
         far = to_key(far[0], 2)
-        near, sums = grads_call(curs[1:3], hists[1:3], queries, stats, sums[0])
+        near, sums = grads_call(curs[1:3], hists[1:3], queries, stats, tiles(1, 2), sums[0])
         near = [to_key(block, offset) for block, offset in zip(near, OFFSETS[1:3])]
-        own, sums = grads_call(curs[:1], hists[:1], queries, stats, sums[0], far)
+        own, sums = grads_call(curs[:1], hists[:1], queries, stats, tiles(0), sums[0], far)
         query_parts = [sums[0]] + [to_query(sums[i], OFFSETS[i]) for i in range(1, 4)]
 
         back = add_call(query_parts, own + near, sizes)

time: 112 us -> 108 us (0.964)
  Pallas kernels: 33.6 us -> 28.8 us
  waiting for transfers between devices: 36.1 us -> 38.1 us
    pallas_call x12, Pallas kernels: 31.2 us -> 26.3 us  [call(): pl.pallas_call(kernel, out_shape=outs, in_specs=[VMEM] * len(args), out_s...]
    ppermute x9, waiting for transfers between devices: 10.6 us -> 12.1 us  [to_key(): return lax.ppermute(value, AXES, key_move(step))]
  transfers between devices with their start and end apart: 26 -> 26, of which waited for: 16 -> 16; matrix products, arithmetic and copies ran while one was open for 0% -> 0% of each run, Pallas kernels for 19% -> 17%
where the time goes in v5:
time: 108 us
  starting transfers between devices  39 us (36%)
  waiting for transfers between devices  38.1 us (35%)
  Pallas kernels  28.8 us (27%)
  between operations  1.41 us (1%)
    pallas_call x12, Pallas kernels, call(): pl.pallas_call(kernel, out_shape=outs, in_specs=[VMEM] * len(args), out_s...  26.3 us
    ppermute x9, starting transfers between devices, to_key(): return lax.ppermute(value, AXES, key_move(step))  12.2 us
    ppermute x9, waiting for transfers between devices, to_key(): return lax.ppermute(value, AXES, key_move(step))  12.1 us
    all_to_all x1, waiting for transfers between devices, shards(): back = lax.all_to_all(back, ('x', 'c'), 0, 0, tiled=True)  9.38 us
    all_to_all x1, starting transfers between devices, shards(): back = lax.all_to_all(back, ('x', 'c'), 0, 0, tiled=True)  9.11 us
    ppermute x9, waiting for transfers between devices, to_query(): return lax.ppermute(value, AXES, query_move(step))  9.07 us
    ppermute x9, starting transfers between devices, to_query(): return lax.ppermute(value, AXES, query_move(step))  8.9 us
    ppermute x6, waiting for transfers between devices, exchange(): lax.ppermute(p, AXES, chip_move(d))  7.55 us
  transfers between devices with their start and end apart: 26, of which 16 were waited for; matrix products, arithmetic and copies ran while one was open for 0% of the time, Pallas kernels for 17%

profile of v5, /device:TPU:1, one launch (start us, length us, event | category | flops | bytes accessed | tf_op | source)
XLA Modules:
  0.0 108.2 jit_solution(7588750167891129436)
XLA Ops:
  1.3 2.4 %shard_map.110 = (bf16[2,4,2,32,384]{4,3,2,1,0:T(8,128)(2,1)}, bf16[2,4,2,32,384]{4,3,2,1,0:T(8,128)(2,1)}, bf16[528,384]{1,0:T(8,128)(2,1)}) custom-call(bf16[32,3072]{1,0:T(8,128)(2,1)} %refs_0_.1, bf16[32,3072]{1,0:T(8,128)(2,1)} %refs_1_.1, bf16[32,3072]{1,0:T(8,128)(2,1)} %refs_2_.1, bf16[32,3072]{1,0:T(8,128)(2,1)} %refs_3_.1, ...), custom_call_target="tpu_custom_call" | custom-call | tf_op jit(solution)/shard_map/pallas_call | solution.py:296
  3.7 1.5 %collective-permute-start = (bf16[2,4,2,32,384]{4,3,2,1,0:T(8,128)(2,1)}, bf16[2,4,2,32,384]{4,3,2,1,0:T(8,128)(2,1)S(1)}, u32[]{:S(2)}, u32[]{:S(2)}) collective-permute-start(bf16[2,4,2,32,384]{4,3,2,1,0:T(8,128)(2,1)} %get-tuple-element.59), channel_id=1, source_target_pairs={{0,1},{1,0},{2,3},{3,2},{4,5},{5,4},{6,7},{7,6},{8,9},{9,8},{10,11... | collective-permute-start | bytes 1179656 | tf_op jit(solution)/shard_map/ppermute | solution.py:427
  5.2 3.8 %collective-permute-start.2 = (bf16[528,384]{1,0:T(8,128)(2,1)}, bf16[528,384]{1,0:T(8,128)(2,1)S(1)}, u32[]{:S(2)}, u32[]{:S(2)}) collective-permute-start(bf16[528,384]{1,0:T(8,128)(2,1)} %get-tuple-element.64.refs_1_), channel_id=1, source_target_pairs={{0,24},{1,97},{2,26},{3,99},{4,28},{5,101},{6,30},{7,103},{8,0},{9... | collective-permute-start | bytes 1216520 | tf_op jit(solution)/shard_map/ppermute | solution.py:418
  10.1 1.3 %collective-permute-start.6 = (bf16[2,64,384]{2,1,0:T(8,128)(2,1)S(1)}, bf16[2,64,384]{2,1,0:T(8,128)(2,1)S(1)}, u32[]{:S(2)}, u32[]{:S(2)}) collective-permute-start(bf16[2,64,384]{2,1,0:T(8,128)(2,1)S(1)} %get-tuple-element.70), channel_id=1, source_target_pairs={{0,2},{1,3},{2,4},{3,5},{4,6},{5,7},{6,0},{7,1},{8,10},{9,11},{10,... | collective-permute-start | bytes 294920 | tf_op jit(solution)/shard_map/ppermute | solution.py:434
  11.4 1.5 %collective-permute-start.7 = (bf16[2,64,384]{2,1,0:T(8,128)(2,1)S(1)}, bf16[2,64,384]{2,1,0:T(8,128)(2,1)S(1)}, u32[]{:S(2)}, u32[]{:S(2)}) collective-permute-start(bf16[2,64,384]{2,1,0:T(8,128)(2,1)S(1)} %get-tuple-element.71), channel_id=1, source_target_pairs={{0,6},{1,7},{2,0},{3,1},{4,2},{5,3},{6,4},{7,5},{8,14},{9,15},{10,... | collective-permute-start | bytes 294920 | tf_op jit(solution)/shard_map/ppermute | solution.py:434
  12.9 1.5 %collective-permute-start.8 = (bf16[2,64,384]{2,1,0:T(8,128)(2,1)S(1)}, bf16[2,64,384]{2,1,0:T(8,128)(2,1)S(1)}, u32[]{:S(2)}, u32[]{:S(2)}) collective-permute-start(bf16[2,64,384]{2,1,0:T(8,128)(2,1)S(1)} %get-tuple-element.72), channel_id=1, source_target_pairs={{0,4},{1,5},{2,6},{3,7},{4,0},{5,1},{6,2},{7,3},{8,12},{9,13},{10,... | collective-permute-start | bytes 294920 | tf_op jit(solution)/shard_map/ppermute | solution.py:434
  14.4 1.6 %collective-permute-done.6.refs_1_ = bf16[2,64,384]{2,1,0:T(8,128)(2,1)S(1)} collective-permute-done((bf16[2,64,384]{2,1,0:T(8,128)(2,1)S(1)}, bf16[2,64,384]{2,1,0:T(8,128)(2,1)S(1)}, u32[]{:S(2)}, u32[]{:S(2)}) %collective-permute-start.6) | collective-permute-done | bytes 98336 | tf_op jit(solution)/shard_map/ppermute | solution.py:434
  16.3 2.7 %collective-permute-done.8.refs_3_ = bf16[2,64,384]{2,1,0:T(8,128)(2,1)S(1)} collective-permute-done((bf16[2,64,384]{2,1,0:T(8,128)(2,1)S(1)}, bf16[2,64,384]{2,1,0:T(8,128)(2,1)S(1)}, u32[]{:S(2)}, u32[]{:S(2)}) %collective-permute-start.8) | collective-permute-done | bytes 98336 | tf_op jit(solution)/shard_map/ppermute | solution.py:434
  19.0 2.3 %collective-permute-start.11 = (bf16[2,256,384]{2,1,0:T(8,128)(2,1)S(1)}, bf16[2,256,384]{2,1,0:T(8,128)(2,1)S(1)}, u32[]{:S(2)}, u32[]{:S(2)}) collective-permute-start(bf16[2,256,384]{2,1,0:T(8,128)(2,1)S(1)} %shard_map.113.refs_5_.refs_3_.refs_2_.refs_4_), channel_id=1, source_target_pairs={{0,64},{1,17},{2,66},{3,19},{4,68},{5,21},{6,70},{7,23},{8,72},{9,... | collective-permute-start | bytes 1179656 | tf_op jit(solution)/shard_map/ppermute | solution.py:421
  22.3 1.7 %collective-permute-start.4 = (bf16[2,64,384]{2,1,0:T(8,128)(2,1)S(1)}, bf16[2,64,384]{2,1,0:T(8,128)(2,1)S(1)}, u32[]{:S(2)}, u32[]{:S(2)}) collective-permute-start(bf16[2,64,384]{2,1,0:T(8,128)(2,1)S(1)} %get-tuple-element.67), channel_id=1, source_target_pairs={{0,6},{1,7},{2,0},{3,1},{4,2},{5,3},{6,4},{7,5},{8,14},{9,15},{10,... | collective-permute-start | bytes 294920 | tf_op jit(solution)/shard_map/ppermute | solution.py:434
  24.3 2.0 %collective-permute-done.3.refs_1_ = bf16[2,64,384]{2,1,0:T(8,128)(2,1)S(1)} collective-permute-done((bf16[2,64,384]{2,1,0:T(8,128)(2,1)S(1)}, bf16[2,64,384]{2,1,0:T(8,128)(2,1)S(1)}, u32[]{:S(2)}, u32[]{:S(2)}) %collective-permute-start.3) | collective-permute-done | bytes 98336 | tf_op jit(solution)/shard_map/ppermute | solution.py:434
  27.8 1.3 %collective-permute-done.5.refs_3_ = bf16[2,64,384]{2,1,0:T(8,128)(2,1)S(1)} collective-permute-done((bf16[2,64,384]{2,1,0:T(8,128)(2,1)S(1)}, bf16[2,64,384]{2,1,0:T(8,128)(2,1)S(1)}, u32[]{:S(2)}, u32[]{:S(2)}) %collective-permute-start.5) | collective-permute-done | bytes 98336 | tf_op jit(solution)/shard_map/ppermute | solution.py:434
  29.1 1.4 %collective-permute-start.14 = (bf16[2,256,384]{2,1,0:T(8,128)(2,1)S(1)}, bf16[2,256,384]{2,1,0:T(8,128)(2,1)S(1)}, u32[]{:S(2)}, u32[]{:S(2)}) collective-permute-start(bf16[2,256,384]{2,1,0:T(8,128)(2,1)S(1)} %shard_map.112.refs_0_), channel_id=1, source_target_pairs={{0,16},{1,65},{2,18},{3,67},{4,20},{5,69},{6,22},{7,71},{8,24},{9,... | collective-permute-start | bytes 1179656 | tf_op jit(solution)/shard_map/ppermute | solution.py:418
  30.5 3.0 %collective-permute-start.13 = (bf16[2,256,384]{2,1,0:T(8,128)(2,1)S(1)}, bf16[2,256,384]{2,1,0:T(8,128)(2,1)S(1)}, u32[]{:S(2)}, u32[]{:S(2)}) collective-permute-start(bf16[2,256,384]{2,1,0:T(8,128)(2,1)S(1)} %shard_map.112.refs_0_), channel_id=1, source_target_pairs={{0,24},{1,97},{2,26},{3,99},{4,28},{5,101},{6,30},{7,103},{8,0},{9... | collective-permute-start | bytes 1179656 | tf_op jit(solution)/shard_map/ppermute | solution.py:418
  34.1 3.4 %shard_map.114 = (f32[3,16,256]{2,1,0:T(8,128)S(1)}, f32[3,256,512]{2,1,0:T(8,128)S(1)}, f32[3,256,512]{2,1,0:T(8,128)S(1)}, f32[3,256,512]{2,1,0:T(8,128)S(1)},...) custom-call(bf16[2,256,384]{2,1,0:T(8,128)(2,1)S(1)} %shard_map.112.refs_0_, ...), custom_call_target="tpu_custom_call" | custom-call | flops 31457280 | bytes 43776 | tf_op jit(solution)/shard_map/pallas_call | solution.py:36
  37.5 3.4 %shard_map.115 = (f32[3,16,256]{2,1,0:T(8,128)S(1)}, f32[3,256,512]{2,1,0:T(8,128)S(1)}, f32[3,256,512]{2,1,0:T(8,128)S(1)}, f32[3,256,512]{2,1,0:T(8,128)S(1)},...) custom-call(bf16[2,256,384]{2,1,0:T(8,128)(2,1)S(1)} %shard_map.112.refs_0_, ...), custom_call_target="tpu_custom_call" | custom-call | flops 31457280 | bytes 44544 | tf_op jit(solution)/shard_map/pallas_call | solution.py:36
  41.0 4.7 %collective-permute-done.13.refs_1_ = bf16[2,256,384]{2,1,0:T(8,128)(2,1)S(1)} collective-permute-done((bf16[2,256,384]{2,1,0:T(8,128)(2,1)S(1)}, bf16[2,256,384]{2,1,0:T(8,128)(2,1)S(1)}, u32[]{:S(2)}, u32[]{:S(2)}) %collective-permute-start.13) | collective-permute-done | bytes 393248 | tf_op jit(solution)/shard_map/ppermute | solution.py:418
  45.8 3.3 %shard_map.116 = (f32[3,16,256]{2,1,0:T(8,128)S(1)}, f32[3,256,1024]{2,1,0:T(8,128)S(1)}, f32[3,256,1024]{2,1,0:T(8,128)S(1)}, f32[3,256,1024]{2,1,0:T(8,128)S(1...) custom-call(bf16[2,256,384]{2,1,0:T(8,128)(2,1)S(1)} %collective-permute-done.12.refs_0_, ...), custom_call_target="tpu_custom_call" | custom-call | flops 37748736 | bytes 43776 | tf_op jit(solution)/shard_map/pallas_call | solution.py:36
  49.1 1.9 %collective-permute-start.18 = (f32[3,16,256]{2,1,0:T(8,128)S(1)}, f32[3,16,256]{2,1,0:T(8,128)S(1)}, u32[]{:S(2)}, u32[]{:S(2)}) collective-permute-start(f32[3,16,256]{2,1,0:T(8,128)S(1)} %get-tuple-element.77.refs_6_.refs_8_), channel_id=1, source_target_pairs={{0,64},{1,17},{2,66},{3,19},{4,68},{5,21},{6,70},{7,23},{8,72},{9,... | collective-permute-start | bytes 147464 | tf_op jit(solution)/shard_map/ppermute | solution.py:421
  51.0 1.7 %collective-permute-start.17 = (f32[3,16,256]{2,1,0:T(8,128)S(1)}, f32[3,16,256]{2,1,0:T(8,128)S(1)}, u32[]{:S(2)}, u32[]{:S(2)}) collective-permute-start(f32[3,16,256]{2,1,0:T(8,128)S(1)} %get-tuple-element.77.refs_6_.refs_8_), channel_id=1, source_target_pairs={{0,96},{1,25},{2,98},{3,27},{4,100},{5,29},{6,102},{7,31},{8,104},... | collective-permute-start | bytes 147464 | tf_op jit(solution)/shard_map/ppermute | solution.py:421
  53.9 3.0 %collective-permute-done.16.refs_7_.refs_9_ = f32[3,16,256]{2,1,0:T(8,128)S(1)} collective-permute-done((f32[3,16,256]{2,1,0:T(8,128)S(1)}, f32[3,16,256]{2,1,0:T(8,128)S(1)}, u32[]{:S(2)}, u32[]{:S(2)}) %collective-permute-start.16) | collective-permute-done | bytes 49184 | tf_op jit(solution)/shard_map/ppermute | solution.py:421
  56.9 2.9 %shard_map.117 = (bf16[4,256,384]{2,1,0:T(8,128)(2,1)S(1)}, f32[3,128,1024]{2,1,0:T(8,128)S(1)}) custom-call(bf16[2,256,384]{2,1,0:T(8,128)(2,1)S(1)} %collective-permute-done.14.refs_2_.refs_0_, bf16[528,384]{1,0:T(8,128)(2,1)S(1)} %collective-permute-done.15.refs_4_.refs_1_, bf16[2,256,384]{2,1,0:T(8,128)(2,1)S(1)} %shard_map.113.refs_5_.refs_3_.refs_2_.refs_4_, ...), custom_call_target="tpu_custom_call" | custom-call | flops 62914560 | bytes 236736 | tf_op jit(solution)/shard_map/pallas_call | solution.py:36
  59.9 1.6 %collective-permute-start.19 = (bf16[4,256,384]{2,1,0:T(8,128)(2,1)S(1)}, bf16[4,256,384]{2,1,0:T(8,128)(2,1)S(1)}, u32[]{:S(2)}, u32[]{:S(2)}) collective-permute-start(bf16[4,256,384]{2,1,0:T(8,128)(2,1)S(1)} %get-tuple-element.98), channel_id=1, source_target_pairs={{0,16},{1,65},{2,18},{3,67},{4,20},{5,69},{6,22},{7,71},{8,24},{9,... | collective-permute-start | bytes 2359304 | tf_op jit(solution)/shard_map/ppermute | solution.py:418
  61.5 7.1 %shard_map.118 = (bf16[4,256,384]{2,1,0:T(8,128)(2,1)S(1)}, bf16[4,256,384]{2,1,0:T(8,128)(2,1)S(1)}, f32[3,128,1024]{2,1,0:T(8,128)S(1)}) custom-call(bf16[2,256,384]{2,1,0:T(8,128)(2,1)S(1)} %collective-permute-done.12.refs_0_, bf16[2,256,384]{2,1,0:T(8,128)(2,1)S(1)} %collective-permute-done.13.refs_1_, ...), custom_call_target="tpu_custom_call" | custom-call | flops 125829120 | bytes 273792 | tf_op jit(solution)/shard_map/pallas_call | solution.py:36
  70.1 2.7 %collective-permute-done.19.refs_19_ = bf16[4,256,384]{2,1,0:T(8,128)(2,1)S(1)} collective-permute-done((bf16[4,256,384]{2,1,0:T(8,128)(2,1)S(1)}, bf16[4,256,384]{2,1,0:T(8,128)(2,1)S(1)}, u32[]{:S(2)}, u32[]{:S(2)}) %collective-permute-start.19) | collective-permute-done | bytes 786464 | tf_op jit(solution)/shard_map/ppermute | solution.py:418
  72.8 3.3 %shard_map.119 = (bf16[4,256,384]{2,1,0:T(8,128)(2,1)S(1)}, bf16[256,384]{1,0:T(8,128)(2,1)S(1)}, bf16[256,384]{1,0:T(8,128)(2,1)S(1)}, bf16[256,384]{1,0:T(8,128)(2,1)S(1)}, bf16[256,384]{1,0:T(8,128)(2,1)S(1)}) custom-call(bf16[2,256,384]{2,1,0:T(8,128)(2,1)S(1)} %shard_map.112.refs_0_, bf16[528,384]{1,0:T(8,128)(2,1)S(1)} %copy-done, ...), custom_call_target="tpu_custom_call" | custom-call | flops 62914560 | bytes 273600 | tf_op jit(solution)/shard_map/pallas_call | solution.py:36
  76.2 1.5 %collective-permute-start.21 = (bf16[256,384]{1,0:T(8,128)(2,1)S(1)}, bf16[256,384]{1,0:T(8,128)(2,1)S(1)}, u32[]{:S(2)}, u32[]{:S(2)}) collective-permute-start(bf16[256,384]{1,0:T(8,128)(2,1)S(1)} %get-tuple-element.101), channel_id=1, source_target_pairs={{0,32},{1,9},{2,34},{3,11},{4,36},{5,13},{6,38},{7,15},{8,40},{9,1... | collective-permute-start | bytes 589832 | tf_op jit(solution)/shard_map/ppermute | solution.py:421
  77.6 2.1 %collective-permute-done.23.refs_5_.refs_1_ = bf16[4,256,384]{2,1,0:T(8,128)(2,1)S(1)} collective-permute-done((bf16[4,256,384]{2,1,0:T(8,128)(2,1)S(1)}, bf16[4,256,384]{2,1,0:T(8,128)(2,1)S(1)}, u32[]{:S(2)}, u32[]{:S(2)}) %collective-permute-start.23) | collective-permute-done | bytes 786464 | tf_op jit(solution)/shard_map/ppermute | solution.py:418
  79.7 2.4 %collective-permute-done.24.refs_6_.refs_2_ = bf16[4,256,384]{2,1,0:T(8,128)(2,1)S(1)} collective-permute-done((bf16[4,256,384]{2,1,0:T(8,128)(2,1)S(1)}, bf16[4,256,384]{2,1,0:T(8,128)(2,1)S(1)}, u32[]{:S(2)}, u32[]{:S(2)}) %collective-permute-start.24) | collective-permute-done | bytes 786464 | tf_op jit(solution)/shard_map/ppermute | solution.py:418
  83.2 2.7 %collective-permute-done.21.refs_2_ = bf16[256,384]{1,0:T(8,128)(2,1)S(1)} collective-permute-done((bf16[256,384]{1,0:T(8,128)(2,1)S(1)}, bf16[256,384]{1,0:T(8,128)(2,1)S(1)}, u32[]{:S(2)}, u32[]{:S(2)}) %collective-permute-start.21) | collective-permute-done | bytes 196640 | tf_op jit(solution)/shard_map/ppermute | solution.py:421
  88.0 9.1 %all-to-all-start = ((bf16[8,96,384]{2,1,0:T(8,128)(2,1)}), bf16[8,96,384]{2,1,0:T(8,128)(2,1)S(1)}, u32[]{:S(2)}, u32[]{:S(2)}) async-start(bf16[8,96,384]{2,1,0:T(8,128)(2,1)} %shard_map.120), calls=%async_computation | async-start | bytes 1179648 | tf_op jit(solution)/shard_map/all_to_all | solution.py:469
  98.0 9.4 %all-to-all-done.ref = bf16[8,96,384]{2,1,0:T(8,128)(2,1)S(1)} async-done(((bf16[8,96,384]{2,1,0:T(8,128)(2,1)}), bf16[8,96,384]{2,1,0:T(8,128)(2,1)S(1)}, u32[]{:S(2)}, u32[]{:S(2)}) %all-to-all-start) | async-done | bytes 589856 | tf_op jit(solution)/shard_map/all_to_all | solution.py:469
  (37 shorter events, 12.6 us)
Async XLA Ops:
  3.7 30.4 %copy-start = (bf16[528,384]{1,0:T(8,128)(2,1)S(1)}, bf16[528,384]{1,0:T(8,128)(2,1)}, u32[]{:S(2)}) copy-start(bf16[528,384]{1,0:T(8,128)(2,1)} %get-tuple-element.64.refs_1_) | copy-start | bytes 1216516
  3.7 5.3 %collective-permute-start = (bf16[2,4,2,32,384]{4,3,2,1,0:T(8,128)(2,1)}, bf16[2,4,2,32,384]{4,3,2,1,0:T(8,128)(2,1)S(1)}, u32[]{:S(2)}, u32[]{:S(2)}) collective-permute-start(bf16[2,4,2,32,384]{4,3,2,1,0:T(8,128)(2,1)} %get-tuple-element.59), channel_id=1, source_target_pairs={{0,1},{1,0},{2,3},{3,2},{4,5},{5,4},{6,7},{7,6},{8,9},{9,8},{10,11... | collective-permute-start | bytes 1179656 | tf_op jit(solution)/shard_map/ppermute | solution.py:427
  5.2 16.1 %collective-permute-start.2 = (bf16[528,384]{1,0:T(8,128)(2,1)}, bf16[528,384]{1,0:T(8,128)(2,1)S(1)}, u32[]{:S(2)}, u32[]{:S(2)}) collective-permute-start(bf16[528,384]{1,0:T(8,128)(2,1)} %get-tuple-element.64.refs_1_), channel_id=1, source_target_pairs={{0,24},{1,97},{2,26},{3,99},{4,28},{5,101},{6,30},{7,103},{8,0},{9... | collective-permute-start | bytes 1216520 | tf_op jit(solution)/shard_map/ppermute | solution.py:418
  9.1 12.3 %collective-permute-start.1 = (bf16[528,384]{1,0:T(8,128)(2,1)}, bf16[528,384]{1,0:T(8,128)(2,1)S(1)}, u32[]{:S(2)}, u32[]{:S(2)}) collective-permute-start(bf16[528,384]{1,0:T(8,128)(2,1)} %get-tuple-element.64.refs_1_), channel_id=1, source_target_pairs={{0,8},{1,33},{2,10},{3,35},{4,12},{5,37},{6,14},{7,39},{8,16},{9,4... | collective-permute-start | bytes 1216520 | tf_op jit(solution)/shard_map/ppermute | solution.py:418
  9.1 1.0 copy-start.1
  10.1 5.9 %collective-permute-start.6 = (bf16[2,64,384]{2,1,0:T(8,128)(2,1)S(1)}, bf16[2,64,384]{2,1,0:T(8,128)(2,1)S(1)}, u32[]{:S(2)}, u32[]{:S(2)}) collective-permute-start(bf16[2,64,384]{2,1,0:T(8,128)(2,1)S(1)} %get-tuple-element.70), channel_id=1, source_target_pairs={{0,2},{1,3},{2,4},{3,5},{4,6},{5,7},{6,0},{7,1},{8,10},{9,11},{10,... | collective-permute-start | bytes 294920 | tf_op jit(solution)/shard_map/ppermute | solution.py:434
  11.4 4.9 %collective-permute-start.7 = (bf16[2,64,384]{2,1,0:T(8,128)(2,1)S(1)}, bf16[2,64,384]{2,1,0:T(8,128)(2,1)S(1)}, u32[]{:S(2)}, u32[]{:S(2)}) collective-permute-start(bf16[2,64,384]{2,1,0:T(8,128)(2,1)S(1)} %get-tuple-element.71), channel_id=1, source_target_pairs={{0,6},{1,7},{2,0},{3,1},{4,2},{5,3},{6,4},{7,5},{8,14},{9,15},{10,... | collective-permute-start | bytes 294920 | tf_op jit(solution)/shard_map/ppermute | solution.py:434
  12.9 6.1 %collective-permute-start.8 = (bf16[2,64,384]{2,1,0:T(8,128)(2,1)S(1)}, bf16[2,64,384]{2,1,0:T(8,128)(2,1)S(1)}, u32[]{:S(2)}, u32[]{:S(2)}) collective-permute-start(bf16[2,64,384]{2,1,0:T(8,128)(2,1)S(1)} %get-tuple-element.72), channel_id=1, source_target_pairs={{0,4},{1,5},{2,6},{3,7},{4,0},{5,1},{6,2},{7,3},{8,12},{9,13},{10,... | collective-permute-start | bytes 294920 | tf_op jit(solution)/shard_map/ppermute | solution.py:434
  16.0 14.4 %collective-permute-start.15 = (bf16[528,384]{1,0:T(8,128)(2,1)}, bf16[528,384]{1,0:T(8,128)(2,1)S(1)}, u32[]{:S(2)}, u32[]{:S(2)}) collective-permute-start(bf16[528,384]{1,0:T(8,128)(2,1)} %get-tuple-element.64.refs_1_), channel_id=1, source_target_pairs={{0,16},{1,65},{2,18},{3,67},{4,20},{5,69},{6,22},{7,71},{8,24},{9,... | collective-permute-start | bytes 1216520 | tf_op jit(solution)/shard_map/ppermute | solution.py:418
  19.0 14.5 %collective-permute-start.11 = (bf16[2,256,384]{2,1,0:T(8,128)(2,1)S(1)}, bf16[2,256,384]{2,1,0:T(8,128)(2,1)S(1)}, u32[]{:S(2)}, u32[]{:S(2)}) collective-permute-start(bf16[2,256,384]{2,1,0:T(8,128)(2,1)S(1)} %shard_map.113.refs_5_.refs_3_.refs_2_.refs_4_), channel_id=1, source_target_pairs={{0,64},{1,17},{2,66},{3,19},{4,68},{5,21},{6,70},{7,23},{8,72},{9,... | collective-permute-start | bytes 1179656 | tf_op jit(solution)/shard_map/ppermute | solution.py:421
  21.3 5.0 %collective-permute-start.3 = (bf16[2,64,384]{2,1,0:T(8,128)(2,1)S(1)}, bf16[2,64,384]{2,1,0:T(8,128)(2,1)S(1)}, u32[]{:S(2)}, u32[]{:S(2)}) collective-permute-start(bf16[2,64,384]{2,1,0:T(8,128)(2,1)S(1)} %get-tuple-element.66), channel_id=1, source_target_pairs={{0,2},{1,3},{2,4},{3,5},{4,6},{5,7},{6,0},{7,1},{8,10},{9,11},{10,... | collective-permute-start | bytes 294920 | tf_op jit(solution)/shard_map/ppermute | solution.py:434
  22.3 4.8 %collective-permute-start.4 = (bf16[2,64,384]{2,1,0:T(8,128)(2,1)S(1)}, bf16[2,64,384]{2,1,0:T(8,128)(2,1)S(1)}, u32[]{:S(2)}, u32[]{:S(2)}) collective-permute-start(bf16[2,64,384]{2,1,0:T(8,128)(2,1)S(1)} %get-tuple-element.67), channel_id=1, source_target_pairs={{0,6},{1,7},{2,0},{3,1},{4,2},{5,3},{6,4},{7,5},{8,14},{9,15},{10,... | collective-permute-start | bytes 294920 | tf_op jit(solution)/shard_map/ppermute | solution.py:434
  24.0 5.1 %collective-permute-start.5 = (bf16[2,64,384]{2,1,0:T(8,128)(2,1)S(1)}, bf16[2,64,384]{2,1,0:T(8,128)(2,1)S(1)}, u32[]{:S(2)}, u32[]{:S(2)}) collective-permute-start(bf16[2,64,384]{2,1,0:T(8,128)(2,1)S(1)} %get-tuple-element.68), channel_id=1, source_target_pairs={{0,4},{1,5},{2,6},{3,7},{4,0},{5,1},{6,2},{7,3},{8,12},{9,13},{10,... | collective-permute-start | bytes 294920 | tf_op jit(solution)/shard_map/ppermute | solution.py:434
  26.3 11.2 %collective-permute-start.10 = (bf16[2,256,384]{2,1,0:T(8,128)(2,1)S(1)}, bf16[2,256,384]{2,1,0:T(8,128)(2,1)S(1)}, u32[]{:S(2)}, u32[]{:S(2)}) collective-permute-start(bf16[2,256,384]{2,1,0:T(8,128)(2,1)S(1)} %shard_map.113.refs_5_.refs_3_.refs_2_.refs_4_), channel_id=1, source_target_pairs={{0,96},{1,25},{2,98},{3,27},{4,100},{5,29},{6,102},{7,31},{8,104},... | collective-permute-start | bytes 1179656 | tf_op jit(solution)/shard_map/ppermute | solution.py:421
  27.1 10.4 %collective-permute-start.9 = (bf16[2,256,384]{2,1,0:T(8,128)(2,1)S(1)}, bf16[2,256,384]{2,1,0:T(8,128)(2,1)S(1)}, u32[]{:S(2)}, u32[]{:S(2)}) collective-permute-start(bf16[2,256,384]{2,1,0:T(8,128)(2,1)S(1)} %shard_map.113.refs_5_.refs_3_.refs_2_.refs_4_), channel_id=1, source_target_pairs={{0,32},{1,9},{2,34},{3,11},{4,36},{5,13},{6,38},{7,15},{8,40},{9,1... | collective-permute-start | bytes 1179656 | tf_op jit(solution)/shard_map/ppermute | solution.py:421
  29.1 11.9 %collective-permute-start.14 = (bf16[2,256,384]{2,1,0:T(8,128)(2,1)S(1)}, bf16[2,256,384]{2,1,0:T(8,128)(2,1)S(1)}, u32[]{:S(2)}, u32[]{:S(2)}) collective-permute-start(bf16[2,256,384]{2,1,0:T(8,128)(2,1)S(1)} %shard_map.112.refs_0_), channel_id=1, source_target_pairs={{0,16},{1,65},{2,18},{3,67},{4,20},{5,69},{6,22},{7,71},{8,24},{9,... | collective-permute-start | bytes 1179656 | tf_op jit(solution)/shard_map/ppermute | solution.py:418
  30.5 15.2 %collective-permute-start.13 = (bf16[2,256,384]{2,1,0:T(8,128)(2,1)S(1)}, bf16[2,256,384]{2,1,0:T(8,128)(2,1)S(1)}, u32[]{:S(2)}, u32[]{:S(2)}) collective-permute-start(bf16[2,256,384]{2,1,0:T(8,128)(2,1)S(1)} %shard_map.112.refs_0_), channel_id=1, source_target_pairs={{0,24},{1,97},{2,26},{3,99},{4,28},{5,101},{6,30},{7,103},{8,0},{9... | collective-permute-start | bytes 1179656 | tf_op jit(solution)/shard_map/ppermute | solution.py:418
  33.5 12.3 %collective-permute-start.12 = (bf16[2,256,384]{2,1,0:T(8,128)(2,1)S(1)}, bf16[2,256,384]{2,1,0:T(8,128)(2,1)S(1)}, u32[]{:S(2)}, u32[]{:S(2)}) collective-permute-start(bf16[2,256,384]{2,1,0:T(8,128)(2,1)S(1)} %shard_map.112.refs_0_), channel_id=1, source_target_pairs={{0,8},{1,33},{2,10},{3,35},{4,12},{5,37},{6,14},{7,39},{8,16},{9,4... | collective-permute-start | bytes 1179656 | tf_op jit(solution)/shard_map/ppermute | solution.py:418
  49.1 4.5 %collective-permute-start.18 = (f32[3,16,256]{2,1,0:T(8,128)S(1)}, f32[3,16,256]{2,1,0:T(8,128)S(1)}, u32[]{:S(2)}, u32[]{:S(2)}) collective-permute-start(f32[3,16,256]{2,1,0:T(8,128)S(1)} %get-tuple-element.77.refs_6_.refs_8_), channel_id=1, source_target_pairs={{0,64},{1,17},{2,66},{3,19},{4,68},{5,21},{6,70},{7,23},{8,72},{9,... | collective-permute-start | bytes 147464 | tf_op jit(solution)/shard_map/ppermute | solution.py:421
  51.0 2.9 %collective-permute-start.17 = (f32[3,16,256]{2,1,0:T(8,128)S(1)}, f32[3,16,256]{2,1,0:T(8,128)S(1)}, u32[]{:S(2)}, u32[]{:S(2)}) collective-permute-start(f32[3,16,256]{2,1,0:T(8,128)S(1)} %get-tuple-element.77.refs_6_.refs_8_), channel_id=1, source_target_pairs={{0,96},{1,25},{2,98},{3,27},{4,100},{5,29},{6,102},{7,31},{8,104},... | collective-permute-start | bytes 147464 | tf_op jit(solution)/shard_map/ppermute | solution.py:421
  52.7 4.2 %collective-permute-start.16 = (f32[3,16,256]{2,1,0:T(8,128)S(1)}, f32[3,16,256]{2,1,0:T(8,128)S(1)}, u32[]{:S(2)}, u32[]{:S(2)}) collective-permute-start(f32[3,16,256]{2,1,0:T(8,128)S(1)} %get-tuple-element.77.refs_6_.refs_8_), channel_id=1, source_target_pairs={{0,32},{1,9},{2,34},{3,11},{4,36},{5,13},{6,38},{7,15},{8,40},{9,1... | collective-permute-start | bytes 147464 | tf_op jit(solution)/shard_map/ppermute | solution.py:421
  59.9 12.9 %collective-permute-start.19 = (bf16[4,256,384]{2,1,0:T(8,128)(2,1)S(1)}, bf16[4,256,384]{2,1,0:T(8,128)(2,1)S(1)}, u32[]{:S(2)}, u32[]{:S(2)}) collective-permute-start(bf16[4,256,384]{2,1,0:T(8,128)(2,1)S(1)} %get-tuple-element.98), channel_id=1, source_target_pairs={{0,16},{1,65},{2,18},{3,67},{4,20},{5,69},{6,22},{7,71},{8,24},{9,... | collective-permute-start | bytes 2359304 | tf_op jit(solution)/shard_map/ppermute | solution.py:418
  68.5 11.2 %collective-permute-start.23 = (bf16[4,256,384]{2,1,0:T(8,128)(2,1)S(1)}, bf16[4,256,384]{2,1,0:T(8,128)(2,1)S(1)}, u32[]{:S(2)}, u32[]{:S(2)}) collective-permute-start(bf16[4,256,384]{2,1,0:T(8,128)(2,1)S(1)} %get-tuple-element.104), channel_id=1, source_target_pairs={{0,24},{1,97},{2,26},{3,99},{4,28},{5,101},{6,30},{7,103},{8,0},{9... | collective-permute-start | bytes 2359304 | tf_op jit(solution)/shard_map/ppermute | solution.py:418
  69.8 12.3 %collective-permute-start.24 = (bf16[4,256,384]{2,1,0:T(8,128)(2,1)S(1)}, bf16[4,256,384]{2,1,0:T(8,128)(2,1)S(1)}, u32[]{:S(2)}, u32[]{:S(2)}) collective-permute-start(bf16[4,256,384]{2,1,0:T(8,128)(2,1)S(1)} %get-tuple-element.105), channel_id=1, source_target_pairs={{0,8},{1,33},{2,10},{3,35},{4,12},{5,37},{6,14},{7,39},{8,16},{9,4... | collective-permute-start | bytes 2359304 | tf_op jit(solution)/shard_map/ppermute | solution.py:418
  76.1 7.1 %collective-permute-start.20 = (bf16[256,384]{1,0:T(8,128)(2,1)S(1)}, bf16[256,384]{1,0:T(8,128)(2,1)S(1)}, u32[]{:S(2)}, u32[]{:S(2)}) collective-permute-start(bf16[256,384]{1,0:T(8,128)(2,1)S(1)} %get-tuple-element.100), channel_id=1, source_target_pairs={{0,96},{1,25},{2,98},{3,27},{4,100},{5,29},{6,102},{7,31},{8,104},... | collective-permute-start | bytes 589832 | tf_op jit(solution)/shard_map/ppermute | solution.py:421
  76.2 9.7 %collective-permute-start.21 = (bf16[256,384]{1,0:T(8,128)(2,1)S(1)}, bf16[256,384]{1,0:T(8,128)(2,1)S(1)}, u32[]{:S(2)}, u32[]{:S(2)}) collective-permute-start(bf16[256,384]{1,0:T(8,128)(2,1)S(1)} %get-tuple-element.101), channel_id=1, source_target_pairs={{0,32},{1,9},{2,34},{3,11},{4,36},{5,13},{6,38},{7,15},{8,40},{9,1... | collective-permute-start | bytes 589832 | tf_op jit(solution)/shard_map/ppermute | solution.py:421
  77.6 9.3 %collective-permute-start.22 = (bf16[256,384]{1,0:T(8,128)(2,1)S(1)}, bf16[256,384]{1,0:T(8,128)(2,1)S(1)}, u32[]{:S(2)}, u32[]{:S(2)}) collective-permute-start(bf16[256,384]{1,0:T(8,128)(2,1)S(1)} %get-tuple-element.102), channel_id=1, source_target_pairs={{0,64},{1,17},{2,66},{3,19},{4,68},{5,21},{6,70},{7,23},{8,72},{9,... | collective-permute-start | bytes 589832 | tf_op jit(solution)/shard_map/ppermute | solution.py:421
  88.0 19.3 %all-to-all-start = ((bf16[8,96,384]{2,1,0:T(8,128)(2,1)}), bf16[8,96,384]{2,1,0:T(8,128)(2,1)S(1)}, u32[]{:S(2)}, u32[]{:S(2)}) async-start(bf16[8,96,384]{2,1,0:T(8,128)(2,1)} %shard_map.120), calls=%async_computation | async-start | bytes 1179648 | tf_op jit(solution)/shard_map/all_to_all | solution.py:469

commit v6 on v5

--- a/solution.py
+++ b/solution.py
@@ -159,13 +159,12 @@
             delta_ref[head, 0:1, at] = dots / total
 
 
-def grads_call(curs, hists, queries, stats, tiles, sums_in=None, far=None):
+def grads_call(curs, hists, queries, stats, tiles, sums_in=None, last=False, whole=()):
     nk, nq = len(curs), len(queries)
     tokens, feat = queries[0].shape[1:]
     rows = tokens
     heads = feat // HS
     width = nq * tokens
-    last = far is not None
     held = [a for pieces in tiles.values() for pair, _ in pieces for a in pair]
 
     def kernel(*refs):
@@ -180,9 +179,7 @@
         }
         if sums_in is not None:
             old, refs = refs[0], refs[1:]
-        if last:
-            far_in, refs = refs[0], refs[1:]
-        key_out, sum_out = refs[:nk], refs[nk:-2]
+        key_out, sum_out = refs[:n_out], refs[n_out:-2]
         base, delta = refs[-2:]
         combine_stats(stat, base, delta, heads)
 
@@ -227,10 +224,11 @@
                     )
                     all_scores.append(score_grad)
                     for j in range(2):
-                        value = both[j]
-                        if last:
-                            value = value + far_in[2 * i + j, :, lanes].astype(F32)
-                        key_out[kb][2 * i + j, :, lanes] = value.astype(BF16)
+                        at = firsts[kb]
+                        if kb in whole:
+                            key_out[at][2 * i + j, :, lanes] = both[j].astype(BF16)
+                        else:
+                            key_out[at + i][j, :, lanes] = both[j].astype(BF16)
                 add = plain_dot(
                     jnp.concatenate([keys for keys, _, _ in blocks], axis=0).T,
                     jnp.concatenate(all_scores, axis=0),
@@ -246,23 +244,31 @@
 
         lax.fori_loop(0, heads, step, 0)
 
-    block = jax.ShapeDtypeStruct((4, rows, feat), BF16)
+    blocks, firsts = [], []
+    for kb in range(nk):
+        firsts.append(len(blocks))
+        if kb in whole:
+            blocks.append(jax.ShapeDtypeStruct((4, rows, feat), BF16))
+        else:
+            blocks += [jax.ShapeDtypeStruct((2, rows, feat), BF16)] * 2
+    n_out = len(blocks)
     if last:
         sums = [jax.ShapeDtypeStruct((tokens, feat), BF16)] * nq
     else:
         sums = [jax.ShapeDtypeStruct((heads, HS, width), F32)]
     args = list(curs) + list(hists) + list(queries) + list(stats) + held
-    args += [a for a in (sums_in, far) if a is not None]
+    if sums_in is not None:
+        args.append(sums_in)
     work = nk * 2 * rows * width
     outs = call(
         kernel,
-        [block] * nk + sums,
+        blocks + sums,
         args,
         flops=2 * 5 * 2 * work * feat,
         exps=work * heads,
         scratch=[pltpu.VMEM((heads, 8, width), F32)] * 2,
     )
-    return list(outs[:nk]), list(outs[nk:])
+    return list(outs[:n_out]), list(outs[n_out:])
 
 
 def pack_call(arrays, key_hist, value_hist, hist_len, sizes):
@@ -371,14 +377,17 @@
     return call(kernel, shape, list(query_parts) + list(cur_parts))
 
 
-def add_hist_call(key_parts):
-    _, rows, feat = key_parts[0].shape
+def add_hist_call(parts, whole):
+    _, rows, feat = parts[0].shape
+    n = len(parts)
 
     def kernel(*refs):
         for i, out in enumerate(refs[-2:]):
-            out[...] = sum(ref[2 + i].astype(F32) for ref in refs[:-2]).astype(BF16)
-
-    return call(kernel, [jax.ShapeDtypeStruct((rows, feat), BF16)] * 2, list(key_parts))
+            total = sum(ref[i].astype(F32) for ref in refs[:n])
+            total = total + sum(ref[2 + i].astype(F32) for ref in refs[n:-2])
+            out[...] = total.astype(BF16)
+
+    return call(kernel, [jax.ShapeDtypeStruct((rows, feat), BF16)] * 2, [*parts, *whole])
 
 
 def ring_moves(sizes):
@@ -458,17 +467,22 @@
             names = [(kind, b) for b in blocks for kind in ("cur", "hist")]
             return {i: held[name] for i, name in enumerate(names) if name in held}
 
-        far, sums = grads_call(curs[3:], hists[3:], queries, stats, tiles(3))
+        far, sums = grads_call(curs[3:], hists[3:], queries, stats, tiles(3), whole=(0,))
         far = to_key(far[0], 2)
-        near, sums = grads_call(curs[1:3], hists[1:3], queries, stats, tiles(1, 2), sums[0])
-        near = [to_key(block, offset) for block, offset in zip(near, OFFSETS[1:3])]
-        own, sums = grads_call(curs[:1], hists[:1], queries, stats, tiles(0), sums[0], far)
+        (near_m, near_cur, near_hist), sums = grads_call(
+            curs[1:3], hists[1:3], queries, stats, tiles(1, 2), sums[0], whole=(0,)
+        )
+        near_m, near_cur = to_key(near_m, OFFSETS[1]), to_key(near_cur, OFFSETS[2])
+        own, sums = grads_call(curs[:1], hists[:1], queries, stats, tiles(0), sums[0], True)
+        sums, far = lax.optimization_barrier((sums, far))
         query_parts = [sums[0]] + [to_query(sums[i], OFFSETS[i]) for i in range(1, 4)]
 
-        back = add_call(query_parts, own + near, sizes)
+        back = add_call(query_parts, [own[0], far, near_m, near_cur], sizes)
+        back, near_hist = lax.optimization_barrier((back, near_hist))
+        near_hist = to_key(near_hist, OFFSETS[2])
         back = lax.all_to_all(back, ("x", "c"), 0, 0, tiled=True)
         outs = unpack_call(back, 3)
-        grad_k, grad_v = add_hist_call(own + near)
+        grad_k, grad_v = add_hist_call([own[1], near_hist], [far, near_m])
         return outs[0], outs[1], outs[2], grad_k, grad_v
 
     return shards

time: 108 us -> 105 us (0.972)
  waiting for transfers between devices: 38.1 us -> 34.2 us
    all_to_all x1, waiting for transfers between devices: 9.38 us -> 1.19 us  [shards(): back = lax.all_to_all(back, ('x', 'c'), 0, 0, tiled=True)]
    ppermute x9 -> x10, waiting for transfers between devices: 12.1 us -> 18.1 us  [to_key(): return lax.ppermute(value, AXES, key_move(step))]
    ppermute x9, waiting for transfers between devices: 9.07 us -> 7.41 us  [to_query(): return lax.ppermute(value, AXES, query_move(step))]
    ppermute x9 -> x10, starting transfers between devices: 12.2 us -> 12.2 us  [to_key(): return lax.ppermute(value, AXES, key_move(step))]
  transfers between devices with their start and end apart: 26 -> 27, of which waited for: 16 -> 15; matrix products, arithmetic and copies ran while one was open for 0% -> 0% of each run, Pallas kernels for 17% -> 17%
where the time goes in v6:
time: 105 us
  starting transfers between devices  39.9 us (38%)
  waiting for transfers between devices  34.2 us (33%)
  Pallas kernels  28.6 us (27%)
  between operations  1.42 us (1%)
    pallas_call x12, Pallas kernels, call(): pl.pallas_call(kernel, out_shape=outs, in_specs=[VMEM] * len(args), out_s...  26.2 us
    ppermute x10, waiting for transfers between devices, to_key(): return lax.ppermute(value, AXES, key_move(step))  18.1 us
    ppermute x10, starting transfers between devices, to_key(): return lax.ppermute(value, AXES, key_move(step))  12.2 us
    all_to_all x1, starting transfers between devices, shards(): back = lax.all_to_all(back, ('x', 'c'), 0, 0, tiled=True)  10.1 us
    ppermute x9, starting transfers between devices, to_query(): return lax.ppermute(value, AXES, query_move(step))  8.91 us
    ppermute x6, waiting for transfers between devices, exchange(): lax.ppermute(p, AXES, chip_move(d))  7.55 us
    ppermute x9, waiting for transfers between devices, to_query(): return lax.ppermute(value, AXES, query_move(step))  7.41 us
    ppermute x6, starting transfers between devices, exchange(): lax.ppermute(p, AXES, chip_move(d))  7.28 us
  transfers between devices with their start and end apart: 27, of which 15 were waited for; matrix products, arithmetic and copies ran while one was open for 0% of the time, Pallas kernels for 17%

profile of v6, /device:TPU:1, one launch (start us, length us, event | category | flops | bytes accessed | tf_op | source)
XLA Modules:
  0.0 105.2 jit_solution(6271554929532116401)
XLA Ops:
  1.3 2.4 %shard_map.110 = (bf16[2,4,2,32,384]{4,3,2,1,0:T(8,128)(2,1)}, bf16[2,4,2,32,384]{4,3,2,1,0:T(8,128)(2,1)}, bf16[528,384]{1,0:T(8,128)(2,1)}) custom-call(bf16[32,3072]{1,0:T(8,128)(2,1)} %refs_0_.1, bf16[32,3072]{1,0:T(8,128)(2,1)} %refs_1_.1, bf16[32,3072]{1,0:T(8,128)(2,1)} %refs_2_.1, bf16[32,3072]{1,0:T(8,128)(2,1)} %refs_3_.1, ...), custom_call_target="tpu_custom_call" | custom-call | tf_op jit(solution)/shard_map/pallas_call | solution.py:302
  3.7 1.5 %collective-permute-start = (bf16[2,4,2,32,384]{4,3,2,1,0:T(8,128)(2,1)}, bf16[2,4,2,32,384]{4,3,2,1,0:T(8,128)(2,1)S(1)}, u32[]{:S(2)}, u32[]{:S(2)}) collective-permute-start(bf16[2,4,2,32,384]{4,3,2,1,0:T(8,128)(2,1)} %get-tuple-element.68), channel_id=1, source_target_pairs={{0,1},{1,0},{2,3},{3,2},{4,5},{5,4},{6,7},{7,6},{8,9},{9,8},{10,11... | collective-permute-start | bytes 1179656 | tf_op jit(solution)/shard_map/ppermute | solution.py:436
  5.2 3.8 %collective-permute-start.2 = (bf16[528,384]{1,0:T(8,128)(2,1)}, bf16[528,384]{1,0:T(8,128)(2,1)S(1)}, u32[]{:S(2)}, u32[]{:S(2)}) collective-permute-start(bf16[528,384]{1,0:T(8,128)(2,1)} %get-tuple-element.73.refs_1_), channel_id=1, source_target_pairs={{0,24},{1,97},{2,26},{3,99},{4,28},{5,101},{6,30},{7,103},{8,0},{9... | collective-permute-start | bytes 1216520 | tf_op jit(solution)/shard_map/ppermute | solution.py:427
  10.1 1.3 %collective-permute-start.6 = (bf16[2,64,384]{2,1,0:T(8,128)(2,1)S(1)}, bf16[2,64,384]{2,1,0:T(8,128)(2,1)S(1)}, u32[]{:S(2)}, u32[]{:S(2)}) collective-permute-start(bf16[2,64,384]{2,1,0:T(8,128)(2,1)S(1)} %get-tuple-element.79), channel_id=1, source_target_pairs={{0,2},{1,3},{2,4},{3,5},{4,6},{5,7},{6,0},{7,1},{8,10},{9,11},{10,... | collective-permute-start | bytes 294920 | tf_op jit(solution)/shard_map/ppermute | solution.py:443
  11.4 1.5 %collective-permute-start.7 = (bf16[2,64,384]{2,1,0:T(8,128)(2,1)S(1)}, bf16[2,64,384]{2,1,0:T(8,128)(2,1)S(1)}, u32[]{:S(2)}, u32[]{:S(2)}) collective-permute-start(bf16[2,64,384]{2,1,0:T(8,128)(2,1)S(1)} %get-tuple-element.80), channel_id=1, source_target_pairs={{0,6},{1,7},{2,0},{3,1},{4,2},{5,3},{6,4},{7,5},{8,14},{9,15},{10,... | collective-permute-start | bytes 294920 | tf_op jit(solution)/shard_map/ppermute | solution.py:443
  12.9 1.5 %collective-permute-start.8 = (bf16[2,64,384]{2,1,0:T(8,128)(2,1)S(1)}, bf16[2,64,384]{2,1,0:T(8,128)(2,1)S(1)}, u32[]{:S(2)}, u32[]{:S(2)}) collective-permute-start(bf16[2,64,384]{2,1,0:T(8,128)(2,1)S(1)} %get-tuple-element.81), channel_id=1, source_target_pairs={{0,4},{1,5},{2,6},{3,7},{4,0},{5,1},{6,2},{7,3},{8,12},{9,13},{10,... | collective-permute-start | bytes 294920 | tf_op jit(solution)/shard_map/ppermute | solution.py:443
  14.4 1.6 %collective-permute-done.6.refs_1_ = bf16[2,64,384]{2,1,0:T(8,128)(2,1)S(1)} collective-permute-done((bf16[2,64,384]{2,1,0:T(8,128)(2,1)S(1)}, bf16[2,64,384]{2,1,0:T(8,128)(2,1)S(1)}, u32[]{:S(2)}, u32[]{:S(2)}) %collective-permute-start.6) | collective-permute-done | bytes 98336 | tf_op jit(solution)/shard_map/ppermute | solution.py:443
  16.3 2.7 %collective-permute-done.8.refs_3_ = bf16[2,64,384]{2,1,0:T(8,128)(2,1)S(1)} collective-permute-done((bf16[2,64,384]{2,1,0:T(8,128)(2,1)S(1)}, bf16[2,64,384]{2,1,0:T(8,128)(2,1)S(1)}, u32[]{:S(2)}, u32[]{:S(2)}) %collective-permute-start.8) | collective-permute-done | bytes 98336 | tf_op jit(solution)/shard_map/ppermute | solution.py:443
  19.0 2.3 %collective-permute-start.11 = (bf16[2,256,384]{2,1,0:T(8,128)(2,1)S(1)}, bf16[2,256,384]{2,1,0:T(8,128)(2,1)S(1)}, u32[]{:S(2)}, u32[]{:S(2)}) collective-permute-start(bf16[2,256,384]{2,1,0:T(8,128)(2,1)S(1)} %shard_map.113.refs_5_.refs_3_.refs_2_.refs_4_), channel_id=1, source_target_pairs={{0,64},{1,17},{2,66},{3,19},{4,68},{5,21},{6,70},{7,23},{8,72},{9,... | collective-permute-start | bytes 1179656 | tf_op jit(solution)/shard_map/ppermute | solution.py:430
  22.3 1.7 %collective-permute-start.4 = (bf16[2,64,384]{2,1,0:T(8,128)(2,1)S(1)}, bf16[2,64,384]{2,1,0:T(8,128)(2,1)S(1)}, u32[]{:S(2)}, u32[]{:S(2)}) collective-permute-start(bf16[2,64,384]{2,1,0:T(8,128)(2,1)S(1)} %get-tuple-element.76), channel_id=1, source_target_pairs={{0,6},{1,7},{2,0},{3,1},{4,2},{5,3},{6,4},{7,5},{8,14},{9,15},{10,... | collective-permute-start | bytes 294920 | tf_op jit(solution)/shard_map/ppermute | solution.py:443
  24.3 2.0 %collective-permute-done.3.refs_1_ = bf16[2,64,384]{2,1,0:T(8,128)(2,1)S(1)} collective-permute-done((bf16[2,64,384]{2,1,0:T(8,128)(2,1)S(1)}, bf16[2,64,384]{2,1,0:T(8,128)(2,1)S(1)}, u32[]{:S(2)}, u32[]{:S(2)}) %collective-permute-start.3) | collective-permute-done | bytes 98336 | tf_op jit(solution)/shard_map/ppermute | solution.py:443
  27.8 1.3 %collective-permute-done.5.refs_3_ = bf16[2,64,384]{2,1,0:T(8,128)(2,1)S(1)} collective-permute-done((bf16[2,64,384]{2,1,0:T(8,128)(2,1)S(1)}, bf16[2,64,384]{2,1,0:T(8,128)(2,1)S(1)}, u32[]{:S(2)}, u32[]{:S(2)}) %collective-permute-start.5) | collective-permute-done | bytes 98336 | tf_op jit(solution)/shard_map/ppermute | solution.py:443
  29.1 1.4 %collective-permute-start.14 = (bf16[2,256,384]{2,1,0:T(8,128)(2,1)S(1)}, bf16[2,256,384]{2,1,0:T(8,128)(2,1)S(1)}, u32[]{:S(2)}, u32[]{:S(2)}) collective-permute-start(bf16[2,256,384]{2,1,0:T(8,128)(2,1)S(1)} %shard_map.112.refs_0_), channel_id=1, source_target_pairs={{0,16},{1,65},{2,18},{3,67},{4,20},{5,69},{6,22},{7,71},{8,24},{9,... | collective-permute-start | bytes 1179656 | tf_op jit(solution)/shard_map/ppermute | solution.py:427
  30.5 3.0 %collective-permute-start.13 = (bf16[2,256,384]{2,1,0:T(8,128)(2,1)S(1)}, bf16[2,256,384]{2,1,0:T(8,128)(2,1)S(1)}, u32[]{:S(2)}, u32[]{:S(2)}) collective-permute-start(bf16[2,256,384]{2,1,0:T(8,128)(2,1)S(1)} %shard_map.112.refs_0_), channel_id=1, source_target_pairs={{0,24},{1,97},{2,26},{3,99},{4,28},{5,101},{6,30},{7,103},{8,0},{9... | collective-permute-start | bytes 1179656 | tf_op jit(solution)/shard_map/ppermute | solution.py:427
  34.1 3.4 %shard_map.114 = (f32[3,16,256]{2,1,0:T(8,128)S(1)}, f32[3,256,512]{2,1,0:T(8,128)S(1)}, f32[3,256,512]{2,1,0:T(8,128)S(1)}, f32[3,256,512]{2,1,0:T(8,128)S(1)},...) custom-call(bf16[2,256,384]{2,1,0:T(8,128)(2,1)S(1)} %shard_map.112.refs_0_, ...), custom_call_target="tpu_custom_call" | custom-call | flops 31457280 | bytes 43776 | tf_op jit(solution)/shard_map/pallas_call | solution.py:36
  37.5 3.4 %shard_map.115 = (f32[3,16,256]{2,1,0:T(8,128)S(1)}, f32[3,256,512]{2,1,0:T(8,128)S(1)}, f32[3,256,512]{2,1,0:T(8,128)S(1)}, f32[3,256,512]{2,1,0:T(8,128)S(1)},...) custom-call(bf16[2,256,384]{2,1,0:T(8,128)(2,1)S(1)} %shard_map.112.refs_0_, ...), custom_call_target="tpu_custom_call" | custom-call | flops 31457280 | bytes 44544 | tf_op jit(solution)/shard_map/pallas_call | solution.py:36
  41.0 4.7 %collective-permute-done.13.refs_1_ = bf16[2,256,384]{2,1,0:T(8,128)(2,1)S(1)} collective-permute-done((bf16[2,256,384]{2,1,0:T(8,128)(2,1)S(1)}, bf16[2,256,384]{2,1,0:T(8,128)(2,1)S(1)}, u32[]{:S(2)}, u32[]{:S(2)}) %collective-permute-start.13) | collective-permute-done | bytes 393248 | tf_op jit(solution)/shard_map/ppermute | solution.py:427
  45.8 3.3 %shard_map.116 = (f32[3,16,256]{2,1,0:T(8,128)S(1)}, f32[3,256,1024]{2,1,0:T(8,128)S(1)}, f32[3,256,1024]{2,1,0:T(8,128)S(1)}, f32[3,256,1024]{2,1,0:T(8,128)S(1...) custom-call(bf16[2,256,384]{2,1,0:T(8,128)(2,1)S(1)} %collective-permute-done.12.refs_0_, ...), custom_call_target="tpu_custom_call" | custom-call | flops 37748736 | bytes 43776 | tf_op jit(solution)/shard_map/pallas_call | solution.py:36
  49.1 1.9 %collective-permute-start.18 = (f32[3,16,256]{2,1,0:T(8,128)S(1)}, f32[3,16,256]{2,1,0:T(8,128)S(1)}, u32[]{:S(2)}, u32[]{:S(2)}) collective-permute-start(f32[3,16,256]{2,1,0:T(8,128)S(1)} %get-tuple-element.86.refs_6_.refs_8_), channel_id=1, source_target_pairs={{0,64},{1,17},{2,66},{3,19},{4,68},{5,21},{6,70},{7,23},{8,72},{9,... | collective-permute-start | bytes 147464 | tf_op jit(solution)/shard_map/ppermute | solution.py:430
  51.0 1.7 %collective-permute-start.17 = (f32[3,16,256]{2,1,0:T(8,128)S(1)}, f32[3,16,256]{2,1,0:T(8,128)S(1)}, u32[]{:S(2)}, u32[]{:S(2)}) collective-permute-start(f32[3,16,256]{2,1,0:T(8,128)S(1)} %get-tuple-element.86.refs_6_.refs_8_), channel_id=1, source_target_pairs={{0,96},{1,25},{2,98},{3,27},{4,100},{5,29},{6,102},{7,31},{8,104},... | collective-permute-start | bytes 147464 | tf_op jit(solution)/shard_map/ppermute | solution.py:430
  53.9 3.0 %collective-permute-done.16.refs_7_.refs_9_ = f32[3,16,256]{2,1,0:T(8,128)S(1)} collective-permute-done((f32[3,16,256]{2,1,0:T(8,128)S(1)}, f32[3,16,256]{2,1,0:T(8,128)S(1)}, u32[]{:S(2)}, u32[]{:S(2)}) %collective-permute-start.16) | collective-permute-done | bytes 49184 | tf_op jit(solution)/shard_map/ppermute | solution.py:430
  56.9 2.9 %shard_map.117 = (bf16[4,256,384]{2,1,0:T(8,128)(2,1)S(1)}, f32[3,128,1024]{2,1,0:T(8,128)S(1)}) custom-call(bf16[2,256,384]{2,1,0:T(8,128)(2,1)S(1)} %collective-permute-done.14.refs_2_.refs_0_, bf16[528,384]{1,0:T(8,128)(2,1)S(1)} %collective-permute-done.15.refs_4_.refs_1_, bf16[2,256,384]{2,1,0:T(8,128)(2,1)S(1)} %shard_map.113.refs_5_.refs_3_.refs_2_.refs_4_, ...), custom_call_target="tpu_custom_call" | custom-call | flops 62914560 | bytes 236736 | tf_op jit(solution)/shard_map/pallas_call | solution.py:36
  59.9 1.6 %collective-permute-start.19 = (bf16[4,256,384]{2,1,0:T(8,128)(2,1)S(1)}, bf16[4,256,384]{2,1,0:T(8,128)(2,1)S(1)}, u32[]{:S(2)}, u32[]{:S(2)}) collective-permute-start(bf16[4,256,384]{2,1,0:T(8,128)(2,1)S(1)} %get-tuple-element.111), channel_id=1, source_target_pairs={{0,16},{1,65},{2,18},{3,67},{4,20},{5,69},{6,22},{7,71},{8,24},{9,... | collective-permute-start | bytes 2359304 | tf_op jit(solution)/shard_map/ppermute | solution.py:427
  61.5 7.1 %shard_map.118 = (bf16[4,256,384]{2,1,0:T(8,128)(2,1)S(1)}, bf16[2,256,384]{2,1,0:T(8,128)(2,1)S(1)}, bf16[2,256,384]{2,1,0:T(8,128)(2,1)S(1)}, f32[3,128,1024]{2,1,0:T(8,128)S(1)}) custom-call(bf16[2,256,384]{2,1,0:T(8,128)(2,1)S(1)} %collective-permute-done.12.refs_0_, bf16[2,256,384]{2,1,0:T(8,128)(2,1)S(1)} %collective-permute-done.13.refs_1_, ...), custom_call_target="tpu_custom_call" | custom-call | flops 125829120 | bytes 273792 | tf_op jit(solution)/shard_map/pallas_call | solution.py:36
  68.5 1.3 %collective-permute-start.23 = (bf16[4,256,384]{2,1,0:T(8,128)(2,1)S(1)}, bf16[4,256,384]{2,1,0:T(8,128)(2,1)S(1)}, u32[]{:S(2)}, u32[]{:S(2)}) collective-permute-start(bf16[4,256,384]{2,1,0:T(8,128)(2,1)S(1)} %get-tuple-element.118), channel_id=1, source_target_pairs={{0,24},{1,97},{2,26},{3,99},{4,28},{5,101},{6,30},{7,103},{8,0},{9... | collective-permute-start | bytes 2359304 | tf_op jit(solution)/shard_map/ppermute | solution.py:427
  70.1 3.0 %shard_map.119 = (bf16[2,256,384]{2,1,0:T(8,128)(2,1)S(1)}, bf16[2,256,384]{2,1,0:T(8,128)(2,1)S(1)}, bf16[256,384]{1,0:T(8,128)(2,1)S(1)}, bf16[256,384]{1,0:T(...) custom-call(bf16[2,256,384]{2,1,0:T(8,128)(2,1)S(1)} %shard_map.112.refs_0_, ...), custom_call_target="tpu_custom_call" | custom-call | flops 62914560 | bytes 261312 | tf_op jit(solution)/shard_map/pallas_call | solution.py:36
  73.2 1.5 %collective-permute-start.21 = (bf16[256,384]{1,0:T(8,128)(2,1)S(1)}, bf16[256,384]{1,0:T(8,128)(2,1)S(1)}, u32[]{:S(2)}, u32[]{:S(2)}) collective-permute-start(bf16[256,384]{1,0:T(8,128)(2,1)S(1)} %get-tuple-element.114), channel_id=1, source_target_pairs={{0,32},{1,9},{2,34},{3,11},{4,36},{5,13},{6,38},{7,15},{8,40},{9,1... | collective-permute-start | bytes 589832 | tf_op jit(solution)/shard_map/ppermute | solution.py:430
  74.7 3.0 %collective-permute-done.24.refs_7_ = bf16[2,256,384]{2,1,0:T(8,128)(2,1)S(1)} collective-permute-done((bf16[2,256,384]{2,1,0:T(8,128)(2,1)S(1)}, bf16[2,256,384]{2,1,0:T(8,128)(2,1)S(1)}, u32[]{:S(2)}, u32[]{:S(2)}) %collective-permute-start.24) | collective-permute-done | bytes 393248 | tf_op jit(solution)/shard_map/ppermute | solution.py:427
  77.7 2.1 %collective-permute-done.23.refs_6_.refs_3_ = bf16[4,256,384]{2,1,0:T(8,128)(2,1)S(1)} collective-permute-done((bf16[4,256,384]{2,1,0:T(8,128)(2,1)S(1)}, bf16[4,256,384]{2,1,0:T(8,128)(2,1)S(1)}, u32[]{:S(2)}, u32[]{:S(2)}) %collective-permute-start.23) | collective-permute-done | bytes 786464 | tf_op jit(solution)/shard_map/ppermute | solution.py:427
  80.2 2.7 %collective-permute-done.22.refs_3_ = bf16[256,384]{1,0:T(8,128)(2,1)S(1)} collective-permute-done((bf16[256,384]{1,0:T(8,128)(2,1)S(1)}, bf16[256,384]{1,0:T(8,128)(2,1)S(1)}, u32[]{:S(2)}, u32[]{:S(2)}) %collective-permute-start.22) | collective-permute-done | bytes 196640 | tf_op jit(solution)/shard_map/ppermute | solution.py:430
  84.1 10.1 %all-to-all-start = ((bf16[8,96,384]{2,1,0:T(8,128)(2,1)}), bf16[8,96,384]{2,1,0:T(8,128)(2,1)S(1)}, u32[]{:S(2)}, u32[]{:S(2)}) async-start(bf16[8,96,384]{2,1,0:T(8,128)(2,1)} %shard_map.120), calls=%async_computation | async-start | bytes 1179648 | tf_op jit(solution)/shard_map/all_to_all | solution.py:483
  94.1 8.1 %collective-permute-done.25.refs_1_ = bf16[2,256,384]{2,1,0:T(8,128)(2,1)S(1)} collective-permute-done((bf16[2,256,384]{2,1,0:T(8,128)(2,1)S(1)}, bf16[2,256,384]{2,1,0:T(8,128)(2,1)S(1)}, u32[]{:S(2)}, u32[]{:S(2)}) %collective-permute-start.25) | collective-permute-done | bytes 393248 | tf_op jit(solution)/shard_map/ppermute | solution.py:427
  (39 shorter events, 11.0 us)
Async XLA Ops:
  3.7 30.4 %copy-start = (bf16[528,384]{1,0:T(8,128)(2,1)S(1)}, bf16[528,384]{1,0:T(8,128)(2,1)}, u32[]{:S(2)}) copy-start(bf16[528,384]{1,0:T(8,128)(2,1)} %get-tuple-element.73.refs_1_) | copy-start | bytes 1216516
  3.7 5.3 %collective-permute-start = (bf16[2,4,2,32,384]{4,3,2,1,0:T(8,128)(2,1)}, bf16[2,4,2,32,384]{4,3,2,1,0:T(8,128)(2,1)S(1)}, u32[]{:S(2)}, u32[]{:S(2)}) collective-permute-start(bf16[2,4,2,32,384]{4,3,2,1,0:T(8,128)(2,1)} %get-tuple-element.68), channel_id=1, source_target_pairs={{0,1},{1,0},{2,3},{3,2},{4,5},{5,4},{6,7},{7,6},{8,9},{9,8},{10,11... | collective-permute-start | bytes 1179656 | tf_op jit(solution)/shard_map/ppermute | solution.py:436
  5.2 16.1 %collective-permute-start.2 = (bf16[528,384]{1,0:T(8,128)(2,1)}, bf16[528,384]{1,0:T(8,128)(2,1)S(1)}, u32[]{:S(2)}, u32[]{:S(2)}) collective-permute-start(bf16[528,384]{1,0:T(8,128)(2,1)} %get-tuple-element.73.refs_1_), channel_id=1, source_target_pairs={{0,24},{1,97},{2,26},{3,99},{4,28},{5,101},{6,30},{7,103},{8,0},{9... | collective-permute-start | bytes 1216520 | tf_op jit(solution)/shard_map/ppermute | solution.py:427
  9.1 12.3 %collective-permute-start.1 = (bf16[528,384]{1,0:T(8,128)(2,1)}, bf16[528,384]{1,0:T(8,128)(2,1)S(1)}, u32[]{:S(2)}, u32[]{:S(2)}) collective-permute-start(bf16[528,384]{1,0:T(8,128)(2,1)} %get-tuple-element.73.refs_1_), channel_id=1, source_target_pairs={{0,8},{1,33},{2,10},{3,35},{4,12},{5,37},{6,14},{7,39},{8,16},{9,4... | collective-permute-start | bytes 1216520 | tf_op jit(solution)/shard_map/ppermute | solution.py:427
  9.1 1.0 copy-start.1
  10.1 5.9 %collective-permute-start.6 = (bf16[2,64,384]{2,1,0:T(8,128)(2,1)S(1)}, bf16[2,64,384]{2,1,0:T(8,128)(2,1)S(1)}, u32[]{:S(2)}, u32[]{:S(2)}) collective-permute-start(bf16[2,64,384]{2,1,0:T(8,128)(2,1)S(1)} %get-tuple-element.79), channel_id=1, source_target_pairs={{0,2},{1,3},{2,4},{3,5},{4,6},{5,7},{6,0},{7,1},{8,10},{9,11},{10,... | collective-permute-start | bytes 294920 | tf_op jit(solution)/shard_map/ppermute | solution.py:443
  11.4 4.9 %collective-permute-start.7 = (bf16[2,64,384]{2,1,0:T(8,128)(2,1)S(1)}, bf16[2,64,384]{2,1,0:T(8,128)(2,1)S(1)}, u32[]{:S(2)}, u32[]{:S(2)}) collective-permute-start(bf16[2,64,384]{2,1,0:T(8,128)(2,1)S(1)} %get-tuple-element.80), channel_id=1, source_target_pairs={{0,6},{1,7},{2,0},{3,1},{4,2},{5,3},{6,4},{7,5},{8,14},{9,15},{10,... | collective-permute-start | bytes 294920 | tf_op jit(solution)/shard_map/ppermute | solution.py:443
  12.9 6.1 %collective-permute-start.8 = (bf16[2,64,384]{2,1,0:T(8,128)(2,1)S(1)}, bf16[2,64,384]{2,1,0:T(8,128)(2,1)S(1)}, u32[]{:S(2)}, u32[]{:S(2)}) collective-permute-start(bf16[2,64,384]{2,1,0:T(8,128)(2,1)S(1)} %get-tuple-element.81), channel_id=1, source_target_pairs={{0,4},{1,5},{2,6},{3,7},{4,0},{5,1},{6,2},{7,3},{8,12},{9,13},{10,... | collective-permute-start | bytes 294920 | tf_op jit(solution)/shard_map/ppermute | solution.py:443
  16.0 14.4 %collective-permute-start.15 = (bf16[528,384]{1,0:T(8,128)(2,1)}, bf16[528,384]{1,0:T(8,128)(2,1)S(1)}, u32[]{:S(2)}, u32[]{:S(2)}) collective-permute-start(bf16[528,384]{1,0:T(8,128)(2,1)} %get-tuple-element.73.refs_1_), channel_id=1, source_target_pairs={{0,16},{1,65},{2,18},{3,67},{4,20},{5,69},{6,22},{7,71},{8,24},{9,... | collective-permute-start | bytes 1216520 | tf_op jit(solution)/shard_map/ppermute | solution.py:427
  19.0 14.5 %collective-permute-start.11 = (bf16[2,256,384]{2,1,0:T(8,128)(2,1)S(1)}, bf16[2,256,384]{2,1,0:T(8,128)(2,1)S(1)}, u32[]{:S(2)}, u32[]{:S(2)}) collective-permute-start(bf16[2,256,384]{2,1,0:T(8,128)(2,1)S(1)} %shard_map.113.refs_5_.refs_3_.refs_2_.refs_4_), channel_id=1, source_target_pairs={{0,64},{1,17},{2,66},{3,19},{4,68},{5,21},{6,70},{7,23},{8,72},{9,... | collective-permute-start | bytes 1179656 | tf_op jit(solution)/shard_map/ppermute | solution.py:430
  21.3 5.0 %collective-permute-start.3 = (bf16[2,64,384]{2,1,0:T(8,128)(2,1)S(1)}, bf16[2,64,384]{2,1,0:T(8,128)(2,1)S(1)}, u32[]{:S(2)}, u32[]{:S(2)}) collective-permute-start(bf16[2,64,384]{2,1,0:T(8,128)(2,1)S(1)} %get-tuple-element.75), channel_id=1, source_target_pairs={{0,2},{1,3},{2,4},{3,5},{4,6},{5,7},{6,0},{7,1},{8,10},{9,11},{10,... | collective-permute-start | bytes 294920 | tf_op jit(solution)/shard_map/ppermute | solution.py:443
  22.3 4.8 %collective-permute-start.4 = (bf16[2,64,384]{2,1,0:T(8,128)(2,1)S(1)}, bf16[2,64,384]{2,1,0:T(8,128)(2,1)S(1)}, u32[]{:S(2)}, u32[]{:S(2)}) collective-permute-start(bf16[2,64,384]{2,1,0:T(8,128)(2,1)S(1)} %get-tuple-element.76), channel_id=1, source_target_pairs={{0,6},{1,7},{2,0},{3,1},{4,2},{5,3},{6,4},{7,5},{8,14},{9,15},{10,... | collective-permute-start | bytes 294920 | tf_op jit(solution)/shard_map/ppermute | solution.py:443
  24.0 5.1 %collective-permute-start.5 = (bf16[2,64,384]{2,1,0:T(8,128)(2,1)S(1)}, bf16[2,64,384]{2,1,0:T(8,128)(2,1)S(1)}, u32[]{:S(2)}, u32[]{:S(2)}) collective-permute-start(bf16[2,64,384]{2,1,0:T(8,128)(2,1)S(1)} %get-tuple-element.77), channel_id=1, source_target_pairs={{0,4},{1,5},{2,6},{3,7},{4,0},{5,1},{6,2},{7,3},{8,12},{9,13},{10,... | collective-permute-start | bytes 294920 | tf_op jit(solution)/shard_map/ppermute | solution.py:443
  26.3 11.2 %collective-permute-start.10 = (bf16[2,256,384]{2,1,0:T(8,128)(2,1)S(1)}, bf16[2,256,384]{2,1,0:T(8,128)(2,1)S(1)}, u32[]{:S(2)}, u32[]{:S(2)}) collective-permute-start(bf16[2,256,384]{2,1,0:T(8,128)(2,1)S(1)} %shard_map.113.refs_5_.refs_3_.refs_2_.refs_4_), channel_id=1, source_target_pairs={{0,96},{1,25},{2,98},{3,27},{4,100},{5,29},{6,102},{7,31},{8,104},... | collective-permute-start | bytes 1179656 | tf_op jit(solution)/shard_map/ppermute | solution.py:430
  27.1 10.4 %collective-permute-start.9 = (bf16[2,256,384]{2,1,0:T(8,128)(2,1)S(1)}, bf16[2,256,384]{2,1,0:T(8,128)(2,1)S(1)}, u32[]{:S(2)}, u32[]{:S(2)}) collective-permute-start(bf16[2,256,384]{2,1,0:T(8,128)(2,1)S(1)} %shard_map.113.refs_5_.refs_3_.refs_2_.refs_4_), channel_id=1, source_target_pairs={{0,32},{1,9},{2,34},{3,11},{4,36},{5,13},{6,38},{7,15},{8,40},{9,1... | collective-permute-start | bytes 1179656 | tf_op jit(solution)/shard_map/ppermute | solution.py:430
  29.1 11.9 %collective-permute-start.14 = (bf16[2,256,384]{2,1,0:T(8,128)(2,1)S(1)}, bf16[2,256,384]{2,1,0:T(8,128)(2,1)S(1)}, u32[]{:S(2)}, u32[]{:S(2)}) collective-permute-start(bf16[2,256,384]{2,1,0:T(8,128)(2,1)S(1)} %shard_map.112.refs_0_), channel_id=1, source_target_pairs={{0,16},{1,65},{2,18},{3,67},{4,20},{5,69},{6,22},{7,71},{8,24},{9,... | collective-permute-start | bytes 1179656 | tf_op jit(solution)/shard_map/ppermute | solution.py:427
  30.5 15.2 %collective-permute-start.13 = (bf16[2,256,384]{2,1,0:T(8,128)(2,1)S(1)}, bf16[2,256,384]{2,1,0:T(8,128)(2,1)S(1)}, u32[]{:S(2)}, u32[]{:S(2)}) collective-permute-start(bf16[2,256,384]{2,1,0:T(8,128)(2,1)S(1)} %shard_map.112.refs_0_), channel_id=1, source_target_pairs={{0,24},{1,97},{2,26},{3,99},{4,28},{5,101},{6,30},{7,103},{8,0},{9... | collective-permute-start | bytes 1179656 | tf_op jit(solution)/shard_map/ppermute | solution.py:427
  33.5 12.3 %collective-permute-start.12 = (bf16[2,256,384]{2,1,0:T(8,128)(2,1)S(1)}, bf16[2,256,384]{2,1,0:T(8,128)(2,1)S(1)}, u32[]{:S(2)}, u32[]{:S(2)}) collective-permute-start(bf16[2,256,384]{2,1,0:T(8,128)(2,1)S(1)} %shard_map.112.refs_0_), channel_id=1, source_target_pairs={{0,8},{1,33},{2,10},{3,35},{4,12},{5,37},{6,14},{7,39},{8,16},{9,4... | collective-permute-start | bytes 1179656 | tf_op jit(solution)/shard_map/ppermute | solution.py:427
  49.1 4.5 %collective-permute-start.18 = (f32[3,16,256]{2,1,0:T(8,128)S(1)}, f32[3,16,256]{2,1,0:T(8,128)S(1)}, u32[]{:S(2)}, u32[]{:S(2)}) collective-permute-start(f32[3,16,256]{2,1,0:T(8,128)S(1)} %get-tuple-element.86.refs_6_.refs_8_), channel_id=1, source_target_pairs={{0,64},{1,17},{2,66},{3,19},{4,68},{5,21},{6,70},{7,23},{8,72},{9,... | collective-permute-start | bytes 147464 | tf_op jit(solution)/shard_map/ppermute | solution.py:430
  51.0 2.9 %collective-permute-start.17 = (f32[3,16,256]{2,1,0:T(8,128)S(1)}, f32[3,16,256]{2,1,0:T(8,128)S(1)}, u32[]{:S(2)}, u32[]{:S(2)}) collective-permute-start(f32[3,16,256]{2,1,0:T(8,128)S(1)} %get-tuple-element.86.refs_6_.refs_8_), channel_id=1, source_target_pairs={{0,96},{1,25},{2,98},{3,27},{4,100},{5,29},{6,102},{7,31},{8,104},... | collective-permute-start | bytes 147464 | tf_op jit(solution)/shard_map/ppermute | solution.py:430
  52.7 4.2 %collective-permute-start.16 = (f32[3,16,256]{2,1,0:T(8,128)S(1)}, f32[3,16,256]{2,1,0:T(8,128)S(1)}, u32[]{:S(2)}, u32[]{:S(2)}) collective-permute-start(f32[3,16,256]{2,1,0:T(8,128)S(1)} %get-tuple-element.86.refs_6_.refs_8_), channel_id=1, source_target_pairs={{0,32},{1,9},{2,34},{3,11},{4,36},{5,13},{6,38},{7,15},{8,40},{9,1... | collective-permute-start | bytes 147464 | tf_op jit(solution)/shard_map/ppermute | solution.py:430
  59.9 13.2 %collective-permute-start.19 = (bf16[4,256,384]{2,1,0:T(8,128)(2,1)S(1)}, bf16[4,256,384]{2,1,0:T(8,128)(2,1)S(1)}, u32[]{:S(2)}, u32[]{:S(2)}) collective-permute-start(bf16[4,256,384]{2,1,0:T(8,128)(2,1)S(1)} %get-tuple-element.111), channel_id=1, source_target_pairs={{0,16},{1,65},{2,18},{3,67},{4,20},{5,69},{6,22},{7,71},{8,24},{9,... | collective-permute-start | bytes 2359304 | tf_op jit(solution)/shard_map/ppermute | solution.py:427
  68.5 11.2 %collective-permute-start.23 = (bf16[4,256,384]{2,1,0:T(8,128)(2,1)S(1)}, bf16[4,256,384]{2,1,0:T(8,128)(2,1)S(1)}, u32[]{:S(2)}, u32[]{:S(2)}) collective-permute-start(bf16[4,256,384]{2,1,0:T(8,128)(2,1)S(1)} %get-tuple-element.118), channel_id=1, source_target_pairs={{0,24},{1,97},{2,26},{3,99},{4,28},{5,101},{6,30},{7,103},{8,0},{9... | collective-permute-start | bytes 2359304 | tf_op jit(solution)/shard_map/ppermute | solution.py:427
  69.8 7.8 %collective-permute-start.24 = (bf16[2,256,384]{2,1,0:T(8,128)(2,1)S(1)}, bf16[2,256,384]{2,1,0:T(8,128)(2,1)S(1)}, u32[]{:S(2)}, u32[]{:S(2)}) collective-permute-start(bf16[2,256,384]{2,1,0:T(8,128)(2,1)S(1)} %get-tuple-element.119), channel_id=1, source_target_pairs={{0,8},{1,33},{2,10},{3,35},{4,12},{5,37},{6,14},{7,39},{8,16},{9,4... | collective-permute-start | bytes 1179656 | tf_op jit(solution)/shard_map/ppermute | solution.py:427
  73.1 7.1 %collective-permute-start.20 = (bf16[256,384]{1,0:T(8,128)(2,1)S(1)}, bf16[256,384]{1,0:T(8,128)(2,1)S(1)}, u32[]{:S(2)}, u32[]{:S(2)}) collective-permute-start(bf16[256,384]{1,0:T(8,128)(2,1)S(1)} %get-tuple-element.113), channel_id=1, source_target_pairs={{0,96},{1,25},{2,98},{3,27},{4,100},{5,29},{6,102},{7,31},{8,104},... | collective-permute-start | bytes 589832 | tf_op jit(solution)/shard_map/ppermute | solution.py:430
  73.2 7.0 %collective-permute-start.21 = (bf16[256,384]{1,0:T(8,128)(2,1)S(1)}, bf16[256,384]{1,0:T(8,128)(2,1)S(1)}, u32[]{:S(2)}, u32[]{:S(2)}) collective-permute-start(bf16[256,384]{1,0:T(8,128)(2,1)S(1)} %get-tuple-element.114), channel_id=1, source_target_pairs={{0,32},{1,9},{2,34},{3,11},{4,36},{5,13},{6,38},{7,15},{8,40},{9,1... | collective-permute-start | bytes 589832 | tf_op jit(solution)/shard_map/ppermute | solution.py:430
  74.7 8.2 %collective-permute-start.22 = (bf16[256,384]{1,0:T(8,128)(2,1)S(1)}, bf16[256,384]{1,0:T(8,128)(2,1)S(1)}, u32[]{:S(2)}, u32[]{:S(2)}) collective-permute-start(bf16[256,384]{1,0:T(8,128)(2,1)S(1)} %get-tuple-element.115), channel_id=1, source_target_pairs={{0,64},{1,17},{2,66},{3,19},{4,68},{5,21},{6,70},{7,23},{8,72},{9,... | collective-permute-start | bytes 589832 | tf_op jit(solution)/shard_map/ppermute | solution.py:430
  84.1 20.3 %all-to-all-start = ((bf16[8,96,384]{2,1,0:T(8,128)(2,1)}), bf16[8,96,384]{2,1,0:T(8,128)(2,1)S(1)}, u32[]{:S(2)}, u32[]{:S(2)}) async-start(bf16[8,96,384]{2,1,0:T(8,128)(2,1)} %shard_map.120), calls=%async_computation | async-start | bytes 1179648 | tf_op jit(solution)/shard_map/all_to_all | solution.py:483
  94.1 8.1 %collective-permute-start.25 = (bf16[2,256,384]{2,1,0:T(8,128)(2,1)S(1)}, bf16[2,256,384]{2,1,0:T(8,128)(2,1)S(1)}, u32[]{:S(2)}, u32[]{:S(2)}) collective-permute-start(bf16[2,256,384]{2,1,0:T(8,128)(2,1)S(1)} %get-tuple-element.126), channel_id=1, source_target_pairs={{0,8},{1,33},{2,10},{3,35},{4,12},{5,37},{6,14},{7,39},{8,16},{9,4... | collective-permute-start | bytes 1179656 | tf_op jit(solution)/shard_map/ppermute | solution.py:427

commit v7 on v6

--- a/solution.py
+++ b/solution.py
@@ -338,56 +338,63 @@
     return call(kernel, shape, blocks)
 
 
-def unpack_call(array, count):
-    parts, rows, feat = array.shape
-    rows //= count
-
-    def kernel(ref, *outs):
-        for i, out in enumerate(outs):
-            for p in range(parts):
-                out[:, p * feat : (p + 1) * feat] = ref[p, i * rows : (i + 1) * rows, :]
-
-    return call(kernel, [jax.ShapeDtypeStruct((rows, parts * feat), BF16)] * count, [array])
-
-
-def add_call(query_parts, cur_parts, sizes):
+def finish_call(pieces, other, sizes, parts, whole):
+    nx, count, rows, feat = other.shape
+    nc = sizes[3]
+    old = whole[0].shape[1]
+    n = len(parts)
+
+    def kernel(*refs):
+        mine, rest, refs = refs[:nx], refs[nx], refs[nx + 1 :]
+        terms, outs, sums = refs[: -count - 2], refs[-count - 2 : -2], refs[-2:]
+        x, core = lax.axis_index("x"), lax.axis_index("c")
+        for i, out in enumerate(sums):
+            total = sum(term[i].astype(F32) for term in terms[:n])
+            total = total + sum(term[2 + i].astype(F32) for term in terms[n:])
+            out[...] = total.astype(BF16)
+        for j, step in enumerate(X_STEPS):
+            for k in range(nc):
+                part = lax.rem(x + step, nx) * nc + lax.rem(core + k, nc)
+                at = pl.ds(pl.multiple_of(part * feat, feat), feat)
+                for i, out in enumerate(outs):
+                    out[:, at] = mine[j][i, 0:rows] if k == 0 else rest[j, i]
+
+    shapes = [jax.ShapeDtypeStruct((rows, nx * nc * feat), BF16)] * count
+    shapes += [jax.ShapeDtypeStruct((old, feat), BF16)] * 2
+    return call(kernel, shapes, [*pieces, other, *parts, *whole])
+
+
+def add_call(query_parts, cur_parts, pieces):
     tokens, feat = query_parts[0].shape
-    nx, nc = sizes[2:]
-    parts = nx * nc
-    rows = tokens // parts
+    rows = tokens // pieces
     nq = len(query_parts)
 
     def kernel(*refs):
-        out = refs[-1]
-        x, core = lax.axis_index("x"), lax.axis_index("c")
+        ins, outs = refs[:-pieces], refs[-pieces:]
         sums = [
-            sum(ref[...].astype(F32) for ref in refs[:nq]),
-            sum(ref[0].astype(F32) for ref in refs[nq:-1]),
-            sum(ref[1].astype(F32) for ref in refs[nq:-1]),
+            sum(ref[...].astype(F32) for ref in ins[:nq]),
+            sum(ref[0].astype(F32) for ref in ins[nq:]),
+            sum(ref[1].astype(F32) for ref in ins[nq:]),
         ]
         for i, total in enumerate(sums):
             low = total.astype(BF16)
-            for j, step in enumerate(X_STEPS):
-                for k in range(nc):
-                    owner = lax.rem(x + nx - step, nx) * nc + lax.rem(core + k, nc)
-                    first = (j * nc + k) * rows
-                    out[owner, i * rows : (i + 1) * rows, :] = low[first : first + rows]
-
-    shape = jax.ShapeDtypeStruct((parts, 3 * rows, feat), BF16)
-    return call(kernel, shape, list(query_parts) + list(cur_parts))
-
-
-def add_hist_call(parts, whole):
-    _, rows, feat = parts[0].shape
-    n = len(parts)
-
-    def kernel(*refs):
-        for i, out in enumerate(refs[-2:]):
-            total = sum(ref[i].astype(F32) for ref in refs[:n])
-            total = total + sum(ref[2 + i].astype(F32) for ref in refs[n:-2])
-            out[...] = total.astype(BF16)
-
-    return call(kernel, [jax.ShapeDtypeStruct((rows, feat), BF16)] * 2, [*parts, *whole])
+            for j, out in enumerate(outs):
+                out[i] = low[j * rows : (j + 1) * rows]
+
+    shape = jax.ShapeDtypeStruct((3, rows, feat), BF16)
+    return list(call(kernel, [shape] * pieces, list(query_parts) + list(cur_parts)))
+
+
+def other_call(pieces):
+    count, rows, feat = pieces[0].shape
+    rows //= 2
+
+    def kernel(*refs):
+        for j, ref in enumerate(refs[:-1]):
+            refs[-1][j] = ref[:, rows:, :]
+
+    shape = jax.ShapeDtypeStruct((len(pieces), count, rows, feat), BF16)
+    return call(kernel, shape, list(pieces))
 
 
 def ring_moves(sizes):
@@ -477,13 +484,13 @@
         sums, far = lax.optimization_barrier((sums, far))
         query_parts = [sums[0]] + [to_query(sums[i], OFFSETS[i]) for i in range(1, 4)]
 
-        back = add_call(query_parts, [own[0], far, near_m, near_cur], sizes)
+        back = add_call(query_parts, [own[0], far, near_m, near_cur], sizes[2])
         back, near_hist = lax.optimization_barrier((back, near_hist))
         near_hist = to_key(near_hist, OFFSETS[2])
-        back = lax.all_to_all(back, ("x", "c"), 0, 0, tiled=True)
-        outs = unpack_call(back, 3)
-        grad_k, grad_v = add_hist_call([own[1], near_hist], [far, near_m])
-        return outs[0], outs[1], outs[2], grad_k, grad_v
+        moved = [lax.ppermute(p, AXES, chip_move(-d)) for p, d in zip(back[1:], X_STEPS[1:])]
+        back = back[:1] + moved
+        other = lax.ppermute(other_call(back), AXES, core_move())
+        return tuple(finish_call(back, other, sizes, [own[1], near_hist], [far, near_m]))
 
     return shards
 

time: 105 us -> 102 us (0.971); the launches traced: 105 us -> 101 us
  waiting for transfers between devices: 34.2 us -> 30.1 us
  starting transfers between devices: 39.9 us -> 41.3 us
  Pallas kernels: 28.6 us -> 27.3 us
    all_to_all x1 -> x0, starting transfers between devices: 10.1 us -> none  [shards(): back = lax.all_to_all(back, ('x', 'c'), 0, 0, tiled=True)]
    ppermute x0 -> x4, starting transfers between devices: none -> 9.94 us  [the longest x3 5.66 us: shards(): lax.ppermute(p, AXES, chip_move(-d))]
    ppermute x10, waiting for transfers between devices: 18.1 us -> 9.93 us  [to_key(): return lax.ppermute(value, AXES, key_move(step))]
    ppermute x0 -> x4, waiting for transfers between devices: none -> 5.22 us  [the longest x3 4.02 us: shards(): lax.ppermute(p, AXES, chip_move(-d))]
    ppermute x10, starting transfers between devices: 12.2 us -> 13.7 us  [to_key(): return lax.ppermute(value, AXES, key_move(step))]
    pallas_call x12, Pallas kernels: 26.2 us -> 24.9 us  [call(): pl.pallas_call(kernel, out_shape=outs, in_specs=[VMEM] * len(args), out_s...]
    all_to_all x1 -> x0, waiting for transfers between devices: 1.19 us -> none  [shards(): back = lax.all_to_all(back, ('x', 'c'), 0, 0, tiled=True)]
  transfers between devices with their start and end apart: 27 -> 30, of which waited for: 15 -> 15; matrix products, arithmetic and copies ran while one was open for 0% -> 0% of each run, Pallas kernels for 17% -> 17%
where the time goes in v7:
time: 102 us; the launch traced here: 101 us
  starting transfers between devices  41.3 us (40%)
  waiting for transfers between devices  30.1 us (30%)
  Pallas kernels  27.3 us (27%)
  between operations  1.43 us (1%)
    pallas_call x12, Pallas kernels, call(): pl.pallas_call(kernel, out_shape=outs, in_specs=[VMEM] * len(args), out_s...  24.9 us
    ppermute x10, starting transfers between devices, to_key(): return lax.ppermute(value, AXES, key_move(step))  13.7 us
    ppermute x10, waiting for transfers between devices, to_key(): return lax.ppermute(value, AXES, key_move(step))  9.93 us
    ppermute x9, starting transfers between devices, to_query(): return lax.ppermute(value, AXES, query_move(step))  8.9 us
    ppermute x6, waiting for transfers between devices, exchange(): lax.ppermute(p, AXES, chip_move(d))  7.55 us
    ppermute x9, waiting for transfers between devices, to_query(): return lax.ppermute(value, AXES, query_move(step))  7.36 us
    ppermute x6, starting transfers between devices, exchange(): lax.ppermute(p, AXES, chip_move(d))  7.28 us
    ppermute x3, starting transfers between devices, shards(): lax.ppermute(p, AXES, chip_move(-d))  5.66 us
  transfers between devices with their start and end apart: 30, of which 15 were waited for; matrix products, arithmetic and copies ran while one was open for 0% of the time, Pallas kernels for 17%

profile of v7, /device:TPU:1, one launch (start us, length us, event | category | flops | bytes accessed | tf_op | source)
XLA Modules:
  0.0 101.1 jit_solution(7252447382411966137)
XLA Ops:
  1.3 2.4 %shard_map.110 = (bf16[2,4,2,32,384]{4,3,2,1,0:T(8,128)(2,1)}, bf16[2,4,2,32,384]{4,3,2,1,0:T(8,128)(2,1)}, bf16[528,384]{1,0:T(8,128)(2,1)}) custom-call(bf16[32,3072]{1,0:T(8,128)(2,1)} %refs_0_.1, bf16[32,3072]{1,0:T(8,128)(2,1)} %refs_1_.1, bf16[32,3072]{1,0:T(8,128)(2,1)} %refs_2_.1, bf16[32,3072]{1,0:T(8,128)(2,1)} %refs_3_.1, ...), custom_call_target="tpu_custom_call" | custom-call | tf_op jit(solution)/shard_map/pallas_call | solution.py:302
  3.7 1.5 %collective-permute-start = (bf16[2,4,2,32,384]{4,3,2,1,0:T(8,128)(2,1)}, bf16[2,4,2,32,384]{4,3,2,1,0:T(8,128)(2,1)S(1)}, u32[]{:S(2)}, u32[]{:S(2)}) collective-permute-start(bf16[2,4,2,32,384]{4,3,2,1,0:T(8,128)(2,1)} %get-tuple-element.70), channel_id=1, source_target_pairs={{0,1},{1,0},{2,3},{3,2},{4,5},{5,4},{6,7},{7,6},{8,9},{9,8},{10,11... | collective-permute-start | bytes 1179656 | tf_op jit(solution)/shard_map/ppermute | solution.py:443
  5.2 3.8 %collective-permute-start.2 = (bf16[528,384]{1,0:T(8,128)(2,1)}, bf16[528,384]{1,0:T(8,128)(2,1)S(1)}, u32[]{:S(2)}, u32[]{:S(2)}) collective-permute-start(bf16[528,384]{1,0:T(8,128)(2,1)} %get-tuple-element.75.refs_1_), channel_id=1, source_target_pairs={{0,24},{1,97},{2,26},{3,99},{4,28},{5,101},{6,30},{7,103},{8,0},{9... | collective-permute-start | bytes 1216520 | tf_op jit(solution)/shard_map/ppermute | solution.py:434
  11.4 1.5 %collective-permute-start.7 = (bf16[2,64,384]{2,1,0:T(8,128)(2,1)S(1)}, bf16[2,64,384]{2,1,0:T(8,128)(2,1)S(1)}, u32[]{:S(2)}, u32[]{:S(2)}) collective-permute-start(bf16[2,64,384]{2,1,0:T(8,128)(2,1)S(1)} %get-tuple-element.82), channel_id=1, source_target_pairs={{0,6},{1,7},{2,0},{3,1},{4,2},{5,3},{6,4},{7,5},{8,14},{9,15},{10,... | collective-permute-start | bytes 294920 | tf_op jit(solution)/shard_map/ppermute | solution.py:450
  12.9 1.5 %collective-permute-start.8 = (bf16[2,64,384]{2,1,0:T(8,128)(2,1)S(1)}, bf16[2,64,384]{2,1,0:T(8,128)(2,1)S(1)}, u32[]{:S(2)}, u32[]{:S(2)}) collective-permute-start(bf16[2,64,384]{2,1,0:T(8,128)(2,1)S(1)} %get-tuple-element.83), channel_id=1, source_target_pairs={{0,4},{1,5},{2,6},{3,7},{4,0},{5,1},{6,2},{7,3},{8,12},{9,13},{10,... | collective-permute-start | bytes 294920 | tf_op jit(solution)/shard_map/ppermute | solution.py:450
  14.4 1.6 %collective-permute-done.6.refs_1_ = bf16[2,64,384]{2,1,0:T(8,128)(2,1)S(1)} collective-permute-done((bf16[2,64,384]{2,1,0:T(8,128)(2,1)S(1)}, bf16[2,64,384]{2,1,0:T(8,128)(2,1)S(1)}, u32[]{:S(2)}, u32[]{:S(2)}) %collective-permute-start.6) | collective-permute-done | bytes 98336 | tf_op jit(solution)/shard_map/ppermute | solution.py:450
  16.3 2.7 %collective-permute-done.8.refs_3_ = bf16[2,64,384]{2,1,0:T(8,128)(2,1)S(1)} collective-permute-done((bf16[2,64,384]{2,1,0:T(8,128)(2,1)S(1)}, bf16[2,64,384]{2,1,0:T(8,128)(2,1)S(1)}, u32[]{:S(2)}, u32[]{:S(2)}) %collective-permute-start.8) | collective-permute-done | bytes 98336 | tf_op jit(solution)/shard_map/ppermute | solution.py:450
  19.0 2.3 %collective-permute-start.11 = (bf16[2,256,384]{2,1,0:T(8,128)(2,1)S(1)}, bf16[2,256,384]{2,1,0:T(8,128)(2,1)S(1)}, u32[]{:S(2)}, u32[]{:S(2)}) collective-permute-start(bf16[2,256,384]{2,1,0:T(8,128)(2,1)S(1)} %shard_map.113.refs_5_.refs_3_.refs_2_.refs_4_), channel_id=1, source_target_pairs={{0,64},{1,17},{2,66},{3,19},{4,68},{5,21},{6,70},{7,23},{8,72},{9,... | collective-permute-start | bytes 1179656 | tf_op jit(solution)/shard_map/ppermute | solution.py:437
  22.3 1.7 %collective-permute-start.4 = (bf16[2,64,384]{2,1,0:T(8,128)(2,1)S(1)}, bf16[2,64,384]{2,1,0:T(8,128)(2,1)S(1)}, u32[]{:S(2)}, u32[]{:S(2)}) collective-permute-start(bf16[2,64,384]{2,1,0:T(8,128)(2,1)S(1)} %get-tuple-element.78), channel_id=1, source_target_pairs={{0,6},{1,7},{2,0},{3,1},{4,2},{5,3},{6,4},{7,5},{8,14},{9,15},{10,... | collective-permute-start | bytes 294920 | tf_op jit(solution)/shard_map/ppermute | solution.py:450
  24.3 2.0 %collective-permute-done.3.refs_1_ = bf16[2,64,384]{2,1,0:T(8,128)(2,1)S(1)} collective-permute-done((bf16[2,64,384]{2,1,0:T(8,128)(2,1)S(1)}, bf16[2,64,384]{2,1,0:T(8,128)(2,1)S(1)}, u32[]{:S(2)}, u32[]{:S(2)}) %collective-permute-start.3) | collective-permute-done | bytes 98336 | tf_op jit(solution)/shard_map/ppermute | solution.py:450
  27.8 1.3 %collective-permute-done.5.refs_3_ = bf16[2,64,384]{2,1,0:T(8,128)(2,1)S(1)} collective-permute-done((bf16[2,64,384]{2,1,0:T(8,128)(2,1)S(1)}, bf16[2,64,384]{2,1,0:T(8,128)(2,1)S(1)}, u32[]{:S(2)}, u32[]{:S(2)}) %collective-permute-start.5) | collective-permute-done | bytes 98336 | tf_op jit(solution)/shard_map/ppermute | solution.py:450
  29.1 1.4 %collective-permute-start.14 = (bf16[2,256,384]{2,1,0:T(8,128)(2,1)S(1)}, bf16[2,256,384]{2,1,0:T(8,128)(2,1)S(1)}, u32[]{:S(2)}, u32[]{:S(2)}) collective-permute-start(bf16[2,256,384]{2,1,0:T(8,128)(2,1)S(1)} %shard_map.112.refs_0_), channel_id=1, source_target_pairs={{0,16},{1,65},{2,18},{3,67},{4,20},{5,69},{6,22},{7,71},{8,24},{9,... | collective-permute-start | bytes 1179656 | tf_op jit(solution)/shard_map/ppermute | solution.py:434
  30.5 3.0 %collective-permute-start.13 = (bf16[2,256,384]{2,1,0:T(8,128)(2,1)S(1)}, bf16[2,256,384]{2,1,0:T(8,128)(2,1)S(1)}, u32[]{:S(2)}, u32[]{:S(2)}) collective-permute-start(bf16[2,256,384]{2,1,0:T(8,128)(2,1)S(1)} %shard_map.112.refs_0_), channel_id=1, source_target_pairs={{0,24},{1,97},{2,26},{3,99},{4,28},{5,101},{6,30},{7,103},{8,0},{9... | collective-permute-start | bytes 1179656 | tf_op jit(solution)/shard_map/ppermute | solution.py:434
  34.1 3.4 %shard_map.114 = (f32[3,16,256]{2,1,0:T(8,128)S(1)}, f32[3,256,512]{2,1,0:T(8,128)S(1)}, f32[3,256,512]{2,1,0:T(8,128)S(1)}, f32[3,256,512]{2,1,0:T(8,128)S(1)},...) custom-call(bf16[2,256,384]{2,1,0:T(8,128)(2,1)S(1)} %shard_map.112.refs_0_, ...), custom_call_target="tpu_custom_call" | custom-call | flops 31457280 | bytes 43776 | tf_op jit(solution)/shard_map/pallas_call | solution.py:36
  37.5 3.4 %shard_map.115 = (f32[3,16,256]{2,1,0:T(8,128)S(1)}, f32[3,256,512]{2,1,0:T(8,128)S(1)}, f32[3,256,512]{2,1,0:T(8,128)S(1)}, f32[3,256,512]{2,1,0:T(8,128)S(1)},...) custom-call(bf16[2,256,384]{2,1,0:T(8,128)(2,1)S(1)} %shard_map.112.refs_0_, ...), custom_call_target="tpu_custom_call" | custom-call | flops 31457280 | bytes 44544 | tf_op jit(solution)/shard_map/pallas_call | solution.py:36
  41.0 4.7 %collective-permute-done.13.refs_1_ = bf16[2,256,384]{2,1,0:T(8,128)(2,1)S(1)} collective-permute-done((bf16[2,256,384]{2,1,0:T(8,128)(2,1)S(1)}, bf16[2,256,384]{2,1,0:T(8,128)(2,1)S(1)}, u32[]{:S(2)}, u32[]{:S(2)}) %collective-permute-start.13) | collective-permute-done | bytes 393248 | tf_op jit(solution)/shard_map/ppermute | solution.py:434
  45.8 3.4 %shard_map.116 = (f32[3,16,256]{2,1,0:T(8,128)S(1)}, f32[3,256,1024]{2,1,0:T(8,128)S(1)}, f32[3,256,1024]{2,1,0:T(8,128)S(1)}, f32[3,256,1024]{2,1,0:T(8,128)S(1...) custom-call(bf16[2,256,384]{2,1,0:T(8,128)(2,1)S(1)} %collective-permute-done.12.refs_0_, ...), custom_call_target="tpu_custom_call" | custom-call | flops 37748736 | bytes 43776 | tf_op jit(solution)/shard_map/pallas_call | solution.py:36
  49.2 1.9 %collective-permute-start.18 = (f32[3,16,256]{2,1,0:T(8,128)S(1)}, f32[3,16,256]{2,1,0:T(8,128)S(1)}, u32[]{:S(2)}, u32[]{:S(2)}) collective-permute-start(f32[3,16,256]{2,1,0:T(8,128)S(1)} %get-tuple-element.88.refs_6_.refs_8_), channel_id=1, source_target_pairs={{0,64},{1,17},{2,66},{3,19},{4,68},{5,21},{6,70},{7,23},{8,72},{9,... | collective-permute-start | bytes 147464 | tf_op jit(solution)/shard_map/ppermute | solution.py:437
  51.0 1.7 %collective-permute-start.17 = (f32[3,16,256]{2,1,0:T(8,128)S(1)}, f32[3,16,256]{2,1,0:T(8,128)S(1)}, u32[]{:S(2)}, u32[]{:S(2)}) collective-permute-start(f32[3,16,256]{2,1,0:T(8,128)S(1)} %get-tuple-element.88.refs_6_.refs_8_), channel_id=1, source_target_pairs={{0,96},{1,25},{2,98},{3,27},{4,100},{5,29},{6,102},{7,31},{8,104},... | collective-permute-start | bytes 147464 | tf_op jit(solution)/shard_map/ppermute | solution.py:437
  54.0 3.0 %collective-permute-done.16.refs_7_.refs_9_ = f32[3,16,256]{2,1,0:T(8,128)S(1)} collective-permute-done((f32[3,16,256]{2,1,0:T(8,128)S(1)}, f32[3,16,256]{2,1,0:T(8,128)S(1)}, u32[]{:S(2)}, u32[]{:S(2)}) %collective-permute-start.16) | collective-permute-done | bytes 49184 | tf_op jit(solution)/shard_map/ppermute | solution.py:437
  57.0 2.9 %shard_map.117 = (bf16[4,256,384]{2,1,0:T(8,128)(2,1)S(1)}, f32[3,128,1024]{2,1,0:T(8,128)S(1)}) custom-call(bf16[2,256,384]{2,1,0:T(8,128)(2,1)S(1)} %collective-permute-done.14.refs_2_.refs_0_, bf16[528,384]{1,0:T(8,128)(2,1)S(1)} %collective-permute-done.15.refs_4_.refs_1_, bf16[2,256,384]{2,1,0:T(8,128)(2,1)S(1)} %shard_map.113.refs_5_.refs_3_.refs_2_.refs_4_, ...), custom_call_target="tpu_custom_call" | custom-call | flops 62914560 | bytes 236736 | tf_op jit(solution)/shard_map/pallas_call | solution.py:36
  59.9 1.6 %collective-permute-start.19 = (bf16[4,256,384]{2,1,0:T(8,128)(2,1)S(1)}, bf16[4,256,384]{2,1,0:T(8,128)(2,1)S(1)}, u32[]{:S(2)}, u32[]{:S(2)}) collective-permute-start(bf16[4,256,384]{2,1,0:T(8,128)(2,1)S(1)} %get-tuple-element.113), channel_id=1, source_target_pairs={{0,16},{1,65},{2,18},{3,67},{4,20},{5,69},{6,22},{7,71},{8,24},{9,... | collective-permute-start | bytes 2359304 | tf_op jit(solution)/shard_map/ppermute | solution.py:434
  61.5 7.1 %shard_map.118 = (bf16[4,256,384]{2,1,0:T(8,128)(2,1)S(1)}, bf16[2,256,384]{2,1,0:T(8,128)(2,1)S(1)}, bf16[2,256,384]{2,1,0:T(8,128)(2,1)S(1)}, f32[3,128,1024]{2,1,0:T(8,128)S(1)}) custom-call(bf16[2,256,384]{2,1,0:T(8,128)(2,1)S(1)} %collective-permute-done.12.refs_0_, bf16[2,256,384]{2,1,0:T(8,128)(2,1)S(1)} %collective-permute-done.13.refs_1_, ...), custom_call_target="tpu_custom_call" | custom-call | flops 125829120 | bytes 273792 | tf_op jit(solution)/shard_map/pallas_call | solution.py:36
  70.1 3.0 %shard_map.119 = (bf16[2,256,384]{2,1,0:T(8,128)(2,1)S(1)}, bf16[2,256,384]{2,1,0:T(8,128)(2,1)S(1)}, bf16[256,384]{1,0:T(8,128)(2,1)S(1)}, bf16[256,384]{1,0:T(...) custom-call(bf16[2,256,384]{2,1,0:T(8,128)(2,1)S(1)} %shard_map.112.refs_0_, ...), custom_call_target="tpu_custom_call" | custom-call | flops 62914560 | bytes 261312 | tf_op jit(solution)/shard_map/pallas_call | solution.py:36
  73.3 1.5 %collective-permute-start.21 = (bf16[256,384]{1,0:T(8,128)(2,1)S(1)}, bf16[256,384]{1,0:T(8,128)(2,1)S(1)}, u32[]{:S(2)}, u32[]{:S(2)}) collective-permute-start(bf16[256,384]{1,0:T(8,128)(2,1)S(1)} %get-tuple-element.116), channel_id=1, source_target_pairs={{0,32},{1,9},{2,34},{3,11},{4,36},{5,13},{6,38},{7,15},{8,40},{9,1... | collective-permute-start | bytes 589832 | tf_op jit(solution)/shard_map/ppermute | solution.py:437
  74.7 3.0 %collective-permute-done.24.refs_7_ = bf16[2,256,384]{2,1,0:T(8,128)(2,1)S(1)} collective-permute-done((bf16[2,256,384]{2,1,0:T(8,128)(2,1)S(1)}, bf16[2,256,384]{2,1,0:T(8,128)(2,1)S(1)}, u32[]{:S(2)}, u32[]{:S(2)}) %collective-permute-start.24) | collective-permute-done | bytes 393248 | tf_op jit(solution)/shard_map/ppermute | solution.py:434
  77.7 2.1 %collective-permute-done.23.refs_6_.refs_8_ = bf16[4,256,384]{2,1,0:T(8,128)(2,1)S(1)} collective-permute-done((bf16[4,256,384]{2,1,0:T(8,128)(2,1)S(1)}, bf16[4,256,384]{2,1,0:T(8,128)(2,1)S(1)}, u32[]{:S(2)}, u32[]{:S(2)}) %collective-permute-start.23) | collective-permute-done | bytes 786464 | tf_op jit(solution)/shard_map/ppermute | solution.py:434
  80.3 2.7 %collective-permute-done.22.refs_3_ = bf16[256,384]{1,0:T(8,128)(2,1)S(1)} collective-permute-done((bf16[256,384]{1,0:T(8,128)(2,1)S(1)}, bf16[256,384]{1,0:T(8,128)(2,1)S(1)}, u32[]{:S(2)}, u32[]{:S(2)}) %collective-permute-start.22) | collective-permute-done | bytes 196640 | tf_op jit(solution)/shard_map/ppermute | solution.py:437
  83.3 4.4 %collective-permute-start.25 = (bf16[3,64,384]{2,1,0:T(8,128)(2,1)S(1)}, bf16[3,64,384]{2,1,0:T(8,128)(2,1)S(1)}, u32[]{:S(2)}, u32[]{:S(2)}) collective-permute-start(bf16[3,64,384]{2,1,0:T(8,128)(2,1)S(1)} %get-tuple-element.128), channel_id=1, source_target_pairs={{0,6},{1,7},{2,0},{3,1},{4,2},{5,3},{6,4},{7,5},{8,14},{9,15},{10,... | collective-permute-start | bytes 442376 | tf_op jit(solution)/shard_map/ppermute | solution.py:490
  88.9 1.5 %collective-permute-start.29 = (bf16[2,256,384]{2,1,0:T(8,128)(2,1)S(1)}, bf16[2,256,384]{2,1,0:T(8,128)(2,1)S(1)}, u32[]{:S(2)}, u32[]{:S(2)}) collective-permute-start(bf16[2,256,384]{2,1,0:T(8,128)(2,1)S(1)} %get-tuple-element.132), channel_id=1, source_target_pairs={{0,8},{1,33},{2,10},{3,35},{4,12},{5,37},{6,14},{7,39},{8,16},{9,4... | collective-permute-start | bytes 1179656 | tf_op jit(solution)/shard_map/ppermute | solution.py:434
  90.4 4.0 %collective-permute-done.26.refs_2_ = bf16[3,64,384]{2,1,0:T(8,128)(2,1)S(1)} collective-permute-done((bf16[3,64,384]{2,1,0:T(8,128)(2,1)S(1)}, bf16[3,64,384]{2,1,0:T(8,128)(2,1)S(1)}, u32[]{:S(2)}, u32[]{:S(2)}) %collective-permute-start.26) | collective-permute-done | bytes 147488 | tf_op jit(solution)/shard_map/ppermute | solution.py:490
  94.5 4.3 %collective-permute-start.28 = (bf16[4,3,32,384]{3,2,1,0:T(8,128)(2,1)S(1)}, bf16[4,3,32,384]{3,2,1,0:T(8,128)(2,1)S(1)}, u32[]{:S(2)}, u32[]{:S(2)}) collective-permute-start(bf16[4,3,32,384]{3,2,1,0:T(8,128)(2,1)S(1)} %shard_map.121), channel_id=1, source_target_pairs={{0,1},{1,0},{2,3},{3,2},{4,5},{5,4},{6,7},{7,6},{8,9},{9,8},{10,11... | collective-permute-start | bytes 884744 | tf_op jit(solution)/shard_map/ppermute | solution.py:492
  (45 shorter events, 13.4 us)
Async XLA Ops:
  3.7 30.4 %copy-start = (bf16[528,384]{1,0:T(8,128)(2,1)S(1)}, bf16[528,384]{1,0:T(8,128)(2,1)}, u32[]{:S(2)}) copy-start(bf16[528,384]{1,0:T(8,128)(2,1)} %get-tuple-element.75.refs_1_) | copy-start | bytes 1216516
  3.7 5.3 %collective-permute-start = (bf16[2,4,2,32,384]{4,3,2,1,0:T(8,128)(2,1)}, bf16[2,4,2,32,384]{4,3,2,1,0:T(8,128)(2,1)S(1)}, u32[]{:S(2)}, u32[]{:S(2)}) collective-permute-start(bf16[2,4,2,32,384]{4,3,2,1,0:T(8,128)(2,1)} %get-tuple-element.70), channel_id=1, source_target_pairs={{0,1},{1,0},{2,3},{3,2},{4,5},{5,4},{6,7},{7,6},{8,9},{9,8},{10,11... | collective-permute-start | bytes 1179656 | tf_op jit(solution)/shard_map/ppermute | solution.py:443
  5.2 16.1 %collective-permute-start.2 = (bf16[528,384]{1,0:T(8,128)(2,1)}, bf16[528,384]{1,0:T(8,128)(2,1)S(1)}, u32[]{:S(2)}, u32[]{:S(2)}) collective-permute-start(bf16[528,384]{1,0:T(8,128)(2,1)} %get-tuple-element.75.refs_1_), channel_id=1, source_target_pairs={{0,24},{1,97},{2,26},{3,99},{4,28},{5,101},{6,30},{7,103},{8,0},{9... | collective-permute-start | bytes 1216520 | tf_op jit(solution)/shard_map/ppermute | solution.py:434
  9.1 12.3 %collective-permute-start.1 = (bf16[528,384]{1,0:T(8,128)(2,1)}, bf16[528,384]{1,0:T(8,128)(2,1)S(1)}, u32[]{:S(2)}, u32[]{:S(2)}) collective-permute-start(bf16[528,384]{1,0:T(8,128)(2,1)} %get-tuple-element.75.refs_1_), channel_id=1, source_target_pairs={{0,8},{1,33},{2,10},{3,35},{4,12},{5,37},{6,14},{7,39},{8,16},{9,4... | collective-permute-start | bytes 1216520 | tf_op jit(solution)/shard_map/ppermute | solution.py:434
  9.1 1.0 copy-start.1
  10.2 5.9 %collective-permute-start.6 = (bf16[2,64,384]{2,1,0:T(8,128)(2,1)S(1)}, bf16[2,64,384]{2,1,0:T(8,128)(2,1)S(1)}, u32[]{:S(2)}, u32[]{:S(2)}) collective-permute-start(bf16[2,64,384]{2,1,0:T(8,128)(2,1)S(1)} %get-tuple-element.81), channel_id=1, source_target_pairs={{0,2},{1,3},{2,4},{3,5},{4,6},{5,7},{6,0},{7,1},{8,10},{9,11},{10,... | collective-permute-start | bytes 294920 | tf_op jit(solution)/shard_map/ppermute | solution.py:450
  11.4 4.9 %collective-permute-start.7 = (bf16[2,64,384]{2,1,0:T(8,128)(2,1)S(1)}, bf16[2,64,384]{2,1,0:T(8,128)(2,1)S(1)}, u32[]{:S(2)}, u32[]{:S(2)}) collective-permute-start(bf16[2,64,384]{2,1,0:T(8,128)(2,1)S(1)} %get-tuple-element.82), channel_id=1, source_target_pairs={{0,6},{1,7},{2,0},{3,1},{4,2},{5,3},{6,4},{7,5},{8,14},{9,15},{10,... | collective-permute-start | bytes 294920 | tf_op jit(solution)/shard_map/ppermute | solution.py:450
  12.9 6.1 %collective-permute-start.8 = (bf16[2,64,384]{2,1,0:T(8,128)(2,1)S(1)}, bf16[2,64,384]{2,1,0:T(8,128)(2,1)S(1)}, u32[]{:S(2)}, u32[]{:S(2)}) collective-permute-start(bf16[2,64,384]{2,1,0:T(8,128)(2,1)S(1)} %get-tuple-element.83), channel_id=1, source_target_pairs={{0,4},{1,5},{2,6},{3,7},{4,0},{5,1},{6,2},{7,3},{8,12},{9,13},{10,... | collective-permute-start | bytes 294920 | tf_op jit(solution)/shard_map/ppermute | solution.py:450
  16.0 14.4 %collective-permute-start.15 = (bf16[528,384]{1,0:T(8,128)(2,1)}, bf16[528,384]{1,0:T(8,128)(2,1)S(1)}, u32[]{:S(2)}, u32[]{:S(2)}) collective-permute-start(bf16[528,384]{1,0:T(8,128)(2,1)} %get-tuple-element.75.refs_1_), channel_id=1, source_target_pairs={{0,16},{1,65},{2,18},{3,67},{4,20},{5,69},{6,22},{7,71},{8,24},{9,... | collective-permute-start | bytes 1216520 | tf_op jit(solution)/shard_map/ppermute | solution.py:434
  19.0 14.5 %collective-permute-start.11 = (bf16[2,256,384]{2,1,0:T(8,128)(2,1)S(1)}, bf16[2,256,384]{2,1,0:T(8,128)(2,1)S(1)}, u32[]{:S(2)}, u32[]{:S(2)}) collective-permute-start(bf16[2,256,384]{2,1,0:T(8,128)(2,1)S(1)} %shard_map.113.refs_5_.refs_3_.refs_2_.refs_4_), channel_id=1, source_target_pairs={{0,64},{1,17},{2,66},{3,19},{4,68},{5,21},{6,70},{7,23},{8,72},{9,... | collective-permute-start | bytes 1179656 | tf_op jit(solution)/shard_map/ppermute | solution.py:437
  21.3 5.0 %collective-permute-start.3 = (bf16[2,64,384]{2,1,0:T(8,128)(2,1)S(1)}, bf16[2,64,384]{2,1,0:T(8,128)(2,1)S(1)}, u32[]{:S(2)}, u32[]{:S(2)}) collective-permute-start(bf16[2,64,384]{2,1,0:T(8,128)(2,1)S(1)} %get-tuple-element.77), channel_id=1, source_target_pairs={{0,2},{1,3},{2,4},{3,5},{4,6},{5,7},{6,0},{7,1},{8,10},{9,11},{10,... | collective-permute-start | bytes 294920 | tf_op jit(solution)/shard_map/ppermute | solution.py:450
  22.3 4.8 %collective-permute-start.4 = (bf16[2,64,384]{2,1,0:T(8,128)(2,1)S(1)}, bf16[2,64,384]{2,1,0:T(8,128)(2,1)S(1)}, u32[]{:S(2)}, u32[]{:S(2)}) collective-permute-start(bf16[2,64,384]{2,1,0:T(8,128)(2,1)S(1)} %get-tuple-element.78), channel_id=1, source_target_pairs={{0,6},{1,7},{2,0},{3,1},{4,2},{5,3},{6,4},{7,5},{8,14},{9,15},{10,... | collective-permute-start | bytes 294920 | tf_op jit(solution)/shard_map/ppermute | solution.py:450
  24.0 5.1 %collective-permute-start.5 = (bf16[2,64,384]{2,1,0:T(8,128)(2,1)S(1)}, bf16[2,64,384]{2,1,0:T(8,128)(2,1)S(1)}, u32[]{:S(2)}, u32[]{:S(2)}) collective-permute-start(bf16[2,64,384]{2,1,0:T(8,128)(2,1)S(1)} %get-tuple-element.79), channel_id=1, source_target_pairs={{0,4},{1,5},{2,6},{3,7},{4,0},{5,1},{6,2},{7,3},{8,12},{9,13},{10,... | collective-permute-start | bytes 294920 | tf_op jit(solution)/shard_map/ppermute | solution.py:450
  26.3 11.2 %collective-permute-start.10 = (bf16[2,256,384]{2,1,0:T(8,128)(2,1)S(1)}, bf16[2,256,384]{2,1,0:T(8,128)(2,1)S(1)}, u32[]{:S(2)}, u32[]{:S(2)}) collective-permute-start(bf16[2,256,384]{2,1,0:T(8,128)(2,1)S(1)} %shard_map.113.refs_5_.refs_3_.refs_2_.refs_4_), channel_id=1, source_target_pairs={{0,96},{1,25},{2,98},{3,27},{4,100},{5,29},{6,102},{7,31},{8,104},... | collective-permute-start | bytes 1179656 | tf_op jit(solution)/shard_map/ppermute | solution.py:437
  27.1 10.4 %collective-permute-start.9 = (bf16[2,256,384]{2,1,0:T(8,128)(2,1)S(1)}, bf16[2,256,384]{2,1,0:T(8,128)(2,1)S(1)}, u32[]{:S(2)}, u32[]{:S(2)}) collective-permute-start(bf16[2,256,384]{2,1,0:T(8,128)(2,1)S(1)} %shard_map.113.refs_5_.refs_3_.refs_2_.refs_4_), channel_id=1, source_target_pairs={{0,32},{1,9},{2,34},{3,11},{4,36},{5,13},{6,38},{7,15},{8,40},{9,1... | collective-permute-start | bytes 1179656 | tf_op jit(solution)/shard_map/ppermute | solution.py:437
  29.1 11.9 %collective-permute-start.14 = (bf16[2,256,384]{2,1,0:T(8,128)(2,1)S(1)}, bf16[2,256,384]{2,1,0:T(8,128)(2,1)S(1)}, u32[]{:S(2)}, u32[]{:S(2)}) collective-permute-start(bf16[2,256,384]{2,1,0:T(8,128)(2,1)S(1)} %shard_map.112.refs_0_), channel_id=1, source_target_pairs={{0,16},{1,65},{2,18},{3,67},{4,20},{5,69},{6,22},{7,71},{8,24},{9,... | collective-permute-start | bytes 1179656 | tf_op jit(solution)/shard_map/ppermute | solution.py:434
  30.5 15.2 %collective-permute-start.13 = (bf16[2,256,384]{2,1,0:T(8,128)(2,1)S(1)}, bf16[2,256,384]{2,1,0:T(8,128)(2,1)S(1)}, u32[]{:S(2)}, u32[]{:S(2)}) collective-permute-start(bf16[2,256,384]{2,1,0:T(8,128)(2,1)S(1)} %shard_map.112.refs_0_), channel_id=1, source_target_pairs={{0,24},{1,97},{2,26},{3,99},{4,28},{5,101},{6,30},{7,103},{8,0},{9... | collective-permute-start | bytes 1179656 | tf_op jit(solution)/shard_map/ppermute | solution.py:434
  33.5 12.3 %collective-permute-start.12 = (bf16[2,256,384]{2,1,0:T(8,128)(2,1)S(1)}, bf16[2,256,384]{2,1,0:T(8,128)(2,1)S(1)}, u32[]{:S(2)}, u32[]{:S(2)}) collective-permute-start(bf16[2,256,384]{2,1,0:T(8,128)(2,1)S(1)} %shard_map.112.refs_0_), channel_id=1, source_target_pairs={{0,8},{1,33},{2,10},{3,35},{4,12},{5,37},{6,14},{7,39},{8,16},{9,4... | collective-permute-start | bytes 1179656 | tf_op jit(solution)/shard_map/ppermute | solution.py:434
  49.2 4.5 %collective-permute-start.18 = (f32[3,16,256]{2,1,0:T(8,128)S(1)}, f32[3,16,256]{2,1,0:T(8,128)S(1)}, u32[]{:S(2)}, u32[]{:S(2)}) collective-permute-start(f32[3,16,256]{2,1,0:T(8,128)S(1)} %get-tuple-element.88.refs_6_.refs_8_), channel_id=1, source_target_pairs={{0,64},{1,17},{2,66},{3,19},{4,68},{5,21},{6,70},{7,23},{8,72},{9,... | collective-permute-start | bytes 147464 | tf_op jit(solution)/shard_map/ppermute | solution.py:437
  51.0 2.9 %collective-permute-start.17 = (f32[3,16,256]{2,1,0:T(8,128)S(1)}, f32[3,16,256]{2,1,0:T(8,128)S(1)}, u32[]{:S(2)}, u32[]{:S(2)}) collective-permute-start(f32[3,16,256]{2,1,0:T(8,128)S(1)} %get-tuple-element.88.refs_6_.refs_8_), channel_id=1, source_target_pairs={{0,96},{1,25},{2,98},{3,27},{4,100},{5,29},{6,102},{7,31},{8,104},... | collective-permute-start | bytes 147464 | tf_op jit(solution)/shard_map/ppermute | solution.py:437
  52.7 4.2 %collective-permute-start.16 = (f32[3,16,256]{2,1,0:T(8,128)S(1)}, f32[3,16,256]{2,1,0:T(8,128)S(1)}, u32[]{:S(2)}, u32[]{:S(2)}) collective-permute-start(f32[3,16,256]{2,1,0:T(8,128)S(1)} %get-tuple-element.88.refs_6_.refs_8_), channel_id=1, source_target_pairs={{0,32},{1,9},{2,34},{3,11},{4,36},{5,13},{6,38},{7,15},{8,40},{9,1... | collective-permute-start | bytes 147464 | tf_op jit(solution)/shard_map/ppermute | solution.py:437
  59.9 13.3 %collective-permute-start.19 = (bf16[4,256,384]{2,1,0:T(8,128)(2,1)S(1)}, bf16[4,256,384]{2,1,0:T(8,128)(2,1)S(1)}, u32[]{:S(2)}, u32[]{:S(2)}) collective-permute-start(bf16[4,256,384]{2,1,0:T(8,128)(2,1)S(1)} %get-tuple-element.113), channel_id=1, source_target_pairs={{0,16},{1,65},{2,18},{3,67},{4,20},{5,69},{6,22},{7,71},{8,24},{9,... | collective-permute-start | bytes 2359304 | tf_op jit(solution)/shard_map/ppermute | solution.py:434
  68.6 11.2 %collective-permute-start.23 = (bf16[4,256,384]{2,1,0:T(8,128)(2,1)S(1)}, bf16[4,256,384]{2,1,0:T(8,128)(2,1)S(1)}, u32[]{:S(2)}, u32[]{:S(2)}) collective-permute-start(bf16[4,256,384]{2,1,0:T(8,128)(2,1)S(1)} %get-tuple-element.120), channel_id=1, source_target_pairs={{0,24},{1,97},{2,26},{3,99},{4,28},{5,101},{6,30},{7,103},{8,0},{9... | collective-permute-start | bytes 2359304 | tf_op jit(solution)/shard_map/ppermute | solution.py:434
  69.9 7.8 %collective-permute-start.24 = (bf16[2,256,384]{2,1,0:T(8,128)(2,1)S(1)}, bf16[2,256,384]{2,1,0:T(8,128)(2,1)S(1)}, u32[]{:S(2)}, u32[]{:S(2)}) collective-permute-start(bf16[2,256,384]{2,1,0:T(8,128)(2,1)S(1)} %get-tuple-element.121), channel_id=1, source_target_pairs={{0,8},{1,33},{2,10},{3,35},{4,12},{5,37},{6,14},{7,39},{8,16},{9,4... | collective-permute-start | bytes 1179656 | tf_op jit(solution)/shard_map/ppermute | solution.py:434
  73.2 7.1 %collective-permute-start.20 = (bf16[256,384]{1,0:T(8,128)(2,1)S(1)}, bf16[256,384]{1,0:T(8,128)(2,1)S(1)}, u32[]{:S(2)}, u32[]{:S(2)}) collective-permute-start(bf16[256,384]{1,0:T(8,128)(2,1)S(1)} %get-tuple-element.115), channel_id=1, source_target_pairs={{0,96},{1,25},{2,98},{3,27},{4,100},{5,29},{6,102},{7,31},{8,104},... | collective-permute-start | bytes 589832 | tf_op jit(solution)/shard_map/ppermute | solution.py:437
  73.3 7.0 %collective-permute-start.21 = (bf16[256,384]{1,0:T(8,128)(2,1)S(1)}, bf16[256,384]{1,0:T(8,128)(2,1)S(1)}, u32[]{:S(2)}, u32[]{:S(2)}) collective-permute-start(bf16[256,384]{1,0:T(8,128)(2,1)S(1)} %get-tuple-element.116), channel_id=1, source_target_pairs={{0,32},{1,9},{2,34},{3,11},{4,36},{5,13},{6,38},{7,15},{8,40},{9,1... | collective-permute-start | bytes 589832 | tf_op jit(solution)/shard_map/ppermute | solution.py:437
  74.7 8.2 %collective-permute-start.22 = (bf16[256,384]{1,0:T(8,128)(2,1)S(1)}, bf16[256,384]{1,0:T(8,128)(2,1)S(1)}, u32[]{:S(2)}, u32[]{:S(2)}) collective-permute-start(bf16[256,384]{1,0:T(8,128)(2,1)S(1)} %get-tuple-element.117), channel_id=1, source_target_pairs={{0,64},{1,17},{2,66},{3,19},{4,68},{5,21},{6,70},{7,23},{8,72},{9,... | collective-permute-start | bytes 589832 | tf_op jit(solution)/shard_map/ppermute | solution.py:437
  83.3 7.2 %collective-permute-start.25 = (bf16[3,64,384]{2,1,0:T(8,128)(2,1)S(1)}, bf16[3,64,384]{2,1,0:T(8,128)(2,1)S(1)}, u32[]{:S(2)}, u32[]{:S(2)}) collective-permute-start(bf16[3,64,384]{2,1,0:T(8,128)(2,1)S(1)} %get-tuple-element.128), channel_id=1, source_target_pairs={{0,6},{1,7},{2,0},{3,1},{4,2},{5,3},{6,4},{7,5},{8,14},{9,15},{10,... | collective-permute-start | bytes 442376 | tf_op jit(solution)/shard_map/ppermute | solution.py:490
  87.7 6.8 %collective-permute-start.26 = (bf16[3,64,384]{2,1,0:T(8,128)(2,1)S(1)}, bf16[3,64,384]{2,1,0:T(8,128)(2,1)S(1)}, u32[]{:S(2)}, u32[]{:S(2)}) collective-permute-start(bf16[3,64,384]{2,1,0:T(8,128)(2,1)S(1)} %get-tuple-element.129), channel_id=1, source_target_pairs={{0,2},{1,3},{2,4},{3,5},{4,6},{5,7},{6,0},{7,1},{8,10},{9,11},{10,... | collective-permute-start | bytes 442376 | tf_op jit(solution)/shard_map/ppermute | solution.py:490
  87.7 6.8 %collective-permute-start.27 = (bf16[3,64,384]{2,1,0:T(8,128)(2,1)S(1)}, bf16[3,64,384]{2,1,0:T(8,128)(2,1)S(1)}, u32[]{:S(2)}, u32[]{:S(2)}) collective-permute-start(bf16[3,64,384]{2,1,0:T(8,128)(2,1)S(1)} %get-tuple-element.130), channel_id=1, source_target_pairs={{0,4},{1,5},{2,6},{3,7},{4,0},{5,1},{6,2},{7,3},{8,12},{9,13},{10,... | collective-permute-start | bytes 442376 | tf_op jit(solution)/shard_map/ppermute | solution.py:490
  88.9 9.8 %collective-permute-start.29 = (bf16[2,256,384]{2,1,0:T(8,128)(2,1)S(1)}, bf16[2,256,384]{2,1,0:T(8,128)(2,1)S(1)}, u32[]{:S(2)}, u32[]{:S(2)}) collective-permute-start(bf16[2,256,384]{2,1,0:T(8,128)(2,1)S(1)} %get-tuple-element.132), channel_id=1, source_target_pairs={{0,8},{1,33},{2,10},{3,35},{4,12},{5,37},{6,14},{7,39},{8,16},{9,4... | collective-permute-start | bytes 1179656 | tf_op jit(solution)/shard_map/ppermute | solution.py:434
  94.5 5.5 %collective-permute-start.28 = (bf16[4,3,32,384]{3,2,1,0:T(8,128)(2,1)S(1)}, bf16[4,3,32,384]{3,2,1,0:T(8,128)(2,1)S(1)}, u32[]{:S(2)}, u32[]{:S(2)}) collective-permute-start(bf16[4,3,32,384]{3,2,1,0:T(8,128)(2,1)S(1)} %shard_map.121), channel_id=1, source_target_pairs={{0,1},{1,0},{2,3},{3,2},{4,5},{5,4},{6,7},{7,6},{8,9},{9,8},{10,11... | collective-permute-start | bytes 884744 | tf_op jit(solution)/shard_map/ppermute | solution.py:492

commit v8 on v7

--- a/solution.py
+++ b/solution.py
@@ -476,21 +476,21 @@
 
         far, sums = grads_call(curs[3:], hists[3:], queries, stats, tiles(3), whole=(0,))
         far = to_key(far[0], 2)
-        (near_m, near_cur, near_hist), sums = grads_call(
-            curs[1:3], hists[1:3], queries, stats, tiles(1, 2), sums[0], whole=(0,)
+        (near_cur, near_hist, near_p), sums = grads_call(
+            curs[1:3], hists[1:3], queries, stats, tiles(1, 2), sums[0], whole=(1,)
         )
-        near_m, near_cur = to_key(near_m, OFFSETS[1]), to_key(near_cur, OFFSETS[2])
+        near_cur, near_p = to_key(near_cur, OFFSETS[1]), to_key(near_p, OFFSETS[2])
         own, sums = grads_call(curs[:1], hists[:1], queries, stats, tiles(0), sums[0], True)
         sums, far = lax.optimization_barrier((sums, far))
         query_parts = [sums[0]] + [to_query(sums[i], OFFSETS[i]) for i in range(1, 4)]
 
-        back = add_call(query_parts, [own[0], far, near_m, near_cur], sizes[2])
+        back = add_call(query_parts, [own[0], far, near_cur, near_p], sizes[2])
         back, near_hist = lax.optimization_barrier((back, near_hist))
-        near_hist = to_key(near_hist, OFFSETS[2])
+        near_hist = to_key(near_hist, OFFSETS[1])
         moved = [lax.ppermute(p, AXES, chip_move(-d)) for p, d in zip(back[1:], X_STEPS[1:])]
         back = back[:1] + moved
         other = lax.ppermute(other_call(back), AXES, core_move())
-        return tuple(finish_call(back, other, sizes, [own[1], near_hist], [far, near_m]))
+        return tuple(finish_call(back, other, sizes, [own[1], near_hist], [far, near_p]))
 
     return shards
 

time: 102 us -> 102 us (level); the launches traced: 101 us -> 102 us
    ppermute x10, starting transfers between devices: 13.7 us -> 15.1 us  [to_key(): return lax.ppermute(value, AXES, key_move(step))]
    ppermute x3, starting transfers between devices: 5.66 us -> 4.31 us  [shards(): lax.ppermute(p, AXES, chip_move(-d))]
where the time goes in v8:
time: 102 us
  starting transfers between devices  41.9 us (41%)
  waiting for transfers between devices  30.6 us (30%)
  Pallas kernels  27.3 us (27%)
  between operations  1.44 us (1%)
    pallas_call x12, Pallas kernels, call(): pl.pallas_call(kernel, out_shape=outs, in_specs=[VMEM] * len(args), out_s...  24.9 us
    ppermute x10, starting transfers between devices, to_key(): return lax.ppermute(value, AXES, key_move(step))  15.1 us
    ppermute x10, waiting for transfers between devices, to_key(): return lax.ppermute(value, AXES, key_move(step))  10.2 us
    ppermute x9, starting transfers between devices, to_query(): return lax.ppermute(value, AXES, query_move(step))  8.9 us
    ppermute x9, waiting for transfers between devices, to_query(): return lax.ppermute(value, AXES, query_move(step))  7.93 us
    ppermute x6, waiting for transfers between devices, exchange(): lax.ppermute(p, AXES, chip_move(d))  7.55 us
    ppermute x6, starting transfers between devices, exchange(): lax.ppermute(p, AXES, chip_move(d))  7.28 us
    ppermute x1, starting transfers between devices, shards(): other = lax.ppermute(other_call(back), AXES, core_move())  4.81 us
  transfers between devices with their start and end apart: 30, of which 15 were waited for; matrix products, arithmetic and copies ran while one was open for 0% of the time, Pallas kernels for 17%

profile of v8, /device:TPU:1, one launch (start us, length us, event | category | flops | bytes accessed | tf_op | source)
XLA Modules:
  0.0 102.3 jit_solution(2439202396046113181)
XLA Ops:
  1.3 2.4 %shard_map.110 = (bf16[2,4,2,32,384]{4,3,2,1,0:T(8,128)(2,1)}, bf16[2,4,2,32,384]{4,3,2,1,0:T(8,128)(2,1)}, bf16[528,384]{1,0:T(8,128)(2,1)}) custom-call(bf16[32,3072]{1,0:T(8,128)(2,1)} %refs_0_.1, bf16[32,3072]{1,0:T(8,128)(2,1)} %refs_1_.1, bf16[32,3072]{1,0:T(8,128)(2,1)} %refs_2_.1, bf16[32,3072]{1,0:T(8,128)(2,1)} %refs_3_.1, ...), custom_call_target="tpu_custom_call" | custom-call | tf_op jit(solution)/shard_map/pallas_call | solution.py:302
  3.7 1.5 %collective-permute-start = (bf16[2,4,2,32,384]{4,3,2,1,0:T(8,128)(2,1)}, bf16[2,4,2,32,384]{4,3,2,1,0:T(8,128)(2,1)S(1)}, u32[]{:S(2)}, u32[]{:S(2)}) collective-permute-start(bf16[2,4,2,32,384]{4,3,2,1,0:T(8,128)(2,1)} %get-tuple-element.70), channel_id=1, source_target_pairs={{0,1},{1,0},{2,3},{3,2},{4,5},{5,4},{6,7},{7,6},{8,9},{9,8},{10,11... | collective-permute-start | bytes 1179656 | tf_op jit(solution)/shard_map/ppermute | solution.py:443
  5.2 3.8 %collective-permute-start.2 = (bf16[528,384]{1,0:T(8,128)(2,1)}, bf16[528,384]{1,0:T(8,128)(2,1)S(1)}, u32[]{:S(2)}, u32[]{:S(2)}) collective-permute-start(bf16[528,384]{1,0:T(8,128)(2,1)} %get-tuple-element.75.refs_1_), channel_id=1, source_target_pairs={{0,24},{1,97},{2,26},{3,99},{4,28},{5,101},{6,30},{7,103},{8,0},{9... | collective-permute-start | bytes 1216520 | tf_op jit(solution)/shard_map/ppermute | solution.py:434
  11.4 1.5 %collective-permute-start.7 = (bf16[2,64,384]{2,1,0:T(8,128)(2,1)S(1)}, bf16[2,64,384]{2,1,0:T(8,128)(2,1)S(1)}, u32[]{:S(2)}, u32[]{:S(2)}) collective-permute-start(bf16[2,64,384]{2,1,0:T(8,128)(2,1)S(1)} %get-tuple-element.82), channel_id=1, source_target_pairs={{0,6},{1,7},{2,0},{3,1},{4,2},{5,3},{6,4},{7,5},{8,14},{9,15},{10,... | collective-permute-start | bytes 294920 | tf_op jit(solution)/shard_map/ppermute | solution.py:450
  12.9 1.5 %collective-permute-start.8 = (bf16[2,64,384]{2,1,0:T(8,128)(2,1)S(1)}, bf16[2,64,384]{2,1,0:T(8,128)(2,1)S(1)}, u32[]{:S(2)}, u32[]{:S(2)}) collective-permute-start(bf16[2,64,384]{2,1,0:T(8,128)(2,1)S(1)} %get-tuple-element.83), channel_id=1, source_target_pairs={{0,4},{1,5},{2,6},{3,7},{4,0},{5,1},{6,2},{7,3},{8,12},{9,13},{10,... | collective-permute-start | bytes 294920 | tf_op jit(solution)/shard_map/ppermute | solution.py:450
  14.4 1.6 %collective-permute-done.6.refs_1_ = bf16[2,64,384]{2,1,0:T(8,128)(2,1)S(1)} collective-permute-done((bf16[2,64,384]{2,1,0:T(8,128)(2,1)S(1)}, bf16[2,64,384]{2,1,0:T(8,128)(2,1)S(1)}, u32[]{:S(2)}, u32[]{:S(2)}) %collective-permute-start.6) | collective-permute-done | bytes 98336 | tf_op jit(solution)/shard_map/ppermute | solution.py:450
  16.3 2.7 %collective-permute-done.8.refs_3_ = bf16[2,64,384]{2,1,0:T(8,128)(2,1)S(1)} collective-permute-done((bf16[2,64,384]{2,1,0:T(8,128)(2,1)S(1)}, bf16[2,64,384]{2,1,0:T(8,128)(2,1)S(1)}, u32[]{:S(2)}, u32[]{:S(2)}) %collective-permute-start.8) | collective-permute-done | bytes 98336 | tf_op jit(solution)/shard_map/ppermute | solution.py:450
  19.0 2.3 %collective-permute-start.11 = (bf16[2,256,384]{2,1,0:T(8,128)(2,1)S(1)}, bf16[2,256,384]{2,1,0:T(8,128)(2,1)S(1)}, u32[]{:S(2)}, u32[]{:S(2)}) collective-permute-start(bf16[2,256,384]{2,1,0:T(8,128)(2,1)S(1)} %shard_map.113.refs_5_.refs_3_.refs_2_.refs_4_), channel_id=1, source_target_pairs={{0,64},{1,17},{2,66},{3,19},{4,68},{5,21},{6,70},{7,23},{8,72},{9,... | collective-permute-start | bytes 1179656 | tf_op jit(solution)/shard_map/ppermute | solution.py:437
  22.3 1.7 %collective-permute-start.4 = (bf16[2,64,384]{2,1,0:T(8,128)(2,1)S(1)}, bf16[2,64,384]{2,1,0:T(8,128)(2,1)S(1)}, u32[]{:S(2)}, u32[]{:S(2)}) collective-permute-start(bf16[2,64,384]{2,1,0:T(8,128)(2,1)S(1)} %get-tuple-element.78), channel_id=1, source_target_pairs={{0,6},{1,7},{2,0},{3,1},{4,2},{5,3},{6,4},{7,5},{8,14},{9,15},{10,... | collective-permute-start | bytes 294920 | tf_op jit(solution)/shard_map/ppermute | solution.py:450
  24.3 2.0 %collective-permute-done.3.refs_1_ = bf16[2,64,384]{2,1,0:T(8,128)(2,1)S(1)} collective-permute-done((bf16[2,64,384]{2,1,0:T(8,128)(2,1)S(1)}, bf16[2,64,384]{2,1,0:T(8,128)(2,1)S(1)}, u32[]{:S(2)}, u32[]{:S(2)}) %collective-permute-start.3) | collective-permute-done | bytes 98336 | tf_op jit(solution)/shard_map/ppermute | solution.py:450
  27.8 1.3 %collective-permute-done.5.refs_3_ = bf16[2,64,384]{2,1,0:T(8,128)(2,1)S(1)} collective-permute-done((bf16[2,64,384]{2,1,0:T(8,128)(2,1)S(1)}, bf16[2,64,384]{2,1,0:T(8,128)(2,1)S(1)}, u32[]{:S(2)}, u32[]{:S(2)}) %collective-permute-start.5) | collective-permute-done | bytes 98336 | tf_op jit(solution)/shard_map/ppermute | solution.py:450
  29.1 1.4 %collective-permute-start.14 = (bf16[2,256,384]{2,1,0:T(8,128)(2,1)S(1)}, bf16[2,256,384]{2,1,0:T(8,128)(2,1)S(1)}, u32[]{:S(2)}, u32[]{:S(2)}) collective-permute-start(bf16[2,256,384]{2,1,0:T(8,128)(2,1)S(1)} %shard_map.112.refs_0_), channel_id=1, source_target_pairs={{0,16},{1,65},{2,18},{3,67},{4,20},{5,69},{6,22},{7,71},{8,24},{9,... | collective-permute-start | bytes 1179656 | tf_op jit(solution)/shard_map/ppermute | solution.py:434
  30.5 3.0 %collective-permute-start.13 = (bf16[2,256,384]{2,1,0:T(8,128)(2,1)S(1)}, bf16[2,256,384]{2,1,0:T(8,128)(2,1)S(1)}, u32[]{:S(2)}, u32[]{:S(2)}) collective-permute-start(bf16[2,256,384]{2,1,0:T(8,128)(2,1)S(1)} %shard_map.112.refs_0_), channel_id=1, source_target_pairs={{0,24},{1,97},{2,26},{3,99},{4,28},{5,101},{6,30},{7,103},{8,0},{9... | collective-permute-start | bytes 1179656 | tf_op jit(solution)/shard_map/ppermute | solution.py:434
  34.1 3.4 %shard_map.114 = (f32[3,16,256]{2,1,0:T(8,128)S(1)}, f32[3,256,512]{2,1,0:T(8,128)S(1)}, f32[3,256,512]{2,1,0:T(8,128)S(1)}, f32[3,256,512]{2,1,0:T(8,128)S(1)},...) custom-call(bf16[2,256,384]{2,1,0:T(8,128)(2,1)S(1)} %shard_map.112.refs_0_, ...), custom_call_target="tpu_custom_call" | custom-call | flops 31457280 | bytes 43776 | tf_op jit(solution)/shard_map/pallas_call | solution.py:36
  37.5 3.4 %shard_map.115 = (f32[3,16,256]{2,1,0:T(8,128)S(1)}, f32[3,256,512]{2,1,0:T(8,128)S(1)}, f32[3,256,512]{2,1,0:T(8,128)S(1)}, f32[3,256,512]{2,1,0:T(8,128)S(1)},...) custom-call(bf16[2,256,384]{2,1,0:T(8,128)(2,1)S(1)} %shard_map.112.refs_0_, ...), custom_call_target="tpu_custom_call" | custom-call | flops 31457280 | bytes 44544 | tf_op jit(solution)/shard_map/pallas_call | solution.py:36
  41.0 4.7 %collective-permute-done.13.refs_1_ = bf16[2,256,384]{2,1,0:T(8,128)(2,1)S(1)} collective-permute-done((bf16[2,256,384]{2,1,0:T(8,128)(2,1)S(1)}, bf16[2,256,384]{2,1,0:T(8,128)(2,1)S(1)}, u32[]{:S(2)}, u32[]{:S(2)}) %collective-permute-start.13) | collective-permute-done | bytes 393248 | tf_op jit(solution)/shard_map/ppermute | solution.py:434
  45.8 3.4 %shard_map.116 = (f32[3,16,256]{2,1,0:T(8,128)S(1)}, f32[3,256,1024]{2,1,0:T(8,128)S(1)}, f32[3,256,1024]{2,1,0:T(8,128)S(1)}, f32[3,256,1024]{2,1,0:T(8,128)S(1...) custom-call(bf16[2,256,384]{2,1,0:T(8,128)(2,1)S(1)} %collective-permute-done.12.refs_0_, ...), custom_call_target="tpu_custom_call" | custom-call | flops 37748736 | bytes 43776 | tf_op jit(solution)/shard_map/pallas_call | solution.py:36
  49.2 1.9 %collective-permute-start.18 = (f32[3,16,256]{2,1,0:T(8,128)S(1)}, f32[3,16,256]{2,1,0:T(8,128)S(1)}, u32[]{:S(2)}, u32[]{:S(2)}) collective-permute-start(f32[3,16,256]{2,1,0:T(8,128)S(1)} %get-tuple-element.88.refs_6_.refs_8_), channel_id=1, source_target_pairs={{0,64},{1,17},{2,66},{3,19},{4,68},{5,21},{6,70},{7,23},{8,72},{9,... | collective-permute-start | bytes 147464 | tf_op jit(solution)/shard_map/ppermute | solution.py:437
  51.0 1.7 %collective-permute-start.17 = (f32[3,16,256]{2,1,0:T(8,128)S(1)}, f32[3,16,256]{2,1,0:T(8,128)S(1)}, u32[]{:S(2)}, u32[]{:S(2)}) collective-permute-start(f32[3,16,256]{2,1,0:T(8,128)S(1)} %get-tuple-element.88.refs_6_.refs_8_), channel_id=1, source_target_pairs={{0,96},{1,25},{2,98},{3,27},{4,100},{5,29},{6,102},{7,31},{8,104},... | collective-permute-start | bytes 147464 | tf_op jit(solution)/shard_map/ppermute | solution.py:437
  54.0 3.0 %collective-permute-done.16.refs_7_.refs_9_ = f32[3,16,256]{2,1,0:T(8,128)S(1)} collective-permute-done((f32[3,16,256]{2,1,0:T(8,128)S(1)}, f32[3,16,256]{2,1,0:T(8,128)S(1)}, u32[]{:S(2)}, u32[]{:S(2)}) %collective-permute-start.16) | collective-permute-done | bytes 49184 | tf_op jit(solution)/shard_map/ppermute | solution.py:437
  57.0 2.9 %shard_map.117 = (bf16[4,256,384]{2,1,0:T(8,128)(2,1)S(1)}, f32[3,128,1024]{2,1,0:T(8,128)S(1)}) custom-call(bf16[2,256,384]{2,1,0:T(8,128)(2,1)S(1)} %collective-permute-done.14.refs_2_.refs_0_, bf16[528,384]{1,0:T(8,128)(2,1)S(1)} %collective-permute-done.15.refs_4_.refs_1_, bf16[2,256,384]{2,1,0:T(8,128)(2,1)S(1)} %shard_map.113.refs_5_.refs_3_.refs_2_.refs_4_, ...), custom_call_target="tpu_custom_call" | custom-call | flops 62914560 | bytes 236736 | tf_op jit(solution)/shard_map/pallas_call | solution.py:36
  59.9 1.6 %collective-permute-start.19 = (bf16[4,256,384]{2,1,0:T(8,128)(2,1)S(1)}, bf16[4,256,384]{2,1,0:T(8,128)(2,1)S(1)}, u32[]{:S(2)}, u32[]{:S(2)}) collective-permute-start(bf16[4,256,384]{2,1,0:T(8,128)(2,1)S(1)} %get-tuple-element.113), channel_id=1, source_target_pairs={{0,16},{1,65},{2,18},{3,67},{4,20},{5,69},{6,22},{7,71},{8,24},{9,... | collective-permute-start | bytes 2359304 | tf_op jit(solution)/shard_map/ppermute | solution.py:434
  61.5 7.1 %shard_map.118 = (bf16[2,256,384]{2,1,0:T(8,128)(2,1)S(1)}, bf16[2,256,384]{2,1,0:T(8,128)(2,1)S(1)}, bf16[4,256,384]{2,1,0:T(8,128)(2,1)S(1)}, f32[3,128,1024]{2,1,0:T(8,128)S(1)}) custom-call(bf16[2,256,384]{2,1,0:T(8,128)(2,1)S(1)} %collective-permute-done.12.refs_0_, bf16[2,256,384]{2,1,0:T(8,128)(2,1)S(1)} %collective-permute-done.13.refs_1_, ...), custom_call_target="tpu_custom_call" | custom-call | flops 125829120 | bytes 273792 | tf_op jit(solution)/shard_map/pallas_call | solution.py:36
  68.7 2.7 %collective-permute-start.23 = (bf16[2,256,384]{2,1,0:T(8,128)(2,1)S(1)}, bf16[2,256,384]{2,1,0:T(8,128)(2,1)S(1)}, u32[]{:S(2)}, u32[]{:S(2)}) collective-permute-start(bf16[2,256,384]{2,1,0:T(8,128)(2,1)S(1)} %get-tuple-element.120), channel_id=1, source_target_pairs={{0,24},{1,97},{2,26},{3,99},{4,28},{5,101},{6,30},{7,103},{8,0},{9... | collective-permute-start | bytes 1179656 | tf_op jit(solution)/shard_map/ppermute | solution.py:434
  71.4 3.0 %shard_map.119 = (bf16[2,256,384]{2,1,0:T(8,128)(2,1)S(1)}, bf16[2,256,384]{2,1,0:T(8,128)(2,1)S(1)}, bf16[256,384]{1,0:T(8,128)(2,1)S(1)}, bf16[256,384]{1,0:T(...) custom-call(bf16[2,256,384]{2,1,0:T(8,128)(2,1)S(1)} %shard_map.112.refs_0_, ...), custom_call_target="tpu_custom_call" | custom-call | flops 62914560 | bytes 261312 | tf_op jit(solution)/shard_map/pallas_call | solution.py:36
  74.5 1.5 %collective-permute-start.21 = (bf16[256,384]{1,0:T(8,128)(2,1)S(1)}, bf16[256,384]{1,0:T(8,128)(2,1)S(1)}, u32[]{:S(2)}, u32[]{:S(2)}) collective-permute-start(bf16[256,384]{1,0:T(8,128)(2,1)S(1)} %get-tuple-element.116), channel_id=1, source_target_pairs={{0,32},{1,9},{2,34},{3,11},{4,36},{5,13},{6,38},{7,15},{8,40},{9,1... | collective-permute-start | bytes 589832 | tf_op jit(solution)/shard_map/ppermute | solution.py:437
  76.1 5.2 %collective-permute-done.24.refs_7_.refs_8_ = bf16[4,256,384]{2,1,0:T(8,128)(2,1)S(1)} collective-permute-done((bf16[4,256,384]{2,1,0:T(8,128)(2,1)S(1)}, bf16[4,256,384]{2,1,0:T(8,128)(2,1)S(1)}, u32[]{:S(2)}, u32[]{:S(2)}) %collective-permute-start.24) | collective-permute-done | bytes 786464 | tf_op jit(solution)/shard_map/ppermute | solution.py:434
  81.3 3.5 %collective-permute-done.21.refs_2_ = bf16[256,384]{1,0:T(8,128)(2,1)S(1)} collective-permute-done((bf16[256,384]{1,0:T(8,128)(2,1)S(1)}, bf16[256,384]{1,0:T(8,128)(2,1)S(1)}, u32[]{:S(2)}, u32[]{:S(2)}) %collective-permute-start.21) | collective-permute-done | bytes 196640 | tf_op jit(solution)/shard_map/ppermute | solution.py:437
  85.3 3.0 %collective-permute-start.25 = (bf16[3,64,384]{2,1,0:T(8,128)(2,1)S(1)}, bf16[3,64,384]{2,1,0:T(8,128)(2,1)S(1)}, u32[]{:S(2)}, u32[]{:S(2)}) collective-permute-start(bf16[3,64,384]{2,1,0:T(8,128)(2,1)S(1)} %get-tuple-element.128), channel_id=1, source_target_pairs={{0,6},{1,7},{2,0},{3,1},{4,2},{5,3},{6,4},{7,5},{8,14},{9,15},{10,... | collective-permute-start | bytes 442376 | tf_op jit(solution)/shard_map/ppermute | solution.py:490
  89.6 1.8 %collective-permute-start.29 = (bf16[2,256,384]{2,1,0:T(8,128)(2,1)S(1)}, bf16[2,256,384]{2,1,0:T(8,128)(2,1)S(1)}, u32[]{:S(2)}, u32[]{:S(2)}) collective-permute-start(bf16[2,256,384]{2,1,0:T(8,128)(2,1)S(1)} %get-tuple-element.132), channel_id=1, source_target_pairs={{0,24},{1,97},{2,26},{3,99},{4,28},{5,101},{6,30},{7,103},{8,0},{9... | collective-permute-start | bytes 1179656 | tf_op jit(solution)/shard_map/ppermute | solution.py:434
  91.3 3.7 %collective-permute-done.26.refs_2_ = bf16[3,64,384]{2,1,0:T(8,128)(2,1)S(1)} collective-permute-done((bf16[3,64,384]{2,1,0:T(8,128)(2,1)S(1)}, bf16[3,64,384]{2,1,0:T(8,128)(2,1)S(1)}, u32[]{:S(2)}, u32[]{:S(2)}) %collective-permute-start.26) | collective-permute-done | bytes 147488 | tf_op jit(solution)/shard_map/ppermute | solution.py:490
  95.1 4.8 %collective-permute-start.28 = (bf16[4,3,32,384]{3,2,1,0:T(8,128)(2,1)S(1)}, bf16[4,3,32,384]{3,2,1,0:T(8,128)(2,1)S(1)}, u32[]{:S(2)}, u32[]{:S(2)}) collective-permute-start(bf16[4,3,32,384]{3,2,1,0:T(8,128)(2,1)S(1)} %shard_map.121), channel_id=1, source_target_pairs={{0,1},{1,0},{2,3},{3,2},{4,5},{5,4},{6,7},{7,6},{8,9},{9,8},{10,11... | collective-permute-start | bytes 884744 | tf_op jit(solution)/shard_map/ppermute | solution.py:492
  (45 shorter events, 11.9 us)
Async XLA Ops:
  3.7 30.4 %copy-start = (bf16[528,384]{1,0:T(8,128)(2,1)S(1)}, bf16[528,384]{1,0:T(8,128)(2,1)}, u32[]{:S(2)}) copy-start(bf16[528,384]{1,0:T(8,128)(2,1)} %get-tuple-element.75.refs_1_) | copy-start | bytes 1216516
  3.7 5.3 %collective-permute-start = (bf16[2,4,2,32,384]{4,3,2,1,0:T(8,128)(2,1)}, bf16[2,4,2,32,384]{4,3,2,1,0:T(8,128)(2,1)S(1)}, u32[]{:S(2)}, u32[]{:S(2)}) collective-permute-start(bf16[2,4,2,32,384]{4,3,2,1,0:T(8,128)(2,1)} %get-tuple-element.70), channel_id=1, source_target_pairs={{0,1},{1,0},{2,3},{3,2},{4,5},{5,4},{6,7},{7,6},{8,9},{9,8},{10,11... | collective-permute-start | bytes 1179656 | tf_op jit(solution)/shard_map/ppermute | solution.py:443
  5.2 16.1 %collective-permute-start.2 = (bf16[528,384]{1,0:T(8,128)(2,1)}, bf16[528,384]{1,0:T(8,128)(2,1)S(1)}, u32[]{:S(2)}, u32[]{:S(2)}) collective-permute-start(bf16[528,384]{1,0:T(8,128)(2,1)} %get-tuple-element.75.refs_1_), channel_id=1, source_target_pairs={{0,24},{1,97},{2,26},{3,99},{4,28},{5,101},{6,30},{7,103},{8,0},{9... | collective-permute-start | bytes 1216520 | tf_op jit(solution)/shard_map/ppermute | solution.py:434
  9.1 12.3 %collective-permute-start.1 = (bf16[528,384]{1,0:T(8,128)(2,1)}, bf16[528,384]{1,0:T(8,128)(2,1)S(1)}, u32[]{:S(2)}, u32[]{:S(2)}) collective-permute-start(bf16[528,384]{1,0:T(8,128)(2,1)} %get-tuple-element.75.refs_1_), channel_id=1, source_target_pairs={{0,8},{1,33},{2,10},{3,35},{4,12},{5,37},{6,14},{7,39},{8,16},{9,4... | collective-permute-start | bytes 1216520 | tf_op jit(solution)/shard_map/ppermute | solution.py:434
  9.1 1.0 copy-start.1
  10.2 5.9 %collective-permute-start.6 = (bf16[2,64,384]{2,1,0:T(8,128)(2,1)S(1)}, bf16[2,64,384]{2,1,0:T(8,128)(2,1)S(1)}, u32[]{:S(2)}, u32[]{:S(2)}) collective-permute-start(bf16[2,64,384]{2,1,0:T(8,128)(2,1)S(1)} %get-tuple-element.81), channel_id=1, source_target_pairs={{0,2},{1,3},{2,4},{3,5},{4,6},{5,7},{6,0},{7,1},{8,10},{9,11},{10,... | collective-permute-start | bytes 294920 | tf_op jit(solution)/shard_map/ppermute | solution.py:450
  11.4 4.9 %collective-permute-start.7 = (bf16[2,64,384]{2,1,0:T(8,128)(2,1)S(1)}, bf16[2,64,384]{2,1,0:T(8,128)(2,1)S(1)}, u32[]{:S(2)}, u32[]{:S(2)}) collective-permute-start(bf16[2,64,384]{2,1,0:T(8,128)(2,1)S(1)} %get-tuple-element.82), channel_id=1, source_target_pairs={{0,6},{1,7},{2,0},{3,1},{4,2},{5,3},{6,4},{7,5},{8,14},{9,15},{10,... | collective-permute-start | bytes 294920 | tf_op jit(solution)/shard_map/ppermute | solution.py:450
  12.9 6.1 %collective-permute-start.8 = (bf16[2,64,384]{2,1,0:T(8,128)(2,1)S(1)}, bf16[2,64,384]{2,1,0:T(8,128)(2,1)S(1)}, u32[]{:S(2)}, u32[]{:S(2)}) collective-permute-start(bf16[2,64,384]{2,1,0:T(8,128)(2,1)S(1)} %get-tuple-element.83), channel_id=1, source_target_pairs={{0,4},{1,5},{2,6},{3,7},{4,0},{5,1},{6,2},{7,3},{8,12},{9,13},{10,... | collective-permute-start | bytes 294920 | tf_op jit(solution)/shard_map/ppermute | solution.py:450
  16.0 14.4 %collective-permute-start.15 = (bf16[528,384]{1,0:T(8,128)(2,1)}, bf16[528,384]{1,0:T(8,128)(2,1)S(1)}, u32[]{:S(2)}, u32[]{:S(2)}) collective-permute-start(bf16[528,384]{1,0:T(8,128)(2,1)} %get-tuple-element.75.refs_1_), channel_id=1, source_target_pairs={{0,16},{1,65},{2,18},{3,67},{4,20},{5,69},{6,22},{7,71},{8,24},{9,... | collective-permute-start | bytes 1216520 | tf_op jit(solution)/shard_map/ppermute | solution.py:434
  19.0 14.5 %collective-permute-start.11 = (bf16[2,256,384]{2,1,0:T(8,128)(2,1)S(1)}, bf16[2,256,384]{2,1,0:T(8,128)(2,1)S(1)}, u32[]{:S(2)}, u32[]{:S(2)}) collective-permute-start(bf16[2,256,384]{2,1,0:T(8,128)(2,1)S(1)} %shard_map.113.refs_5_.refs_3_.refs_2_.refs_4_), channel_id=1, source_target_pairs={{0,64},{1,17},{2,66},{3,19},{4,68},{5,21},{6,70},{7,23},{8,72},{9,... | collective-permute-start | bytes 1179656 | tf_op jit(solution)/shard_map/ppermute | solution.py:437
  21.3 5.0 %collective-permute-start.3 = (bf16[2,64,384]{2,1,0:T(8,128)(2,1)S(1)}, bf16[2,64,384]{2,1,0:T(8,128)(2,1)S(1)}, u32[]{:S(2)}, u32[]{:S(2)}) collective-permute-start(bf16[2,64,384]{2,1,0:T(8,128)(2,1)S(1)} %get-tuple-element.77), channel_id=1, source_target_pairs={{0,2},{1,3},{2,4},{3,5},{4,6},{5,7},{6,0},{7,1},{8,10},{9,11},{10,... | collective-permute-start | bytes 294920 | tf_op jit(solution)/shard_map/ppermute | solution.py:450
  22.3 4.8 %collective-permute-start.4 = (bf16[2,64,384]{2,1,0:T(8,128)(2,1)S(1)}, bf16[2,64,384]{2,1,0:T(8,128)(2,1)S(1)}, u32[]{:S(2)}, u32[]{:S(2)}) collective-permute-start(bf16[2,64,384]{2,1,0:T(8,128)(2,1)S(1)} %get-tuple-element.78), channel_id=1, source_target_pairs={{0,6},{1,7},{2,0},{3,1},{4,2},{5,3},{6,4},{7,5},{8,14},{9,15},{10,... | collective-permute-start | bytes 294920 | tf_op jit(solution)/shard_map/ppermute | solution.py:450
  24.0 5.1 %collective-permute-start.5 = (bf16[2,64,384]{2,1,0:T(8,128)(2,1)S(1)}, bf16[2,64,384]{2,1,0:T(8,128)(2,1)S(1)}, u32[]{:S(2)}, u32[]{:S(2)}) collective-permute-start(bf16[2,64,384]{2,1,0:T(8,128)(2,1)S(1)} %get-tuple-element.79), channel_id=1, source_target_pairs={{0,4},{1,5},{2,6},{3,7},{4,0},{5,1},{6,2},{7,3},{8,12},{9,13},{10,... | collective-permute-start | bytes 294920 | tf_op jit(solution)/shard_map/ppermute | solution.py:450
  26.3 11.2 %collective-permute-start.10 = (bf16[2,256,384]{2,1,0:T(8,128)(2,1)S(1)}, bf16[2,256,384]{2,1,0:T(8,128)(2,1)S(1)}, u32[]{:S(2)}, u32[]{:S(2)}) collective-permute-start(bf16[2,256,384]{2,1,0:T(8,128)(2,1)S(1)} %shard_map.113.refs_5_.refs_3_.refs_2_.refs_4_), channel_id=1, source_target_pairs={{0,96},{1,25},{2,98},{3,27},{4,100},{5,29},{6,102},{7,31},{8,104},... | collective-permute-start | bytes 1179656 | tf_op jit(solution)/shard_map/ppermute | solution.py:437
  27.1 10.4 %collective-permute-start.9 = (bf16[2,256,384]{2,1,0:T(8,128)(2,1)S(1)}, bf16[2,256,384]{2,1,0:T(8,128)(2,1)S(1)}, u32[]{:S(2)}, u32[]{:S(2)}) collective-permute-start(bf16[2,256,384]{2,1,0:T(8,128)(2,1)S(1)} %shard_map.113.refs_5_.refs_3_.refs_2_.refs_4_), channel_id=1, source_target_pairs={{0,32},{1,9},{2,34},{3,11},{4,36},{5,13},{6,38},{7,15},{8,40},{9,1... | collective-permute-start | bytes 1179656 | tf_op jit(solution)/shard_map/ppermute | solution.py:437
  29.1 11.9 %collective-permute-start.14 = (bf16[2,256,384]{2,1,0:T(8,128)(2,1)S(1)}, bf16[2,256,384]{2,1,0:T(8,128)(2,1)S(1)}, u32[]{:S(2)}, u32[]{:S(2)}) collective-permute-start(bf16[2,256,384]{2,1,0:T(8,128)(2,1)S(1)} %shard_map.112.refs_0_), channel_id=1, source_target_pairs={{0,16},{1,65},{2,18},{3,67},{4,20},{5,69},{6,22},{7,71},{8,24},{9,... | collective-permute-start | bytes 1179656 | tf_op jit(solution)/shard_map/ppermute | solution.py:434
  30.5 15.2 %collective-permute-start.13 = (bf16[2,256,384]{2,1,0:T(8,128)(2,1)S(1)}, bf16[2,256,384]{2,1,0:T(8,128)(2,1)S(1)}, u32[]{:S(2)}, u32[]{:S(2)}) collective-permute-start(bf16[2,256,384]{2,1,0:T(8,128)(2,1)S(1)} %shard_map.112.refs_0_), channel_id=1, source_target_pairs={{0,24},{1,97},{2,26},{3,99},{4,28},{5,101},{6,30},{7,103},{8,0},{9... | collective-permute-start | bytes 1179656 | tf_op jit(solution)/shard_map/ppermute | solution.py:434
  33.5 12.3 %collective-permute-start.12 = (bf16[2,256,384]{2,1,0:T(8,128)(2,1)S(1)}, bf16[2,256,384]{2,1,0:T(8,128)(2,1)S(1)}, u32[]{:S(2)}, u32[]{:S(2)}) collective-permute-start(bf16[2,256,384]{2,1,0:T(8,128)(2,1)S(1)} %shard_map.112.refs_0_), channel_id=1, source_target_pairs={{0,8},{1,33},{2,10},{3,35},{4,12},{5,37},{6,14},{7,39},{8,16},{9,4... | collective-permute-start | bytes 1179656 | tf_op jit(solution)/shard_map/ppermute | solution.py:434
  49.2 4.5 %collective-permute-start.18 = (f32[3,16,256]{2,1,0:T(8,128)S(1)}, f32[3,16,256]{2,1,0:T(8,128)S(1)}, u32[]{:S(2)}, u32[]{:S(2)}) collective-permute-start(f32[3,16,256]{2,1,0:T(8,128)S(1)} %get-tuple-element.88.refs_6_.refs_8_), channel_id=1, source_target_pairs={{0,64},{1,17},{2,66},{3,19},{4,68},{5,21},{6,70},{7,23},{8,72},{9,... | collective-permute-start | bytes 147464 | tf_op jit(solution)/shard_map/ppermute | solution.py:437
  51.0 2.9 %collective-permute-start.17 = (f32[3,16,256]{2,1,0:T(8,128)S(1)}, f32[3,16,256]{2,1,0:T(8,128)S(1)}, u32[]{:S(2)}, u32[]{:S(2)}) collective-permute-start(f32[3,16,256]{2,1,0:T(8,128)S(1)} %get-tuple-element.88.refs_6_.refs_8_), channel_id=1, source_target_pairs={{0,96},{1,25},{2,98},{3,27},{4,100},{5,29},{6,102},{7,31},{8,104},... | collective-permute-start | bytes 147464 | tf_op jit(solution)/shard_map/ppermute | solution.py:437
  52.7 4.2 %collective-permute-start.16 = (f32[3,16,256]{2,1,0:T(8,128)S(1)}, f32[3,16,256]{2,1,0:T(8,128)S(1)}, u32[]{:S(2)}, u32[]{:S(2)}) collective-permute-start(f32[3,16,256]{2,1,0:T(8,128)S(1)} %get-tuple-element.88.refs_6_.refs_8_), channel_id=1, source_target_pairs={{0,32},{1,9},{2,34},{3,11},{4,36},{5,13},{6,38},{7,15},{8,40},{9,1... | collective-permute-start | bytes 147464 | tf_op jit(solution)/shard_map/ppermute | solution.py:437
  59.9 14.5 %collective-permute-start.19 = (bf16[4,256,384]{2,1,0:T(8,128)(2,1)S(1)}, bf16[4,256,384]{2,1,0:T(8,128)(2,1)S(1)}, u32[]{:S(2)}, u32[]{:S(2)}) collective-permute-start(bf16[4,256,384]{2,1,0:T(8,128)(2,1)S(1)} %get-tuple-element.113), channel_id=1, source_target_pairs={{0,16},{1,65},{2,18},{3,67},{4,20},{5,69},{6,22},{7,71},{8,24},{9,... | collective-permute-start | bytes 2359304 | tf_op jit(solution)/shard_map/ppermute | solution.py:434
  68.6 12.6 %collective-permute-start.24 = (bf16[4,256,384]{2,1,0:T(8,128)(2,1)S(1)}, bf16[4,256,384]{2,1,0:T(8,128)(2,1)S(1)}, u32[]{:S(2)}, u32[]{:S(2)}) collective-permute-start(bf16[4,256,384]{2,1,0:T(8,128)(2,1)S(1)} %get-tuple-element.121), channel_id=1, source_target_pairs={{0,8},{1,33},{2,10},{3,35},{4,12},{5,37},{6,14},{7,39},{8,16},{9,4... | collective-permute-start | bytes 2359304 | tf_op jit(solution)/shard_map/ppermute | solution.py:434
  68.7 7.4 %collective-permute-start.23 = (bf16[2,256,384]{2,1,0:T(8,128)(2,1)S(1)}, bf16[2,256,384]{2,1,0:T(8,128)(2,1)S(1)}, u32[]{:S(2)}, u32[]{:S(2)}) collective-permute-start(bf16[2,256,384]{2,1,0:T(8,128)(2,1)S(1)} %get-tuple-element.120), channel_id=1, source_target_pairs={{0,24},{1,97},{2,26},{3,99},{4,28},{5,101},{6,30},{7,103},{8,0},{9... | collective-permute-start | bytes 1179656 | tf_op jit(solution)/shard_map/ppermute | solution.py:434
  74.4 6.9 %collective-permute-start.20 = (bf16[256,384]{1,0:T(8,128)(2,1)S(1)}, bf16[256,384]{1,0:T(8,128)(2,1)S(1)}, u32[]{:S(2)}, u32[]{:S(2)}) collective-permute-start(bf16[256,384]{1,0:T(8,128)(2,1)S(1)} %get-tuple-element.115), channel_id=1, source_target_pairs={{0,96},{1,25},{2,98},{3,27},{4,100},{5,29},{6,102},{7,31},{8,104},... | collective-permute-start | bytes 589832 | tf_op jit(solution)/shard_map/ppermute | solution.py:437
  74.5 10.3 %collective-permute-start.21 = (bf16[256,384]{1,0:T(8,128)(2,1)S(1)}, bf16[256,384]{1,0:T(8,128)(2,1)S(1)}, u32[]{:S(2)}, u32[]{:S(2)}) collective-permute-start(bf16[256,384]{1,0:T(8,128)(2,1)S(1)} %get-tuple-element.116), channel_id=1, source_target_pairs={{0,32},{1,9},{2,34},{3,11},{4,36},{5,13},{6,38},{7,15},{8,40},{9,1... | collective-permute-start | bytes 589832 | tf_op jit(solution)/shard_map/ppermute | solution.py:437
  75.9 9.0 %collective-permute-start.22 = (bf16[256,384]{1,0:T(8,128)(2,1)S(1)}, bf16[256,384]{1,0:T(8,128)(2,1)S(1)}, u32[]{:S(2)}, u32[]{:S(2)}) collective-permute-start(bf16[256,384]{1,0:T(8,128)(2,1)S(1)} %get-tuple-element.117), channel_id=1, source_target_pairs={{0,64},{1,17},{2,66},{3,19},{4,68},{5,21},{6,70},{7,23},{8,72},{9,... | collective-permute-start | bytes 589832 | tf_op jit(solution)/shard_map/ppermute | solution.py:437
  85.3 6.1 %collective-permute-start.25 = (bf16[3,64,384]{2,1,0:T(8,128)(2,1)S(1)}, bf16[3,64,384]{2,1,0:T(8,128)(2,1)S(1)}, u32[]{:S(2)}, u32[]{:S(2)}) collective-permute-start(bf16[3,64,384]{2,1,0:T(8,128)(2,1)S(1)} %get-tuple-element.128), channel_id=1, source_target_pairs={{0,6},{1,7},{2,0},{3,1},{4,2},{5,3},{6,4},{7,5},{8,14},{9,15},{10,... | collective-permute-start | bytes 442376 | tf_op jit(solution)/shard_map/ppermute | solution.py:490
  88.3 6.8 %collective-permute-start.26 = (bf16[3,64,384]{2,1,0:T(8,128)(2,1)S(1)}, bf16[3,64,384]{2,1,0:T(8,128)(2,1)S(1)}, u32[]{:S(2)}, u32[]{:S(2)}) collective-permute-start(bf16[3,64,384]{2,1,0:T(8,128)(2,1)S(1)} %get-tuple-element.129), channel_id=1, source_target_pairs={{0,2},{1,3},{2,4},{3,5},{4,6},{5,7},{6,0},{7,1},{8,10},{9,11},{10,... | collective-permute-start | bytes 442376 | tf_op jit(solution)/shard_map/ppermute | solution.py:490
  88.3 6.8 %collective-permute-start.27 = (bf16[3,64,384]{2,1,0:T(8,128)(2,1)S(1)}, bf16[3,64,384]{2,1,0:T(8,128)(2,1)S(1)}, u32[]{:S(2)}, u32[]{:S(2)}) collective-permute-start(bf16[3,64,384]{2,1,0:T(8,128)(2,1)S(1)} %get-tuple-element.130), channel_id=1, source_target_pairs={{0,4},{1,5},{2,6},{3,7},{4,0},{5,1},{6,2},{7,3},{8,12},{9,13},{10,... | collective-permute-start | bytes 442376 | tf_op jit(solution)/shard_map/ppermute | solution.py:490
  89.6 10.4 %collective-permute-start.29 = (bf16[2,256,384]{2,1,0:T(8,128)(2,1)S(1)}, bf16[2,256,384]{2,1,0:T(8,128)(2,1)S(1)}, u32[]{:S(2)}, u32[]{:S(2)}) collective-permute-start(bf16[2,256,384]{2,1,0:T(8,128)(2,1)S(1)} %get-tuple-element.132), channel_id=1, source_target_pairs={{0,24},{1,97},{2,26},{3,99},{4,28},{5,101},{6,30},{7,103},{8,0},{9... | collective-permute-start | bytes 1179656 | tf_op jit(solution)/shard_map/ppermute | solution.py:434
  95.1 6.0 %collective-permute-start.28 = (bf16[4,3,32,384]{3,2,1,0:T(8,128)(2,1)S(1)}, bf16[4,3,32,384]{3,2,1,0:T(8,128)(2,1)S(1)}, u32[]{:S(2)}, u32[]{:S(2)}) collective-permute-start(bf16[4,3,32,384]{3,2,1,0:T(8,128)(2,1)S(1)} %shard_map.121), channel_id=1, source_target_pairs={{0,1},{1,0},{2,3},{3,2},{4,5},{5,4},{6,7},{7,6},{8,9},{9,8},{10,11... | collective-permute-start | bytes 884744 | tf_op jit(solution)/shard_map/ppermute | solution.py:492

commit v9 on v8

--- a/solution.py
+++ b/solution.py
@@ -12,9 +12,9 @@
 SCALE = 1.0 / math.sqrt(HS)
 EXP2_SCALE = SCALE * math.log2(math.e)
 LOW = -1e30
-VMEM_LIMIT = 12 * 1024 * 1024
+VMEM_LIMIT = 6 * 1024 * 1024
 PACK_LIMIT = 56 * 1024 * 1024
-SAVED = (0, 1, 4)
+SAVED = (0, 1, 2, 4)
 AXES = ("z", "y", "x", "c")
 OFFSETS = (0, -1, 1, 2)
 X_STEPS = (0, 1, 3, 2)

time: 102 us -> 102 us (level)
  transfers between devices with their start and end apart: 30 -> 30, of which waited for: 15 -> 14; matrix products, arithmetic and copies ran while one was open for 0% -> 0% of each run, Pallas kernels for 17% -> 17%
where the time goes in v9:
time: 102 us
  starting transfers between devices  41.8 us (41%)
  waiting for transfers between devices  30.4 us (30%)
  Pallas kernels  27.2 us (27%)
  between operations  1.44 us (1%)
    pallas_call x12, Pallas kernels, call(): pl.pallas_call(kernel, out_shape=outs, in_specs=[VMEM] * len(args), out_s...  24.7 us
    ppermute x10, starting transfers between devices, to_key(): return lax.ppermute(value, AXES, key_move(step))  15.3 us
    ppermute x10, waiting for transfers between devices, to_key(): return lax.ppermute(value, AXES, key_move(step))  10.4 us
    ppermute x9, starting transfers between devices, to_query(): return lax.ppermute(value, AXES, query_move(step))  8.89 us
    ppermute x9, waiting for transfers between devices, to_query(): return lax.ppermute(value, AXES, query_move(step))  7.69 us
    ppermute x6, waiting for transfers between devices, exchange(): lax.ppermute(p, AXES, chip_move(d))  7.55 us
    ppermute x6, starting transfers between devices, exchange(): lax.ppermute(p, AXES, chip_move(d))  7.28 us
    ppermute x1, starting transfers between devices, shards(): other = lax.ppermute(other_call(back), AXES, core_move())  4.47 us
  transfers between devices with their start and end apart: 30, of which 14 were waited for; matrix products, arithmetic and copies ran while one was open for 0% of the time, Pallas kernels for 17%

profile of v9, /device:TPU:1, one launch (start us, length us, event | category | flops | bytes accessed | tf_op | source)
XLA Modules:
  0.0 101.9 jit_solution(14417478559453421767)
XLA Ops:
  1.3 2.4 %shard_map.110 = (bf16[2,4,2,32,384]{4,3,2,1,0:T(8,128)(2,1)}, bf16[2,4,2,32,384]{4,3,2,1,0:T(8,128)(2,1)}, bf16[528,384]{1,0:T(8,128)(2,1)}) custom-call(bf16[32,3072]{1,0:T(8,128)(2,1)} %refs_0_.1, bf16[32,3072]{1,0:T(8,128)(2,1)} %refs_1_.1, bf16[32,3072]{1,0:T(8,128)(2,1)} %refs_2_.1, bf16[32,3072]{1,0:T(8,128)(2,1)} %refs_3_.1, ...), custom_call_target="tpu_custom_call" | custom-call | tf_op jit(solution)/shard_map/pallas_call | solution.py:302
  3.7 1.5 %collective-permute-start = (bf16[2,4,2,32,384]{4,3,2,1,0:T(8,128)(2,1)}, bf16[2,4,2,32,384]{4,3,2,1,0:T(8,128)(2,1)S(1)}, u32[]{:S(2)}, u32[]{:S(2)}) collective-permute-start(bf16[2,4,2,32,384]{4,3,2,1,0:T(8,128)(2,1)} %get-tuple-element.74), channel_id=1, source_target_pairs={{0,1},{1,0},{2,3},{3,2},{4,5},{5,4},{6,7},{7,6},{8,9},{9,8},{10,11... | collective-permute-start | bytes 1179656 | tf_op jit(solution)/shard_map/ppermute | solution.py:443
  5.2 3.8 %collective-permute-start.2 = (bf16[528,384]{1,0:T(8,128)(2,1)}, bf16[528,384]{1,0:T(8,128)(2,1)S(1)}, u32[]{:S(2)}, u32[]{:S(2)}) collective-permute-start(bf16[528,384]{1,0:T(8,128)(2,1)} %get-tuple-element.79.refs_1_), channel_id=1, source_target_pairs={{0,24},{1,97},{2,26},{3,99},{4,28},{5,101},{6,30},{7,103},{8,0},{9... | collective-permute-start | bytes 1216520 | tf_op jit(solution)/shard_map/ppermute | solution.py:434
  11.4 1.5 %collective-permute-start.7 = (bf16[2,64,384]{2,1,0:T(8,128)(2,1)S(1)}, bf16[2,64,384]{2,1,0:T(8,128)(2,1)S(1)}, u32[]{:S(2)}, u32[]{:S(2)}) collective-permute-start(bf16[2,64,384]{2,1,0:T(8,128)(2,1)S(1)} %get-tuple-element.86), channel_id=1, source_target_pairs={{0,6},{1,7},{2,0},{3,1},{4,2},{5,3},{6,4},{7,5},{8,14},{9,15},{10,... | collective-permute-start | bytes 294920 | tf_op jit(solution)/shard_map/ppermute | solution.py:450
  12.9 1.5 %collective-permute-start.8 = (bf16[2,64,384]{2,1,0:T(8,128)(2,1)S(1)}, bf16[2,64,384]{2,1,0:T(8,128)(2,1)S(1)}, u32[]{:S(2)}, u32[]{:S(2)}) collective-permute-start(bf16[2,64,384]{2,1,0:T(8,128)(2,1)S(1)} %get-tuple-element.87), channel_id=1, source_target_pairs={{0,4},{1,5},{2,6},{3,7},{4,0},{5,1},{6,2},{7,3},{8,12},{9,13},{10,... | collective-permute-start | bytes 294920 | tf_op jit(solution)/shard_map/ppermute | solution.py:450
  14.4 1.6 %collective-permute-done.6.refs_1_ = bf16[2,64,384]{2,1,0:T(8,128)(2,1)S(1)} collective-permute-done((bf16[2,64,384]{2,1,0:T(8,128)(2,1)S(1)}, bf16[2,64,384]{2,1,0:T(8,128)(2,1)S(1)}, u32[]{:S(2)}, u32[]{:S(2)}) %collective-permute-start.6) | collective-permute-done | bytes 98336 | tf_op jit(solution)/shard_map/ppermute | solution.py:450
  16.3 2.7 %collective-permute-done.8.refs_3_ = bf16[2,64,384]{2,1,0:T(8,128)(2,1)S(1)} collective-permute-done((bf16[2,64,384]{2,1,0:T(8,128)(2,1)S(1)}, bf16[2,64,384]{2,1,0:T(8,128)(2,1)S(1)}, u32[]{:S(2)}, u32[]{:S(2)}) %collective-permute-start.8) | collective-permute-done | bytes 98336 | tf_op jit(solution)/shard_map/ppermute | solution.py:450
  19.0 2.3 %collective-permute-start.11 = (bf16[2,256,384]{2,1,0:T(8,128)(2,1)S(1)}, bf16[2,256,384]{2,1,0:T(8,128)(2,1)S(1)}, u32[]{:S(2)}, u32[]{:S(2)}) collective-permute-start(bf16[2,256,384]{2,1,0:T(8,128)(2,1)S(1)} %shard_map.113.refs_5_.refs_3_.refs_2_.refs_4_), channel_id=1, source_target_pairs={{0,64},{1,17},{2,66},{3,19},{4,68},{5,21},{6,70},{7,23},{8,72},{9,... | collective-permute-start | bytes 1179656 | tf_op jit(solution)/shard_map/ppermute | solution.py:437
  22.3 1.7 %collective-permute-start.4 = (bf16[2,64,384]{2,1,0:T(8,128)(2,1)S(1)}, bf16[2,64,384]{2,1,0:T(8,128)(2,1)S(1)}, u32[]{:S(2)}, u32[]{:S(2)}) collective-permute-start(bf16[2,64,384]{2,1,0:T(8,128)(2,1)S(1)} %get-tuple-element.82), channel_id=1, source_target_pairs={{0,6},{1,7},{2,0},{3,1},{4,2},{5,3},{6,4},{7,5},{8,14},{9,15},{10,... | collective-permute-start | bytes 294920 | tf_op jit(solution)/shard_map/ppermute | solution.py:450
  24.3 2.0 %collective-permute-done.3.refs_1_ = bf16[2,64,384]{2,1,0:T(8,128)(2,1)S(1)} collective-permute-done((bf16[2,64,384]{2,1,0:T(8,128)(2,1)S(1)}, bf16[2,64,384]{2,1,0:T(8,128)(2,1)S(1)}, u32[]{:S(2)}, u32[]{:S(2)}) %collective-permute-start.3) | collective-permute-done | bytes 98336 | tf_op jit(solution)/shard_map/ppermute | solution.py:450
  27.8 1.3 %collective-permute-done.5.refs_3_ = bf16[2,64,384]{2,1,0:T(8,128)(2,1)S(1)} collective-permute-done((bf16[2,64,384]{2,1,0:T(8,128)(2,1)S(1)}, bf16[2,64,384]{2,1,0:T(8,128)(2,1)S(1)}, u32[]{:S(2)}, u32[]{:S(2)}) %collective-permute-start.5) | collective-permute-done | bytes 98336 | tf_op jit(solution)/shard_map/ppermute | solution.py:450
  29.1 1.4 %collective-permute-start.14 = (bf16[2,256,384]{2,1,0:T(8,128)(2,1)S(1)}, bf16[2,256,384]{2,1,0:T(8,128)(2,1)S(1)}, u32[]{:S(2)}, u32[]{:S(2)}) collective-permute-start(bf16[2,256,384]{2,1,0:T(8,128)(2,1)S(1)} %shard_map.112.refs_0_), channel_id=1, source_target_pairs={{0,16},{1,65},{2,18},{3,67},{4,20},{5,69},{6,22},{7,71},{8,24},{9,... | collective-permute-start | bytes 1179656 | tf_op jit(solution)/shard_map/ppermute | solution.py:434
  30.5 3.0 %collective-permute-start.13 = (bf16[2,256,384]{2,1,0:T(8,128)(2,1)S(1)}, bf16[2,256,384]{2,1,0:T(8,128)(2,1)S(1)}, u32[]{:S(2)}, u32[]{:S(2)}) collective-permute-start(bf16[2,256,384]{2,1,0:T(8,128)(2,1)S(1)} %shard_map.112.refs_0_), channel_id=1, source_target_pairs={{0,24},{1,97},{2,26},{3,99},{4,28},{5,101},{6,30},{7,103},{8,0},{9... | collective-permute-start | bytes 1179656 | tf_op jit(solution)/shard_map/ppermute | solution.py:434
  34.1 3.4 %shard_map.114 = (f32[3,16,256]{2,1,0:T(8,128)S(1)}, f32[3,256,512]{2,1,0:T(8,128)S(1)}, f32[3,256,512]{2,1,0:T(8,128)S(1)}, f32[3,256,512]{2,1,0:T(8,128)S(1)},...) custom-call(bf16[2,256,384]{2,1,0:T(8,128)(2,1)S(1)} %shard_map.112., ...), custom_call_target="tpu_custom_call" | custom-call | flops 31457280 | bytes 43776 | tf_op jit(solution)/shard_map/pallas_call | solution.py:36
  37.5 3.4 %shard_map.115 = (f32[3,16,256]{2,1,0:T(8,128)S(1)}, f32[3,256,512]{2,1,0:T(8,128)S(1)}, f32[3,256,512]{2,1,0:T(8,128)S(1)}, f32[3,256,512]{2,1,0:T(8,128)S(1)},...) custom-call(bf16[2,256,384]{2,1,0:T(8,128)(2,1)S(1)} %shard_map.112., ...), custom_call_target="tpu_custom_call" | custom-call | flops 31457280 | bytes 44544 | tf_op jit(solution)/shard_map/pallas_call | solution.py:36
  41.0 4.7 %collective-permute-done.13.refs_1_ = bf16[2,256,384]{2,1,0:T(8,128)(2,1)S(1)} collective-permute-done((bf16[2,256,384]{2,1,0:T(8,128)(2,1)S(1)}, bf16[2,256,384]{2,1,0:T(8,128)(2,1)S(1)}, u32[]{:S(2)}, u32[]{:S(2)}) %collective-permute-start.13) | collective-permute-done | bytes 393248 | tf_op jit(solution)/shard_map/ppermute | solution.py:434
  45.8 3.4 %shard_map.116 = (f32[3,16,256]{2,1,0:T(8,128)S(1)}, f32[3,256,1024]{2,1,0:T(8,128)S(1)}, f32[3,256,1024]{2,1,0:T(8,128)S(1)}, f32[3,256,1024]{2,1,0:T(8,128)S(1...) custom-call(bf16[2,256,384]{2,1,0:T(8,128)(2,1)S(1)} %collective-permute-done.12.refs_0_, ...), custom_call_target="tpu_custom_call" | custom-call | flops 37748736 | bytes 43776 | tf_op jit(solution)/shard_map/pallas_call | solution.py:36
  49.2 1.9 %collective-permute-start.18 = (f32[3,16,256]{2,1,0:T(8,128)S(1)}, f32[3,16,256]{2,1,0:T(8,128)S(1)}, u32[]{:S(2)}, u32[]{:S(2)}) collective-permute-start(f32[3,16,256]{2,1,0:T(8,128)S(1)} %get-tuple-element.92.refs_6_.refs_8_), channel_id=1, source_target_pairs={{0,64},{1,17},{2,66},{3,19},{4,68},{5,21},{6,70},{7,23},{8,72},{9,... | collective-permute-start | bytes 147464 | tf_op jit(solution)/shard_map/ppermute | solution.py:437
  51.1 1.7 %collective-permute-start.17 = (f32[3,16,256]{2,1,0:T(8,128)S(1)}, f32[3,16,256]{2,1,0:T(8,128)S(1)}, u32[]{:S(2)}, u32[]{:S(2)}) collective-permute-start(f32[3,16,256]{2,1,0:T(8,128)S(1)} %get-tuple-element.92.refs_6_.refs_8_), channel_id=1, source_target_pairs={{0,96},{1,25},{2,98},{3,27},{4,100},{5,29},{6,102},{7,31},{8,104},... | collective-permute-start | bytes 147464 | tf_op jit(solution)/shard_map/ppermute | solution.py:437
  54.0 3.0 %collective-permute-done.16.refs_7_.refs_9_ = f32[3,16,256]{2,1,0:T(8,128)S(1)} collective-permute-done((f32[3,16,256]{2,1,0:T(8,128)S(1)}, f32[3,16,256]{2,1,0:T(8,128)S(1)}, u32[]{:S(2)}, u32[]{:S(2)}) %collective-permute-start.16) | collective-permute-done | bytes 49184 | tf_op jit(solution)/shard_map/ppermute | solution.py:437
  57.0 3.0 %shard_map.117 = (bf16[4,256,384]{2,1,0:T(8,128)(2,1)S(1)}, f32[3,128,1024]{2,1,0:T(8,128)S(1)}) custom-call(bf16[2,256,384]{2,1,0:T(8,128)(2,1)S(1)} %collective-permute-done.14.refs_2_.refs_0_, bf16[528,384]{1,0:T(8,128)(2,1)S(1)} %collective-permute-done.15.refs_4_.refs_1_, bf16[2,256,384]{2,1,0:T(8,128)(2,1)S(1)} %shard_map.113.refs_5_.refs_3_.refs_2_.refs_4_, ...), custom_call_target="tpu_custom_call" | custom-call | flops 62914560 | bytes 236736 | tf_op jit(solution)/shard_map/pallas_call | solution.py:36
  60.1 1.6 %collective-permute-start.19 = (bf16[4,256,384]{2,1,0:T(8,128)(2,1)S(1)}, bf16[4,256,384]{2,1,0:T(8,128)(2,1)S(1)}, u32[]{:S(2)}, u32[]{:S(2)}) collective-permute-start(bf16[4,256,384]{2,1,0:T(8,128)(2,1)S(1)} %get-tuple-element.121), channel_id=1, source_target_pairs={{0,16},{1,65},{2,18},{3,67},{4,20},{5,69},{6,22},{7,71},{8,24},{9,... | collective-permute-start | bytes 2359304 | tf_op jit(solution)/shard_map/ppermute | solution.py:434
  61.6 6.6 %shard_map.118 = (bf16[2,256,384]{2,1,0:T(8,128)(2,1)S(1)}, bf16[2,256,384]{2,1,0:T(8,128)(2,1)S(1)}, bf16[4,256,384]{2,1,0:T(8,128)(2,1)S(1)}, f32[3,128,1024]{2,1,0:T(8,128)S(1)}) custom-call(bf16[2,256,384]{2,1,0:T(8,128)(2,1)S(1)} %collective-permute-done.12.refs_0_, bf16[2,256,384]{2,1,0:T(8,128)(2,1)S(1)} %collective-permute-done.13.refs_1_, ...), custom_call_target="tpu_custom_call" | custom-call | flops 125829120 | bytes 372096 | tf_op jit(solution)/shard_map/pallas_call | solution.py:36
  68.3 2.7 %collective-permute-start.23 = (bf16[2,256,384]{2,1,0:T(8,128)(2,1)S(1)}, bf16[2,256,384]{2,1,0:T(8,128)(2,1)S(1)}, u32[]{:S(2)}, u32[]{:S(2)}) collective-permute-start(bf16[2,256,384]{2,1,0:T(8,128)(2,1)S(1)} %get-tuple-element.128), channel_id=1, source_target_pairs={{0,24},{1,97},{2,26},{3,99},{4,28},{5,101},{6,30},{7,103},{8,0},{9... | collective-permute-start | bytes 1179656 | tf_op jit(solution)/shard_map/ppermute | solution.py:434
  71.0 3.3 %shard_map.119 = (bf16[2,256,384]{2,1,0:T(8,128)(2,1)S(1)}, bf16[2,256,384]{2,1,0:T(8,128)(2,1)S(1)}, bf16[256,384]{1,0:T(8,128)(2,1)S(1)}, bf16[256,384]{1,0:T(...) custom-call(bf16[2,256,384]{2,1,0:T(8,128)(2,1)S(1)} %shard_map.112.refs_0_, ...), custom_call_target="tpu_custom_call" | custom-call | flops 62914560 | bytes 261312 | tf_op jit(solution)/shard_map/pallas_call | solution.py:36
  74.4 1.5 %collective-permute-start.21 = (bf16[256,384]{1,0:T(8,128)(2,1)S(1)}, bf16[256,384]{1,0:T(8,128)(2,1)S(1)}, u32[]{:S(2)}, u32[]{:S(2)}) collective-permute-start(bf16[256,384]{1,0:T(8,128)(2,1)S(1)} %get-tuple-element.124), channel_id=1, source_target_pairs={{0,32},{1,9},{2,34},{3,11},{4,36},{5,13},{6,38},{7,15},{8,40},{9,1... | collective-permute-start | bytes 589832 | tf_op jit(solution)/shard_map/ppermute | solution.py:437
  75.8 5.5 %collective-permute-done.24.refs_7_.refs_8_ = bf16[4,256,384]{2,1,0:T(8,128)(2,1)S(1)} collective-permute-done((bf16[4,256,384]{2,1,0:T(8,128)(2,1)S(1)}, bf16[4,256,384]{2,1,0:T(8,128)(2,1)S(1)}, u32[]{:S(2)}, u32[]{:S(2)}) %collective-permute-start.24) | collective-permute-done | bytes 786464 | tf_op jit(solution)/shard_map/ppermute | solution.py:434
  81.4 3.3 %collective-permute-done.21.refs_2_ = bf16[256,384]{1,0:T(8,128)(2,1)S(1)} collective-permute-done((bf16[256,384]{1,0:T(8,128)(2,1)S(1)}, bf16[256,384]{1,0:T(8,128)(2,1)S(1)}, u32[]{:S(2)}, u32[]{:S(2)}) %collective-permute-start.21) | collective-permute-done | bytes 196640 | tf_op jit(solution)/shard_map/ppermute | solution.py:437
  85.1 3.1 %collective-permute-start.25 = (bf16[3,64,384]{2,1,0:T(8,128)(2,1)S(1)}, bf16[3,64,384]{2,1,0:T(8,128)(2,1)S(1)}, u32[]{:S(2)}, u32[]{:S(2)}) collective-permute-start(bf16[3,64,384]{2,1,0:T(8,128)(2,1)S(1)} %get-tuple-element.136), channel_id=1, source_target_pairs={{0,6},{1,7},{2,0},{3,1},{4,2},{5,3},{6,4},{7,5},{8,14},{9,15},{10,... | collective-permute-start | bytes 442376 | tf_op jit(solution)/shard_map/ppermute | solution.py:490
  89.5 2.0 %collective-permute-start.29 = (bf16[2,256,384]{2,1,0:T(8,128)(2,1)S(1)}, bf16[2,256,384]{2,1,0:T(8,128)(2,1)S(1)}, u32[]{:S(2)}, u32[]{:S(2)}) collective-permute-start(bf16[2,256,384]{2,1,0:T(8,128)(2,1)S(1)} %get-tuple-element.140), channel_id=1, source_target_pairs={{0,24},{1,97},{2,26},{3,99},{4,28},{5,101},{6,30},{7,103},{8,0},{9... | collective-permute-start | bytes 1179656 | tf_op jit(solution)/shard_map/ppermute | solution.py:434
  91.5 3.5 %collective-permute-done.26.refs_2_ = bf16[3,64,384]{2,1,0:T(8,128)(2,1)S(1)} collective-permute-done((bf16[3,64,384]{2,1,0:T(8,128)(2,1)S(1)}, bf16[3,64,384]{2,1,0:T(8,128)(2,1)S(1)}, u32[]{:S(2)}, u32[]{:S(2)}) %collective-permute-start.26) | collective-permute-done | bytes 147488 | tf_op jit(solution)/shard_map/ppermute | solution.py:490
  95.0 4.5 %collective-permute-start.28 = (bf16[4,3,32,384]{3,2,1,0:T(8,128)(2,1)S(1)}, bf16[4,3,32,384]{3,2,1,0:T(8,128)(2,1)S(1)}, u32[]{:S(2)}, u32[]{:S(2)}) collective-permute-start(bf16[4,3,32,384]{3,2,1,0:T(8,128)(2,1)S(1)} %shard_map.121), channel_id=1, source_target_pairs={{0,1},{1,0},{2,3},{3,2},{4,5},{5,4},{6,7},{7,6},{8,9},{9,8},{10,11... | collective-permute-start | bytes 884744 | tf_op jit(solution)/shard_map/ppermute | solution.py:492
  (45 shorter events, 11.7 us)
Async XLA Ops:
  3.7 30.4 %copy-start = (bf16[528,384]{1,0:T(8,128)(2,1)S(1)}, bf16[528,384]{1,0:T(8,128)(2,1)}, u32[]{:S(2)}) copy-start(bf16[528,384]{1,0:T(8,128)(2,1)} %get-tuple-element.79.refs_1_) | copy-start | bytes 1216516
  3.7 5.3 %collective-permute-start = (bf16[2,4,2,32,384]{4,3,2,1,0:T(8,128)(2,1)}, bf16[2,4,2,32,384]{4,3,2,1,0:T(8,128)(2,1)S(1)}, u32[]{:S(2)}, u32[]{:S(2)}) collective-permute-start(bf16[2,4,2,32,384]{4,3,2,1,0:T(8,128)(2,1)} %get-tuple-element.74), channel_id=1, source_target_pairs={{0,1},{1,0},{2,3},{3,2},{4,5},{5,4},{6,7},{7,6},{8,9},{9,8},{10,11... | collective-permute-start | bytes 1179656 | tf_op jit(solution)/shard_map/ppermute | solution.py:443
  5.2 16.1 %collective-permute-start.2 = (bf16[528,384]{1,0:T(8,128)(2,1)}, bf16[528,384]{1,0:T(8,128)(2,1)S(1)}, u32[]{:S(2)}, u32[]{:S(2)}) collective-permute-start(bf16[528,384]{1,0:T(8,128)(2,1)} %get-tuple-element.79.refs_1_), channel_id=1, source_target_pairs={{0,24},{1,97},{2,26},{3,99},{4,28},{5,101},{6,30},{7,103},{8,0},{9... | collective-permute-start | bytes 1216520 | tf_op jit(solution)/shard_map/ppermute | solution.py:434
  9.1 12.3 %collective-permute-start.1 = (bf16[528,384]{1,0:T(8,128)(2,1)}, bf16[528,384]{1,0:T(8,128)(2,1)S(1)}, u32[]{:S(2)}, u32[]{:S(2)}) collective-permute-start(bf16[528,384]{1,0:T(8,128)(2,1)} %get-tuple-element.79.refs_1_), channel_id=1, source_target_pairs={{0,8},{1,33},{2,10},{3,35},{4,12},{5,37},{6,14},{7,39},{8,16},{9,4... | collective-permute-start | bytes 1216520 | tf_op jit(solution)/shard_map/ppermute | solution.py:434
  9.1 1.0 copy-start.1
  10.2 5.9 %collective-permute-start.6 = (bf16[2,64,384]{2,1,0:T(8,128)(2,1)S(1)}, bf16[2,64,384]{2,1,0:T(8,128)(2,1)S(1)}, u32[]{:S(2)}, u32[]{:S(2)}) collective-permute-start(bf16[2,64,384]{2,1,0:T(8,128)(2,1)S(1)} %get-tuple-element.85), channel_id=1, source_target_pairs={{0,2},{1,3},{2,4},{3,5},{4,6},{5,7},{6,0},{7,1},{8,10},{9,11},{10,... | collective-permute-start | bytes 294920 | tf_op jit(solution)/shard_map/ppermute | solution.py:450
  11.4 4.9 %collective-permute-start.7 = (bf16[2,64,384]{2,1,0:T(8,128)(2,1)S(1)}, bf16[2,64,384]{2,1,0:T(8,128)(2,1)S(1)}, u32[]{:S(2)}, u32[]{:S(2)}) collective-permute-start(bf16[2,64,384]{2,1,0:T(8,128)(2,1)S(1)} %get-tuple-element.86), channel_id=1, source_target_pairs={{0,6},{1,7},{2,0},{3,1},{4,2},{5,3},{6,4},{7,5},{8,14},{9,15},{10,... | collective-permute-start | bytes 294920 | tf_op jit(solution)/shard_map/ppermute | solution.py:450
  12.9 6.1 %collective-permute-start.8 = (bf16[2,64,384]{2,1,0:T(8,128)(2,1)S(1)}, bf16[2,64,384]{2,1,0:T(8,128)(2,1)S(1)}, u32[]{:S(2)}, u32[]{:S(2)}) collective-permute-start(bf16[2,64,384]{2,1,0:T(8,128)(2,1)S(1)} %get-tuple-element.87), channel_id=1, source_target_pairs={{0,4},{1,5},{2,6},{3,7},{4,0},{5,1},{6,2},{7,3},{8,12},{9,13},{10,... | collective-permute-start | bytes 294920 | tf_op jit(solution)/shard_map/ppermute | solution.py:450
  16.0 14.4 %collective-permute-start.15 = (bf16[528,384]{1,0:T(8,128)(2,1)}, bf16[528,384]{1,0:T(8,128)(2,1)S(1)}, u32[]{:S(2)}, u32[]{:S(2)}) collective-permute-start(bf16[528,384]{1,0:T(8,128)(2,1)} %get-tuple-element.79.refs_1_), channel_id=1, source_target_pairs={{0,16},{1,65},{2,18},{3,67},{4,20},{5,69},{6,22},{7,71},{8,24},{9,... | collective-permute-start | bytes 1216520 | tf_op jit(solution)/shard_map/ppermute | solution.py:434
  19.0 14.5 %collective-permute-start.11 = (bf16[2,256,384]{2,1,0:T(8,128)(2,1)S(1)}, bf16[2,256,384]{2,1,0:T(8,128)(2,1)S(1)}, u32[]{:S(2)}, u32[]{:S(2)}) collective-permute-start(bf16[2,256,384]{2,1,0:T(8,128)(2,1)S(1)} %shard_map.113.refs_5_.refs_3_.refs_2_.refs_4_), channel_id=1, source_target_pairs={{0,64},{1,17},{2,66},{3,19},{4,68},{5,21},{6,70},{7,23},{8,72},{9,... | collective-permute-start | bytes 1179656 | tf_op jit(solution)/shard_map/ppermute | solution.py:437
  21.3 5.0 %collective-permute-start.3 = (bf16[2,64,384]{2,1,0:T(8,128)(2,1)S(1)}, bf16[2,64,384]{2,1,0:T(8,128)(2,1)S(1)}, u32[]{:S(2)}, u32[]{:S(2)}) collective-permute-start(bf16[2,64,384]{2,1,0:T(8,128)(2,1)S(1)} %get-tuple-element.81), channel_id=1, source_target_pairs={{0,2},{1,3},{2,4},{3,5},{4,6},{5,7},{6,0},{7,1},{8,10},{9,11},{10,... | collective-permute-start | bytes 294920 | tf_op jit(solution)/shard_map/ppermute | solution.py:450
  22.3 4.8 %collective-permute-start.4 = (bf16[2,64,384]{2,1,0:T(8,128)(2,1)S(1)}, bf16[2,64,384]{2,1,0:T(8,128)(2,1)S(1)}, u32[]{:S(2)}, u32[]{:S(2)}) collective-permute-start(bf16[2,64,384]{2,1,0:T(8,128)(2,1)S(1)} %get-tuple-element.82), channel_id=1, source_target_pairs={{0,6},{1,7},{2,0},{3,1},{4,2},{5,3},{6,4},{7,5},{8,14},{9,15},{10,... | collective-permute-start | bytes 294920 | tf_op jit(solution)/shard_map/ppermute | solution.py:450
  24.0 5.1 %collective-permute-start.5 = (bf16[2,64,384]{2,1,0:T(8,128)(2,1)S(1)}, bf16[2,64,384]{2,1,0:T(8,128)(2,1)S(1)}, u32[]{:S(2)}, u32[]{:S(2)}) collective-permute-start(bf16[2,64,384]{2,1,0:T(8,128)(2,1)S(1)} %get-tuple-element.83), channel_id=1, source_target_pairs={{0,4},{1,5},{2,6},{3,7},{4,0},{5,1},{6,2},{7,3},{8,12},{9,13},{10,... | collective-permute-start | bytes 294920 | tf_op jit(solution)/shard_map/ppermute | solution.py:450
  26.3 11.2 %collective-permute-start.10 = (bf16[2,256,384]{2,1,0:T(8,128)(2,1)S(1)}, bf16[2,256,384]{2,1,0:T(8,128)(2,1)S(1)}, u32[]{:S(2)}, u32[]{:S(2)}) collective-permute-start(bf16[2,256,384]{2,1,0:T(8,128)(2,1)S(1)} %shard_map.113.refs_5_.refs_3_.refs_2_.refs_4_), channel_id=1, source_target_pairs={{0,96},{1,25},{2,98},{3,27},{4,100},{5,29},{6,102},{7,31},{8,104},... | collective-permute-start | bytes 1179656 | tf_op jit(solution)/shard_map/ppermute | solution.py:437
  27.1 10.4 %collective-permute-start.9 = (bf16[2,256,384]{2,1,0:T(8,128)(2,1)S(1)}, bf16[2,256,384]{2,1,0:T(8,128)(2,1)S(1)}, u32[]{:S(2)}, u32[]{:S(2)}) collective-permute-start(bf16[2,256,384]{2,1,0:T(8,128)(2,1)S(1)} %shard_map.113.refs_5_.refs_3_.refs_2_.refs_4_), channel_id=1, source_target_pairs={{0,32},{1,9},{2,34},{3,11},{4,36},{5,13},{6,38},{7,15},{8,40},{9,1... | collective-permute-start | bytes 1179656 | tf_op jit(solution)/shard_map/ppermute | solution.py:437
  29.1 11.9 %collective-permute-start.14 = (bf16[2,256,384]{2,1,0:T(8,128)(2,1)S(1)}, bf16[2,256,384]{2,1,0:T(8,128)(2,1)S(1)}, u32[]{:S(2)}, u32[]{:S(2)}) collective-permute-start(bf16[2,256,384]{2,1,0:T(8,128)(2,1)S(1)} %shard_map.112.refs_0_), channel_id=1, source_target_pairs={{0,16},{1,65},{2,18},{3,67},{4,20},{5,69},{6,22},{7,71},{8,24},{9,... | collective-permute-start | bytes 1179656 | tf_op jit(solution)/shard_map/ppermute | solution.py:434
  30.5 15.2 %collective-permute-start.13 = (bf16[2,256,384]{2,1,0:T(8,128)(2,1)S(1)}, bf16[2,256,384]{2,1,0:T(8,128)(2,1)S(1)}, u32[]{:S(2)}, u32[]{:S(2)}) collective-permute-start(bf16[2,256,384]{2,1,0:T(8,128)(2,1)S(1)} %shard_map.112.refs_0_), channel_id=1, source_target_pairs={{0,24},{1,97},{2,26},{3,99},{4,28},{5,101},{6,30},{7,103},{8,0},{9... | collective-permute-start | bytes 1179656 | tf_op jit(solution)/shard_map/ppermute | solution.py:434
  33.5 12.3 %collective-permute-start.12 = (bf16[2,256,384]{2,1,0:T(8,128)(2,1)S(1)}, bf16[2,256,384]{2,1,0:T(8,128)(2,1)S(1)}, u32[]{:S(2)}, u32[]{:S(2)}) collective-permute-start(bf16[2,256,384]{2,1,0:T(8,128)(2,1)S(1)} %shard_map.112.refs_0_), channel_id=1, source_target_pairs={{0,8},{1,33},{2,10},{3,35},{4,12},{5,37},{6,14},{7,39},{8,16},{9,4... | collective-permute-start | bytes 1179656 | tf_op jit(solution)/shard_map/ppermute | solution.py:434
  49.2 4.5 %collective-permute-start.18 = (f32[3,16,256]{2,1,0:T(8,128)S(1)}, f32[3,16,256]{2,1,0:T(8,128)S(1)}, u32[]{:S(2)}, u32[]{:S(2)}) collective-permute-start(f32[3,16,256]{2,1,0:T(8,128)S(1)} %get-tuple-element.92.refs_6_.refs_8_), channel_id=1, source_target_pairs={{0,64},{1,17},{2,66},{3,19},{4,68},{5,21},{6,70},{7,23},{8,72},{9,... | collective-permute-start | bytes 147464 | tf_op jit(solution)/shard_map/ppermute | solution.py:437
  51.1 2.9 %collective-permute-start.17 = (f32[3,16,256]{2,1,0:T(8,128)S(1)}, f32[3,16,256]{2,1,0:T(8,128)S(1)}, u32[]{:S(2)}, u32[]{:S(2)}) collective-permute-start(f32[3,16,256]{2,1,0:T(8,128)S(1)} %get-tuple-element.92.refs_6_.refs_8_), channel_id=1, source_target_pairs={{0,96},{1,25},{2,98},{3,27},{4,100},{5,29},{6,102},{7,31},{8,104},... | collective-permute-start | bytes 147464 | tf_op jit(solution)/shard_map/ppermute | solution.py:437
  52.8 4.2 %collective-permute-start.16 = (f32[3,16,256]{2,1,0:T(8,128)S(1)}, f32[3,16,256]{2,1,0:T(8,128)S(1)}, u32[]{:S(2)}, u32[]{:S(2)}) collective-permute-start(f32[3,16,256]{2,1,0:T(8,128)S(1)} %get-tuple-element.92.refs_6_.refs_8_), channel_id=1, source_target_pairs={{0,32},{1,9},{2,34},{3,11},{4,36},{5,13},{6,38},{7,15},{8,40},{9,1... | collective-permute-start | bytes 147464 | tf_op jit(solution)/shard_map/ppermute | solution.py:437
  60.1 14.2 %collective-permute-start.19 = (bf16[4,256,384]{2,1,0:T(8,128)(2,1)S(1)}, bf16[4,256,384]{2,1,0:T(8,128)(2,1)S(1)}, u32[]{:S(2)}, u32[]{:S(2)}) collective-permute-start(bf16[4,256,384]{2,1,0:T(8,128)(2,1)S(1)} %get-tuple-element.121), channel_id=1, source_target_pairs={{0,16},{1,65},{2,18},{3,67},{4,20},{5,69},{6,22},{7,71},{8,24},{9,... | collective-permute-start | bytes 2359304 | tf_op jit(solution)/shard_map/ppermute | solution.py:434
  68.2 13.2 %collective-permute-start.24 = (bf16[4,256,384]{2,1,0:T(8,128)(2,1)S(1)}, bf16[4,256,384]{2,1,0:T(8,128)(2,1)S(1)}, u32[]{:S(2)}, u32[]{:S(2)}) collective-permute-start(bf16[4,256,384]{2,1,0:T(8,128)(2,1)S(1)} %get-tuple-element.129), channel_id=1, source_target_pairs={{0,8},{1,33},{2,10},{3,35},{4,12},{5,37},{6,14},{7,39},{8,16},{9,4... | collective-permute-start | bytes 2359304 | tf_op jit(solution)/shard_map/ppermute | solution.py:434
  68.3 7.6 %collective-permute-start.23 = (bf16[2,256,384]{2,1,0:T(8,128)(2,1)S(1)}, bf16[2,256,384]{2,1,0:T(8,128)(2,1)S(1)}, u32[]{:S(2)}, u32[]{:S(2)}) collective-permute-start(bf16[2,256,384]{2,1,0:T(8,128)(2,1)S(1)} %get-tuple-element.128), channel_id=1, source_target_pairs={{0,24},{1,97},{2,26},{3,99},{4,28},{5,101},{6,30},{7,103},{8,0},{9... | collective-permute-start | bytes 1179656 | tf_op jit(solution)/shard_map/ppermute | solution.py:434
  74.3 7.1 %collective-permute-start.20 = (bf16[256,384]{1,0:T(8,128)(2,1)S(1)}, bf16[256,384]{1,0:T(8,128)(2,1)S(1)}, u32[]{:S(2)}, u32[]{:S(2)}) collective-permute-start(bf16[256,384]{1,0:T(8,128)(2,1)S(1)} %get-tuple-element.123), channel_id=1, source_target_pairs={{0,96},{1,25},{2,98},{3,27},{4,100},{5,29},{6,102},{7,31},{8,104},... | collective-permute-start | bytes 589832 | tf_op jit(solution)/shard_map/ppermute | solution.py:437
  74.4 10.3 %collective-permute-start.21 = (bf16[256,384]{1,0:T(8,128)(2,1)S(1)}, bf16[256,384]{1,0:T(8,128)(2,1)S(1)}, u32[]{:S(2)}, u32[]{:S(2)}) collective-permute-start(bf16[256,384]{1,0:T(8,128)(2,1)S(1)} %get-tuple-element.124), channel_id=1, source_target_pairs={{0,32},{1,9},{2,34},{3,11},{4,36},{5,13},{6,38},{7,15},{8,40},{9,1... | collective-permute-start | bytes 589832 | tf_op jit(solution)/shard_map/ppermute | solution.py:437
  75.8 9.0 %collective-permute-start.22 = (bf16[256,384]{1,0:T(8,128)(2,1)S(1)}, bf16[256,384]{1,0:T(8,128)(2,1)S(1)}, u32[]{:S(2)}, u32[]{:S(2)}) collective-permute-start(bf16[256,384]{1,0:T(8,128)(2,1)S(1)} %get-tuple-element.125), channel_id=1, source_target_pairs={{0,64},{1,17},{2,66},{3,19},{4,68},{5,21},{6,70},{7,23},{8,72},{9,... | collective-permute-start | bytes 589832 | tf_op jit(solution)/shard_map/ppermute | solution.py:437
  85.1 6.3 %collective-permute-start.25 = (bf16[3,64,384]{2,1,0:T(8,128)(2,1)S(1)}, bf16[3,64,384]{2,1,0:T(8,128)(2,1)S(1)}, u32[]{:S(2)}, u32[]{:S(2)}) collective-permute-start(bf16[3,64,384]{2,1,0:T(8,128)(2,1)S(1)} %get-tuple-element.136), channel_id=1, source_target_pairs={{0,6},{1,7},{2,0},{3,1},{4,2},{5,3},{6,4},{7,5},{8,14},{9,15},{10,... | collective-permute-start | bytes 442376 | tf_op jit(solution)/shard_map/ppermute | solution.py:490
  88.2 6.8 %collective-permute-start.26 = (bf16[3,64,384]{2,1,0:T(8,128)(2,1)S(1)}, bf16[3,64,384]{2,1,0:T(8,128)(2,1)S(1)}, u32[]{:S(2)}, u32[]{:S(2)}) collective-permute-start(bf16[3,64,384]{2,1,0:T(8,128)(2,1)S(1)} %get-tuple-element.137), channel_id=1, source_target_pairs={{0,2},{1,3},{2,4},{3,5},{4,6},{5,7},{6,0},{7,1},{8,10},{9,11},{10,... | collective-permute-start | bytes 442376 | tf_op jit(solution)/shard_map/ppermute | solution.py:490
  88.2 6.8 %collective-permute-start.27 = (bf16[3,64,384]{2,1,0:T(8,128)(2,1)S(1)}, bf16[3,64,384]{2,1,0:T(8,128)(2,1)S(1)}, u32[]{:S(2)}, u32[]{:S(2)}) collective-permute-start(bf16[3,64,384]{2,1,0:T(8,128)(2,1)S(1)} %get-tuple-element.138), channel_id=1, source_target_pairs={{0,4},{1,5},{2,6},{3,7},{4,0},{5,1},{6,2},{7,3},{8,12},{9,13},{10,... | collective-permute-start | bytes 442376 | tf_op jit(solution)/shard_map/ppermute | solution.py:490
  89.5 10.0 %collective-permute-start.29 = (bf16[2,256,384]{2,1,0:T(8,128)(2,1)S(1)}, bf16[2,256,384]{2,1,0:T(8,128)(2,1)S(1)}, u32[]{:S(2)}, u32[]{:S(2)}) collective-permute-start(bf16[2,256,384]{2,1,0:T(8,128)(2,1)S(1)} %get-tuple-element.140), channel_id=1, source_target_pairs={{0,24},{1,97},{2,26},{3,99},{4,28},{5,101},{6,30},{7,103},{8,0},{9... | collective-permute-start | bytes 1179656 | tf_op jit(solution)/shard_map/ppermute | solution.py:434
  95.0 5.7 %collective-permute-start.28 = (bf16[4,3,32,384]{3,2,1,0:T(8,128)(2,1)S(1)}, bf16[4,3,32,384]{3,2,1,0:T(8,128)(2,1)S(1)}, u32[]{:S(2)}, u32[]{:S(2)}) collective-permute-start(bf16[4,3,32,384]{3,2,1,0:T(8,128)(2,1)S(1)} %shard_map.121), channel_id=1, source_target_pairs={{0,1},{1,0},{2,3},{3,2},{4,5},{5,4},{6,7},{7,6},{8,9},{9,8},{10,11... | collective-permute-start | bytes 884744 | tf_op jit(solution)/shard_map/ppermute | solution.py:492

commit v10 on v9

--- a/solution.py
+++ b/solution.py
@@ -481,7 +481,6 @@
         )
         near_cur, near_p = to_key(near_cur, OFFSETS[1]), to_key(near_p, OFFSETS[2])
         own, sums = grads_call(curs[:1], hists[:1], queries, stats, tiles(0), sums[0], True)
-        sums, far = lax.optimization_barrier((sums, far))
         query_parts = [sums[0]] + [to_query(sums[i], OFFSETS[i]) for i in range(1, 4)]
 
         back = add_call(query_parts, [own[0], far, near_cur, near_p], sizes[2])

time: 102 us -> 108 us (1.059)
  waiting for transfers between devices: 30.4 us -> 36.9 us
    ppermute x9, waiting for transfers between devices: 7.69 us -> 15.7 us  [to_query(): return lax.ppermute(value, AXES, query_move(step))]
    ppermute x10, waiting for transfers between devices: 10.4 us -> 6.87 us  [to_key(): return lax.ppermute(value, AXES, key_move(step))]
    ppermute x10, starting transfers between devices: 15.3 us -> 12 us  [to_key(): return lax.ppermute(value, AXES, key_move(step))]
    ppermute x3, starting transfers between devices: 4.35 us -> 7.53 us  [shards(): lax.ppermute(p, AXES, chip_move(-d))]
    ppermute x3, waiting for transfers between devices: 3.55 us -> 5.52 us  [shards(): lax.ppermute(p, AXES, chip_move(-d))]
  transfers between devices with their start and end apart: 30 -> 30, of which waited for: 14 -> 16; matrix products, arithmetic and copies ran while one was open for 0% -> 0% of each run, Pallas kernels for 17% -> 10%
where the time goes in v10:
time: 108 us
  starting transfers between devices  41.7 us (39%)
  waiting for transfers between devices  36.9 us (34%)
  Pallas kernels  27.1 us (25%)
  between operations  1.41 us (1%)
    pallas_call x12, Pallas kernels, call(): pl.pallas_call(kernel, out_shape=outs, in_specs=[VMEM] * len(args), out_s...  24.7 us
    ppermute x9, waiting for transfers between devices, to_query(): return lax.ppermute(value, AXES, query_move(step))  15.7 us
    ppermute x10, starting transfers between devices, to_key(): return lax.ppermute(value, AXES, key_move(step))  12 us
    ppermute x9, starting transfers between devices, to_query(): return lax.ppermute(value, AXES, query_move(step))  9.42 us
    ppermute x6, waiting for transfers between devices, exchange(): lax.ppermute(p, AXES, chip_move(d))  7.55 us
    ppermute x3, starting transfers between devices, shards(): lax.ppermute(p, AXES, chip_move(-d))  7.53 us
    ppermute x6, starting transfers between devices, exchange(): lax.ppermute(p, AXES, chip_move(d))  7.28 us
    ppermute x10, waiting for transfers between devices, to_key(): return lax.ppermute(value, AXES, key_move(step))  6.87 us
  transfers between devices with their start and end apart: 30, of which 16 were waited for; matrix products, arithmetic and copies ran while one was open for 0% of the time, Pallas kernels for 10%

profile of v10, /device:TPU:1, one launch (start us, length us, event | category | flops | bytes accessed | tf_op | source)
XLA Modules:
  0.0 108.1 jit_solution(15524563335524556422)
XLA Ops:
  1.3 2.4 %shard_map.110 = (bf16[2,4,2,32,384]{4,3,2,1,0:T(8,128)(2,1)}, bf16[2,4,2,32,384]{4,3,2,1,0:T(8,128)(2,1)}, bf16[528,384]{1,0:T(8,128)(2,1)}) custom-call(bf16[32,3072]{1,0:T(8,128)(2,1)} %refs_0_.1, bf16[32,3072]{1,0:T(8,128)(2,1)} %refs_1_.1, bf16[32,3072]{1,0:T(8,128)(2,1)} %refs_2_.1, bf16[32,3072]{1,0:T(8,128)(2,1)} %refs_3_.1, ...), custom_call_target="tpu_custom_call" | custom-call | tf_op jit(solution)/shard_map/pallas_call | solution.py:302
  3.7 1.5 %collective-permute-start = (bf16[2,4,2,32,384]{4,3,2,1,0:T(8,128)(2,1)}, bf16[2,4,2,32,384]{4,3,2,1,0:T(8,128)(2,1)S(1)}, u32[]{:S(2)}, u32[]{:S(2)}) collective-permute-start(bf16[2,4,2,32,384]{4,3,2,1,0:T(8,128)(2,1)} %get-tuple-element.69), channel_id=1, source_target_pairs={{0,1},{1,0},{2,3},{3,2},{4,5},{5,4},{6,7},{7,6},{8,9},{9,8},{10,11... | collective-permute-start | bytes 1179656 | tf_op jit(solution)/shard_map/ppermute | solution.py:443
  5.2 3.8 %collective-permute-start.2 = (bf16[528,384]{1,0:T(8,128)(2,1)}, bf16[528,384]{1,0:T(8,128)(2,1)S(1)}, u32[]{:S(2)}, u32[]{:S(2)}) collective-permute-start(bf16[528,384]{1,0:T(8,128)(2,1)} %get-tuple-element.74.refs_1_), channel_id=1, source_target_pairs={{0,24},{1,97},{2,26},{3,99},{4,28},{5,101},{6,30},{7,103},{8,0},{9... | collective-permute-start | bytes 1216520 | tf_op jit(solution)/shard_map/ppermute | solution.py:434
  11.4 1.5 %collective-permute-start.7 = (bf16[2,64,384]{2,1,0:T(8,128)(2,1)S(1)}, bf16[2,64,384]{2,1,0:T(8,128)(2,1)S(1)}, u32[]{:S(2)}, u32[]{:S(2)}) collective-permute-start(bf16[2,64,384]{2,1,0:T(8,128)(2,1)S(1)} %get-tuple-element.81), channel_id=1, source_target_pairs={{0,6},{1,7},{2,0},{3,1},{4,2},{5,3},{6,4},{7,5},{8,14},{9,15},{10,... | collective-permute-start | bytes 294920 | tf_op jit(solution)/shard_map/ppermute | solution.py:450
  12.9 1.5 %collective-permute-start.8 = (bf16[2,64,384]{2,1,0:T(8,128)(2,1)S(1)}, bf16[2,64,384]{2,1,0:T(8,128)(2,1)S(1)}, u32[]{:S(2)}, u32[]{:S(2)}) collective-permute-start(bf16[2,64,384]{2,1,0:T(8,128)(2,1)S(1)} %get-tuple-element.82), channel_id=1, source_target_pairs={{0,4},{1,5},{2,6},{3,7},{4,0},{5,1},{6,2},{7,3},{8,12},{9,13},{10,... | collective-permute-start | bytes 294920 | tf_op jit(solution)/shard_map/ppermute | solution.py:450
  14.4 1.6 %collective-permute-done.6.refs_1_ = bf16[2,64,384]{2,1,0:T(8,128)(2,1)S(1)} collective-permute-done((bf16[2,64,384]{2,1,0:T(8,128)(2,1)S(1)}, bf16[2,64,384]{2,1,0:T(8,128)(2,1)S(1)}, u32[]{:S(2)}, u32[]{:S(2)}) %collective-permute-start.6) | collective-permute-done | bytes 98336 | tf_op jit(solution)/shard_map/ppermute | solution.py:450
  16.3 2.7 %collective-permute-done.8.refs_3_ = bf16[2,64,384]{2,1,0:T(8,128)(2,1)S(1)} collective-permute-done((bf16[2,64,384]{2,1,0:T(8,128)(2,1)S(1)}, bf16[2,64,384]{2,1,0:T(8,128)(2,1)S(1)}, u32[]{:S(2)}, u32[]{:S(2)}) %collective-permute-start.8) | collective-permute-done | bytes 98336 | tf_op jit(solution)/shard_map/ppermute | solution.py:450
  19.0 2.3 %collective-permute-start.11 = (bf16[2,256,384]{2,1,0:T(8,128)(2,1)S(1)}, bf16[2,256,384]{2,1,0:T(8,128)(2,1)S(1)}, u32[]{:S(2)}, u32[]{:S(2)}) collective-permute-start(bf16[2,256,384]{2,1,0:T(8,128)(2,1)S(1)} %shard_map.113.refs_5_.refs_3_.refs_2_.refs_4_), channel_id=1, source_target_pairs={{0,64},{1,17},{2,66},{3,19},{4,68},{5,21},{6,70},{7,23},{8,72},{9,... | collective-permute-start | bytes 1179656 | tf_op jit(solution)/shard_map/ppermute | solution.py:437
  22.3 1.7 %collective-permute-start.4 = (bf16[2,64,384]{2,1,0:T(8,128)(2,1)S(1)}, bf16[2,64,384]{2,1,0:T(8,128)(2,1)S(1)}, u32[]{:S(2)}, u32[]{:S(2)}) collective-permute-start(bf16[2,64,384]{2,1,0:T(8,128)(2,1)S(1)} %get-tuple-element.77), channel_id=1, source_target_pairs={{0,6},{1,7},{2,0},{3,1},{4,2},{5,3},{6,4},{7,5},{8,14},{9,15},{10,... | collective-permute-start | bytes 294920 | tf_op jit(solution)/shard_map/ppermute | solution.py:450
  24.3 2.0 %collective-permute-done.3.refs_1_ = bf16[2,64,384]{2,1,0:T(8,128)(2,1)S(1)} collective-permute-done((bf16[2,64,384]{2,1,0:T(8,128)(2,1)S(1)}, bf16[2,64,384]{2,1,0:T(8,128)(2,1)S(1)}, u32[]{:S(2)}, u32[]{:S(2)}) %collective-permute-start.3) | collective-permute-done | bytes 98336 | tf_op jit(solution)/shard_map/ppermute | solution.py:450
  29.1 1.4 %collective-permute-start.14 = (bf16[2,256,384]{2,1,0:T(8,128)(2,1)S(1)}, bf16[2,256,384]{2,1,0:T(8,128)(2,1)S(1)}, u32[]{:S(2)}, u32[]{:S(2)}) collective-permute-start(bf16[2,256,384]{2,1,0:T(8,128)(2,1)S(1)} %shard_map.112.refs_0_), channel_id=1, source_target_pairs={{0,16},{1,65},{2,18},{3,67},{4,20},{5,69},{6,22},{7,71},{8,24},{9,... | collective-permute-start | bytes 1179656 | tf_op jit(solution)/shard_map/ppermute | solution.py:434
  30.5 3.0 %collective-permute-start.13 = (bf16[2,256,384]{2,1,0:T(8,128)(2,1)S(1)}, bf16[2,256,384]{2,1,0:T(8,128)(2,1)S(1)}, u32[]{:S(2)}, u32[]{:S(2)}) collective-permute-start(bf16[2,256,384]{2,1,0:T(8,128)(2,1)S(1)} %shard_map.112.refs_0_), channel_id=1, source_target_pairs={{0,24},{1,97},{2,26},{3,99},{4,28},{5,101},{6,30},{7,103},{8,0},{9... | collective-permute-start | bytes 1179656 | tf_op jit(solution)/shard_map/ppermute | solution.py:434
  34.1 3.4 %shard_map.114 = (f32[3,16,256]{2,1,0:T(8,128)S(1)}, f32[3,256,512]{2,1,0:T(8,128)S(1)}, f32[3,256,512]{2,1,0:T(8,128)S(1)}, f32[3,256,512]{2,1,0:T(8,128)S(1)},...) custom-call(bf16[2,256,384]{2,1,0:T(8,128)(2,1)S(1)} %shard_map.112., ...), custom_call_target="tpu_custom_call" | custom-call | flops 31457280 | bytes 43776 | tf_op jit(solution)/shard_map/pallas_call | solution.py:36
  37.5 3.4 %shard_map.115 = (f32[3,16,256]{2,1,0:T(8,128)S(1)}, f32[3,256,512]{2,1,0:T(8,128)S(1)}, f32[3,256,512]{2,1,0:T(8,128)S(1)}, f32[3,256,512]{2,1,0:T(8,128)S(1)},...) custom-call(bf16[2,256,384]{2,1,0:T(8,128)(2,1)S(1)} %shard_map.112., ...), custom_call_target="tpu_custom_call" | custom-call | flops 31457280 | bytes 44544 | tf_op jit(solution)/shard_map/pallas_call | solution.py:36
  41.0 4.7 %collective-permute-done.13.refs_1_ = bf16[2,256,384]{2,1,0:T(8,128)(2,1)S(1)} collective-permute-done((bf16[2,256,384]{2,1,0:T(8,128)(2,1)S(1)}, bf16[2,256,384]{2,1,0:T(8,128)(2,1)S(1)}, u32[]{:S(2)}, u32[]{:S(2)}) %collective-permute-start.13) | collective-permute-done | bytes 393248 | tf_op jit(solution)/shard_map/ppermute | solution.py:434
  45.8 3.4 %shard_map.116 = (f32[3,16,256]{2,1,0:T(8,128)S(1)}, f32[3,256,1024]{2,1,0:T(8,128)S(1)}, f32[3,256,1024]{2,1,0:T(8,128)S(1)}, f32[3,256,1024]{2,1,0:T(8,128)S(1...) custom-call(bf16[2,256,384]{2,1,0:T(8,128)(2,1)S(1)} %collective-permute-done.12.refs_0_, ...), custom_call_target="tpu_custom_call" | custom-call | flops 37748736 | bytes 43776 | tf_op jit(solution)/shard_map/pallas_call | solution.py:36
  49.2 1.9 %collective-permute-start.18 = (f32[3,16,256]{2,1,0:T(8,128)S(1)}, f32[3,16,256]{2,1,0:T(8,128)S(1)}, u32[]{:S(2)}, u32[]{:S(2)}) collective-permute-start(f32[3,16,256]{2,1,0:T(8,128)S(1)} %get-tuple-element.87.refs_6_.refs_8_), channel_id=1, source_target_pairs={{0,64},{1,17},{2,66},{3,19},{4,68},{5,21},{6,70},{7,23},{8,72},{9,... | collective-permute-start | bytes 147464 | tf_op jit(solution)/shard_map/ppermute | solution.py:437
  51.1 1.7 %collective-permute-start.17 = (f32[3,16,256]{2,1,0:T(8,128)S(1)}, f32[3,16,256]{2,1,0:T(8,128)S(1)}, u32[]{:S(2)}, u32[]{:S(2)}) collective-permute-start(f32[3,16,256]{2,1,0:T(8,128)S(1)} %get-tuple-element.87.refs_6_.refs_8_), channel_id=1, source_target_pairs={{0,96},{1,25},{2,98},{3,27},{4,100},{5,29},{6,102},{7,31},{8,104},... | collective-permute-start | bytes 147464 | tf_op jit(solution)/shard_map/ppermute | solution.py:437
  54.0 3.0 %collective-permute-done.16.refs_7_.refs_9_ = f32[3,16,256]{2,1,0:T(8,128)S(1)} collective-permute-done((f32[3,16,256]{2,1,0:T(8,128)S(1)}, f32[3,16,256]{2,1,0:T(8,128)S(1)}, u32[]{:S(2)}, u32[]{:S(2)}) %collective-permute-start.16) | collective-permute-done | bytes 49184 | tf_op jit(solution)/shard_map/ppermute | solution.py:437
  57.0 3.0 %shard_map.117 = (bf16[4,256,384]{2,1,0:T(8,128)(2,1)S(1)}, f32[3,128,1024]{2,1,0:T(8,128)S(1)}) custom-call(bf16[2,256,384]{2,1,0:T(8,128)(2,1)S(1)} %collective-permute-done.14.refs_2_.refs_0_, bf16[528,384]{1,0:T(8,128)(2,1)S(1)} %collective-permute-done.15.refs_4_.refs_1_, bf16[2,256,384]{2,1,0:T(8,128)(2,1)S(1)} %shard_map.113.refs_5_.refs_3_.refs_2_.refs_4_, ...), custom_call_target="tpu_custom_call" | custom-call | flops 62914560 | bytes 236736 | tf_op jit(solution)/shard_map/pallas_call | solution.py:36
  60.0 6.6 %shard_map.118 = (bf16[2,256,384]{2,1,0:T(8,128)(2,1)S(1)}, bf16[2,256,384]{2,1,0:T(8,128)(2,1)S(1)}, bf16[4,256,384]{2,1,0:T(8,128)(2,1)S(1)}, f32[3,128,1024]{2,1,0:T(8,128)S(1)}) custom-call(bf16[2,256,384]{2,1,0:T(8,128)(2,1)S(1)} %collective-permute-done.12.refs_0_, bf16[2,256,384]{2,1,0:T(8,128)(2,1)S(1)} %collective-permute-done.13.refs_1_, ...), custom_call_target="tpu_custom_call" | custom-call | flops 125829120 | bytes 372096 | tf_op jit(solution)/shard_map/pallas_call | solution.py:36
  66.7 1.4 %collective-permute-start.22 = (bf16[4,256,384]{2,1,0:T(8,128)(2,1)S(1)}, bf16[4,256,384]{2,1,0:T(8,128)(2,1)S(1)}, u32[]{:S(2)}, u32[]{:S(2)}) collective-permute-start(bf16[4,256,384]{2,1,0:T(8,128)(2,1)S(1)} %get-tuple-element.117), channel_id=1, source_target_pairs={{0,16},{1,65},{2,18},{3,67},{4,20},{5,69},{6,22},{7,71},{8,24},{9,... | collective-permute-start | bytes 2359304 | tf_op jit(solution)/shard_map/ppermute | solution.py:434
  68.1 3.3 %shard_map.119 = (bf16[2,256,384]{2,1,0:T(8,128)(2,1)S(1)}, bf16[2,256,384]{2,1,0:T(8,128)(2,1)S(1)}, bf16[256,384]{1,0:T(8,128)(2,1)S(1)}, bf16[256,384]{1,0:T(...) custom-call(bf16[2,256,384]{2,1,0:T(8,128)(2,1)S(1)} %shard_map.112.refs_0_, ...), custom_call_target="tpu_custom_call" | custom-call | flops 62914560 | bytes 261312 | tf_op jit(solution)/shard_map/pallas_call | solution.py:36
  72.1 1.4 %collective-permute-start.23 = (bf16[2,256,384]{2,1,0:T(8,128)(2,1)S(1)}, bf16[2,256,384]{2,1,0:T(8,128)(2,1)S(1)}, u32[]{:S(2)}, u32[]{:S(2)}) collective-permute-start(bf16[2,256,384]{2,1,0:T(8,128)(2,1)S(1)} %get-tuple-element.118), channel_id=1, source_target_pairs={{0,24},{1,97},{2,26},{3,99},{4,28},{5,101},{6,30},{7,103},{8,0},{9... | collective-permute-start | bytes 1179656 | tf_op jit(solution)/shard_map/ppermute | solution.py:434
  73.5 1.4 %collective-permute-start.20 = (bf16[256,384]{1,0:T(8,128)(2,1)S(1)}, bf16[256,384]{1,0:T(8,128)(2,1)S(1)}, u32[]{:S(2)}, u32[]{:S(2)}) collective-permute-start(bf16[256,384]{1,0:T(8,128)(2,1)S(1)} %get-tuple-element.114), channel_id=1, source_target_pairs={{0,32},{1,9},{2,34},{3,11},{4,36},{5,13},{6,38},{7,15},{8,40},{9,1... | collective-permute-start | bytes 589832 | tf_op jit(solution)/shard_map/ppermute | solution.py:437
  74.9 3.3 %collective-permute-done.19.refs_1_ = bf16[256,384]{1,0:T(8,128)(2,1)S(1)} collective-permute-done((bf16[256,384]{1,0:T(8,128)(2,1)S(1)}, bf16[256,384]{1,0:T(8,128)(2,1)S(1)}, u32[]{:S(2)}, u32[]{:S(2)}) %collective-permute-start.19) | collective-permute-done | bytes 196640 | tf_op jit(solution)/shard_map/ppermute | solution.py:437
  78.2 3.5 %collective-permute-done.20.refs_2_ = bf16[256,384]{1,0:T(8,128)(2,1)S(1)} collective-permute-done((bf16[256,384]{1,0:T(8,128)(2,1)S(1)}, bf16[256,384]{1,0:T(8,128)(2,1)S(1)}, u32[]{:S(2)}, u32[]{:S(2)}) %collective-permute-start.20) | collective-permute-done | bytes 196640 | tf_op jit(solution)/shard_map/ppermute | solution.py:437
  81.7 4.7 %collective-permute-done.21.refs_3_ = bf16[256,384]{1,0:T(8,128)(2,1)S(1)} collective-permute-done((bf16[256,384]{1,0:T(8,128)(2,1)S(1)}, bf16[256,384]{1,0:T(8,128)(2,1)S(1)}, u32[]{:S(2)}, u32[]{:S(2)}) %collective-permute-start.21) | collective-permute-done | bytes 196640 | tf_op jit(solution)/shard_map/ppermute | solution.py:437
  86.4 2.0 %collective-permute-done.22.refs_5_.refs_7_ = bf16[4,256,384]{2,1,0:T(8,128)(2,1)S(1)} collective-permute-done((bf16[4,256,384]{2,1,0:T(8,128)(2,1)S(1)}, bf16[4,256,384]{2,1,0:T(8,128)(2,1)S(1)}, u32[]{:S(2)}, u32[]{:S(2)}) %collective-permute-start.22) | collective-permute-done | bytes 786464 | tf_op jit(solution)/shard_map/ppermute | solution.py:434
  88.7 6.3 %collective-permute-start.25 = (bf16[3,64,384]{2,1,0:T(8,128)(2,1)S(1)}, bf16[3,64,384]{2,1,0:T(8,128)(2,1)S(1)}, u32[]{:S(2)}, u32[]{:S(2)}) collective-permute-start(bf16[3,64,384]{2,1,0:T(8,128)(2,1)S(1)} %get-tuple-element.126), channel_id=1, source_target_pairs={{0,6},{1,7},{2,0},{3,1},{4,2},{5,3},{6,4},{7,5},{8,14},{9,15},{10,... | collective-permute-start | bytes 442376 | tf_op jit(solution)/shard_map/ppermute | solution.py:489
  97.0 4.7 %collective-permute-done.26.refs_2_ = bf16[3,64,384]{2,1,0:T(8,128)(2,1)S(1)} collective-permute-done((bf16[3,64,384]{2,1,0:T(8,128)(2,1)S(1)}, bf16[3,64,384]{2,1,0:T(8,128)(2,1)S(1)}, u32[]{:S(2)}, u32[]{:S(2)}) %collective-permute-start.26) | collective-permute-done | bytes 147488 | tf_op jit(solution)/shard_map/ppermute | solution.py:489
  101.8 4.0 %collective-permute-start.28 = (bf16[4,3,32,384]{3,2,1,0:T(8,128)(2,1)S(1)}, bf16[4,3,32,384]{3,2,1,0:T(8,128)(2,1)S(1)}, u32[]{:S(2)}, u32[]{:S(2)}) collective-permute-start(bf16[4,3,32,384]{3,2,1,0:T(8,128)(2,1)S(1)} %shard_map.121), channel_id=1, source_target_pairs={{0,1},{1,0},{2,3},{3,2},{4,5},{5,4},{6,7},{7,6},{8,9},{9,8},{10,11... | collective-permute-start | bytes 884744 | tf_op jit(solution)/shard_map/ppermute | solution.py:491
  (45 shorter events, 14.4 us)
Async XLA Ops:
  3.7 30.4 %copy-start = (bf16[528,384]{1,0:T(8,128)(2,1)S(1)}, bf16[528,384]{1,0:T(8,128)(2,1)}, u32[]{:S(2)}) copy-start(bf16[528,384]{1,0:T(8,128)(2,1)} %get-tuple-element.74.refs_1_) | copy-start | bytes 1216516
  3.7 5.3 %collective-permute-start = (bf16[2,4,2,32,384]{4,3,2,1,0:T(8,128)(2,1)}, bf16[2,4,2,32,384]{4,3,2,1,0:T(8,128)(2,1)S(1)}, u32[]{:S(2)}, u32[]{:S(2)}) collective-permute-start(bf16[2,4,2,32,384]{4,3,2,1,0:T(8,128)(2,1)} %get-tuple-element.69), channel_id=1, source_target_pairs={{0,1},{1,0},{2,3},{3,2},{4,5},{5,4},{6,7},{7,6},{8,9},{9,8},{10,11... | collective-permute-start | bytes 1179656 | tf_op jit(solution)/shard_map/ppermute | solution.py:443
  5.2 16.1 %collective-permute-start.2 = (bf16[528,384]{1,0:T(8,128)(2,1)}, bf16[528,384]{1,0:T(8,128)(2,1)S(1)}, u32[]{:S(2)}, u32[]{:S(2)}) collective-permute-start(bf16[528,384]{1,0:T(8,128)(2,1)} %get-tuple-element.74.refs_1_), channel_id=1, source_target_pairs={{0,24},{1,97},{2,26},{3,99},{4,28},{5,101},{6,30},{7,103},{8,0},{9... | collective-permute-start | bytes 1216520 | tf_op jit(solution)/shard_map/ppermute | solution.py:434
  9.1 12.3 %collective-permute-start.1 = (bf16[528,384]{1,0:T(8,128)(2,1)}, bf16[528,384]{1,0:T(8,128)(2,1)S(1)}, u32[]{:S(2)}, u32[]{:S(2)}) collective-permute-start(bf16[528,384]{1,0:T(8,128)(2,1)} %get-tuple-element.74.refs_1_), channel_id=1, source_target_pairs={{0,8},{1,33},{2,10},{3,35},{4,12},{5,37},{6,14},{7,39},{8,16},{9,4... | collective-permute-start | bytes 1216520 | tf_op jit(solution)/shard_map/ppermute | solution.py:434
  9.1 1.0 copy-start.1
  10.2 5.9 %collective-permute-start.6 = (bf16[2,64,384]{2,1,0:T(8,128)(2,1)S(1)}, bf16[2,64,384]{2,1,0:T(8,128)(2,1)S(1)}, u32[]{:S(2)}, u32[]{:S(2)}) collective-permute-start(bf16[2,64,384]{2,1,0:T(8,128)(2,1)S(1)} %get-tuple-element.80), channel_id=1, source_target_pairs={{0,2},{1,3},{2,4},{3,5},{4,6},{5,7},{6,0},{7,1},{8,10},{9,11},{10,... | collective-permute-start | bytes 294920 | tf_op jit(solution)/shard_map/ppermute | solution.py:450
  11.4 4.9 %collective-permute-start.7 = (bf16[2,64,384]{2,1,0:T(8,128)(2,1)S(1)}, bf16[2,64,384]{2,1,0:T(8,128)(2,1)S(1)}, u32[]{:S(2)}, u32[]{:S(2)}) collective-permute-start(bf16[2,64,384]{2,1,0:T(8,128)(2,1)S(1)} %get-tuple-element.81), channel_id=1, source_target_pairs={{0,6},{1,7},{2,0},{3,1},{4,2},{5,3},{6,4},{7,5},{8,14},{9,15},{10,... | collective-permute-start | bytes 294920 | tf_op jit(solution)/shard_map/ppermute | solution.py:450
  12.9 6.1 %collective-permute-start.8 = (bf16[2,64,384]{2,1,0:T(8,128)(2,1)S(1)}, bf16[2,64,384]{2,1,0:T(8,128)(2,1)S(1)}, u32[]{:S(2)}, u32[]{:S(2)}) collective-permute-start(bf16[2,64,384]{2,1,0:T(8,128)(2,1)S(1)} %get-tuple-element.82), channel_id=1, source_target_pairs={{0,4},{1,5},{2,6},{3,7},{4,0},{5,1},{6,2},{7,3},{8,12},{9,13},{10,... | collective-permute-start | bytes 294920 | tf_op jit(solution)/shard_map/ppermute | solution.py:450
  16.0 14.4 %collective-permute-start.15 = (bf16[528,384]{1,0:T(8,128)(2,1)}, bf16[528,384]{1,0:T(8,128)(2,1)S(1)}, u32[]{:S(2)}, u32[]{:S(2)}) collective-permute-start(bf16[528,384]{1,0:T(8,128)(2,1)} %get-tuple-element.74.refs_1_), channel_id=1, source_target_pairs={{0,16},{1,65},{2,18},{3,67},{4,20},{5,69},{6,22},{7,71},{8,24},{9,... | collective-permute-start | bytes 1216520 | tf_op jit(solution)/shard_map/ppermute | solution.py:434
  19.0 14.5 %collective-permute-start.11 = (bf16[2,256,384]{2,1,0:T(8,128)(2,1)S(1)}, bf16[2,256,384]{2,1,0:T(8,128)(2,1)S(1)}, u32[]{:S(2)}, u32[]{:S(2)}) collective-permute-start(bf16[2,256,384]{2,1,0:T(8,128)(2,1)S(1)} %shard_map.113.refs_5_.refs_3_.refs_2_.refs_4_), channel_id=1, source_target_pairs={{0,64},{1,17},{2,66},{3,19},{4,68},{5,21},{6,70},{7,23},{8,72},{9,... | collective-permute-start | bytes 1179656 | tf_op jit(solution)/shard_map/ppermute | solution.py:437
  21.3 5.0 %collective-permute-start.3 = (bf16[2,64,384]{2,1,0:T(8,128)(2,1)S(1)}, bf16[2,64,384]{2,1,0:T(8,128)(2,1)S(1)}, u32[]{:S(2)}, u32[]{:S(2)}) collective-permute-start(bf16[2,64,384]{2,1,0:T(8,128)(2,1)S(1)} %get-tuple-element.76), channel_id=1, source_target_pairs={{0,2},{1,3},{2,4},{3,5},{4,6},{5,7},{6,0},{7,1},{8,10},{9,11},{10,... | collective-permute-start | bytes 294920 | tf_op jit(solution)/shard_map/ppermute | solution.py:450
  22.3 4.8 %collective-permute-start.4 = (bf16[2,64,384]{2,1,0:T(8,128)(2,1)S(1)}, bf16[2,64,384]{2,1,0:T(8,128)(2,1)S(1)}, u32[]{:S(2)}, u32[]{:S(2)}) collective-permute-start(bf16[2,64,384]{2,1,0:T(8,128)(2,1)S(1)} %get-tuple-element.77), channel_id=1, source_target_pairs={{0,6},{1,7},{2,0},{3,1},{4,2},{5,3},{6,4},{7,5},{8,14},{9,15},{10,... | collective-permute-start | bytes 294920 | tf_op jit(solution)/shard_map/ppermute | solution.py:450
  24.0 5.1 %collective-permute-start.5 = (bf16[2,64,384]{2,1,0:T(8,128)(2,1)S(1)}, bf16[2,64,384]{2,1,0:T(8,128)(2,1)S(1)}, u32[]{:S(2)}, u32[]{:S(2)}) collective-permute-start(bf16[2,64,384]{2,1,0:T(8,128)(2,1)S(1)} %get-tuple-element.78), channel_id=1, source_target_pairs={{0,4},{1,5},{2,6},{3,7},{4,0},{5,1},{6,2},{7,3},{8,12},{9,13},{10,... | collective-permute-start | bytes 294920 | tf_op jit(solution)/shard_map/ppermute | solution.py:450
  26.3 11.2 %collective-permute-start.10 = (bf16[2,256,384]{2,1,0:T(8,128)(2,1)S(1)}, bf16[2,256,384]{2,1,0:T(8,128)(2,1)S(1)}, u32[]{:S(2)}, u32[]{:S(2)}) collective-permute-start(bf16[2,256,384]{2,1,0:T(8,128)(2,1)S(1)} %shard_map.113.refs_5_.refs_3_.refs_2_.refs_4_), channel_id=1, source_target_pairs={{0,96},{1,25},{2,98},{3,27},{4,100},{5,29},{6,102},{7,31},{8,104},... | collective-permute-start | bytes 1179656 | tf_op jit(solution)/shard_map/ppermute | solution.py:437
  27.1 10.4 %collective-permute-start.9 = (bf16[2,256,384]{2,1,0:T(8,128)(2,1)S(1)}, bf16[2,256,384]{2,1,0:T(8,128)(2,1)S(1)}, u32[]{:S(2)}, u32[]{:S(2)}) collective-permute-start(bf16[2,256,384]{2,1,0:T(8,128)(2,1)S(1)} %shard_map.113.refs_5_.refs_3_.refs_2_.refs_4_), channel_id=1, source_target_pairs={{0,32},{1,9},{2,34},{3,11},{4,36},{5,13},{6,38},{7,15},{8,40},{9,1... | collective-permute-start | bytes 1179656 | tf_op jit(solution)/shard_map/ppermute | solution.py:437
  29.1 11.9 %collective-permute-start.14 = (bf16[2,256,384]{2,1,0:T(8,128)(2,1)S(1)}, bf16[2,256,384]{2,1,0:T(8,128)(2,1)S(1)}, u32[]{:S(2)}, u32[]{:S(2)}) collective-permute-start(bf16[2,256,384]{2,1,0:T(8,128)(2,1)S(1)} %shard_map.112.refs_0_), channel_id=1, source_target_pairs={{0,16},{1,65},{2,18},{3,67},{4,20},{5,69},{6,22},{7,71},{8,24},{9,... | collective-permute-start | bytes 1179656 | tf_op jit(solution)/shard_map/ppermute | solution.py:434
  30.5 15.2 %collective-permute-start.13 = (bf16[2,256,384]{2,1,0:T(8,128)(2,1)S(1)}, bf16[2,256,384]{2,1,0:T(8,128)(2,1)S(1)}, u32[]{:S(2)}, u32[]{:S(2)}) collective-permute-start(bf16[2,256,384]{2,1,0:T(8,128)(2,1)S(1)} %shard_map.112.refs_0_), channel_id=1, source_target_pairs={{0,24},{1,97},{2,26},{3,99},{4,28},{5,101},{6,30},{7,103},{8,0},{9... | collective-permute-start | bytes 1179656 | tf_op jit(solution)/shard_map/ppermute | solution.py:434
  33.5 12.3 %collective-permute-start.12 = (bf16[2,256,384]{2,1,0:T(8,128)(2,1)S(1)}, bf16[2,256,384]{2,1,0:T(8,128)(2,1)S(1)}, u32[]{:S(2)}, u32[]{:S(2)}) collective-permute-start(bf16[2,256,384]{2,1,0:T(8,128)(2,1)S(1)} %shard_map.112.refs_0_), channel_id=1, source_target_pairs={{0,8},{1,33},{2,10},{3,35},{4,12},{5,37},{6,14},{7,39},{8,16},{9,4... | collective-permute-start | bytes 1179656 | tf_op jit(solution)/shard_map/ppermute | solution.py:434
  49.2 4.5 %collective-permute-start.18 = (f32[3,16,256]{2,1,0:T(8,128)S(1)}, f32[3,16,256]{2,1,0:T(8,128)S(1)}, u32[]{:S(2)}, u32[]{:S(2)}) collective-permute-start(f32[3,16,256]{2,1,0:T(8,128)S(1)} %get-tuple-element.87.refs_6_.refs_8_), channel_id=1, source_target_pairs={{0,64},{1,17},{2,66},{3,19},{4,68},{5,21},{6,70},{7,23},{8,72},{9,... | collective-permute-start | bytes 147464 | tf_op jit(solution)/shard_map/ppermute | solution.py:437
  51.1 2.9 %collective-permute-start.17 = (f32[3,16,256]{2,1,0:T(8,128)S(1)}, f32[3,16,256]{2,1,0:T(8,128)S(1)}, u32[]{:S(2)}, u32[]{:S(2)}) collective-permute-start(f32[3,16,256]{2,1,0:T(8,128)S(1)} %get-tuple-element.87.refs_6_.refs_8_), channel_id=1, source_target_pairs={{0,96},{1,25},{2,98},{3,27},{4,100},{5,29},{6,102},{7,31},{8,104},... | collective-permute-start | bytes 147464 | tf_op jit(solution)/shard_map/ppermute | solution.py:437
  52.8 4.2 %collective-permute-start.16 = (f32[3,16,256]{2,1,0:T(8,128)S(1)}, f32[3,16,256]{2,1,0:T(8,128)S(1)}, u32[]{:S(2)}, u32[]{:S(2)}) collective-permute-start(f32[3,16,256]{2,1,0:T(8,128)S(1)} %get-tuple-element.87.refs_6_.refs_8_), channel_id=1, source_target_pairs={{0,32},{1,9},{2,34},{3,11},{4,36},{5,13},{6,38},{7,15},{8,40},{9,1... | collective-permute-start | bytes 147464 | tf_op jit(solution)/shard_map/ppermute | solution.py:437
  66.5 19.8 %collective-permute-start.24 = (bf16[4,256,384]{2,1,0:T(8,128)(2,1)S(1)}, bf16[4,256,384]{2,1,0:T(8,128)(2,1)S(1)}, u32[]{:S(2)}, u32[]{:S(2)}) collective-permute-start(bf16[4,256,384]{2,1,0:T(8,128)(2,1)S(1)} %get-tuple-element.119), channel_id=1, source_target_pairs={{0,8},{1,33},{2,10},{3,35},{4,12},{5,37},{6,14},{7,39},{8,16},{9,4... | collective-permute-start | bytes 2359304 | tf_op jit(solution)/shard_map/ppermute | solution.py:434
  66.7 21.6 %collective-permute-start.22 = (bf16[4,256,384]{2,1,0:T(8,128)(2,1)S(1)}, bf16[4,256,384]{2,1,0:T(8,128)(2,1)S(1)}, u32[]{:S(2)}, u32[]{:S(2)}) collective-permute-start(bf16[4,256,384]{2,1,0:T(8,128)(2,1)S(1)} %get-tuple-element.117), channel_id=1, source_target_pairs={{0,16},{1,65},{2,18},{3,67},{4,20},{5,69},{6,22},{7,71},{8,24},{9,... | collective-permute-start | bytes 2359304 | tf_op jit(solution)/shard_map/ppermute | solution.py:434
  71.5 6.7 %collective-permute-start.19 = (bf16[256,384]{1,0:T(8,128)(2,1)S(1)}, bf16[256,384]{1,0:T(8,128)(2,1)S(1)}, u32[]{:S(2)}, u32[]{:S(2)}) collective-permute-start(bf16[256,384]{1,0:T(8,128)(2,1)S(1)} %get-tuple-element.113), channel_id=1, source_target_pairs={{0,96},{1,25},{2,98},{3,27},{4,100},{5,29},{6,102},{7,31},{8,104},... | collective-permute-start | bytes 589832 | tf_op jit(solution)/shard_map/ppermute | solution.py:437
  72.1 14.2 %collective-permute-start.23 = (bf16[2,256,384]{2,1,0:T(8,128)(2,1)S(1)}, bf16[2,256,384]{2,1,0:T(8,128)(2,1)S(1)}, u32[]{:S(2)}, u32[]{:S(2)}) collective-permute-start(bf16[2,256,384]{2,1,0:T(8,128)(2,1)S(1)} %get-tuple-element.118), channel_id=1, source_target_pairs={{0,24},{1,97},{2,26},{3,99},{4,28},{5,101},{6,30},{7,103},{8,0},{9... | collective-permute-start | bytes 1179656 | tf_op jit(solution)/shard_map/ppermute | solution.py:434
  73.5 8.2 %collective-permute-start.20 = (bf16[256,384]{1,0:T(8,128)(2,1)S(1)}, bf16[256,384]{1,0:T(8,128)(2,1)S(1)}, u32[]{:S(2)}, u32[]{:S(2)}) collective-permute-start(bf16[256,384]{1,0:T(8,128)(2,1)S(1)} %get-tuple-element.114), channel_id=1, source_target_pairs={{0,32},{1,9},{2,34},{3,11},{4,36},{5,13},{6,38},{7,15},{8,40},{9,1... | collective-permute-start | bytes 589832 | tf_op jit(solution)/shard_map/ppermute | solution.py:437
  78.2 8.2 %collective-permute-start.21 = (bf16[256,384]{1,0:T(8,128)(2,1)S(1)}, bf16[256,384]{1,0:T(8,128)(2,1)S(1)}, u32[]{:S(2)}, u32[]{:S(2)}) collective-permute-start(bf16[256,384]{1,0:T(8,128)(2,1)S(1)} %get-tuple-element.115), channel_id=1, source_target_pairs={{0,64},{1,17},{2,66},{3,19},{4,68},{5,21},{6,70},{7,23},{8,72},{9,... | collective-permute-start | bytes 589832 | tf_op jit(solution)/shard_map/ppermute | solution.py:437
  88.7 8.4 %collective-permute-start.25 = (bf16[3,64,384]{2,1,0:T(8,128)(2,1)S(1)}, bf16[3,64,384]{2,1,0:T(8,128)(2,1)S(1)}, u32[]{:S(2)}, u32[]{:S(2)}) collective-permute-start(bf16[3,64,384]{2,1,0:T(8,128)(2,1)S(1)} %get-tuple-element.126), channel_id=1, source_target_pairs={{0,6},{1,7},{2,0},{3,1},{4,2},{5,3},{6,4},{7,5},{8,14},{9,15},{10,... | collective-permute-start | bytes 442376 | tf_op jit(solution)/shard_map/ppermute | solution.py:489
  94.9 6.8 %collective-permute-start.26 = (bf16[3,64,384]{2,1,0:T(8,128)(2,1)S(1)}, bf16[3,64,384]{2,1,0:T(8,128)(2,1)S(1)}, u32[]{:S(2)}, u32[]{:S(2)}) collective-permute-start(bf16[3,64,384]{2,1,0:T(8,128)(2,1)S(1)} %get-tuple-element.127), channel_id=1, source_target_pairs={{0,2},{1,3},{2,4},{3,5},{4,6},{5,7},{6,0},{7,1},{8,10},{9,11},{10,... | collective-permute-start | bytes 442376 | tf_op jit(solution)/shard_map/ppermute | solution.py:489
  94.9 6.8 %collective-permute-start.27 = (bf16[3,64,384]{2,1,0:T(8,128)(2,1)S(1)}, bf16[3,64,384]{2,1,0:T(8,128)(2,1)S(1)}, u32[]{:S(2)}, u32[]{:S(2)}) collective-permute-start(bf16[3,64,384]{2,1,0:T(8,128)(2,1)S(1)} %get-tuple-element.128), channel_id=1, source_target_pairs={{0,4},{1,5},{2,6},{3,7},{4,0},{5,1},{6,2},{7,3},{8,12},{9,13},{10,... | collective-permute-start | bytes 442376 | tf_op jit(solution)/shard_map/ppermute | solution.py:489
  96.2 9.5 %collective-permute-start.29 = (bf16[2,256,384]{2,1,0:T(8,128)(2,1)S(1)}, bf16[2,256,384]{2,1,0:T(8,128)(2,1)S(1)}, u32[]{:S(2)}, u32[]{:S(2)}) collective-permute-start(bf16[2,256,384]{2,1,0:T(8,128)(2,1)S(1)} %get-tuple-element.130), channel_id=1, source_target_pairs={{0,24},{1,97},{2,26},{3,99},{4,28},{5,101},{6,30},{7,103},{8,0},{9... | collective-permute-start | bytes 1179656 | tf_op jit(solution)/shard_map/ppermute | solution.py:434
  101.8 5.2 %collective-permute-start.28 = (bf16[4,3,32,384]{3,2,1,0:T(8,128)(2,1)S(1)}, bf16[4,3,32,384]{3,2,1,0:T(8,128)(2,1)S(1)}, u32[]{:S(2)}, u32[]{:S(2)}) collective-permute-start(bf16[4,3,32,384]{3,2,1,0:T(8,128)(2,1)S(1)} %shard_map.121), channel_id=1, source_target_pairs={{0,1},{1,0},{2,3},{3,2},{4,5},{5,4},{6,7},{7,6},{8,9},{9,8},{10,11... | collective-permute-start | bytes 884744 | tf_op jit(solution)/shard_map/ppermute | solution.py:491
